TPU v7x, 32 devices: a whole 2x2x4 slice. The times are simulated.
32 devices in a mesh: dp: 8 (over z, y), expert: 4 (over x, core).
Axes of the slice: x: 2, y: 2, z: 4, core: 2. Of those that a mesh axis runs over, the one named last changes fastest.
Arguments:
- tokens: bfloat16 [128, 6144], P(('dp', 'expert')), may hold values from -6 to 6
- expert_choice_table: int32 [4, 32], P('expert'), may hold values from 0 to 1, as said below
- gate_weight: bfloat16 [6144, 16384], P(None, ('dp', 'expert')), may hold values from -0.078125 to 0.078125
- up_weight: bfloat16 [6144, 16384], P(None, ('dp', 'expert')), may hold values from -0.078125 to 0.078125
- down_weight: bfloat16 [16384, 6144], P(('dp', 'expert')), may hold values from -0.0625 to 0.0625
- adapter_down_shared: bfloat16 [6144, 64], P('dp'), may hold values from -0.078125 to 0.078125
- adapter_gate_factor: bfloat16 [64, 16384], P(None, ('dp', 'expert')), may hold values from -0.75 to 0.75
- router: bfloat16 [6144, 2], replicated, may hold values from -0.078125 to 0.078125
Outputs:
- mixed: bfloat16 [128, 6144], P(('dp', 'expert'))
- grad_a: float32 [6144, 64], P(('dp', 'expert'))
- grad_b: float32 [16384, 64], P(('dp', 'expert'))
Inputs may be any that keep to these rules, and one draw needn't show every extreme that they name: Every row of expert_choice_table names every expert exactly 2 * 8 times.
All inputs are finite; a program needn't handle non-finite values.
Results may differ from a plain program's by a relative error of at most 0.014.
Values may be sent and summed in bfloat16 or wider, within the bound.
No kernel may reach another device: no remote copies, remote signals or barrier semaphores. Data moves between devices by JAX's collectives and lax.ppermute only.
A program may use at most 128 MiB of HBM per device.

v0:
```python
import math

import jax
import jax.numpy as jnp
from jax import lax
from jax.sharding import PartitionSpec as P

adapter_scale = 0.25


def partner(block, axis, apart):
    count = lax.axis_size(axis)
    route = []
    for low in range(count):
        high = low | 1 << apart
        if high != low and high < count:
            route += [(low, high), (high, low)]
    return lax.ppermute(block, axis, route)


def contract_last(left, right):
    return lax.dot_general(
        left, right, (((1,), (1,)), ((), ())), preferred_element_type=jnp.float32
    )


def pairing_order(lower_member, own_part, other_part, mesh_axis):
    first = jnp.where(lower_member, own_part, other_part)
    second = jnp.where(lower_member, other_part, own_part)
    return jnp.concatenate([first, second], axis=mesh_axis)


def shards(
    tokens,
    expert_choice_table,
    gate_weight,
    up_weight,
    down_weight,
    adapter_down_shared,
    adapter_gate_factor,
    router,
):
    tok_rows, column_width = tokens.shape
    n_data = lax.axis_size("dp")
    n_expert = lax.axis_size("expert")
    groups = n_expert // 2
    place_dp = lax.axis_index("dp")
    member = lax.axis_index("expert")
    group = member // 2
    parity = member % 2
    lower_member = parity == 0
    col_rows = n_data * tok_rows
    capacity = col_rows // n_expert
    units = down_weight.shape[0]
    adapter_rank_value = adapter_down_shared.shape[1]
    loss_weight_factor = math.sqrt(groups / (tok_rows * n_data * n_expert))
    column, factor_a = (
        lax.all_gather(tokens, "dp", axis=0, tiled=True),
        lax.all_gather(adapter_down_shared, "dp", axis=0, tiled=True),
    )
    labels = expert_choice_table[0]
    onehot = (labels[:, None] == jnp.arange(groups, dtype=jnp.int32)[None, :]).astype(jnp.int32)
    earlier = jnp.cumsum(onehot, axis=0) - onehot
    ordinal = jnp.sum(earlier * onehot, axis=1)
    target = (2 * labels + ordinal % 2) * capacity + ordinal // 2
    placer = (jnp.arange(col_rows, dtype=jnp.int32)[:, None] == target[None, :]).astype(
        jnp.bfloat16
    )
    packed = jnp.dot(placer, column, preferred_element_type=jnp.float32).astype(jnp.bfloat16)
    arrived = lax.all_to_all(
        packed.reshape(n_expert, capacity, column_width),
        "expert",
        split_axis=0,
        concat_axis=0,
        tiled=True,
    )
    own_rows = arrived.reshape(col_rows, column_width)
    pair_partner = partner((gate_weight, up_weight, down_weight, adapter_gate_factor), "expert", 0)
    gate_cols = pairing_order(lower_member, gate_weight, pair_partner[0], 1)
    up_cols = pairing_order(lower_member, up_weight, pair_partner[1], 1)
    out_rows = pairing_order(lower_member, down_weight, pair_partner[2], 0)
    latent_columns = pairing_order(lower_member, adapter_gate_factor, pair_partner[3], 1)
    adapter_latent = jnp.dot(own_rows, factor_a, preferred_element_type=jnp.float32).astype(
        jnp.bfloat16
    )
    pre = jnp.dot(
        own_rows, gate_cols, preferred_element_type=jnp.float32
    ) + adapter_scale * jnp.dot(adapter_latent, latent_columns, preferred_element_type=jnp.float32)
    lifted = jnp.dot(own_rows, up_cols, preferred_element_type=jnp.float32)
    hidden = (jax.nn.silu(pre) * lifted).astype(jnp.bfloat16)
    partial_out = jnp.dot(hidden, out_rows, preferred_element_type=jnp.float32)
    picker = (jnp.arange(groups, dtype=jnp.int32) == group).astype(jnp.float32)
    summed = lax.psum(partial_out.astype(jnp.bfloat16), "dp").astype(jnp.float32)
    logits = jnp.dot(own_rows, router, preferred_element_type=jnp.float32)
    gate = jax.nn.sigmoid(jnp.sum(logits * picker[None, :], axis=1))
    mixed_rows = (gate[:, None] * summed).astype(jnp.bfloat16)
    back_rows = (
        loss_weight_factor
        * gate[:, None]
        * (mixed_rows.astype(jnp.float32) - own_rows.astype(jnp.float32))
    ).astype(jnp.bfloat16)
    back_hidden = contract_last(back_rows, out_rows)
    sig = jax.nn.sigmoid(pre)
    back_pre = (back_hidden * lifted * (sig * (1.0 + pre * (1.0 - sig)))).astype(jnp.bfloat16)
    back_low = adapter_scale * contract_last(back_pre, latent_columns)
    grad_a_part = lax.dot_general(
        own_rows.astype(jnp.float32),
        back_low,
        (((0,), (0,)), ((), ())),
        precision=lax.Precision.HIGHEST,
    )
    grad_b_part = adapter_scale * lax.dot_general(
        back_pre, adapter_latent, (((0,), (0,)), ((), ())), preferred_element_type=jnp.float32
    )
    blocks = grad_b_part.reshape(2, units, adapter_rank_value)
    own_block = lax.dynamic_index_in_dim(blocks, parity, 0, keepdims=False)
    other_block = lax.dynamic_index_in_dim(blocks, 1 - parity, 0, keepdims=False)
    grad_b = own_block + partner(other_block.astype(jnp.bfloat16), "expert", 0).astype(
        other_block.dtype
    )
    returned = lax.all_to_all(
        mixed_rows.reshape(n_expert, capacity, column_width),
        "expert",
        split_axis=0,
        concat_axis=0,
        tiled=True,
    )
    unpacked = returned.reshape(col_rows, column_width)
    own_target = lax.dynamic_slice_in_dim(target, place_dp * tok_rows, tok_rows, 0)
    chooser = (own_target[:, None] == jnp.arange(col_rows, dtype=jnp.int32)[None, :]).astype(
        jnp.bfloat16
    )
    result = jnp.dot(chooser, unpacked, preferred_element_type=jnp.float32).astype(jnp.bfloat16)
    whole_a = lax.psum(grad_a_part, ("dp", "expert"))
    place = place_dp * n_expert + member
    share_a = whole_a.shape[0] // (n_data * n_expert)
    grad_a = lax.dynamic_slice_in_dim(whole_a, place * share_a, share_a, 0)
    return (result, grad_a, grad_b)


def solution(mesh):
    return jax.shard_map(
        shards,
        mesh=mesh,
        in_specs=(
            P(("dp", "expert"), None),
            P("expert", None),
            P(None, ("dp", "expert")),
            P(None, ("dp", "expert")),
            P(("dp", "expert"), None),
            P("dp", None),
            P(None, ("dp", "expert")),
            P(),
        ),
        out_specs=(P(("dp", "expert"), None), P(("dp", "expert"), None), P(("dp", "expert"), None)),
        check_vma=False,
    )
```

profile of v0, /device:TPU:0, one launch (start us, length us, event | category | flops | bytes accessed | tf_op | source)
XLA Modules:
  0.0 340.9 jit_solution(11365825241272128652)
XLA Ops:
  7.2 0.5 collective-permute-start
  7.8 0.4 collective-permute-start.3
  8.3 33.0 %all-gather = bf16[8,4,6144]{2,1,0:T(4,128)(2,1)S(1)} all-gather(bf16[1,4,6144]{2,1,0:T(4,128)(2,1)} %bitcast.60), channel_id=1, replica_groups=mesh['dp'=8,'expert'=4] {'dp'}, dimensions={0}, use_global_device_ids=true | all-gather | bytes 442368 | tf_op jit(solution)/shard_map/all_gather | solution.py:58
  41.4 0.7 fusion.31
  42.2 0.8 select_reduce_fusion
  43.0 0.7 add_bitcast_fusion
  43.7 1.0 fusion.11
  44.7 3.5 %all-to-all-start = ((bf16[4,8,6144]{2,1,0:T(8,128)(2,1)}), bf16[4,8,6144]{2,1,0:T(8,128)(2,1)S(1)}, u32[]{:S(2)}, u32[]{:S(2)}) async-start(bf16[4,8,6144]{2,1,0:T(8,128)(2,1)} %fusion.11), calls=%async_computation | async-start | bytes 786432 | tf_op jit(solution)/shard_map/all_to_all | solution.py:70
  48.2 32.4 %all_gather.7 = bf16[6144,64]{0,1:T(8,128)(2,1)S(1)} all-gather(bf16[768,64]{0,1:T(8,128)(2,1)} %param.13), channel_id=1, replica_groups=mesh['dp'=8,'expert'=4] {'dp'}, dimensions={0}, use_global_device_ids=true | all-gather | bytes 884736 | tf_op jit(solution)/shard_map/all_gather | solution.py:59
  80.6 0.7 multiply_add_fusion
  81.3 0.9 broadcast_select_fusion.7
  82.2 0.3 convolution_convert_fusion.2
  82.7 9.1 %broadcast_select_fusion.5 = (bf16[6144,512]{1,0:T(8,128)(2,1)S(1)}, bf16[6144,512]{1,0:T(8,128)(2,1)}) fusion(bf16[6144,512]{1,0:T(8,128)(2,1)} %param.10, bf16[6144,512]{1,0:T(8,128)(2,1)} %collective-permute-done, pred[]{:T(512)S(6)} %eq.70), kind=kLoop, calls=%fused_computation.20 | loop fusion | flops 6291456 | bytes 25165824 | tf_op jit(solution)/shard_map/jit(_where)/select_n | solution.py:28
  91.8 7.5 %broadcast_select_fusion.3 = (bf16[6144,512]{1,0:T(8,128)(2,1)}, bf16[6144,512]{1,0:T(8,128)(2,1)}) fusion(bf16[6144,512]{1,0:T(8,128)(2,1)S(1)} %bitcast.56, bf16[6144,512]{1,0:T(8,128)(2,1)} %collective-permute-done.2, pred[]{:T(512)S(6)} %eq.70), kind=kLoop, calls=%fused_computation.18 | loop fusion | flops 6291456 | bytes 25165824 | tf_op jit(solution)/shard_map/jit(_where)/select_n | solution.py:28
  99.4 3.8 %broadcast_select_fusion.1 = (bf16[512,6144]{1,0:T(8,128)(2,1)S(1)}, bf16[512,6144]{1,0:T(8,128)(2,1)S(1)}) fusion(bf16[512,6144]{1,0:T(8,128)(2,1)S(1)} %bitcast.58, bf16[512,6144]{1,0:T(8,128)(2,1)} %collective-permute-done.3, pred[]{:T(512)S(6)} %eq.70), kind=kLoop, calls=%fused_computation.16 | loop fusion | flops 6291456 | bytes 25165824 | tf_op jit(solution)/shard_map/jit(_where)/select_n | solution.py:28
  103.3 10.2 %fusion.4 = f32[32,1024]{1,0:T(8,128)S(1)} fusion(bf16[6144,512]{1,0:T(8,128)(2,1)} %get-tuple-element.8, bf16[6144,512]{1,0:T(8,128)(2,1)} %get-tuple-element.7, bf16[4,8,6144]{2,1,0:T(8,128)(2,1)S(1)} %all-to-all-done), kind=kOutput, calls=%fused_computation.4 | convolution fusion | flops 427819008 | bytes 13107200 | tf_op jit(solution)/shard_map/dot_general | solution.py:89
  113.4 0.6 copy-done.3
  114.1 2.2 fusion.13
  116.2 3.1 fusion.10
  119.8 72.2 %all-reduce.3.cloned.1.call-done = bf16[32,6144]{1,0:T(8,128)(2,1)} async-done(((bf16[32,6144]{1,0:T(8,128)(2,1)}), bf16[32,6144]{1,0:T(8,128)(2,1)}) %all-reduce.3.cloned.1.call-update) | async-done | bytes 393232 | tf_op jit(solution)/shard_map/psum | solution.py:93
  192.0 7.1 %fusion.17 = bf16[32,1024]{1,0:T(8,128)(2,1)S(1)} fusion(f32[32,1024]{1,0:T(8,128)S(1)} %fusion.4, bf16[512,6144]{1,0:T(8,128)(2,1)} %copy-done.2, bf16[512,6144]{1,0:T(8,128)(2,1)} %copy-done.1, bf16[4,8,6144]{2,1,0:T(8,128)(2,1)S(1)} %all-to-all-done, f32[32]{0:T(128)S(1)} %get-tuple-element.3, bf16[32,6144]{1,0:T(8,128)(2,1)} %all-reduce.3.cloned.1.call-done, ...), kind=kOutput, calls=%fused_computation.26 | convolution fusion | flops 429719552 | bytes 13697280 | tf_op jit(solution)/shard_map/dot_general | solution.py:22
  199.2 2.0 fusion.20
  201.2 0.9 fusion.28
  202.1 0.2 convolution_multiply_fusion
  202.3 3.5 %all-to-all-start.1 = ((bf16[4,8,6144]{2,1,0:T(8,128)(2,1)}), bf16[4,8,6144]{2,1,0:T(8,128)(2,1)S(1)}, u32[]{:S(2)}, u32[]{:S(2)}) async-start(bf16[4,8,6144]{2,1,0:T(8,128)(2,1)} %fusion.28), calls=%async_computation.1 | async-start | bytes 786432 | tf_op jit(solution)/shard_map/all_to_all | solution.py:121
  206.2 0.5 collective-permute-start.4
  206.8 0.8 collective-permute-done.4
  207.6 0.7 bitcast_add_fusion
  208.3 6.0 %all-to-all-done.1 = bf16[4,8,6144]{2,1,0:T(8,128)(2,1)S(1)} async-done(((bf16[4,8,6144]{2,1,0:T(8,128)(2,1)}), bf16[4,8,6144]{2,1,0:T(8,128)(2,1)S(1)}, u32[]{:S(2)}, u32[]{:S(2)}) %all-to-all-start.1) | async-done | bytes 393248 | tf_op jit(solution)/shard_map/all_to_all | solution.py:121
  214.3 0.9 convolution_convert_fusion.1
  215.1 117.3 %all-reduce.5.cloned.1.call-done = f32[6144,64]{0,1:T(8,128)} async-done(((f32[6144,64]{0,1:T(8,128)}), f32[6144,64]{0,1:T(8,128)}) %all-reduce.5.cloned.1.call-update) | async-done | bytes 1572880 | tf_op jit(solution)/shard_map/psum | solution.py:134
  332.4 1.6 constant_dynamic-slice_fusion.1
  (42 shorter events, 1.6 us)
Async XLA Ops:
  7.2 112.4 %copy-start = (bf16[6144,2]{0,1:T(2,128)(2,1)S(1)}, bf16[6144,2]{0,1:T(2,128)(2,1)}, u32[]{:S(2)}) copy-start(bf16[6144,2]{0,1:T(2,128)(2,1)} %param.15) | copy-start | bytes 73732
  7.2 75.5 %collective-permute-start = (bf16[6144,512]{1,0:T(8,128)(2,1)}, bf16[6144,512]{1,0:T(8,128)(2,1)}, u32[]{:S(2)}, u32[]{:S(2)}) collective-permute-start(bf16[6144,512]{1,0:T(8,128)(2,1)} %param.10), channel_id=1, source_target_pairs={{0,1},{1,0},{2,3},{3,2},{4,5},{5,4},{6,7},{7,6},{8,9},{9,8},{10,11... | collective-permute-start | bytes 18874376 | tf_op jit(solution)/shard_map/ppermute | solution.py:18
  7.7 84.1 %collective-permute-start.2 = (bf16[6144,512]{1,0:T(8,128)(2,1)}, bf16[6144,512]{1,0:T(8,128)(2,1)}, u32[]{:S(2)}, u32[]{:S(2)}) collective-permute-start(bf16[6144,512]{1,0:T(8,128)(2,1)} %param.11), channel_id=1, source_target_pairs={{0,1},{1,0},{2,3},{3,2},{4,5},{5,4},{6,7},{7,6},{8,9},{9,8},{10,11... | collective-permute-start | bytes 18874376 | tf_op jit(solution)/shard_map/ppermute | solution.py:18
  7.8 91.6 %collective-permute-start.3 = (bf16[512,6144]{1,0:T(8,128)(2,1)}, bf16[512,6144]{1,0:T(8,128)(2,1)}, u32[]{:S(2)}, u32[]{:S(2)}) collective-permute-start(bf16[512,6144]{1,0:T(8,128)(2,1)} %param.12), channel_id=1, source_target_pairs={{0,1},{1,0},{2,3},{3,2},{4,5},{5,4},{6,7},{7,6},{8,9},{9,8},{10,11... | collective-permute-start | bytes 18874376 | tf_op jit(solution)/shard_map/ppermute | solution.py:18
  8.2 73.1 %collective-permute-start.1 = (bf16[64,512]{1,0:T(8,128)(2,1)}, bf16[64,512]{1,0:T(8,128)(2,1)S(1)}, u32[]{:S(2)}, u32[]{:S(2)}) collective-permute-start(bf16[64,512]{1,0:T(8,128)(2,1)} %param.14), channel_id=1, source_target_pairs={{0,1},{1,0},{2,3},{3,2},{4,5},{5,4},{6,7},{7,6},{8,9},{9,8},{10,11... | collective-permute-start | bytes 196616 | tf_op jit(solution)/shard_map/ppermute | solution.py:18
  44.7 37.5 %all-to-all-start = ((bf16[4,8,6144]{2,1,0:T(8,128)(2,1)}), bf16[4,8,6144]{2,1,0:T(8,128)(2,1)S(1)}, u32[]{:S(2)}, u32[]{:S(2)}) async-start(bf16[4,8,6144]{2,1,0:T(8,128)(2,1)} %fusion.11), calls=%async_computation | async-start | bytes 786432 | tf_op jit(solution)/shard_map/all_to_all | solution.py:70
  48.1 143.8 %all-reduce.3.cloned.1.call-start = ((), (), s32[]{:S(2)}) async-start(), calls=%async_computation.2 | async-start | bytes 786432 | tf_op jit(solution)/shard_map/psum | solution.py:93
  82.5 9.3 %slice-start = ((s8[6291456]{0:T(1024)(128)(4,1)}), s8[4194304]{0:T(1024)(128)(4,1)S(1)}, s32[]{:S(2)}) async-start(s8[6291456]{0:T(1024)(128)(4,1)} %bitcast.55), calls=%async_computation.4 | async-start | bytes 8388608
  82.7 9.1 %slice-start.1 = ((s8[6291456]{0:T(1024)(128)(4,1)}), s8[2097152]{0:T(1024)(128)(4,1)S(1)}, s32[]{:S(2)}) async-start(s8[6291456]{0:T(1024)(128)(4,1)} %bitcast.55), calls=%async_computation.5 | async-start | bytes 4194304
  82.7 16.6 %slice-start.2 = ((s8[6291456]{0:T(1024)(128)(4,1)}), s8[4194304]{0:T(1024)(128)(4,1)S(1)}, s32[]{:S(2)}) async-start(s8[6291456]{0:T(1024)(128)(4,1)} %bitcast.57), calls=%async_computation.6 | async-start | bytes 8388608
  91.8 7.6 %slice-start.3 = ((s8[6291456]{0:T(1024)(128)(4,1)}), s8[2097152]{0:T(1024)(128)(4,1)S(1)}, s32[]{:S(2)}) async-start(s8[6291456]{0:T(1024)(128)(4,1)} %bitcast.57), calls=%async_computation.7 | async-start | bytes 4194304
  103.3 13.0 %copy-start.1 = (bf16[512,6144]{1,0:T(8,128)(2,1)}, bf16[512,6144]{1,0:T(8,128)(2,1)S(1)}, u32[]{:S(2)}) copy-start(bf16[512,6144]{1,0:T(8,128)(2,1)S(1)} %get-tuple-element.9) | copy-start | bytes 18874372
  103.3 13.0 %copy-start.2 = (bf16[512,6144]{1,0:T(8,128)(2,1)}, bf16[512,6144]{1,0:T(8,128)(2,1)S(1)}, u32[]{:S(2)}) copy-start(bf16[512,6144]{1,0:T(8,128)(2,1)S(1)} %get-tuple-element.10) | copy-start | bytes 18874372
  103.3 10.8 %copy-start.3 = (bf16[6144,512]{1,0:T(8,128)(2,1)S(1)}, bf16[6144,512]{1,0:T(8,128)(2,1)}, u32[]{:S(2)}) copy-start(bf16[6144,512]{1,0:T(8,128)(2,1)} %get-tuple-element.6) | copy-start | bytes 18874372
  119.4 213.1 %all-reduce.5.cloned.1.call-start = ((), (), s32[]{:S(2)}) async-start(), calls=%async_computation.3 | async-start | bytes 3145728 | tf_op jit(solution)/shard_map/psum | solution.py:134
  192.0 9.2 %copy-start.4 = (bf16[32,6144]{1,0:T(8,128)(2,1)S(1)}, bf16[32,6144]{1,0:T(8,128)(2,1)}, u32[]{:S(2)}) copy-start(bf16[32,6144]{1,0:T(8,128)(2,1)} %all-reduce.3.cloned.1.call-done) | copy-start | bytes 1179652
  202.3 11.9 %all-to-all-start.1 = ((bf16[4,8,6144]{2,1,0:T(8,128)(2,1)}), bf16[4,8,6144]{2,1,0:T(8,128)(2,1)S(1)}, u32[]{:S(2)}, u32[]{:S(2)}) async-start(bf16[4,8,6144]{2,1,0:T(8,128)(2,1)} %fusion.28), calls=%async_computation.1 | async-start | bytes 786432 | tf_op jit(solution)/shard_map/all_to_all | solution.py:121
  206.2 1.4 collective-permute-start.4
Sparse Core Ops, SparseCore 0:
  119.5 72.4 all-reduce.2
  201.3 131.0 all-reduce.4
where the time goes:
time: 341 us
  waiting for transfers between devices  196 us (57%)
  blocking collectives  65.4 us (19%)
  matrix products  27.4 us (8%)
  other arithmetic  25.9 us (8%)
  between operations  14.3 us (4%)
  starting transfers between devices  8.65 us (3%)
    psum x1, waiting for transfers between devices, shards(): whole_a = lax.psum(grad_a_part, ('dp', 'expert'))  117 us
    psum x1, waiting for transfers between devices, shards(): lax.psum(partial_out.astype(jnp.bfloat16), 'dp').astype(jnp.float32)  72.2 us
    all_gather x1, blocking collectives, shards(): lax.all_gather(tokens, 'dp', axis=0, tiled=True)  33 us
    all_gather x1, blocking collectives, shards(): lax.all_gather(adapter_down_shared, 'dp', axis=0, tiled=True)  32.4 us
    select_n x4, other arithmetic, pairing_order(): first = jnp.where(lower_member, own_part, other_part)  21.3 us
    dot_general x1, matrix products, shards(): lifted = jnp.dot(own_rows, up_cols, preferred_element_type=jnp.float32)  10.2 us
    dot_general x2, matrix products, contract_last(): lax.dot_general(left, right, (((1,), (1,)), ((), ())), preferred_element_...  7.2 us
  transfers between devices with their start and end apart: 9, of which 4 were waited for; matrix products, arithmetic and copies ran while one was open for 7% of the time, Pallas kernels for 0%

commit v1 on v0

v1 whole, which is shorter than its diff:
```python
import math

import jax
import jax.numpy as jnp
from jax import lax
from jax.sharding import Mesh, PartitionSpec as P

adapter_scale = 0.25
bf16, f32 = jnp.bfloat16, jnp.float32


def swap(block, axis):
    return lax.ppermute(block, axis, [(0, 1), (1, 0)])


def exchange(blocks, axis):
    return lax.all_to_all(blocks, axis, 0, 0, tiled=True)


def spread(block, axis):
    count = lax.axis_size(axis)
    return exchange(jnp.broadcast_to(block[None], (count, *block.shape)), axis)


def trade_groups(blocks, axis):
    count = lax.axis_size(axis)
    arrived = [blocks[0]]
    for step in range(1, count):
        route = [(i, (i + step) % count) for i in range(count)]
        arrived.append(lax.ppermute(blocks[step], axis, route))
    return arrived


def dot(left, right):
    return jnp.dot(left, right, preferred_element_type=f32)


def dot_last(left, right):
    return lax.dot_general(left, right, (((1,), (1,)), ((), ())), preferred_element_type=f32)


def dot_first(left, right):
    return lax.dot_general(left, right, (((0,), (0,)), ((), ())), preferred_element_type=f32)


def shards(
    tokens,
    expert_choice_table,
    gate_weight,
    up_weight,
    down_weight,
    adapter_down_shared,
    adapter_gate_factor,
    router,
):
    tok_rows, width = tokens.shape
    n_dp = lax.axis_size("dp")
    groups = lax.axis_size("x")
    place = lax.axis_index("dp")
    group = lax.axis_index("x")
    core = lax.axis_index("core")
    col_rows = n_dp * tok_rows
    capacity = col_rows // groups
    half = groups * capacity
    rank = adapter_down_shared.shape[1]
    depth = adapter_down_shared.shape[0]
    wide = width // n_dp
    share = width // (n_dp * groups * 2)
    loss_factor = math.sqrt(groups / (tok_rows * n_dp * groups * 2))

    column = spread(tokens, "dp").reshape(col_rows, width)
    labels = expert_choice_table[0]
    index = jnp.arange(col_rows, dtype=jnp.int32)
    before = (labels[None, :] == labels[:, None]) & (index[None, :] < index[:, None])
    ordinal = jnp.sum(before.astype(jnp.int32), axis=1)
    ahead = lax.rem(labels - group + groups, groups)
    target = ahead * capacity + ordinal
    placer = (index[:, None] == target[None, :]).astype(bf16)
    packed = dot(placer, column).astype(bf16).reshape(groups, capacity, width)
    own_half = jnp.concatenate(trade_groups(packed, "x"), axis=0)
    rows = jnp.concatenate([own_half, swap(own_half, "core")], axis=0)

    piece = lax.dynamic_slice_in_dim(rows, place * depth, depth, 1)
    low_part = dot(piece, adapter_down_shared)
    low = jnp.sum(spread(low_part, "dp"), axis=0).astype(bf16)

    pre = dot(rows, gate_weight) + adapter_scale * dot(low, adapter_gate_factor)
    lifted = dot(rows, up_weight)
    hidden = (jax.nn.silu(pre) * lifted).astype(bf16)
    partial = dot(hidden, down_weight)

    logits = dot(rows, router)
    picker = (jnp.arange(groups, dtype=jnp.int32) == group).astype(f32)
    gate = jax.nn.sigmoid(jnp.sum(logits * picker[None, :], axis=1))

    summed = (partial[:half] + swap(partial[half:].astype(bf16), "core").astype(f32)).astype(bf16)
    blocks = exchange(summed.reshape(half, n_dp, wide).transpose(1, 0, 2), "dp")
    total = jnp.sum(blocks.astype(f32), axis=0)
    mixed_block = (gate[:half, None] * total).astype(bf16)
    mixed_half = spread(mixed_block, "dp").transpose(1, 0, 2).reshape(half, width)
    mixed = jnp.concatenate([mixed_half, swap(mixed_half, "core")], axis=0)

    back = mixed_half.reshape(groups, capacity, width)
    returned = [back[0]] + [None] * (groups - 1)
    for step in range(1, groups):
        route = [(i, (i - step) % groups) for i in range(groups)]
        returned[step] = lax.ppermute(back[step], "x", route)
    unpacked = jnp.concatenate(returned, axis=0)
    own_target = lax.dynamic_slice_in_dim(target, place * tok_rows, tok_rows, 0)
    chooser = (own_target[:, None] == index[None, :]).astype(bf16)
    result = dot(chooser, unpacked).astype(bf16)

    back_rows = (
        loss_factor * gate[:, None] * (mixed.astype(f32) - rows.astype(f32))
    ).astype(bf16)
    back_hidden = dot_last(back_rows, down_weight)
    sig = jax.nn.sigmoid(pre)
    back_pre = (back_hidden * lifted * (sig * (1.0 + pre * (1.0 - sig)))).astype(bf16)
    back_low = adapter_scale * dot_last(back_pre, adapter_gate_factor)
    grad_b = adapter_scale * dot_first(back_pre, low)

    pieces = []
    for step in range(groups):
        to = lax.rem(group + step, groups)
        at = ((place * groups + to) * 2 + core) * share
        pieces.append(lax.dynamic_slice_in_dim(rows, at, share, 1))
    pieces = trade_groups(pieces, "x")
    gathered = spread(back_low.astype(bf16), ("dp", "x", "core"))
    parts = jnp.sum(
        gathered.reshape(n_dp, groups, 2, 2, half, rank).astype(f32), axis=0
    )
    by_core = jnp.stack([parts[:, 0, 0] + parts[:, 1, 1], parts[:, 0, 1] + parts[:, 1, 0]])
    by_core = jnp.where(core == 0, by_core, by_core[::-1])
    grad_a = jnp.zeros((share, rank), f32)
    for step in range(groups):
        source = lax.rem(group - step + groups, groups)
        low_rows = lax.dynamic_index_in_dim(by_core, source, 1, keepdims=False)
        grad_a = grad_a + lax.dot_general(
            pieces[step].astype(f32),
            low_rows.reshape(2 * half, rank),
            (((0,), (0,)), ((), ())),
            precision=lax.Precision.HIGHEST,
        )
    return (result, grad_a, grad_b)


def solution(mesh):
    n_dp, n_expert = mesh.shape["dp"], mesh.shape["expert"]
    split = Mesh(mesh.devices.reshape(n_dp, n_expert // 2, 2), ("dp", "x", "core"))
    every = ("dp", "x", "core")
    return jax.shard_map(
        shards,
        mesh=split,
        in_specs=(
            P(every, None),
            P(("x", "core"), None),
            P(None, every),
            P(None, every),
            P(every, None),
            P("dp", None),
            P(None, every),
            P(),
        ),
        out_specs=(P(every, None), P(every, None), P(every, None)),
        check_vma=False,
    )
```

time: 341 us -> 111 us (0.33)
  waiting for transfers between devices: 196 us -> 51.6 us
  blocking collectives: 65.4 us -> 0 us
  other arithmetic: 25.9 us -> 3.03 us
  starting transfers between devices: 8.65 us -> 27.6 us
  between operations: 14.3 us -> 0.98 us
  matrix products: 27.4 us -> 20.7 us
  local copies, waits for them, and re-layouts: 2.92 us -> 6.77 us
    psum x2 -> x0, waiting for transfers between devices: 190 us -> none  [the longest x1 117 us: shards(): whole_a = lax.psum(grad_a_part, ('dp', 'expert'))]
    all_gather x2 -> x0, blocking collectives: 65.4 us -> none  [the longest x1 33 us: shards(): lax.all_gather(tokens, 'dp', axis=0, tiled=True)]
    all_to_all x2 -> x5, waiting for transfers between devices: 5.98 us -> 44 us  [exchange(): return lax.all_to_all(blocks, axis, 0, 0, tiled=True)]
    select_n x4 -> x1, other arithmetic: 21.3 us -> 0.01 us  [shards(): by_core = jnp.where(core == 0, by_core, by_core[::-1])]
    all_to_all x2 -> x5, starting transfers between devices: 6.93 us -> 22.4 us  [exchange(): return lax.all_to_all(blocks, axis, 0, 0, tiled=True)]
    ppermute x5 -> x6, waiting for transfers between devices: 0.79 us -> 7.6 us  [the longest x2 4.18 us: trade_groups(): arrived.append(lax.ppermute(blocks[step], axis, route))]
    dot_general x12 -> x13, matrix products: 27.4 us -> 20.7 us  [the longest x8 13.7 us: dot(): return jnp.dot(left, right, preferred_element_type=f32)]
    ppermute x5 -> x6, starting transfers between devices: 1.64 us -> 5.15 us  [the longest x2 3.38 us: trade_groups(): arrived.append(lax.ppermute(blocks[step], axis, route))]
  transfers between devices with their start and end apart: 9 -> 11, of which waited for: 4 -> 8; matrix products, arithmetic and copies ran while one was open for 7% -> 13% of each run, Pallas kernels for 0% -> 0%
where the time goes in v1:
time: 111 us
  waiting for transfers between devices  51.6 us (46%)
  starting transfers between devices  27.6 us (25%)
  matrix products  20.7 us (19%)
  local copies, waits for them, and re-layouts  6.77 us (6%)
  other arithmetic  3.03 us (3%)
    all_to_all x5, waiting for transfers between devices, exchange(): return lax.all_to_all(blocks, axis, 0, 0, tiled=True)  44 us
    all_to_all x5, starting transfers between devices, exchange(): return lax.all_to_all(blocks, axis, 0, 0, tiled=True)  22.4 us
    dot_general x8, matrix products, dot(): return jnp.dot(left, right, preferred_element_type=f32)  13.7 us
    dot_general x2, matrix products, dot_last(): lax.dot_general(left, right, (((1,), (1,)), ((), ())), preferred_element_...  4.98 us
    ppermute x2, waiting for transfers between devices, trade_groups(): arrived.append(lax.ppermute(blocks[step], axis, route))  4.18 us
    ppermute x3, waiting for transfers between devices, swap(): return lax.ppermute(block, axis, [(0, 1), (1, 0)])  3.42 us
    ppermute x2, starting transfers between devices, trade_groups(): arrived.append(lax.ppermute(blocks[step], axis, route))  3.38 us
    broadcast_in_dim x4, local copies, waits for them, and re-layouts, spread(): return exchange(jnp.broadcast_to(block[None], (count, *block.shape)), axis)  2.62 us
  transfers between devices with their start and end apart: 11, of which 8 were waited for; matrix products, arithmetic and copies ran while one was open for 13% of the time, Pallas kernels for 0%

profile of v1, /device:TPU:0, one launch (start us, length us, event | category | flops | bytes accessed | tf_op | source)
XLA Modules:
  0.0 110.7 jit_solution(7862520245130423336)
XLA Ops:
  0.6 1.7 %broadcast_in_dim.8 = bf16[8,4,6144]{2,1,0:T(4,128)(2,1)} broadcast(bf16[4,6144]{1,0:T(4,128)(2,1)} %param.8), dimensions={1,2} | broadcast | bytes 442368 | tf_op jit(solution)/shard_map/broadcast_in_dim | solution.py:22
  2.3 7.3 %all-to-all-start = ((bf16[8,4,6144]{2,1,0:T(4,128)(2,1)}), bf16[8,4,6144]{2,1,0:T(4,128)(2,1)S(1)}, u32[]{:S(2)}, u32[]{:S(2)}) async-start(bf16[8,4,6144]{2,1,0:T(4,128)(2,1)} %broadcast_in_dim.8), calls=%async_computation | async-start | bytes 786432 | tf_op jit(solution)/shard_map/all_to_all | solution.py:17
  9.6 0.9 convert_reduce_fusion.2
  10.5 0.7 fusion.33
  11.2 10.1 %all-to-all-done = bf16[8,4,6144]{2,1,0:T(4,128)(2,1)S(1)} async-done(((bf16[8,4,6144]{2,1,0:T(4,128)(2,1)}), bf16[8,4,6144]{2,1,0:T(4,128)(2,1)S(1)}, u32[]{:S(2)}, u32[]{:S(2)}) %all-to-all-start) | async-done | bytes 393248 | tf_op jit(solution)/shard_map/all_to_all | solution.py:17
  21.7 1.6 %collective-permute-start = (bf16[16,6144]{1,0:T(8,128)(2,1)S(1)}, bf16[16,6144]{1,0:T(8,128)(2,1)S(1)}, u32[]{:S(2)}, u32[]{:S(2)}) collective-permute-start(bf16[16,6144]{1,0:T(8,128)(2,1)S(1)} %get-tuple-element.8), channel_id=1, source_target_pairs={{0,2},{2,0},{1,3},{3,1},{4,6},{6,4},{5,7},{7,5},{8,10},{10,8},{9,1... | collective-permute-start | bytes 589832 | tf_op jit(solution)/shard_map/ppermute | solution.py:30
  23.3 4.2 %collective-permute-done = bf16[16,6144]{1,0:T(8,128)(2,1)S(1)} collective-permute-done((bf16[16,6144]{1,0:T(8,128)(2,1)S(1)}, bf16[16,6144]{1,0:T(8,128)(2,1)S(1)}, u32[]{:S(2)}, u32[]{:S(2)}) %collective-permute-start) | collective-permute-done | bytes 196640 | tf_op jit(solution)/shard_map/ppermute | solution.py:30
  27.5 1.7 %collective-permute-done.1 = bf16[32,6144]{1,0:T(8,128)(2,1)S(1)} collective-permute-done((bf16[32,6144]{1,0:T(8,128)(2,1)S(1)}, bf16[32,6144]{1,0:T(8,128)(2,1)S(1)}, u32[]{:S(2)}, u32[]{:S(2)}) %collective-permute-start.1) | collective-permute-done | bytes 393248 | tf_op jit(solution)/shard_map/ppermute | solution.py:13
  29.5 0.8 reshape.111
  30.3 4.5 %all-to-all-start.1 = ((f32[8,1,4096]{2,1,0:T(1,128)}), f32[8,1,4096]{2,1,0:T(1,128)S(1)}, u32[]{:S(2)}, u32[]{:S(2)}) async-start(f32[8,1,4096]{2,1,0:T(1,128)} %reshape.111), calls=%async_computation.1 | async-start | bytes 262144 | tf_op jit(solution)/shard_map/all_to_all | solution.py:17
  34.8 4.0 %fusion.38 = f32[64,512]{1,0:T(8,128)S(1)} fusion(bf16[64,6144]{1,0:T(8,128)(2,1)S(1)} %pad_maximum_fusion, bf16[6144,512]{1,0:T(8,128)(2,1)} %param.11), kind=kOutput, calls=%fused_computation.79 | convolution fusion | flops 402653184 | bytes 7208960 | tf_op jit(solution)/shard_map/dot_general | solution.py:35
  38.8 3.3 %all-to-all-done.1 = f32[8,1,4096]{2,1,0:T(1,128)S(1)} async-done(((f32[8,1,4096]{2,1,0:T(1,128)}), f32[8,1,4096]{2,1,0:T(1,128)S(1)}, u32[]{:S(2)}, u32[]{:S(2)}) %all-to-all-start.1) | async-done | bytes 131104 | tf_op jit(solution)/shard_map/all_to_all | solution.py:17
  42.1 0.5 broadcast.65
  42.7 1.0 reduce
  43.9 4.0 %convolution_add_fusion = f32[64,512]{1,0:T(8,128)S(1)} fusion(f32[64,512]{1,0:T(8,128)S(1)} %convolution_multiply_fusion.2, bf16[64,6144]{1,0:T(8,128)(2,1)S(1)} %pad_maximum_fusion, bf16[6144,512]{1,0:T(8,128)(2,1)} %param.10), kind=kOutput, calls=%fused_computation.5 | convolution fusion | flops 402685952 | bytes 7340032 | tf_op jit(solution)/shard_map/dot_general | solution.py:35
  47.9 4.0 %fusion.14 = f32[64,6144]{1,0:T(8,128)S(1)} fusion(bf16[512,6144]{1,0:T(8,128)(2,1)} %param.12, f32[64,512]{1,0:T(8,128)S(1)} %fusion.38, f32[64,512]{1,0:T(8,128)S(1)} %convolution_add_fusion), kind=kOutput, calls=%fused_computation.37 | convolution fusion | flops 402849792 | bytes 8126464 | tf_op jit(solution)/shard_map/dot_general | solution.py:35
  52.0 1.7 %collective-permute-done.2 = bf16[32,6144]{1,0:T(8,128)(2,1)S(1)} collective-permute-done((bf16[32,6144]{1,0:T(8,128)(2,1)S(1)}, bf16[32,6144]{1,0:T(8,128)(2,1)S(1)}, u32[]{:S(2)}, u32[]{:S(2)}) %collective-permute-start.2) | collective-permute-done | bytes 393248 | tf_op jit(solution)/shard_map/ppermute | solution.py:13
  53.8 0.8 copy.30
  54.6 3.5 %all-to-all-start.2 = ((bf16[8,32,768]{2,1,0:T(8,128)(2,1)}), bf16[8,32,768]{2,1,0:T(8,128)(2,1)S(1)}, u32[]{:S(2)}, u32[]{:S(2)}) async-start(bf16[8,32,768]{2,1,0:T(8,128)(2,1)} %bitcast.60), calls=%async_computation.2 | async-start | bytes 786432 | tf_op jit(solution)/shard_map/all_to_all | solution.py:17
  58.4 11.8 %all-to-all-done.2 = bf16[8,32,768]{2,1,0:T(8,128)(2,1)S(1)} async-done(((bf16[8,32,768]{2,1,0:T(8,128)(2,1)}), bf16[8,32,768]{2,1,0:T(8,128)(2,1)S(1)}, u32[]{:S(2)}, u32[]{:S(2)}) %all-to-all-start.2) | async-done | bytes 393248 | tf_op jit(solution)/shard_map/all_to_all | solution.py:17
  70.4 0.8 broadcast_in_dim.10
  71.2 3.6 %all-to-all-start.3 = ((bf16[8,32,768]{2,1,0:T(8,128)(2,1)}), bf16[8,32,768]{2,1,0:T(8,128)(2,1)S(1)}, u32[]{:S(2)}, u32[]{:S(2)}) async-start(bf16[8,32,768]{2,1,0:T(8,128)(2,1)} %broadcast_in_dim.10), calls=%async_computation.3 | async-start | bytes 786432 | tf_op jit(solution)/shard_map/all_to_all | solution.py:17
  74.8 11.9 %all-to-all-done.3 = bf16[8,32,768]{2,1,0:T(8,128)(2,1)S(1)} async-done(((bf16[8,32,768]{2,1,0:T(8,128)(2,1)}), bf16[8,32,768]{2,1,0:T(8,128)(2,1)S(1)}, u32[]{:S(2)}, u32[]{:S(2)}) %all-to-all-start.3) | async-done | bytes 393248 | tf_op jit(solution)/shard_map/all_to_all | solution.py:17
  86.9 1.6 %collective-permute-start.3 = (bf16[16,6144]{1,0:T(8,128)(2,1)S(1)}, bf16[16,6144]{1,0:T(8,128)(2,1)S(1)}, u32[]{:S(2)}, u32[]{:S(2)}) collective-permute-start(bf16[16,6144]{1,0:T(8,128)(2,1)S(1)} %bitcast.68), channel_id=1, source_target_pairs={{0,2},{2,0},{1,3},{3,1},{4,6},{6,4},{5,7},{7,5},{8,10},{10,8},{9,1... | collective-permute-start | bytes 589832 | tf_op jit(solution)/shard_map/ppermute | solution.py:107
  88.5 4.8 %fusion.1 = bf16[64,512]{1,0:T(8,128)(2,1)S(1)} fusion(f32[64,512]{1,0:T(8,128)S(1)} %fusion.38, bf16[512,6144]{1,0:T(8,128)(2,1)} %param.12, bf16[64,6144]{1,0:T(8,128)(2,1)S(1)} %pad_maximum_fusion, bf16[32,6144]{1,0:T(8,128)(2,1)S(1)} %collective-permute-done.4, bf16[32,6144]{1,0:T(8,128)(2,1)S(1)} %bitcast.66, f32[64]{0:T(128)S(1)} %get-tuple-element.3, ...), kind=kOutput, calls=%fused_computation.8 | convolution fusion | flops 406126592 | bytes 8192256 | tf_op jit(solution)/shard_map/dot_general | solution.py:39
  93.6 1.1 %reshape.113 = bf16[32,2,2048]{2,1,0:T(2,128)(2,1)} reshape(bf16[32,64,64]{2,1,0:T(8,128)(2,1)S(1)} %broadcast_in_dim.11) | data formatting | bytes 524288
  94.7 3.6 %all-to-all-start.4 = ((bf16[32,2,2048]{2,1,0:T(2,128)(2,1)}), bf16[32,2,2048]{2,1,0:T(2,128)(2,1)S(1)}, u32[]{:S(2)}, u32[]{:S(2)}) async-start(bf16[32,2,2048]{2,1,0:T(2,128)(2,1)} %reshape.113), calls=%async_computation.4 | async-start | bytes 524288 | tf_op jit(solution)/shard_map/all_to_all | solution.py:17
  98.5 1.8 %collective-permute-start.5 = (bf16[64,192]{1,0:T(8,128)(2,1)S(1)}, bf16[64,192]{1,0:T(8,128)(2,1)S(1)}, u32[]{:S(2)}, u32[]{:S(2)}) collective-permute-start(bf16[64,192]{1,0:T(8,128)(2,1)S(1)} %constant_dynamic-slice_fusion.1), channel_id=1, source_target_pairs={{0,2},{2,0},{1,3},{3,1},{4,6},{6,4},{5,7},{7,5},{8,10},{10,8},{9,1... | collective-permute-start | bytes 73736 | tf_op jit(solution)/shard_map/ppermute | solution.py:30
  100.3 0.9 convolution_convert_fusion.1
  101.2 0.9 convolution_multiply_fusion.1
  102.0 6.9 %all-to-all-done.4 = bf16[32,2,2048]{2,1,0:T(2,128)(2,1)S(1)} async-done(((bf16[32,2,2048]{2,1,0:T(2,128)(2,1)}), bf16[32,2,2048]{2,1,0:T(2,128)(2,1)S(1)}, u32[]{:S(2)}, u32[]{:S(2)}) %all-to-all-start.4) | async-done | bytes 262176 | tf_op jit(solution)/shard_map/all_to_all | solution.py:17
  109.8 0.9 convolution_add_fusion.1
  (48 shorter events, 3.0 us)
Async XLA Ops:
  0.6 28.7 %copy-start = (bf16[768,64]{0,1:T(8,128)(2,1)S(1)}, bf16[768,64]{0,1:T(8,128)(2,1)}, u32[]{:S(2)}) copy-start(bf16[768,64]{0,1:T(8,128)(2,1)} %param.13) | copy-start | bytes 294916
  2.3 19.0 %all-to-all-start = ((bf16[8,4,6144]{2,1,0:T(4,128)(2,1)}), bf16[8,4,6144]{2,1,0:T(4,128)(2,1)S(1)}, u32[]{:S(2)}, u32[]{:S(2)}) async-start(bf16[8,4,6144]{2,1,0:T(4,128)(2,1)} %broadcast_in_dim.8), calls=%async_computation | async-start | bytes 786432 | tf_op jit(solution)/shard_map/all_to_all | solution.py:17
  21.7 5.7 %collective-permute-start = (bf16[16,6144]{1,0:T(8,128)(2,1)S(1)}, bf16[16,6144]{1,0:T(8,128)(2,1)S(1)}, u32[]{:S(2)}, u32[]{:S(2)}) collective-permute-start(bf16[16,6144]{1,0:T(8,128)(2,1)S(1)} %get-tuple-element.8), channel_id=1, source_target_pairs={{0,2},{2,0},{1,3},{3,1},{4,6},{6,4},{5,7},{7,5},{8,10},{10,8},{9,1... | collective-permute-start | bytes 589832 | tf_op jit(solution)/shard_map/ppermute | solution.py:30
  27.5 1.8 %collective-permute-start.1 = (bf16[32,6144]{1,0:T(8,128)(2,1)S(1)}, bf16[32,6144]{1,0:T(8,128)(2,1)S(1)}, u32[]{:S(2)}, u32[]{:S(2)}) collective-permute-start(bf16[32,6144]{1,0:T(8,128)(2,1)S(1)} %pad_maximum_fusion.1), channel_id=1, source_target_pairs={{0,1},{1,0},{2,3},{3,2},{4,5},{5,4},{6,7},{7,6},{8,9},{9,8},{10,11... | collective-permute-start | bytes 1179656 | tf_op jit(solution)/shard_map/ppermute | solution.py:13
  30.3 11.8 %all-to-all-start.1 = ((f32[8,1,4096]{2,1,0:T(1,128)}), f32[8,1,4096]{2,1,0:T(1,128)S(1)}, u32[]{:S(2)}, u32[]{:S(2)}) async-start(f32[8,1,4096]{2,1,0:T(1,128)} %reshape.111), calls=%async_computation.1 | async-start | bytes 262144 | tf_op jit(solution)/shard_map/all_to_all | solution.py:17
  34.8 9.0 %copy-start.1 = (bf16[64,512]{1,0:T(8,128)(2,1)S(1)}, bf16[64,512]{1,0:T(8,128)(2,1)}, u32[]{:S(2)}) copy-start(bf16[64,512]{1,0:T(8,128)(2,1)} %param.14) | copy-start | bytes 196612
  51.9 6.2 %copy-start.3 = (bf16[6144,2]{0,1:T(2,128)(2,1)S(1)}, bf16[6144,2]{0,1:T(2,128)(2,1)}, u32[]{:S(2)}) copy-start(bf16[6144,2]{0,1:T(2,128)(2,1)} %param.15) | copy-start | bytes 73732
  51.9 1.8 %collective-permute-start.2 = (bf16[32,6144]{1,0:T(8,128)(2,1)S(1)}, bf16[32,6144]{1,0:T(8,128)(2,1)S(1)}, u32[]{:S(2)}, u32[]{:S(2)}) collective-permute-start(bf16[32,6144]{1,0:T(8,128)(2,1)S(1)} %slice.77), channel_id=1, source_target_pairs={{0,1},{1,0},{2,3},{3,2},{4,5},{5,4},{6,7},{7,6},{8,9},{9,8},{10,11... | collective-permute-start | bytes 1179656 | tf_op jit(solution)/shard_map/ppermute | solution.py:13
  54.6 15.6 %all-to-all-start.2 = ((bf16[8,32,768]{2,1,0:T(8,128)(2,1)}), bf16[8,32,768]{2,1,0:T(8,128)(2,1)S(1)}, u32[]{:S(2)}, u32[]{:S(2)}) async-start(bf16[8,32,768]{2,1,0:T(8,128)(2,1)} %bitcast.60), calls=%async_computation.2 | async-start | bytes 786432 | tf_op jit(solution)/shard_map/all_to_all | solution.py:17
  58.4 28.4 %copy-start.2 = (s32[1,32]{1,0:T(1,128)S(1)}, s32[1,32]{1,0:T(1,128)}, u32[]{:S(2)}) copy-start(s32[1,32]{1,0:T(1,128)} %param.9) | copy-start | bytes 388
  71.2 15.5 %all-to-all-start.3 = ((bf16[8,32,768]{2,1,0:T(8,128)(2,1)}), bf16[8,32,768]{2,1,0:T(8,128)(2,1)S(1)}, u32[]{:S(2)}, u32[]{:S(2)}) async-start(bf16[8,32,768]{2,1,0:T(8,128)(2,1)} %broadcast_in_dim.10), calls=%async_computation.3 | async-start | bytes 786432 | tf_op jit(solution)/shard_map/all_to_all | solution.py:17
  86.7 1.8 %collective-permute-start.4 = (bf16[32,6144]{1,0:T(8,128)(2,1)S(1)}, bf16[32,6144]{1,0:T(8,128)(2,1)S(1)}, u32[]{:S(2)}, u32[]{:S(2)}) collective-permute-start(bf16[32,6144]{1,0:T(8,128)(2,1)S(1)} %bitcast.65), channel_id=1, source_target_pairs={{0,1},{1,0},{2,3},{3,2},{4,5},{5,4},{6,7},{7,6},{8,9},{9,8},{10,11... | collective-permute-start | bytes 1179656 | tf_op jit(solution)/shard_map/ppermute | solution.py:13
  86.9 13.4 %collective-permute-start.3 = (bf16[16,6144]{1,0:T(8,128)(2,1)S(1)}, bf16[16,6144]{1,0:T(8,128)(2,1)S(1)}, u32[]{:S(2)}, u32[]{:S(2)}) collective-permute-start(bf16[16,6144]{1,0:T(8,128)(2,1)S(1)} %bitcast.68), channel_id=1, source_target_pairs={{0,2},{2,0},{1,3},{3,1},{4,6},{6,4},{5,7},{7,5},{8,10},{10,8},{9,1... | collective-permute-start | bytes 589832 | tf_op jit(solution)/shard_map/ppermute | solution.py:107
  94.7 14.2 %all-to-all-start.4 = ((bf16[32,2,2048]{2,1,0:T(2,128)(2,1)}), bf16[32,2,2048]{2,1,0:T(2,128)(2,1)S(1)}, u32[]{:S(2)}, u32[]{:S(2)}) async-start(bf16[32,2,2048]{2,1,0:T(2,128)(2,1)} %reshape.113), calls=%async_computation.4 | async-start | bytes 524288 | tf_op jit(solution)/shard_map/all_to_all | solution.py:17
  98.5 11.1 %collective-permute-start.5 = (bf16[64,192]{1,0:T(8,128)(2,1)S(1)}, bf16[64,192]{1,0:T(8,128)(2,1)S(1)}, u32[]{:S(2)}, u32[]{:S(2)}) collective-permute-start(bf16[64,192]{1,0:T(8,128)(2,1)S(1)} %constant_dynamic-slice_fusion.1), channel_id=1, source_target_pairs={{0,2},{2,0},{1,3},{3,1},{4,6},{6,4},{5,7},{7,5},{8,10},{10,8},{9,1... | collective-permute-start | bytes 73736 | tf_op jit(solution)/shard_map/ppermute | solution.py:30

commit v2 on v1

v2 whole, which is shorter than its diff:
```python
import functools
import math

import jax
import jax.numpy as jnp
from jax import lax
from jax.experimental import pallas as pl
from jax.experimental.pallas import tpu as pltpu
from jax.sharding import Mesh, PartitionSpec as P

adapter_scale = 0.25
bf16, f32 = jnp.bfloat16, jnp.float32
VMEM_LIMIT = 20 * 2**20
every = ("dp", "x", "core")


def swap(block, axis):
    return lax.ppermute(block, axis, [(0, 1), (1, 0)])


def exchange(blocks, axis):
    return lax.all_to_all(blocks, axis, 0, 0, tiled=True)


def dot(left, right):
    return jnp.dot(left, right, preferred_element_type=f32)


def dot_last(left, right):
    return lax.dot_general(left, right, (((1,), (1,)), ((), ())), preferred_element_type=f32)


def dot_first(left, right):
    return lax.dot_general(left, right, (((0,), (0,)), ((), ())), preferred_element_type=f32)


def sigmoid(v):
    return 1.0 / (1.0 + jnp.exp(-v))


def struct(shape, dtype):
    return jax.ShapeDtypeStruct(shape, dtype)


def vmem(count):
    return [pl.BlockSpec(memory_space=pltpu.VMEM)] * count


def params():
    return pltpu.CompilerParams(vmem_limit_bytes=VMEM_LIMIT)


def cost(flops, moved):
    return pl.CostEstimate(flops=int(flops), bytes_accessed=int(moved), transcendentals=0)


def beside(rows):
    half = rows.shape[0] // 2
    return jnp.concatenate([rows[:half], rows[half:]], axis=1)


def apart(wide):
    rank = wide.shape[1] // 2
    return jnp.concatenate([wide[:, :rank], wide[:, rank:]], axis=0)


def low_kernel(n_parts, place_ref, *refs):
    parts, factor_ref, out_ref = refs[:n_parts], refs[n_parts], refs[n_parts + 1]
    depth = factor_ref.shape[1]
    if depth < parts[0].shape[1]:
        at = pl.ds(pl.multiple_of(place_ref[0] * depth, depth), depth)
        rows = jnp.concatenate([r[:, at] for r in parts], axis=0)
    else:
        rows = jnp.concatenate([r[...] for r in parts], axis=0)
    piece = beside(dot_last(rows, factor_ref[...]))
    for i in range(out_ref.shape[0]):
        out_ref[i] = piece


def low_pieces(parts, factor, place, n_dp):
    rank, depth = factor.shape
    half = parts[0].shape[0] * len(parts) // 2
    if depth % 128:
        parts = [lax.dynamic_slice_in_dim(part, place * depth, depth, 1) for part in parts]
    return pl.pallas_call(
        functools.partial(low_kernel, len(parts)),
        in_specs=[pl.BlockSpec(memory_space=pltpu.SMEM)] + vmem(len(parts) + 1),
        out_specs=vmem(1)[0],
        out_shape=struct((n_dp, half, 2 * rank), f32),
        compiler_params=params(),
        name="low_pieces",
    )(place.reshape(1), *parts, factor)


def lift_kernel(n_parts, *refs):
    parts = refs[:n_parts]
    weight_ref, up_ref, route_ref, pre_ref, lifted_ref, gate_ref, weight, up, sems = refs[n_parts:]
    width = parts[0].shape[1]
    steps = sems.shape[1]
    chunk = width // steps
    copies = []
    for k in range(steps):
        at = pl.ds(k * chunk, chunk)
        copies.append(
            (
                pltpu.make_async_copy(weight_ref.at[at], weight.at[at], sems.at[0, k]),
                pltpu.make_async_copy(up_ref.at[at], up.at[at], sems.at[1, k]),
            )
        )
    ahead = 4
    for pair in copies[:ahead]:
        pair[0].start()
        pair[1].start()
    pre = lifted = logit = 0.0
    for k in range(steps):
        at = slice(k * chunk, (k + 1) * chunk)
        for i in (0, 1):
            copies[k][i].wait()
            if k + ahead < steps:
                copies[k + ahead][i].start()
        rows = jnp.concatenate([r[:, at] for r in parts], axis=0)
        pre = pre + dot(rows, weight[at])
        lifted = lifted + dot(rows, up[at])
        logit = logit + jnp.sum(rows.astype(f32) * route_ref[:, at], axis=1, keepdims=True)
    pre_ref[...] = pre
    lifted_ref[...] = lifted
    gate_ref[...] = sigmoid(logit)


def lift(parts, gate_weight, up_weight, route):
    capacity, width = parts[0].shape
    units = gate_weight.shape[1]
    count = capacity * len(parts)
    return pl.pallas_call(
        functools.partial(lift_kernel, len(parts)),
        in_specs=vmem(len(parts)) + [pl.BlockSpec(memory_space=pl.ANY)] * 2 + vmem(1),
        out_specs=vmem(3),
        scratch_shapes=[
            pltpu.VMEM(gate_weight.shape, bf16),
            pltpu.VMEM(up_weight.shape, bf16),
            pltpu.SemaphoreType.DMA((2, 12)),
        ],
        out_shape=(
            struct((count, units), f32),
            struct((count, units), f32),
            struct((count, 1), f32),
        ),
        cost_estimate=cost(4 * count * width * units, 4 * width * units),
        compiler_params=params(),
        name="lift",
    )(
        *parts,
        pltpu.with_memory_space_constraint(gate_weight, pltpu.HBM),
        pltpu.with_memory_space_constraint(up_weight, pltpu.HBM),
        route,
    )


def bring(source, target, sems, blocks, wide):
    copies, ahead = [], 4
    for k in range(blocks):
        at = pl.ds(k * wide, wide)
        copies.append(pltpu.make_async_copy(source.at[:, at], target.at[:, at], sems.at[k]))
    for copy in copies[:ahead]:
        copy.start()

    def arrive(k):
        copies[k].wait()
        if k + ahead < blocks:
            copies[k + ahead].start()

    return arrive


def down_kernel(
    base_ref, lifted_ref, low_ref, factor_ref, weight_ref, own_ref, other_ref, pre_ref, low_out, down_ref, sems
):
    blocks, half, wide = own_ref.shape
    arrive = bring(weight_ref, down_ref, sems, blocks, wide)
    low = apart(jnp.sum(low_ref[...], axis=0)).astype(bf16)
    pre = base_ref[...] + adapter_scale * dot(low, factor_ref[...])
    low_out[...] = low
    pre_ref[...] = pre
    hidden = (pre * sigmoid(pre) * lifted_ref[...]).astype(bf16)
    for k in range(blocks):
        arrive(k)
        partial = dot(hidden, down_ref[:, k * wide : (k + 1) * wide]).astype(bf16)
        own_ref[k] = partial[:half]
        other_ref[k] = partial[half:]


def down(base, lifted, low_parts, factor, down_weight, blocks):
    count, units = base.shape
    half, width = count // 2, down_weight.shape[1]
    shape = struct((blocks, half, width // blocks), bf16)
    return pl.pallas_call(
        down_kernel,
        in_specs=vmem(4) + [pl.BlockSpec(memory_space=pl.ANY)],
        out_specs=vmem(4),
        scratch_shapes=[pltpu.VMEM(down_weight.shape, bf16), pltpu.SemaphoreType.DMA((blocks,))],
        out_shape=(shape, shape, struct((count, units), f32), struct((count, factor.shape[0]), bf16)),
        cost_estimate=cost(2 * count * width * units, 2 * width * units),
        compiler_params=params(),
        name="down",
    )(base, lifted, low_parts, factor, pltpu.with_memory_space_constraint(down_weight, pltpu.HBM))


def mix_kernel(blocks_ref, gate_ref, out_ref):
    half = out_ref.shape[1]
    total = blocks_ref[0].astype(f32)
    for i in range(1, blocks_ref.shape[0]):
        total = total + blocks_ref[i].astype(f32)
    mixed = (gate_ref[:half] * total).astype(bf16)
    for i in range(out_ref.shape[0]):
        out_ref[i] = mixed


def mix(blocks, gate):
    return pl.pallas_call(
        mix_kernel,
        in_specs=vmem(2),
        out_specs=vmem(1)[0],
        out_shape=struct(blocks.shape, bf16),
        compiler_params=params(),
        name="mix",
    )(blocks, gate)


def back_kernel(n_parts, loss_factor, *refs):
    parts = refs[:n_parts]
    (
        own_ref,
        other_ref,
        gate_ref,
        weight_ref,
        pre_ref,
        lifted_ref,
        low_ref,
        factor_ref,
        low_out,
        grad_ref,
        down_ref,
        sems,
    ) = refs[n_parts:]
    blocks, half, wide = own_ref.shape
    arrive = bring(weight_ref, down_ref, sems, blocks, wide)
    scale = loss_factor * gate_ref[...]
    total = 0.0
    for k in range(blocks):
        at = slice(k * wide, (k + 1) * wide)
        mixed = jnp.concatenate([own_ref[k], other_ref[k]], axis=0).astype(f32)
        rows = jnp.concatenate([r[:, at] for r in parts], axis=0).astype(f32)
        back = (scale * (mixed - rows)).astype(bf16)
        arrive(k)
        total = total + dot_last(down_ref[:, at], back)
    pre = pre_ref[...]
    sig = sigmoid(pre)
    slope = sig * (1.0 + pre * (1.0 - sig))
    back_pre = (total.T * lifted_ref[...] * slope).astype(bf16)
    back_low = beside(adapter_scale * dot_last(back_pre, factor_ref[...])).astype(bf16)
    for i in range(low_out.shape[0]):
        low_out[i] = back_low
    grad_ref[...] = adapter_scale * dot_first(low_ref[...], back_pre)


def back(parts, own, other, gate, down_weight, pre, lifted, low, factor, loss_factor, copies):
    width = parts[0].shape[1]
    half = own.shape[1]
    count, units = pre.shape
    rank = factor.shape[0]
    return pl.pallas_call(
        functools.partial(back_kernel, len(parts), loss_factor),
        in_specs=vmem(len(parts) + 3) + [pl.BlockSpec(memory_space=pl.ANY)] + vmem(4),
        out_specs=vmem(2),
        scratch_shapes=[pltpu.VMEM(down_weight.shape, bf16), pltpu.SemaphoreType.DMA((own.shape[0],))],
        out_shape=(struct((copies, half, 2 * rank), bf16), struct((rank, units), f32)),
        cost_estimate=cost(2 * count * width * units, 2 * width * units),
        compiler_params=params(),
        name="back",
    )(
        *parts,
        own,
        other,
        gate,
        pltpu.with_memory_space_constraint(down_weight, pltpu.HBM),
        pre,
        lifted,
        low,
        factor,
    )


def factor_kernel(place_ref, low_ref, piece_ref, out_ref):
    rank = out_ref.shape[0]
    groups = piece_ref.shape[0]
    group, core = place_ref[0], place_ref[1]
    total = 0.0
    for g in range(groups):
        mine = jnp.sum(low_ref[:, g, core].astype(f32), axis=0)
        theirs = jnp.sum(low_ref[:, g, 1 - core].astype(f32), axis=0)
        low = jnp.concatenate(
            [mine[:, :rank] + theirs[:, rank:], mine[:, rank:] + theirs[:, :rank]], axis=0
        )
        high = low.astype(bf16)
        rest = (low - high.astype(f32)).astype(bf16)
        piece = piece_ref[lax.rem(group - g + groups, groups)]
        total = total + dot_first(high, piece) + dot_first(rest, piece)
    out_ref[...] = total


def factor_gradient(lows, pieces, group, core):
    rank, share = lows.shape[-1] // 2, pieces.shape[2]
    return pl.pallas_call(
        factor_kernel,
        in_specs=[pl.BlockSpec(memory_space=pltpu.SMEM)] + vmem(2),
        out_specs=vmem(1)[0],
        out_shape=struct((rank, share), f32),
        compiler_params=params(),
        name="factor_gradient",
    )(jnp.stack([group, core]), lows, pieces)


def shards(
    tokens,
    expert_choice_table,
    gate_weight,
    up_weight,
    down_weight,
    adapter_down_shared,
    adapter_gate_factor,
    router,
):
    tok_rows, width = tokens.shape
    n_dp = lax.axis_size("dp")
    groups = lax.axis_size("x")
    place = lax.axis_index("dp")
    group = lax.axis_index("x")
    core = lax.axis_index("core")
    col_rows = n_dp * tok_rows
    capacity = col_rows // groups
    half = groups * capacity
    wide = width // n_dp
    rank = adapter_down_shared.shape[1]
    devices = n_dp * groups * 2
    share = width // devices
    loss_factor = math.sqrt(groups / (tok_rows * devices))
    blocks = 8

    def regroup(array, pieces):
        if array.shape[0] == pieces:
            return array
        flat = array.transpose(1, 0, 2).reshape(array.shape[1], width)
        return flat.reshape(array.shape[1], pieces, width // pieces).transpose(1, 0, 2)

    column = exchange(jnp.broadcast_to(tokens[None], (n_dp, tok_rows, width)), "dp")
    column = column.reshape(col_rows, width)
    labels = expert_choice_table[0]
    index = jnp.arange(col_rows, dtype=jnp.int32)
    before = (labels[None, :] == labels[:, None]) & (index[None, :] < index[:, None])
    ordinal = jnp.sum(before.astype(jnp.int32), axis=1)
    ahead = lax.rem(labels - group + groups, groups)
    target = ahead * capacity + ordinal
    placer = (index[:, None] == target[None, :]).astype(bf16)
    packed = dot(placer, column).astype(bf16).reshape(groups, capacity, width)
    parts = [packed[0]]
    for step in range(1, groups):
        route = [(i, (i + step) % groups) for i in range(groups)]
        parts.append(lax.ppermute(packed[step], "x", route))
    parts = parts + [swap(part, "core") for part in parts]

    low_parts = exchange(low_pieces(parts, adapter_down_shared.T, place, n_dp), "dp")
    own_route = lax.dynamic_slice_in_dim(router.T, group, 1, 0).astype(f32)
    base, lifted, gate = lift(parts, gate_weight, up_weight, own_route)
    own, other, pre, low = down(base, lifted, low_parts, adapter_gate_factor, down_weight, blocks)

    summed = (own.astype(f32) + swap(other, "core").astype(f32)).astype(bf16)
    rows = jnp.concatenate(parts, axis=0)
    pieces = []
    for step in range(groups):
        to = lax.rem(group + step, groups)
        at = ((place * groups + to) * 2 + core) * share
        piece = lax.dynamic_slice_in_dim(rows, at, share, 1)
        route = [(i, (i + step) % groups) for i in range(groups)]
        pieces.append(lax.ppermute(piece, "x", route) if step else piece)
    pieces = jnp.stack(pieces)

    totals, pieces = lax.optimization_barrier((exchange(regroup(summed, n_dp), "dp"), pieces))
    mixed = mix(totals, gate)
    mixed_half = regroup(exchange(mixed, "dp"), blocks)
    mixed_other = swap(mixed_half, "core")

    back_low, grad_b = back(
        parts,
        mixed_half,
        mixed_other,
        gate,
        down_weight,
        pre,
        lifted,
        low,
        adapter_gate_factor,
        loss_factor,
        devices,
    )
    lows = exchange(back_low, every).reshape(n_dp, groups, 2, half, 2 * rank)

    returned = [mixed_half[:, :capacity]]
    for step in range(1, groups):
        route = [(i, (i - step) % groups) for i in range(groups)]
        part = mixed_half[:, step * capacity : (step + 1) * capacity]
        returned.append(lax.ppermute(part, "x", route))
    own_target = lax.dynamic_slice_in_dim(target, place * tok_rows, tok_rows, 0)
    result = jnp.zeros((tok_rows, width), f32)
    for step in range(groups):
        spot = index[step * capacity : (step + 1) * capacity]
        chooser = (own_target[:, None] == spot[None, :]).astype(bf16)
        chosen = jnp.einsum("ir,brc->ibc", chooser, returned[step], preferred_element_type=f32)
        result = result + chosen.reshape(tok_rows, width)

    grad_a = factor_gradient(lows, pieces, group, core)
    return (result.astype(bf16), grad_a.T, grad_b.T)


def solution(mesh):
    n_dp, n_expert = mesh.shape["dp"], mesh.shape["expert"]
    split = Mesh(mesh.devices.reshape(n_dp, n_expert // 2, 2), every)
    return jax.shard_map(
        shards,
        mesh=split,
        in_specs=(
            P(every, None),
            P(("x", "core"), None),
            P(None, every),
            P(None, every),
            P(every, None),
            P("dp", None),
            P(None, every),
            P(),
        ),
        out_specs=(P(every, None), P(every, None), P(every, None)),
        check_vma=False,
    )
```

time: 111 us -> 104 us (0.937)
  matrix products: 20.7 us -> 1.3 us
  Pallas kernels: 0 us -> 17.8 us
  blocking collectives: 0 us -> 15.7 us
  waiting for transfers between devices: 51.6 us -> 38.7 us
  local copies, waits for them, and re-layouts: 6.77 us -> 2.06 us
  starting transfers between devices: 27.6 us -> 24.3 us
    all_to_all x5 -> x4, waiting for transfers between devices: 44 us -> 19.8 us  [exchange(): return lax.all_to_all(blocks, axis, 0, 0, tiled=True)]
    pallas_call x0 -> x6, Pallas kernels: none -> 17.8 us  [the longest x1 6.11 us: back(): pl.pallas_call(functools.partial(back_kernel, len(parts), loss_factor), i...]
    all_to_all x0 -> x1, blocking collectives: none -> 15.7 us  [exchange(): return lax.all_to_all(blocks, axis, 0, 0, tiled=True)]
    dot_general x8 -> x1, matrix products: 13.7 us -> 0.24 us  [dot(): return jnp.dot(left, right, preferred_element_type=f32)]
    ppermute x3, waiting for transfers between devices: 4.18 us -> 14.1 us  [the longest x1 7.5 us: shards(): returned.append(lax.ppermute(part, 'x', route))]
    dot_general x5 -> x2, matrix products: 6.97 us -> 1.05 us  [shards(): jnp.einsum('ir,brc->ibc', chooser, returned[step], preferred_element_type...]
    all_to_all x5 -> x4, starting transfers between devices: 22.4 us -> 19.3 us  [exchange(): return lax.all_to_all(blocks, axis, 0, 0, tiled=True)]
    unnamed x13 -> x8, local copies, waits for them, and re-layouts: 2.45 us -> 0.02 us
  transfers between devices with their start and end apart: 11 -> 11, of which waited for: 8 -> 9; matrix products, arithmetic and copies ran while one was open for 13% -> 3% of each run, Pallas kernels for 0% -> 5%
where the time goes in v2:
time: 104 us; the launch traced here: 103 us
  waiting for transfers between devices  38.7 us (37%)
  starting transfers between devices  24.3 us (23%)
  Pallas kernels  17.8 us (17%)
  blocking collectives  15.7 us (15%)
  other arithmetic  2.61 us (3%)
  local copies, waits for them, and re-layouts  2.06 us (2%)
  matrix products  1.3 us (1%)
    all_to_all x4, waiting for transfers between devices, exchange(): return lax.all_to_all(blocks, axis, 0, 0, tiled=True)  19.8 us
    all_to_all x4, starting transfers between devices, exchange(): return lax.all_to_all(blocks, axis, 0, 0, tiled=True)  19.3 us
    all_to_all x1, blocking collectives, exchange(): return lax.all_to_all(blocks, axis, 0, 0, tiled=True)  15.7 us
    ppermute x1, waiting for transfers between devices, shards(): returned.append(lax.ppermute(part, 'x', route))  7.5 us
    pallas_call x1, Pallas kernels, back(): pl.pallas_call(functools.partial(back_kernel, len(parts), loss_factor), i...  6.11 us
    pallas_call x1, Pallas kernels, lift(): pl.pallas_call(functools.partial(lift_kernel, len(parts)), in_specs=vmem(...  5.44 us
    ppermute x4, waiting for transfers between devices, swap(): return lax.ppermute(block, axis, [(0, 1), (1, 0)])  4.83 us
    ppermute x1, waiting for transfers between devices, shards(): parts.append(lax.ppermute(packed[step], 'x', route))  4.18 us
  transfers between devices with their start and end apart: 11, of which 9 were waited for; matrix products, arithmetic and copies ran while one was open for 3% of the time, Pallas kernels for 5%

profile of v2, /device:TPU:0, one launch (start us, length us, event | category | flops | bytes accessed | tf_op | source)
XLA Modules:
  0.0 103.2 jit_solution(17035839870067934077)
XLA Ops:
  0.6 1.7 %broadcast_in_dim.2 = bf16[8,4,6144]{2,1,0:T(4,128)(2,1)} broadcast(bf16[4,6144]{1,0:T(4,128)(2,1)} %param.8), dimensions={1,2} | broadcast | bytes 442368 | tf_op jit(solution)/shard_map/broadcast_in_dim | solution.py:355
  2.3 7.4 %all-to-all-start = ((bf16[8,4,6144]{2,1,0:T(4,128)(2,1)}), bf16[8,4,6144]{2,1,0:T(4,128)(2,1)S(1)}, u32[]{:S(2)}, u32[]{:S(2)}) async-start(bf16[8,4,6144]{2,1,0:T(4,128)(2,1)} %broadcast_in_dim.2), calls=%async_computation | async-start | bytes 786432 | tf_op jit(solution)/shard_map/all_to_all | solution.py:22
  9.7 0.9 convert_reduce_fusion
  10.6 0.7 fusion.19
  11.3 10.1 %all-to-all-done = bf16[8,4,6144]{2,1,0:T(4,128)(2,1)S(1)} async-done(((bf16[8,4,6144]{2,1,0:T(4,128)(2,1)}), bf16[8,4,6144]{2,1,0:T(4,128)(2,1)S(1)}, u32[]{:S(2)}, u32[]{:S(2)}) %all-to-all-start) | async-done | bytes 393248 | tf_op jit(solution)/shard_map/all_to_all | solution.py:22
  21.4 0.1 reshape.42
  21.5 0.2 convolution_convert_fusion
  21.8 1.6 %collective-permute-start = (bf16[16,6144]{1,0:T(8,128)(2,1)S(1)}, bf16[16,6144]{1,0:T(8,128)(2,1)S(1)}, u32[]{:S(2)}, u32[]{:S(2)}) collective-permute-start(bf16[16,6144]{1,0:T(8,128)(2,1)S(1)} %get-tuple-element.27), channel_id=1, source_target_pairs={{0,2},{2,0},{1,3},{3,1},{4,6},{6,4},{5,7},{7,5},{8,10},{10,8},{9,1... | collective-permute-start | bytes 589832 | tf_op jit(solution)/shard_map/ppermute | solution.py:368
  23.3 4.2 %collective-permute-done.refs_1_ = bf16[16,6144]{1,0:T(8,128)(2,1)S(1)} collective-permute-done((bf16[16,6144]{1,0:T(8,128)(2,1)S(1)}, bf16[16,6144]{1,0:T(8,128)(2,1)S(1)}, u32[]{:S(2)}, u32[]{:S(2)}) %collective-permute-start) | collective-permute-done | bytes 196640 | tf_op jit(solution)/shard_map/ppermute | solution.py:368
  27.5 1.4 %collective-permute-done.2.refs_3_ = bf16[16,6144]{1,0:T(8,128)(2,1)S(1)} collective-permute-done((bf16[16,6144]{1,0:T(8,128)(2,1)S(1)}, bf16[16,6144]{1,0:T(8,128)(2,1)S(1)}, u32[]{:S(2)}, u32[]{:S(2)}) %collective-permute-start.2) | collective-permute-done | bytes 196640 | tf_op jit(solution)/shard_map/ppermute | solution.py:18
  29.0 0.9 low_pieces.1
  29.9 4.5 %all-to-all-start.1 = ((f32[8,32,128]{2,1,0:T(8,128)}), f32[8,32,128]{2,1,0:T(8,128)S(1)}, u32[]{:S(2)}, u32[]{:S(2)}) async-start(f32[8,32,128]{2,1,0:T(8,128)} %low_pieces.1), calls=%async_computation.1 | async-start | bytes 262144 | tf_op jit(solution)/shard_map/all_to_all | solution.py:22
  34.4 5.4 %lift.1 = (f32[64,512]{1,0:T(8,128)S(1)}, f32[64,512]{1,0:T(8,128)S(1)}, f32[64,1]{1,0:T(8,128)S(1)}) custom-call(bf16[16,6144]{1,0:T(8,128)(2,1)S(1)} %get-tuple-element.28.refs_0_, bf16[16,6144]{1,0:T(8,128)(2,1)S(1)} %collective-permute-done.refs_1_, bf16[16,6144]{1,0:T(8,128)(2,1)S(1)} %collective-permute-done.1.refs_2_, ...), custom_call_target="tpu_custom_call" | custom-call | flops 805306368 | bytes 12582912 | tf_op jit(solution)/shard_map/lift/pallas_call | solution.py:134
  39.8 1.8 %all-to-all-done.1.low_ref = f32[8,32,128]{2,1,0:T(8,128)S(1)} async-done(((f32[8,32,128]{2,1,0:T(8,128)}), f32[8,32,128]{2,1,0:T(8,128)S(1)}, u32[]{:S(2)}, u32[]{:S(2)}) %all-to-all-start.1) | async-done | bytes 131104 | tf_op jit(solution)/shard_map/all_to_all | solution.py:22
  41.7 3.7 %down.1 = (bf16[8,32,768]{2,1,0:T(8,128)(2,1)S(1)}, bf16[8,32,768]{2,1,0:T(8,128)(2,1)S(1)}, f32[64,512]{1,0:T(8,128)S(1)}, bf16[64,64]{1,0:T(8,128)(2,1)S(1)}) custom-call(f32[64,512]{1,0:T(8,128)S(1)} %get-tuple-element.14.base_ref, f32[64,512]{1,0:T(8,128)S(1)} %get-tuple-element.15.lifted_ref.refs_9_, f32[8,32,128]{2,1,0:T(8,128)S(1)} %all-to-all-done.1.low_ref, ...), custom_call_target="tpu_custom_call" | custom-call | flops 402653184 | bytes 6291456 | tf_op jit(solution)/shard_map/down/pallas_call | solution.py:196
  45.5 1.7 %collective-permute-done.3 = bf16[8,32,768]{2,1,0:T(8,128)(2,1)S(1)} collective-permute-done((bf16[8,32,768]{2,1,0:T(8,128)(2,1)S(1)}, bf16[8,32,768]{2,1,0:T(8,128)(2,1)S(1)}, u32[]{:S(2)}, u32[]{:S(2)}) %collective-permute-start.3) | collective-permute-done | bytes 393248 | tf_op jit(solution)/shard_map/ppermute | solution.py:18
  47.1 0.8 add_convert_fusion
  48.0 4.2 %all-to-all-start.2 = ((bf16[8,32,768]{2,1,0:T(8,128)(2,1)}), bf16[8,32,768]{2,1,0:T(8,128)(2,1)S(1)}, u32[]{:S(2)}, u32[]{:S(2)}) async-start(bf16[8,32,768]{2,1,0:T(8,128)(2,1)} %add_convert_fusion), calls=%async_computation.2 | async-start | bytes 786432 | tf_op jit(solution)/shard_map/all_to_all | solution.py:22
  52.2 0.1 dynamic-slice_bitcast_fusion
  52.3 1.6 %collective-permute-start.4 = (bf16[64,192]{1,0:T(8,128)(2,1)S(1)}, bf16[64,192]{1,0:T(8,128)(2,1)S(1)}, u32[]{:S(2)}, u32[]{:S(2)}) collective-permute-start(bf16[64,192]{1,0:T(8,128)(2,1)S(1)} %get-tuple-element.26), channel_id=1, source_target_pairs={{0,2},{2,0},{1,3},{3,1},{4,6},{6,4},{5,7},{7,5},{8,10},{10,8},{9,1... | collective-permute-start | bytes 73736 | tf_op jit(solution)/shard_map/ppermute | solution.py:384
  53.9 2.4 %collective-permute-done.4 = bf16[64,192]{1,0:T(8,128)(2,1)S(1)} collective-permute-done((bf16[64,192]{1,0:T(8,128)(2,1)S(1)}, bf16[64,192]{1,0:T(8,128)(2,1)S(1)}, u32[]{:S(2)}, u32[]{:S(2)}) %collective-permute-start.4) | collective-permute-done | bytes 24608 | tf_op jit(solution)/shard_map/ppermute | solution.py:384
  56.3 7.8 %all-to-all-done.2.blocks_ref = bf16[8,32,768]{2,1,0:T(8,128)(2,1)S(1)} async-done(((bf16[8,32,768]{2,1,0:T(8,128)(2,1)}), bf16[8,32,768]{2,1,0:T(8,128)(2,1)S(1)}, u32[]{:S(2)}, u32[]{:S(2)}) %all-to-all-start.2) | async-done | bytes 393248 | tf_op jit(solution)/shard_map/all_to_all | solution.py:22
  64.1 0.1 mix.1
  64.2 15.7 %all_to_all.25.refs_4_ = bf16[8,32,768]{2,1,0:T(8,128)(2,1)S(1)} all-to-all(bf16[8,32,768]{2,1,0:T(8,128)(2,1)S(1)} %mix.1), channel_id=1, replica_groups=mesh['dp'=8,'x'=2,'core'=2] {'dp'}, dimensions={0} | all-to-all | bytes 786432 | tf_op jit(solution)/shard_map/all_to_all | solution.py:22
  79.9 1.7 %collective-permute-done.6.refs_5_ = bf16[8,32,768]{2,1,0:T(8,128)(2,1)S(1)} collective-permute-done((bf16[8,32,768]{2,1,0:T(8,128)(2,1)S(1)}, bf16[8,32,768]{2,1,0:T(8,128)(2,1)S(1)}, u32[]{:S(2)}, u32[]{:S(2)}) %collective-permute-start.6) | collective-permute-done | bytes 393248 | tf_op jit(solution)/shard_map/ppermute | solution.py:18
  81.6 6.1 %back.1 = (bf16[32,32,128]{2,1,0:T(8,128)(2,1)}, f32[64,512]{1,0:T(8,128)}) custom-call(bf16[16,6144]{1,0:T(8,128)(2,1)S(1)} %get-tuple-element.28.refs_0_, bf16[16,6144]{1,0:T(8,128)(2,1)S(1)} %collective-permute-done.refs_1_, bf16[16,6144]{1,0:T(8,128)(2,1)S(1)} %collective-permute-done.1.refs_2_, bf16[16,6144]{1,0:T(8,128)(2,1)S(1)} %collective-permute-done.2.refs_3_, ...), custom_call_target="tpu_custom_call" | custom-call | flops 402653184 | bytes 6291456 | tf_op jit(solution)/shard_map/back/pallas_call | solution.py:271
  87.7 3.3 %all-to-all-start.4 = ((bf16[32,32,128]{2,1,0:T(8,128)(2,1)}), bf16[32,32,128]{2,1,0:T(8,128)(2,1)S(1)}, u32[]{:S(2)}, u32[]{:S(2)}) async-start(bf16[32,32,128]{2,1,0:T(8,128)(2,1)} %get-tuple-element.22), calls=%async_computation.4 | async-start | bytes 524288 | tf_op jit(solution)/shard_map/all_to_all | solution.py:22
  91.3 1.8 %collective-permute-start.5 = (bf16[8,16,768]{2,1,0:T(8,128)(2,1)S(1)}, bf16[8,16,768]{2,1,0:T(8,128)(2,1)S(1)}, u32[]{:S(2)}, u32[]{:S(2)}) collective-permute-start(bf16[8,16,768]{2,1,0:T(8,128)(2,1)S(1)} %slice.29), channel_id=1, source_target_pairs={{0,2},{2,0},{1,3},{3,1},{4,6},{6,4},{5,7},{7,5},{8,10},{10,8},{9,1... | collective-permute-start | bytes 589832 | tf_op jit(solution)/shard_map/ppermute | solution.py:411
  93.1 0.2 fusion.1
  93.3 7.5 %collective-permute-done.5 = bf16[8,16,768]{2,1,0:T(8,128)(2,1)S(1)} collective-permute-done((bf16[8,16,768]{2,1,0:T(8,128)(2,1)S(1)}, bf16[8,16,768]{2,1,0:T(8,128)(2,1)S(1)}, u32[]{:S(2)}, u32[]{:S(2)}) %collective-permute-start.5) | collective-permute-done | bytes 196640 | tf_op jit(solution)/shard_map/ppermute | solution.py:411
  100.8 0.8 fusion
  101.7 1.5 %factor_gradient.1 = f32[64,192]{1,0:T(8,128)} custom-call(s32[2]{0:T(128)S(1)} %pad_add_fusion.place_ref, bf16[8,2,2,32,128]{4,3,2,1,0:T(8,128)(2,1)S(1)} %bitcast.31, bf16[2,64,192]{2,1,0:T(8,128)(2,1)S(1)} %pad_maximum_fusion.1.piece_ref), custom_call_target="tpu_custom_call" | custom-call | tf_op jit(solution)/shard_map/factor_gradient/pallas_call | solution.py:313
  (25 shorter events, 0.5 us)
Async XLA Ops:
  2.3 26.7 %copy-start.1 = (bf16[768,64]{0,1:T(8,128)(2,1)S(1)}, bf16[768,64]{0,1:T(8,128)(2,1)}, u32[]{:S(2)}) copy-start(bf16[768,64]{0,1:T(8,128)(2,1)} %param.13) | copy-start | bytes 294916
  2.3 19.1 %all-to-all-start = ((bf16[8,4,6144]{2,1,0:T(4,128)(2,1)}), bf16[8,4,6144]{2,1,0:T(4,128)(2,1)S(1)}, u32[]{:S(2)}, u32[]{:S(2)}) async-start(bf16[8,4,6144]{2,1,0:T(4,128)(2,1)} %broadcast_in_dim.2), calls=%async_computation | async-start | bytes 786432 | tf_op jit(solution)/shard_map/all_to_all | solution.py:22
  21.5 12.8 %copy-start.2 = (bf16[6144,2]{0,1:T(2,128)(2,1)S(1)}, bf16[6144,2]{0,1:T(2,128)(2,1)}, u32[]{:S(2)}) copy-start(bf16[6144,2]{0,1:T(2,128)(2,1)} %param.15) | copy-start | bytes 73732
  21.8 5.7 %collective-permute-start = (bf16[16,6144]{1,0:T(8,128)(2,1)S(1)}, bf16[16,6144]{1,0:T(8,128)(2,1)S(1)}, u32[]{:S(2)}, u32[]{:S(2)}) collective-permute-start(bf16[16,6144]{1,0:T(8,128)(2,1)S(1)} %get-tuple-element.27), channel_id=1, source_target_pairs={{0,2},{2,0},{1,3},{3,1},{4,6},{6,4},{5,7},{7,5},{8,10},{10,8},{9,1... | collective-permute-start | bytes 589832 | tf_op jit(solution)/shard_map/ppermute | solution.py:368
  23.3 4.2 %collective-permute-start.1 = (bf16[16,6144]{1,0:T(8,128)(2,1)S(1)}, bf16[16,6144]{1,0:T(8,128)(2,1)S(1)}, u32[]{:S(2)}, u32[]{:S(2)}) collective-permute-start(bf16[16,6144]{1,0:T(8,128)(2,1)S(1)} %get-tuple-element.28.refs_0_), channel_id=1, source_target_pairs={{0,1},{1,0},{2,3},{3,2},{4,5},{5,4},{6,7},{7,6},{8,9},{9,8},{10,11... | collective-permute-start | bytes 589832 | tf_op jit(solution)/shard_map/ppermute | solution.py:18
  27.5 1.4 %collective-permute-start.2 = (bf16[16,6144]{1,0:T(8,128)(2,1)S(1)}, bf16[16,6144]{1,0:T(8,128)(2,1)S(1)}, u32[]{:S(2)}, u32[]{:S(2)}) collective-permute-start(bf16[16,6144]{1,0:T(8,128)(2,1)S(1)} %collective-permute-done.refs_1_), channel_id=1, source_target_pairs={{0,1},{1,0},{2,3},{3,2},{4,5},{5,4},{6,7},{7,6},{8,9},{9,8},{10,11... | collective-permute-start | bytes 589832 | tf_op jit(solution)/shard_map/ppermute | solution.py:18
  29.9 11.8 %all-to-all-start.1 = ((f32[8,32,128]{2,1,0:T(8,128)}), f32[8,32,128]{2,1,0:T(8,128)S(1)}, u32[]{:S(2)}, u32[]{:S(2)}) async-start(f32[8,32,128]{2,1,0:T(8,128)} %low_pieces.1), calls=%async_computation.1 | async-start | bytes 262144 | tf_op jit(solution)/shard_map/all_to_all | solution.py:22
  34.4 7.3 %copy-start = (bf16[64,512]{1,0:T(8,128)(2,1)S(1)}, bf16[64,512]{1,0:T(8,128)(2,1)}, u32[]{:S(2)}) copy-start(bf16[64,512]{1,0:T(8,128)(2,1)} %refs_11_.1) | copy-start | bytes 196612
  45.4 1.8 %collective-permute-start.3 = (bf16[8,32,768]{2,1,0:T(8,128)(2,1)S(1)}, bf16[8,32,768]{2,1,0:T(8,128)(2,1)S(1)}, u32[]{:S(2)}, u32[]{:S(2)}) collective-permute-start(bf16[8,32,768]{2,1,0:T(8,128)(2,1)S(1)} %get-tuple-element.17), channel_id=1, source_target_pairs={{0,1},{1,0},{2,3},{3,2},{4,5},{5,4},{6,7},{7,6},{8,9},{9,8},{10,11... | collective-permute-start | bytes 1179656 | tf_op jit(solution)/shard_map/ppermute | solution.py:18
  48.0 16.1 %all-to-all-start.2 = ((bf16[8,32,768]{2,1,0:T(8,128)(2,1)}), bf16[8,32,768]{2,1,0:T(8,128)(2,1)S(1)}, u32[]{:S(2)}, u32[]{:S(2)}) async-start(bf16[8,32,768]{2,1,0:T(8,128)(2,1)} %add_convert_fusion), calls=%async_computation.2 | async-start | bytes 786432 | tf_op jit(solution)/shard_map/all_to_all | solution.py:22
  52.2 27.8 %copy-start.3 = (s32[1,32]{1,0:T(1,128)S(1)}, s32[1,32]{1,0:T(1,128)}, u32[]{:S(2)}) copy-start(s32[1,32]{1,0:T(1,128)} %param.9) | copy-start | bytes 388
  52.3 4.0 %collective-permute-start.4 = (bf16[64,192]{1,0:T(8,128)(2,1)S(1)}, bf16[64,192]{1,0:T(8,128)(2,1)S(1)}, u32[]{:S(2)}, u32[]{:S(2)}) collective-permute-start(bf16[64,192]{1,0:T(8,128)(2,1)S(1)} %get-tuple-element.26), channel_id=1, source_target_pairs={{0,2},{2,0},{1,3},{3,1},{4,6},{6,4},{5,7},{7,5},{8,10},{10,8},{9,1... | collective-permute-start | bytes 73736 | tf_op jit(solution)/shard_map/ppermute | solution.py:384
  79.9 1.7 %collective-permute-start.6 = (bf16[8,32,768]{2,1,0:T(8,128)(2,1)S(1)}, bf16[8,32,768]{2,1,0:T(8,128)(2,1)S(1)}, u32[]{:S(2)}, u32[]{:S(2)}) collective-permute-start(bf16[8,32,768]{2,1,0:T(8,128)(2,1)S(1)} %all_to_all.25.refs_4_), channel_id=1, source_target_pairs={{0,1},{1,0},{2,3},{3,2},{4,5},{5,4},{6,7},{7,6},{8,9},{9,8},{10,11... | collective-permute-start | bytes 1179656 | tf_op jit(solution)/shard_map/ppermute | solution.py:18
  87.7 13.9 %all-to-all-start.4 = ((bf16[32,32,128]{2,1,0:T(8,128)(2,1)}), bf16[32,32,128]{2,1,0:T(8,128)(2,1)S(1)}, u32[]{:S(2)}, u32[]{:S(2)}) async-start(bf16[32,32,128]{2,1,0:T(8,128)(2,1)} %get-tuple-element.22), calls=%async_computation.4 | async-start | bytes 524288 | tf_op jit(solution)/shard_map/all_to_all | solution.py:22
  91.3 9.5 %collective-permute-start.5 = (bf16[8,16,768]{2,1,0:T(8,128)(2,1)S(1)}, bf16[8,16,768]{2,1,0:T(8,128)(2,1)S(1)}, u32[]{:S(2)}, u32[]{:S(2)}) collective-permute-start(bf16[8,16,768]{2,1,0:T(8,128)(2,1)S(1)} %slice.29), channel_id=1, source_target_pairs={{0,2},{2,0},{1,3},{3,1},{4,6},{6,4},{5,7},{7,5},{8,10},{10,8},{9,1... | collective-permute-start | bytes 589832 | tf_op jit(solution)/shard_map/ppermute | solution.py:411

commit v3 on v2

--- a/solution.py
+++ b/solution.py
@@ -12,10 +12,22 @@
 bf16, f32 = jnp.bfloat16, jnp.float32
 VMEM_LIMIT = 20 * 2**20
 every = ("dp", "x", "core")
+NEAR = (0, 2, 4, 6, 1, 3, 5, 7)
 
 
 def swap(block, axis):
     return lax.ppermute(block, axis, [(0, 1), (1, 0)])
+
+
+def across(block, axis, apart_by):
+    count = lax.axis_size(axis)
+    return lax.ppermute(block, axis, [(i, i ^ apart_by) for i in range(count)])
+
+
+def gather_eight(block):
+    near = across(block, "dp", 1)
+    far = [across(block, "dp", bits) for bits in NEAR[1:4]]
+    return [block, *far, near, *[across(other, "dp", 1) for other in far]]
 
 
 def exchange(blocks, axis):
@@ -62,6 +74,31 @@
 def apart(wide):
     rank = wide.shape[1] // 2
     return jnp.concatenate([wide[:, :rank], wide[:, rank:]], axis=0)
+
+
+def pack_kernel(n_blocks, placer_ref, *refs):
+    blocks = refs[:n_blocks]
+    outs = refs[n_blocks:]
+    capacity, width = outs[0].shape
+    chunk = width // 6
+    for k in range(6):
+        at = slice(k * chunk, (k + 1) * chunk)
+        rows = jnp.concatenate([block[:, at] for block in blocks], axis=0)
+        packed = dot(placer_ref[...], rows).astype(bf16)
+        for step, out in enumerate(outs):
+            out[:, at] = packed[step * capacity : (step + 1) * capacity]
+
+
+def pack(placer, blocks, capacity):
+    count, width = placer.shape[0], blocks[0].shape[1]
+    return pl.pallas_call(
+        functools.partial(pack_kernel, len(blocks)),
+        in_specs=vmem(1 + len(blocks)),
+        out_specs=vmem(count // capacity),
+        out_shape=[struct((capacity, width), bf16)] * (count // capacity),
+        compiler_params=params(),
+        name="pack",
+    )(placer, *blocks)
 
 
 def low_kernel(n_parts, place_ref, *refs):
@@ -69,27 +106,30 @@
     depth = factor_ref.shape[1]
     if depth < parts[0].shape[1]:
         at = pl.ds(pl.multiple_of(place_ref[0] * depth, depth), depth)
-        rows = jnp.concatenate([r[:, at] for r in parts], axis=0)
     else:
-        rows = jnp.concatenate([r[...] for r in parts], axis=0)
-    piece = beside(dot_last(rows, factor_ref[...]))
-    for i in range(out_ref.shape[0]):
-        out_ref[i] = piece
-
-
-def low_pieces(parts, factor, place, n_dp):
+        at = slice(None)
+    for step in range(n_parts):
+        piece = beside(dot_last(parts[step][:, at], factor_ref[...]))
+        group = lax.rem(place_ref[1] + step, n_parts)
+        for i in range(out_ref.shape[0] // (2 * n_parts)):
+            spot = (i * n_parts + group) * 2
+            out_ref[spot] = piece
+            out_ref[spot + 1] = piece
+
+
+def low_pieces(parts, factor, place, group, n_dp):
     rank, depth = factor.shape
-    half = parts[0].shape[0] * len(parts) // 2
+    capacity = parts[0].shape[0]
     if depth % 128:
         parts = [lax.dynamic_slice_in_dim(part, place * depth, depth, 1) for part in parts]
     return pl.pallas_call(
         functools.partial(low_kernel, len(parts)),
         in_specs=[pl.BlockSpec(memory_space=pltpu.SMEM)] + vmem(len(parts) + 1),
         out_specs=vmem(1)[0],
-        out_shape=struct((n_dp, half, 2 * rank), f32),
+        out_shape=struct((n_dp * len(parts) * 2, capacity // 2, 2 * rank), f32),
         compiler_params=params(),
         name="low_pieces",
-    )(place.reshape(1), *parts, factor)
+    )(jnp.stack([place, group]), *parts, factor)
 
 
 def lift_kernel(n_parts, *refs):
@@ -156,133 +196,233 @@
     )
 
 
-def bring(source, target, sems, blocks, wide):
-    copies, ahead = [], 4
-    for k in range(blocks):
-        at = pl.ds(k * wide, wide)
-        copies.append(pltpu.make_async_copy(source.at[:, at], target.at[:, at], sems.at[k]))
-    for copy in copies[:ahead]:
+def bring(source, target, sems, starts):
+    copies = []
+    for k, start in enumerate(starts):
+        at = pl.ds(start, target.shape[2])
+        copies.append(pltpu.make_async_copy(source.at[:, at], target.at[k], sems.at[k]))
+    for copy in copies:
         copy.start()
-
-    def arrive(k):
-        copies[k].wait()
-        if k + ahead < blocks:
-            copies[k + ahead].start()
-
-    return arrive
+    return copies
 
 
 def down_kernel(
-    base_ref, lifted_ref, low_ref, factor_ref, weight_ref, own_ref, other_ref, pre_ref, low_out, down_ref, sems
+    place_ref, base_ref, lifted_ref, low_ref, factor_ref, weight_ref, own_ref, other_ref, pre_ref, low_out, down_ref, sems
 ):
     blocks, half, wide = own_ref.shape
-    arrive = bring(weight_ref, down_ref, sems, blocks, wide)
-    low = apart(jnp.sum(low_ref[...], axis=0)).astype(bf16)
+    copies = bring(weight_ref, down_ref, sems, [k * wide for k in range(blocks)])
+    groups = low_ref.shape[1]
+    sums = []
+    for core in (place_ref[1], 1 - place_ref[1]):
+        for step in range(groups):
+            group = lax.rem(place_ref[0] - step + groups, groups)
+            sums.append(apart(jnp.sum(low_ref[:, group, core], axis=0)))
+    low = jnp.concatenate(sums, axis=0).astype(bf16)
     pre = base_ref[...] + adapter_scale * dot(low, factor_ref[...])
     low_out[...] = low
     pre_ref[...] = pre
     hidden = (pre * sigmoid(pre) * lifted_ref[...]).astype(bf16)
     for k in range(blocks):
-        arrive(k)
-        partial = dot(hidden, down_ref[:, k * wide : (k + 1) * wide]).astype(bf16)
+        if k % 2 == 0:
+            copies[k].wait()
+            copies[k + 1].wait()
+        partial = dot(hidden, down_ref[k]).astype(bf16)
         own_ref[k] = partial[:half]
         other_ref[k] = partial[half:]
 
 
-def down(base, lifted, low_parts, factor, down_weight, blocks):
+def down(base, lifted, low_parts, factor, down_weight, blocks, group, core):
     count, units = base.shape
     half, width = count // 2, down_weight.shape[1]
     shape = struct((blocks, half, width // blocks), bf16)
     return pl.pallas_call(
         down_kernel,
-        in_specs=vmem(4) + [pl.BlockSpec(memory_space=pl.ANY)],
+        in_specs=[pl.BlockSpec(memory_space=pltpu.SMEM)] + vmem(4) + [pl.BlockSpec(memory_space=pl.ANY)],
         out_specs=vmem(4),
-        scratch_shapes=[pltpu.VMEM(down_weight.shape, bf16), pltpu.SemaphoreType.DMA((blocks,))],
+        scratch_shapes=[
+            pltpu.VMEM((blocks, units, width // blocks), bf16),
+            pltpu.SemaphoreType.DMA((blocks,)),
+        ],
         out_shape=(shape, shape, struct((count, units), f32), struct((count, factor.shape[0]), bf16)),
         cost_estimate=cost(2 * count * width * units, 2 * width * units),
         compiler_params=params(),
         name="down",
-    )(base, lifted, low_parts, factor, pltpu.with_memory_space_constraint(down_weight, pltpu.HBM))
-
-
-def mix_kernel(blocks_ref, gate_ref, out_ref):
-    half = out_ref.shape[1]
-    total = blocks_ref[0].astype(f32)
-    for i in range(1, blocks_ref.shape[0]):
-        total = total + blocks_ref[i].astype(f32)
-    mixed = (gate_ref[:half] * total).astype(bf16)
-    for i in range(out_ref.shape[0]):
-        out_ref[i] = mixed
-
-
-def mix(blocks, gate):
-    return pl.pallas_call(
-        mix_kernel,
+    )(
+        jnp.stack([group, core]),
+        base,
+        lifted,
+        low_parts,
+        factor,
+        pltpu.with_memory_space_constraint(down_weight, pltpu.HBM),
+    )
+
+
+def fold_core_kernel(place_ref, own_ref, got_ref, keep_ref, far_ref, near_ref):
+    line, bit = place_ref[0] // 2, lax.rem(place_ref[0], 2)
+
+    def folded(at):
+        return (own_ref[at].astype(f32) + got_ref[at].astype(f32)).astype(bf16)
+
+    for k in range(4):
+        at = 2 * lax.bitwise_xor(line, k)
+        keep_ref[k] = folded(at + bit)
+        out_ref = near_ref if k < 2 else far_ref
+        out_ref[k % 2] = folded(at + 1 - bit)
+
+
+def fold_core(own, got, place):
+    shapes = [struct((count, *own.shape[1:]), bf16) for count in (4, 2, 2)]
+    return pl.pallas_call(
+        fold_core_kernel,
+        in_specs=[pl.BlockSpec(memory_space=pltpu.SMEM)] + vmem(2),
+        out_specs=vmem(3),
+        out_shape=shapes,
+        compiler_params=params(),
+        name="fold_core",
+    )(place.reshape(1), own, got)
+
+
+def fold_near_kernel(first, keep_ref, got_ref, *out_refs):
+    for k, out_ref in enumerate(out_refs):
+        out_ref[...] = (keep_ref[first + k].astype(f32) + got_ref[k].astype(f32)).astype(bf16)
+
+
+def fold_near(keep, got, first):
+    return pl.pallas_call(
+        functools.partial(fold_near_kernel, first),
         in_specs=vmem(2),
+        out_specs=vmem(2),
+        out_shape=[struct(keep.shape[1:], bf16)] * 2,
+        compiler_params=params(),
+        name="fold_near",
+    )(keep, got)
+
+
+def mix_kernel(n_terms, *refs):
+    gate_ref, out_ref = refs[n_terms:]
+    total = refs[0][...].astype(f32)
+    for term in refs[1:n_terms]:
+        total = total + term[...].astype(f32)
+    out_ref[...] = (gate_ref[: out_ref.shape[0]] * total).astype(bf16)
+
+
+def mix(terms, gate):
+    return pl.pallas_call(
+        functools.partial(mix_kernel, len(terms)),
+        in_specs=vmem(len(terms) + 1),
         out_specs=vmem(1)[0],
-        out_shape=struct(blocks.shape, bf16),
+        out_shape=struct(terms[0].shape, bf16),
         compiler_params=params(),
         name="mix",
-    )(blocks, gate)
-
-
-def back_kernel(n_parts, loss_factor, *refs):
-    parts = refs[:n_parts]
-    (
-        own_ref,
-        other_ref,
-        gate_ref,
-        weight_ref,
-        pre_ref,
-        lifted_ref,
-        low_ref,
-        factor_ref,
-        low_out,
-        grad_ref,
-        down_ref,
-        sems,
-    ) = refs[n_parts:]
-    blocks, half, wide = own_ref.shape
-    arrive = bring(weight_ref, down_ref, sems, blocks, wide)
+    )(*terms, gate)
+
+
+def back_sum(parts, owns, others, starts, gate_ref, weight_ref, down_ref, back_ref, sems, loss_factor):
+    wide = owns[0].shape[1]
+    copies = bring(weight_ref, down_ref, sems, starts)
     scale = loss_factor * gate_ref[...]
-    total = 0.0
-    for k in range(blocks):
-        at = slice(k * wide, (k + 1) * wide)
-        mixed = jnp.concatenate([own_ref[k], other_ref[k]], axis=0).astype(f32)
+    for k, (own, other) in enumerate(zip(owns, others)):
+        at = pl.ds(starts[k], wide)
+        mixed = jnp.concatenate([own[...], other[...]], axis=0).astype(f32)
         rows = jnp.concatenate([r[:, at] for r in parts], axis=0).astype(f32)
-        back = (scale * (mixed - rows)).astype(bf16)
-        arrive(k)
-        total = total + dot_last(down_ref[:, at], back)
+        back_ref[k] = (scale * (mixed - rows)).astype(bf16)
+    for copy in copies:
+        copy.wait()
+    total = dot_last(down_ref[0], back_ref[0])
+    for k in range(1, len(copies)):
+        total = total + dot_last(down_ref[k], back_ref[k])
+    return total
+
+
+def back_first_kernel(n_parts, n_blocks, loss_factor, order_ref, *refs):
+    parts, refs = refs[:n_parts], refs[n_parts:]
+    owns, others, refs = refs[:n_blocks], refs[n_blocks : 2 * n_blocks], refs[2 * n_blocks :]
+    gate_ref, weight_ref, out_ref, *scratch = refs
+    wide = owns[0].shape[1]
+    starts = [pl.multiple_of(order_ref[k] * wide, wide) for k in range(n_blocks)]
+    out_ref[...] = back_sum(parts, owns, others, starts, gate_ref, weight_ref, *scratch, loss_factor)
+
+
+def back_last_kernel(n_parts, n_blocks, loss_factor, order_ref, *refs):
+    parts, refs = refs[:n_parts], refs[n_parts:]
+    owns, refs = refs[: 2 * n_blocks], refs[2 * n_blocks :]
+    others, refs = refs[:n_blocks], refs[n_blocks:]
+    gate_ref, weight_ref, first_ref, pre_ref, lifted_ref, low_ref, factor_ref = refs[:7]
+    low_out, grad_ref, *homes = refs[7:-3]
+    half, wide = owns[0].shape
+    capacity = half // len(homes)
+    starts = [pl.multiple_of(order_ref[k] * wide, wide) for k in range(2 * n_blocks)]
     pre = pre_ref[...]
     sig = sigmoid(pre)
-    slope = sig * (1.0 + pre * (1.0 - sig))
-    back_pre = (total.T * lifted_ref[...] * slope).astype(bf16)
+    slope = lifted_ref[...] * (sig * (1.0 + pre * (1.0 - sig)))
+    total = back_sum(
+        parts, owns[n_blocks:], others, starts[n_blocks:], gate_ref, weight_ref, *refs[-3:], loss_factor
+    )
+    back_pre = ((first_ref[...] + total).T * slope).astype(bf16)
     back_low = beside(adapter_scale * dot_last(back_pre, factor_ref[...])).astype(bf16)
     for i in range(low_out.shape[0]):
         low_out[i] = back_low
     grad_ref[...] = adapter_scale * dot_first(low_ref[...], back_pre)
-
-
-def back(parts, own, other, gate, down_weight, pre, lifted, low, factor, loss_factor, copies):
-    width = parts[0].shape[1]
-    half = own.shape[1]
+    for k, own in enumerate(owns):
+        for step, home in enumerate(homes):
+            home[:, pl.ds(starts[k], wide)] = own[step * capacity : (step + 1) * capacity]
+
+
+def back_scratch(blocks, units, count, wide):
+    return [
+        pltpu.VMEM((blocks, units, wide), bf16),
+        pltpu.VMEM((blocks, count, wide), bf16),
+        pltpu.SemaphoreType.DMA((blocks,)),
+    ]
+
+
+def back_first(parts, owns, others, order, gate, down_weight, loss_factor):
+    units = down_weight.shape[0]
+    count, blocks, wide = gate.shape[0], len(owns), owns[0].shape[1]
+    return pl.pallas_call(
+        functools.partial(back_first_kernel, len(parts), blocks, loss_factor),
+        in_specs=[pl.BlockSpec(memory_space=pltpu.SMEM)]
+        + vmem(len(parts) + 2 * blocks + 1)
+        + [pl.BlockSpec(memory_space=pl.ANY)],
+        out_specs=vmem(1)[0],
+        out_shape=struct((units, count), f32),
+        scratch_shapes=back_scratch(blocks, units, count, wide),
+        cost_estimate=cost(2 * count * blocks * wide * units, 2 * blocks * wide * units),
+        compiler_params=params(),
+        name="back_first",
+    )(order, *parts, *owns, *others, gate, pltpu.with_memory_space_constraint(down_weight, pltpu.HBM))
+
+
+def back_last(parts, owns, others, order, gate, down_weight, first, pre, lifted, low, factor, loss_factor, copies):
+    capacity, width = parts[0].shape
+    half, wide = owns[0].shape
     count, units = pre.shape
-    rank = factor.shape[0]
-    return pl.pallas_call(
-        functools.partial(back_kernel, len(parts), loss_factor),
-        in_specs=vmem(len(parts) + 3) + [pl.BlockSpec(memory_space=pl.ANY)] + vmem(4),
-        out_specs=vmem(2),
-        scratch_shapes=[pltpu.VMEM(down_weight.shape, bf16), pltpu.SemaphoreType.DMA((own.shape[0],))],
-        out_shape=(struct((copies, half, 2 * rank), bf16), struct((rank, units), f32)),
-        cost_estimate=cost(2 * count * width * units, 2 * width * units),
-        compiler_params=params(),
-        name="back",
+    rank, blocks = factor.shape[0], len(others)
+    homes = half // capacity
+    return pl.pallas_call(
+        functools.partial(back_last_kernel, len(parts), blocks, loss_factor),
+        in_specs=[pl.BlockSpec(memory_space=pltpu.SMEM)]
+        + vmem(len(parts) + 3 * blocks + 1)
+        + [pl.BlockSpec(memory_space=pl.ANY)]
+        + vmem(5),
+        out_specs=vmem(2 + homes),
+        out_shape=(
+            struct((copies, half, 2 * rank), bf16),
+            struct((rank, units), f32),
+            *[struct((capacity, width), bf16)] * homes,
+        ),
+        scratch_shapes=back_scratch(blocks, units, count, wide),
+        cost_estimate=cost(2 * count * blocks * wide * units, 2 * blocks * wide * units),
+        compiler_params=params(),
+        name="back_last",
     )(
+        order,
         *parts,
-        own,
-        other,
+        *owns,
+        *others,
         gate,
         pltpu.with_memory_space_constraint(down_weight, pltpu.HBM),
+        first,
         pre,
         lifted,
         low,
@@ -345,35 +485,44 @@
     share = width // devices
     loss_factor = math.sqrt(groups / (tok_rows * devices))
     blocks = 8
-
-    def regroup(array, pieces):
-        if array.shape[0] == pieces:
-            return array
-        flat = array.transpose(1, 0, 2).reshape(array.shape[1], width)
-        return flat.reshape(array.shape[1], pieces, width // pieces).transpose(1, 0, 2)
-
-    column = exchange(jnp.broadcast_to(tokens[None], (n_dp, tok_rows, width)), "dp")
-    column = column.reshape(col_rows, width)
+    eight = n_dp == blocks
+
     labels = expert_choice_table[0]
     index = jnp.arange(col_rows, dtype=jnp.int32)
     before = (labels[None, :] == labels[:, None]) & (index[None, :] < index[:, None])
     ordinal = jnp.sum(before.astype(jnp.int32), axis=1)
     ahead = lax.rem(labels - group + groups, groups)
     target = ahead * capacity + ordinal
-    placer = (index[:, None] == target[None, :]).astype(bf16)
-    packed = dot(placer, column).astype(bf16).reshape(groups, capacity, width)
+    if eight:
+        order = lax.bitwise_xor(jnp.array(NEAR, jnp.int32), place)
+        column = gather_eight(tokens)
+        spread_out = target.reshape(n_dp, tok_rows)
+        arrived = jnp.sum(
+            jnp.where(order[:, None, None] == jnp.arange(n_dp)[None, :, None], spread_out[None], 0), axis=1
+        ).reshape(col_rows)
+    else:
+        order = jnp.arange(blocks, dtype=jnp.int32)
+        column = exchange(jnp.broadcast_to(tokens[None], (n_dp, tok_rows, width)), "dp")
+        column = [column.reshape(col_rows, width)]
+        arrived = target
+    placer = (index[:, None] == arrived[None, :]).astype(bf16)
+    own_route = lax.dynamic_slice_in_dim(router.T, group, 1, 0).astype(f32)
+    column, placer, own_route = lax.optimization_barrier((column, placer, own_route))
+    packed = pack(placer, column, capacity)
     parts = [packed[0]]
     for step in range(1, groups):
         route = [(i, (i + step) % groups) for i in range(groups)]
         parts.append(lax.ppermute(packed[step], "x", route))
     parts = parts + [swap(part, "core") for part in parts]
 
-    low_parts = exchange(low_pieces(parts, adapter_down_shared.T, place, n_dp), "dp")
-    own_route = lax.dynamic_slice_in_dim(router.T, group, 1, 0).astype(f32)
+    low_parts = low_pieces(packed, adapter_down_shared.T, place, group, n_dp)
+    low_parts = exchange(low_parts, every).reshape(n_dp, groups, 2, capacity // 2, 2 * rank)
     base, lifted, gate = lift(parts, gate_weight, up_weight, own_route)
-    own, other, pre, low = down(base, lifted, low_parts, adapter_gate_factor, down_weight, blocks)
-
-    summed = (own.astype(f32) + swap(other, "core").astype(f32)).astype(bf16)
+    low_parts, gate = lax.optimization_barrier((low_parts, gate))
+    own, other, pre, low = down(
+        base, lifted, low_parts, adapter_gate_factor, down_weight, blocks, group, core
+    )
+
     rows = jnp.concatenate(parts, axis=0)
     pieces = []
     for step in range(groups):
@@ -384,17 +533,36 @@
         pieces.append(lax.ppermute(piece, "x", route) if step else piece)
     pieces = jnp.stack(pieces)
 
-    totals, pieces = lax.optimization_barrier((exchange(regroup(summed, n_dp), "dp"), pieces))
-    mixed = mix(totals, gate)
-    mixed_half = regroup(exchange(mixed, "dp"), blocks)
-    mixed_other = swap(mixed_half, "core")
-
-    back_low, grad_b = back(
+    got = swap(other, "core")
+    if eight:
+        keep, far, near = fold_core(own, got, place)
+        far, near = across(far, "dp", 1), across(near, "dp", 1)
+        two, three = fold_near(keep, far, 2)
+        mine, one = fold_near(keep, near, 0)
+        terms = [mine, across(one, "dp", 2), across(two, "dp", 4), across(three, "dp", 6)]
+        terms, pieces = lax.optimization_barrier((terms, pieces))
+        owns = gather_eight(mix(terms, gate))
+    else:
+        summed = (own.astype(f32) + got.astype(f32)).astype(bf16)
+        summed = summed.transpose(1, 0, 2).reshape(half, n_dp, wide).transpose(1, 0, 2)
+        summed = exchange(summed, "dp")
+        mixed = mix([summed[i] for i in range(n_dp)], gate)
+        mixed = exchange(jnp.broadcast_to(mixed[None], (n_dp, half, wide)), "dp")
+        mixed = mixed.transpose(1, 0, 2).reshape(half, width)
+        owns = [mixed[:, i * (width // blocks) : (i + 1) * (width // blocks)] for i in range(blocks)]
+    others = [swap(block, "core") for block in owns]
+
+    first = back_first(
+        parts, owns[: blocks // 2], others[: blocks // 2], order, gate, down_weight, loss_factor
+    )
+    back_low, grad_b, *homes = back_last(
         parts,
-        mixed_half,
-        mixed_other,
+        owns,
+        others[blocks // 2 :],
+        order,
         gate,
         down_weight,
+        first,
         pre,
         lifted,
         low,
@@ -404,18 +572,14 @@
     )
     lows = exchange(back_low, every).reshape(n_dp, groups, 2, half, 2 * rank)
 
-    returned = [mixed_half[:, :capacity]]
-    for step in range(1, groups):
-        route = [(i, (i - step) % groups) for i in range(groups)]
-        part = mixed_half[:, step * capacity : (step + 1) * capacity]
-        returned.append(lax.ppermute(part, "x", route))
     own_target = lax.dynamic_slice_in_dim(target, place * tok_rows, tok_rows, 0)
     result = jnp.zeros((tok_rows, width), f32)
     for step in range(groups):
+        route = [(i, (i - step) % groups) for i in range(groups)]
+        returned = lax.ppermute(homes[step], "x", route) if step else homes[0]
         spot = index[step * capacity : (step + 1) * capacity]
         chooser = (own_target[:, None] == spot[None, :]).astype(bf16)
-        chosen = jnp.einsum("ir,brc->ibc", chooser, returned[step], preferred_element_type=f32)
-        result = result + chosen.reshape(tok_rows, width)
+        result = result + dot(chooser, returned)
 
     grad_a = factor_gradient(lows, pieces, group, core)
     return (result.astype(bf16), grad_a.T, grad_b.T)

time: 104 us -> 94 us (0.904)
  blocking collectives: 15.7 us -> 0 us
  starting transfers between devices: 24.3 us -> 38.3 us
  waiting for transfers between devices: 38.7 us -> 26.9 us
  Pallas kernels: 17.8 us -> 20.5 us
    ppermute x1 -> x20, starting transfers between devices: 1.83 us -> 26.4 us  [the longest x19 24.5 us: across(): return lax.ppermute(block, axis, [(i, i ^ apart_by) for i in range(count)])]
    all_to_all x4 -> x2, waiting for transfers between devices: 19.8 us -> 1.3 us  [exchange(): return lax.all_to_all(blocks, axis, 0, 0, tiled=True)]
    all_to_all x1 -> x0, blocking collectives: 15.7 us -> none  [exchange(): return lax.all_to_all(blocks, axis, 0, 0, tiled=True)]
    ppermute x1 -> x20, waiting for transfers between devices: 7.5 us -> 23 us  [the longest x19 15.2 us: across(): return lax.ppermute(block, axis, [(i, i ^ apart_by) for i in range(count)])]
    all_to_all x4 -> x2, starting transfers between devices: 19.3 us -> 8.12 us  [exchange(): return lax.all_to_all(blocks, axis, 0, 0, tiled=True)]
    ppermute x1, waiting for transfers between devices: 4.18 us -> 0.01 us  [shards(): parts.append(lax.ppermute(packed[step], 'x', route))]
    ppermute x1, waiting for transfers between devices: 2.42 us -> 0.01 us  [shards(): pieces.append(lax.ppermute(piece, 'x', route) if step else piece)]
    pallas_call x3 -> x8, Pallas kernels: 9.9 us -> 12.2 us  [the longest x1 4.43 us: back_last(): pl.pallas_call(functools.partial(back_last_kernel, len(parts), blocks, lo...]
  transfers between devices with their start and end apart: 11 -> 35, of which waited for: 9 -> 14; matrix products, arithmetic and copies ran while one was open for 3% -> 6% of each run, Pallas kernels for 5% -> 11%
where the time goes in v3:
time: 94 us; the launch traced here: 93.5 us
  starting transfers between devices  38.3 us (41%)
  waiting for transfers between devices  26.9 us (29%)
  Pallas kernels  20.5 us (22%)
  other arithmetic  3.44 us (4%)
  local copies, waits for them, and re-layouts  2.41 us (3%)
  matrix products  1.06 us (1%)
    ppermute x19, starting transfers between devices, across(): return lax.ppermute(block, axis, [(i, i ^ apart_by) for i in range(count)])  24.5 us
    ppermute x19, waiting for transfers between devices, across(): return lax.ppermute(block, axis, [(i, i ^ apart_by) for i in range(count)])  15.2 us
    all_to_all x2, starting transfers between devices, exchange(): return lax.all_to_all(blocks, axis, 0, 0, tiled=True)  8.12 us
    ppermute x1, waiting for transfers between devices, shards(): returned = lax.ppermute(homes[step], 'x', route) if step else homes[0]  7.79 us
    pallas_call x1, Pallas kernels, lift(): pl.pallas_call(functools.partial(lift_kernel, len(parts)), in_specs=vmem(...  5.41 us
    pallas_call x1, Pallas kernels, back_last(): pl.pallas_call(functools.partial(back_last_kernel, len(parts), blocks, lo...  4.43 us
    pallas_call x1, Pallas kernels, down(): pl.pallas_call(down_kernel, in_specs=[pl.BlockSpec(memory_space=pltpu.SME...  3.86 us
    pallas_call x1, Pallas kernels, back_first(): pl.pallas_call(functools.partial(back_first_kernel, len(parts), blocks, l...  3.4 us
  transfers between devices with their start and end apart: 35, of which 14 were waited for; matrix products, arithmetic and copies ran while one was open for 6% of the time, Pallas kernels for 11%

profile of v3, /device:TPU:0, one launch (start us, length us, event | category | flops | bytes accessed | tf_op | source)
XLA Modules:
  0.0 93.5 jit_solution(16209895451439318806)
XLA Ops:
  0.6 3.1 %collective-permute-start = (bf16[4,6144]{1,0:T(4,128)(2,1)}, bf16[4,6144]{1,0:T(4,128)(2,1)S(1)}, u32[]{:S(2)}, u32[]{:S(2)}) collective-permute-start(bf16[4,6144]{1,0:T(4,128)(2,1)} %refs_0_), channel_id=1, source_target_pairs={{0,8},{4,12},{8,0},{12,4},{16,24},{20,28},{24,16},{28,20},{1,9},{5... | collective-permute-start | bytes 147464 | tf_op jit(solution)/shard_map/ppermute | solution.py:24
  3.7 2.6 %collective-permute-start.1 = (bf16[4,6144]{1,0:T(4,128)(2,1)}, bf16[4,6144]{1,0:T(4,128)(2,1)S(1)}, u32[]{:S(2)}, u32[]{:S(2)}) collective-permute-start(bf16[4,6144]{1,0:T(4,128)(2,1)} %refs_0_), channel_id=1, source_target_pairs={{0,16},{4,20},{8,24},{12,28},{16,0},{20,4},{24,8},{28,12},{1,17},{... | collective-permute-start | bytes 147464 | tf_op jit(solution)/shard_map/ppermute | solution.py:24
  6.3 1.7 %collective-permute-start.3 = (bf16[4,6144]{1,0:T(4,128)(2,1)}, bf16[4,6144]{1,0:T(4,128)(2,1)S(1)}, u32[]{:S(2)}, u32[]{:S(2)}) collective-permute-start(bf16[4,6144]{1,0:T(4,128)(2,1)} %refs_0_), channel_id=1, source_target_pairs={{0,4},{4,0},{8,12},{12,8},{16,20},{20,16},{24,28},{28,24},{1,5},{5... | collective-permute-start | bytes 147464 | tf_op jit(solution)/shard_map/ppermute | solution.py:24
  12.1 1.7 %collective-permute-start.5 = (bf16[4,6144]{1,0:T(4,128)(2,1)S(1)}, bf16[4,6144]{1,0:T(4,128)(2,1)S(1)}, u32[]{:S(2)}, u32[]{:S(2)}) collective-permute-start(bf16[4,6144]{1,0:T(4,128)(2,1)S(1)} %collective-permute-done.1.refs_2_), channel_id=1, source_target_pairs={{0,4},{4,0},{8,12},{12,8},{16,20},{20,16},{24,28},{28,24},{1,5},{5... | collective-permute-start | bytes 147464 | tf_op jit(solution)/shard_map/ppermute | solution.py:24
  14.2 1.7 %collective-permute-done.4.refs_5_ = bf16[4,6144]{1,0:T(4,128)(2,1)S(1)} collective-permute-done((bf16[4,6144]{1,0:T(4,128)(2,1)S(1)}, bf16[4,6144]{1,0:T(4,128)(2,1)S(1)}, u32[]{:S(2)}, u32[]{:S(2)}) %collective-permute-start.4) | collective-permute-done | bytes 49184 | tf_op jit(solution)/shard_map/ppermute | solution.py:24
  16.5 1.5 %collective-permute-done.6.refs_7_ = bf16[4,6144]{1,0:T(4,128)(2,1)S(1)} collective-permute-done((bf16[4,6144]{1,0:T(4,128)(2,1)S(1)}, bf16[4,6144]{1,0:T(4,128)(2,1)S(1)}, u32[]{:S(2)}, u32[]{:S(2)}) %collective-permute-start.6) | collective-permute-done | bytes 49184 | tf_op jit(solution)/shard_map/ppermute | solution.py:24
  19.0 1.6 %collective-permute-start.7 = (bf16[16,6144]{1,0:T(8,128)(2,1)S(1)}, bf16[16,6144]{1,0:T(8,128)(2,1)S(1)}, u32[]{:S(2)}, u32[]{:S(2)}) collective-permute-start(bf16[16,6144]{1,0:T(8,128)(2,1)S(1)} %get-tuple-element.50.refs_1_), channel_id=1, source_target_pairs={{0,2},{2,0},{1,3},{3,1},{4,6},{6,4},{5,7},{7,5},{8,10},{10,8},{9,1... | collective-permute-start | bytes 589832 | tf_op jit(solution)/shard_map/ppermute | solution.py:515
  21.6 1.4 %low_pieces.1 = f32[32,8,128]{2,1,0:T(8,128)} custom-call(s32[2]{0:T(128)S(1)} %pad_add_fusion.1.place_ref, bf16[16,6144]{1,0:T(8,128)(2,1)S(1)} %get-tuple-element.49.refs_0_, bf16[16,6144]{1,0:T(8,128)(2,1)S(1)} %get-tuple-element.50.refs_1_, bf16[64,768]{1,0:T(8,128)(2,1)S(1)} %bitcast.21), custom_call_target="tpu_custom_call" | custom-call | tf_op jit(solution)/shard_map/low_pieces/pallas_call | solution.py:125
  23.0 4.1 %all-to-all-start = ((f32[32,8,128]{2,1,0:T(8,128)}), f32[32,8,128]{2,1,0:T(8,128)S(1)}, u32[]{:S(2)}, u32[]{:S(2)}) async-start(f32[32,8,128]{2,1,0:T(8,128)} %low_pieces.1), calls=%async_computation | async-start | bytes 262144 | tf_op jit(solution)/shard_map/all_to_all | solution.py:34
  27.5 1.1 %collective-permute-done.9.refs_3_ = bf16[16,6144]{1,0:T(8,128)(2,1)S(1)} collective-permute-done((bf16[16,6144]{1,0:T(8,128)(2,1)S(1)}, bf16[16,6144]{1,0:T(8,128)(2,1)S(1)}, u32[]{:S(2)}, u32[]{:S(2)}) %collective-permute-start.9) | collective-permute-done | bytes 196640 | tf_op jit(solution)/shard_map/ppermute | solution.py:19
  28.6 5.4 %lift.1 = (f32[64,512]{1,0:T(8,128)S(1)}, f32[64,512]{1,0:T(8,128)S(1)}, f32[64,1]{1,0:T(8,128)S(1)}) custom-call(bf16[16,6144]{1,0:T(8,128)(2,1)S(1)} %get-tuple-element.49.refs_0_, bf16[16,6144]{1,0:T(8,128)(2,1)S(1)} %collective-permute-done.7.refs_1_, bf16[16,6144]{1,0:T(8,128)(2,1)S(1)} %collective-permute-done.8.refs_2_, ...), custom_call_target="tpu_custom_call" | custom-call | flops 805306368 | bytes 12582912 | tf_op jit(solution)/shard_map/lift/pallas_call | solution.py:174
  34.0 1.3 %all-to-all-done = f32[32,8,128]{2,1,0:T(8,128)S(1)} async-done(((f32[32,8,128]{2,1,0:T(8,128)}), f32[32,8,128]{2,1,0:T(8,128)S(1)}, u32[]{:S(2)}, u32[]{:S(2)}) %all-to-all-start) | async-done | bytes 131104 | tf_op jit(solution)/shard_map/all_to_all | solution.py:34
  35.3 3.9 %down.1 = (bf16[8,32,768]{2,1,0:T(8,128)(2,1)S(1)}, bf16[8,32,768]{2,1,0:T(8,128)(2,1)S(1)}, f32[64,512]{1,0:T(8,128)S(1)}, bf16[64,64]{1,0:T(8,128)(2,1)S(1)}) custom-call(s32[2]{0:T(128)S(1)} %pad_add_fusion.place_ref, f32[64,512]{1,0:T(8,128)S(1)} %get-tuple-element.52.base_ref, f32[64,512]{1,0:T(8,128)S(1)} %get-tuple-element.53.lifted_ref.refs_20_, ...), custom_call_target="tpu_custom_call" | custom-call | flops 402653184 | bytes 6291456 | tf_op jit(solution)/shard_map/down/pallas_call | solution.py:238
  39.5 1.5 %collective-permute-done.10.got_ref = bf16[8,32,768]{2,1,0:T(8,128)(2,1)S(1)} collective-permute-done((bf16[8,32,768]{2,1,0:T(8,128)(2,1)S(1)}, bf16[8,32,768]{2,1,0:T(8,128)(2,1)S(1)}, u32[]{:S(2)}, u32[]{:S(2)}) %collective-permute-start.10) | collective-permute-done | bytes 393248 | tf_op jit(solution)/shard_map/ppermute | solution.py:19
  41.8 1.4 %collective-permute-start.11 = (bf16[2,32,768]{2,1,0:T(8,128)(2,1)S(1)}, bf16[2,32,768]{2,1,0:T(8,128)(2,1)S(1)}, u32[]{:S(2)}, u32[]{:S(2)}) collective-permute-start(bf16[2,32,768]{2,1,0:T(8,128)(2,1)S(1)} %get-tuple-element.59), channel_id=1, source_target_pairs={{0,4},{4,0},{8,12},{12,8},{16,20},{20,16},{24,28},{28,24},{1,5},{5... | collective-permute-start | bytes 294920 | tf_op jit(solution)/shard_map/ppermute | solution.py:24
  43.8 2.9 %collective-permute-done.13.got_ref = bf16[2,32,768]{2,1,0:T(8,128)(2,1)S(1)} collective-permute-done((bf16[2,32,768]{2,1,0:T(8,128)(2,1)S(1)}, bf16[2,32,768]{2,1,0:T(8,128)(2,1)S(1)}, u32[]{:S(2)}, u32[]{:S(2)}) %collective-permute-start.13) | collective-permute-done | bytes 98336 | tf_op jit(solution)/shard_map/ppermute | solution.py:24
  46.8 1.5 %collective-permute-start.14 = (bf16[32,768]{1,0:T(8,128)(2,1)S(1)}, bf16[32,768]{1,0:T(8,128)(2,1)S(1)}, u32[]{:S(2)}, u32[]{:S(2)}) collective-permute-start(bf16[32,768]{1,0:T(8,128)(2,1)S(1)} %get-tuple-element.63), channel_id=1, source_target_pairs={{0,16},{4,20},{8,24},{12,28},{16,0},{20,4},{24,8},{28,12},{1,17},{... | collective-permute-start | bytes 147464 | tf_op jit(solution)/shard_map/ppermute | solution.py:24
  48.3 1.6 %collective-permute-start.15 = (bf16[32,768]{1,0:T(8,128)(2,1)S(1)}, bf16[32,768]{1,0:T(8,128)(2,1)S(1)}, u32[]{:S(2)}, u32[]{:S(2)}) collective-permute-start(bf16[32,768]{1,0:T(8,128)(2,1)S(1)} %get-tuple-element.64), channel_id=1, source_target_pairs={{0,24},{4,28},{8,16},{12,20},{16,8},{20,12},{24,0},{28,4},{1,25},{... | collective-permute-start | bytes 147464 | tf_op jit(solution)/shard_map/ppermute | solution.py:24
  50.5 2.0 %collective-permute-done.14.refs_2_ = bf16[32,768]{1,0:T(8,128)(2,1)S(1)} collective-permute-done((bf16[32,768]{1,0:T(8,128)(2,1)S(1)}, bf16[32,768]{1,0:T(8,128)(2,1)S(1)}, u32[]{:S(2)}, u32[]{:S(2)}) %collective-permute-start.14) | collective-permute-done | bytes 49184 | tf_op jit(solution)/shard_map/ppermute | solution.py:24
  52.5 1.8 %collective-permute-done.15.refs_3_ = bf16[32,768]{1,0:T(8,128)(2,1)S(1)} collective-permute-done((bf16[32,768]{1,0:T(8,128)(2,1)S(1)}, bf16[32,768]{1,0:T(8,128)(2,1)S(1)}, u32[]{:S(2)}, u32[]{:S(2)}) %collective-permute-start.15) | collective-permute-done | bytes 49184 | tf_op jit(solution)/shard_map/ppermute | solution.py:24
  54.9 2.3 %collective-permute-start.18 = (bf16[32,768]{1,0:T(8,128)(2,1)S(1)}, bf16[32,768]{1,0:T(8,128)(2,1)S(1)}, u32[]{:S(2)}, u32[]{:S(2)}) collective-permute-start(bf16[32,768]{1,0:T(8,128)(2,1)S(1)} %mix.1.refs_4_), channel_id=1, source_target_pairs={{0,16},{4,20},{8,24},{12,28},{16,0},{20,4},{24,8},{28,12},{1,17},{... | collective-permute-start | bytes 147464 | tf_op jit(solution)/shard_map/ppermute | solution.py:24
  57.2 2.1 %collective-permute-start.19 = (bf16[32,768]{1,0:T(8,128)(2,1)S(1)}, bf16[32,768]{1,0:T(8,128)(2,1)S(1)}, u32[]{:S(2)}, u32[]{:S(2)}) collective-permute-start(bf16[32,768]{1,0:T(8,128)(2,1)S(1)} %mix.1.refs_4_), channel_id=1, source_target_pairs={{0,24},{4,28},{8,16},{12,20},{16,8},{20,12},{24,0},{28,4},{1,25},{... | collective-permute-start | bytes 147464 | tf_op jit(solution)/shard_map/ppermute | solution.py:24
  60.9 2.1 %collective-permute-done.19.refs_7_ = bf16[32,768]{1,0:T(8,128)(2,1)S(1)} collective-permute-done((bf16[32,768]{1,0:T(8,128)(2,1)S(1)}, bf16[32,768]{1,0:T(8,128)(2,1)S(1)}, u32[]{:S(2)}, u32[]{:S(2)}) %collective-permute-start.19) | collective-permute-done | bytes 49184 | tf_op jit(solution)/shard_map/ppermute | solution.py:24
  63.1 1.5 %collective-permute-start.21 = (bf16[32,768]{1,0:T(8,128)(2,1)S(1)}, bf16[32,768]{1,0:T(8,128)(2,1)S(1)}, u32[]{:S(2)}, u32[]{:S(2)}) collective-permute-start(bf16[32,768]{1,0:T(8,128)(2,1)S(1)} %collective-permute-done.17.refs_5_), channel_id=1, source_target_pairs={{0,4},{4,0},{8,12},{12,8},{16,20},{20,16},{24,28},{28,24},{1,5},{5... | collective-permute-start | bytes 147464 | tf_op jit(solution)/shard_map/ppermute | solution.py:24
  65.1 1.5 %collective-permute-start.23 = (bf16[32,768]{1,0:T(8,128)(2,1)S(1)}, bf16[32,768]{1,0:T(8,128)(2,1)S(1)}, u32[]{:S(2)}, u32[]{:S(2)}) collective-permute-start(bf16[32,768]{1,0:T(8,128)(2,1)S(1)} %collective-permute-done.19.refs_7_), channel_id=1, source_target_pairs={{0,4},{4,0},{8,12},{12,8},{16,20},{20,16},{24,28},{28,24},{1,5},{5... | collective-permute-start | bytes 147464 | tf_op jit(solution)/shard_map/ppermute | solution.py:24
  67.2 1.5 %collective-permute-done.22.refs_10_ = bf16[32,768]{1,0:T(8,128)(2,1)S(1)} collective-permute-done((bf16[32,768]{1,0:T(8,128)(2,1)S(1)}, bf16[32,768]{1,0:T(8,128)(2,1)S(1)}, u32[]{:S(2)}, u32[]{:S(2)}) %collective-permute-start.22) | collective-permute-done | bytes 49184 | tf_op jit(solution)/shard_map/ppermute | solution.py:24
  69.2 3.4 %back_first.1.refs_18_ = f32[512,64]{1,0:T(8,128)S(1)} custom-call(s32[8]{0:T(128)S(1)} %broadcast_xor_fusion.order_ref, bf16[16,6144]{1,0:T(8,128)(2,1)S(1)} %get-tuple-element.49.refs_0_, bf16[16,6144]{1,0:T(8,128)(2,1)S(1)} %collective-permute-done.7.refs_1_, bf16[16,6144]{1,0:T(8,128)(2,1)S(1)} %collective-permute-done.8.refs_2_, ...), custom_call_target="tpu_custom_call" | custom-call | flops 201326592 | bytes 3145728 | tf_op jit(solution)/shard_map/back_first/pallas_call | solution.py:382
  72.6 4.4 %back_last.1 = (bf16[32,32,128]{2,1,0:T(8,128)(2,1)}, f32[64,512]{1,0:T(8,128)}, bf16[16,6144]{1,0:T(8,128)(2,1)S(1)}, bf16[16,6144]{1,0:T(8,128)(2,1)S(1)}) custom-call(s32[8]{0:T(128)S(1)} %broadcast_xor_fusion.order_ref, bf16[16,6144]{1,0:T(8,128)(2,1)S(1)} %get-tuple-element.49.refs_0_, bf16[16,6144]{1,0:T(8,128)(2,1)S(1)} %collective-permute-done.7.refs_1_, ...), custom_call_target="tpu_custom_call" | custom-call | flops 201326592 | bytes 3145728 | tf_op jit(solution)/shard_map/back_last/pallas_call | solution.py:402
  77.1 4.0 %all-to-all-start.1 = ((bf16[32,32,128]{2,1,0:T(8,128)(2,1)}), bf16[32,32,128]{2,1,0:T(8,128)(2,1)S(1)}, u32[]{:S(2)}, u32[]{:S(2)}) async-start(bf16[32,32,128]{2,1,0:T(8,128)(2,1)} %get-tuple-element.74), calls=%async_computation.1 | async-start | bytes 524288 | tf_op jit(solution)/shard_map/all_to_all | solution.py:34
  81.1 1.8 %collective-permute-start.32 = (bf16[16,6144]{1,0:T(8,128)(2,1)S(1)}, bf16[16,6144]{1,0:T(8,128)(2,1)S(1)}, u32[]{:S(2)}, u32[]{:S(2)}) collective-permute-start(bf16[16,6144]{1,0:T(8,128)(2,1)S(1)} %get-tuple-element.73), channel_id=1, source_target_pairs={{0,2},{2,0},{1,3},{3,1},{4,6},{6,4},{5,7},{7,5},{8,10},{10,8},{9,1... | collective-permute-start | bytes 589832 | tf_op jit(solution)/shard_map/ppermute | solution.py:579
  83.1 7.8 %collective-permute-done.32 = bf16[16,6144]{1,0:T(8,128)(2,1)S(1)} collective-permute-done((bf16[16,6144]{1,0:T(8,128)(2,1)S(1)}, bf16[16,6144]{1,0:T(8,128)(2,1)S(1)}, u32[]{:S(2)}, u32[]{:S(2)}) %collective-permute-start.32) | collective-permute-done | bytes 196640 | tf_op jit(solution)/shard_map/ppermute | solution.py:579
  92.0 1.5 %factor_gradient.1 = f32[64,192]{1,0:T(8,128)} custom-call(s32[2]{0:T(128)S(1)} %pad_add_fusion.place_ref, bf16[8,2,2,32,128]{4,3,2,1,0:T(8,128)(2,1)S(1)} %bitcast.19, bf16[2,64,192]{2,1,0:T(8,128)(2,1)S(1)} %pad_maximum_fusion.piece_ref), custom_call_target="tpu_custom_call" | custom-call | tf_op jit(solution)/shard_map/factor_gradient/pallas_call | solution.py:453
  (85 shorter events, 14.8 us)
Async XLA Ops:
  0.6 11.2 %collective-permute-start = (bf16[4,6144]{1,0:T(4,128)(2,1)}, bf16[4,6144]{1,0:T(4,128)(2,1)S(1)}, u32[]{:S(2)}, u32[]{:S(2)}) collective-permute-start(bf16[4,6144]{1,0:T(4,128)(2,1)} %refs_0_), channel_id=1, source_target_pairs={{0,8},{4,12},{8,0},{12,4},{16,24},{20,28},{24,16},{28,20},{1,9},{5... | collective-permute-start | bytes 147464 | tf_op jit(solution)/shard_map/ppermute | solution.py:24
  3.7 8.4 %collective-permute-start.1 = (bf16[4,6144]{1,0:T(4,128)(2,1)}, bf16[4,6144]{1,0:T(4,128)(2,1)S(1)}, u32[]{:S(2)}, u32[]{:S(2)}) collective-permute-start(bf16[4,6144]{1,0:T(4,128)(2,1)} %refs_0_), channel_id=1, source_target_pairs={{0,16},{4,20},{8,24},{12,28},{16,0},{20,4},{24,8},{28,12},{1,17},{... | collective-permute-start | bytes 147464 | tf_op jit(solution)/shard_map/ppermute | solution.py:24
  6.3 7.6 %collective-permute-start.2 = (bf16[4,6144]{1,0:T(4,128)(2,1)}, bf16[4,6144]{1,0:T(4,128)(2,1)S(1)}, u32[]{:S(2)}, u32[]{:S(2)}) collective-permute-start(bf16[4,6144]{1,0:T(4,128)(2,1)} %refs_0_), channel_id=1, source_target_pairs={{0,24},{4,28},{8,16},{12,20},{16,8},{20,12},{24,0},{28,4},{1,25},{... | collective-permute-start | bytes 147464 | tf_op jit(solution)/shard_map/ppermute | solution.py:24
  6.3 7.9 %collective-permute-start.3 = (bf16[4,6144]{1,0:T(4,128)(2,1)}, bf16[4,6144]{1,0:T(4,128)(2,1)S(1)}, u32[]{:S(2)}, u32[]{:S(2)}) collective-permute-start(bf16[4,6144]{1,0:T(4,128)(2,1)} %refs_0_), channel_id=1, source_target_pairs={{0,4},{4,0},{8,12},{12,8},{16,20},{20,16},{24,28},{28,24},{1,5},{5... | collective-permute-start | bytes 147464 | tf_op jit(solution)/shard_map/ppermute | solution.py:24
  11.8 4.1 %collective-permute-start.4 = (bf16[4,6144]{1,0:T(4,128)(2,1)S(1)}, bf16[4,6144]{1,0:T(4,128)(2,1)S(1)}, u32[]{:S(2)}, u32[]{:S(2)}) collective-permute-start(bf16[4,6144]{1,0:T(4,128)(2,1)S(1)} %collective-permute-done.refs_1_), channel_id=1, source_target_pairs={{0,4},{4,0},{8,12},{12,8},{16,20},{20,16},{24,28},{28,24},{1,5},{5... | collective-permute-start | bytes 147464 | tf_op jit(solution)/shard_map/ppermute | solution.py:24
  12.1 4.3 %collective-permute-start.5 = (bf16[4,6144]{1,0:T(4,128)(2,1)S(1)}, bf16[4,6144]{1,0:T(4,128)(2,1)S(1)}, u32[]{:S(2)}, u32[]{:S(2)}) collective-permute-start(bf16[4,6144]{1,0:T(4,128)(2,1)S(1)} %collective-permute-done.1.refs_2_), channel_id=1, source_target_pairs={{0,4},{4,0},{8,12},{12,8},{16,20},{20,16},{24,28},{28,24},{1,5},{5... | collective-permute-start | bytes 147464 | tf_op jit(solution)/shard_map/ppermute | solution.py:24
  13.9 4.1 %collective-permute-start.6 = (bf16[4,6144]{1,0:T(4,128)(2,1)S(1)}, bf16[4,6144]{1,0:T(4,128)(2,1)S(1)}, u32[]{:S(2)}, u32[]{:S(2)}) collective-permute-start(bf16[4,6144]{1,0:T(4,128)(2,1)S(1)} %collective-permute-done.2.refs_3_), channel_id=1, source_target_pairs={{0,4},{4,0},{8,12},{12,8},{16,20},{20,16},{24,28},{28,24},{1,5},{5... | collective-permute-start | bytes 147464 | tf_op jit(solution)/shard_map/ppermute | solution.py:24
  19.0 8.1 %collective-permute-start.7 = (bf16[16,6144]{1,0:T(8,128)(2,1)S(1)}, bf16[16,6144]{1,0:T(8,128)(2,1)S(1)}, u32[]{:S(2)}, u32[]{:S(2)}) collective-permute-start(bf16[16,6144]{1,0:T(8,128)(2,1)S(1)} %get-tuple-element.50.refs_1_), channel_id=1, source_target_pairs={{0,2},{2,0},{1,3},{3,1},{4,6},{6,4},{5,7},{7,5},{8,10},{10,8},{9,1... | collective-permute-start | bytes 589832 | tf_op jit(solution)/shard_map/ppermute | solution.py:515
  20.6 6.8 %collective-permute-start.8 = (bf16[16,6144]{1,0:T(8,128)(2,1)S(1)}, bf16[16,6144]{1,0:T(8,128)(2,1)S(1)}, u32[]{:S(2)}, u32[]{:S(2)}) collective-permute-start(bf16[16,6144]{1,0:T(8,128)(2,1)S(1)} %get-tuple-element.49.refs_0_), channel_id=1, source_target_pairs={{0,1},{1,0},{2,3},{3,2},{4,5},{5,4},{6,7},{7,6},{8,9},{9,8},{10,11... | collective-permute-start | bytes 589832 | tf_op jit(solution)/shard_map/ppermute | solution.py:19
  23.0 12.3 %all-to-all-start = ((f32[32,8,128]{2,1,0:T(8,128)}), f32[32,8,128]{2,1,0:T(8,128)S(1)}, u32[]{:S(2)}, u32[]{:S(2)}) async-start(f32[32,8,128]{2,1,0:T(8,128)} %low_pieces.1), calls=%async_computation | async-start | bytes 262144 | tf_op jit(solution)/shard_map/all_to_all | solution.py:34
  41.1 5.7 %collective-permute-start.13 = (bf16[2,32,768]{2,1,0:T(8,128)(2,1)S(1)}, bf16[2,32,768]{2,1,0:T(8,128)(2,1)S(1)}, u32[]{:S(2)}, u32[]{:S(2)}) collective-permute-start(bf16[2,32,768]{2,1,0:T(8,128)(2,1)S(1)} %get-tuple-element.62), channel_id=1, source_target_pairs={{0,4},{4,0},{8,12},{12,8},{16,20},{20,16},{24,28},{28,24},{1,5},{5... | collective-permute-start | bytes 294920 | tf_op jit(solution)/shard_map/ppermute | solution.py:24
  41.8 8.1 %collective-permute-start.11 = (bf16[2,32,768]{2,1,0:T(8,128)(2,1)S(1)}, bf16[2,32,768]{2,1,0:T(8,128)(2,1)S(1)}, u32[]{:S(2)}, u32[]{:S(2)}) collective-permute-start(bf16[2,32,768]{2,1,0:T(8,128)(2,1)S(1)} %get-tuple-element.59), channel_id=1, source_target_pairs={{0,4},{4,0},{8,12},{12,8},{16,20},{20,16},{24,28},{28,24},{1,5},{5... | collective-permute-start | bytes 294920 | tf_op jit(solution)/shard_map/ppermute | solution.py:24
  43.3 7.2 %collective-permute-start.16 = (bf16[64,192]{1,0:T(8,128)(2,1)S(1)}, bf16[64,192]{1,0:T(8,128)(2,1)S(1)}, u32[]{:S(2)}, u32[]{:S(2)}) collective-permute-start(bf16[64,192]{1,0:T(8,128)(2,1)S(1)} %get-tuple-element.78), channel_id=1, source_target_pairs={{0,2},{2,0},{1,3},{3,1},{4,6},{6,4},{5,7},{7,5},{8,10},{10,8},{9,1... | collective-permute-start | bytes 73736 | tf_op jit(solution)/shard_map/ppermute | solution.py:533
  46.8 5.7 %collective-permute-start.14 = (bf16[32,768]{1,0:T(8,128)(2,1)S(1)}, bf16[32,768]{1,0:T(8,128)(2,1)S(1)}, u32[]{:S(2)}, u32[]{:S(2)}) collective-permute-start(bf16[32,768]{1,0:T(8,128)(2,1)S(1)} %get-tuple-element.63), channel_id=1, source_target_pairs={{0,16},{4,20},{8,24},{12,28},{16,0},{20,4},{24,8},{28,12},{1,17},{... | collective-permute-start | bytes 147464 | tf_op jit(solution)/shard_map/ppermute | solution.py:24
  48.3 6.0 %collective-permute-start.15 = (bf16[32,768]{1,0:T(8,128)(2,1)S(1)}, bf16[32,768]{1,0:T(8,128)(2,1)S(1)}, u32[]{:S(2)}, u32[]{:S(2)}) collective-permute-start(bf16[32,768]{1,0:T(8,128)(2,1)S(1)} %get-tuple-element.64), channel_id=1, source_target_pairs={{0,24},{4,28},{8,16},{12,20},{16,8},{20,12},{24,0},{28,4},{1,25},{... | collective-permute-start | bytes 147464 | tf_op jit(solution)/shard_map/ppermute | solution.py:24
  49.9 4.9 %collective-permute-start.12 = (bf16[32,768]{1,0:T(8,128)(2,1)S(1)}, bf16[32,768]{1,0:T(8,128)(2,1)S(1)}, u32[]{:S(2)}, u32[]{:S(2)}) collective-permute-start(bf16[32,768]{1,0:T(8,128)(2,1)S(1)} %get-tuple-element.61), channel_id=1, source_target_pairs={{0,8},{4,12},{8,0},{12,4},{16,24},{20,28},{24,16},{28,20},{1,9},{5... | collective-permute-start | bytes 147464 | tf_op jit(solution)/shard_map/ppermute | solution.py:24
  54.9 5.5 %collective-permute-start.17 = (bf16[32,768]{1,0:T(8,128)(2,1)S(1)}, bf16[32,768]{1,0:T(8,128)(2,1)S(1)}, u32[]{:S(2)}, u32[]{:S(2)}) collective-permute-start(bf16[32,768]{1,0:T(8,128)(2,1)S(1)} %mix.1.refs_4_), channel_id=1, source_target_pairs={{0,8},{4,12},{8,0},{12,4},{16,24},{20,28},{24,16},{28,20},{1,9},{5... | collective-permute-start | bytes 147464 | tf_op jit(solution)/shard_map/ppermute | solution.py:24
  54.9 5.7 %collective-permute-start.18 = (bf16[32,768]{1,0:T(8,128)(2,1)S(1)}, bf16[32,768]{1,0:T(8,128)(2,1)S(1)}, u32[]{:S(2)}, u32[]{:S(2)}) collective-permute-start(bf16[32,768]{1,0:T(8,128)(2,1)S(1)} %mix.1.refs_4_), channel_id=1, source_target_pairs={{0,16},{4,20},{8,24},{12,28},{16,0},{20,4},{24,8},{28,12},{1,17},{... | collective-permute-start | bytes 147464 | tf_op jit(solution)/shard_map/ppermute | solution.py:24
  57.2 5.9 %collective-permute-start.19 = (bf16[32,768]{1,0:T(8,128)(2,1)S(1)}, bf16[32,768]{1,0:T(8,128)(2,1)S(1)}, u32[]{:S(2)}, u32[]{:S(2)}) collective-permute-start(bf16[32,768]{1,0:T(8,128)(2,1)S(1)} %mix.1.refs_4_), channel_id=1, source_target_pairs={{0,24},{4,28},{8,16},{12,20},{16,8},{20,12},{24,0},{28,4},{1,25},{... | collective-permute-start | bytes 147464 | tf_op jit(solution)/shard_map/ppermute | solution.py:24
  59.3 5.3 %collective-permute-start.28 = (bf16[32,768]{1,0:T(8,128)(2,1)S(1)}, bf16[32,768]{1,0:T(8,128)(2,1)S(1)}, u32[]{:S(2)}, u32[]{:S(2)}) collective-permute-start(bf16[32,768]{1,0:T(8,128)(2,1)S(1)} %mix.1.refs_4_), channel_id=1, source_target_pairs={{0,1},{1,0},{2,3},{3,2},{4,5},{5,4},{6,7},{7,6},{8,9},{9,8},{10,11... | collective-permute-start | bytes 147464 | tf_op jit(solution)/shard_map/ppermute | solution.py:19
  59.3 5.8 %collective-permute-start.20 = (bf16[32,768]{1,0:T(8,128)(2,1)S(1)}, bf16[32,768]{1,0:T(8,128)(2,1)S(1)}, u32[]{:S(2)}, u32[]{:S(2)}) collective-permute-start(bf16[32,768]{1,0:T(8,128)(2,1)S(1)} %mix.1.refs_4_), channel_id=1, source_target_pairs={{0,4},{4,0},{8,12},{12,8},{16,20},{20,16},{24,28},{28,24},{1,5},{5... | collective-permute-start | bytes 147464 | tf_op jit(solution)/shard_map/ppermute | solution.py:24
  60.4 6.2 %collective-permute-start.29 = (bf16[32,768]{1,0:T(8,128)(2,1)S(1)}, bf16[32,768]{1,0:T(8,128)(2,1)S(1)}, u32[]{:S(2)}, u32[]{:S(2)}) collective-permute-start(bf16[32,768]{1,0:T(8,128)(2,1)S(1)} %collective-permute-done.17.refs_5_), channel_id=1, source_target_pairs={{0,1},{1,0},{2,3},{3,2},{4,5},{5,4},{6,7},{7,6},{8,9},{9,8},{10,11... | collective-permute-start | bytes 147464 | tf_op jit(solution)/shard_map/ppermute | solution.py:19
  60.6 6.0 %collective-permute-start.30 = (bf16[32,768]{1,0:T(8,128)(2,1)S(1)}, bf16[32,768]{1,0:T(8,128)(2,1)S(1)}, u32[]{:S(2)}, u32[]{:S(2)}) collective-permute-start(bf16[32,768]{1,0:T(8,128)(2,1)S(1)} %collective-permute-done.18.refs_6_), channel_id=1, source_target_pairs={{0,1},{1,0},{2,3},{3,2},{4,5},{5,4},{6,7},{7,6},{8,9},{9,8},{10,11... | collective-permute-start | bytes 147464 | tf_op jit(solution)/shard_map/ppermute | solution.py:19
  63.1 4.1 %collective-permute-start.21 = (bf16[32,768]{1,0:T(8,128)(2,1)S(1)}, bf16[32,768]{1,0:T(8,128)(2,1)S(1)}, u32[]{:S(2)}, u32[]{:S(2)}) collective-permute-start(bf16[32,768]{1,0:T(8,128)(2,1)S(1)} %collective-permute-done.17.refs_5_), channel_id=1, source_target_pairs={{0,4},{4,0},{8,12},{12,8},{16,20},{20,16},{24,28},{28,24},{1,5},{5... | collective-permute-start | bytes 147464 | tf_op jit(solution)/shard_map/ppermute | solution.py:24
  64.6 4.1 %collective-permute-start.22 = (bf16[32,768]{1,0:T(8,128)(2,1)S(1)}, bf16[32,768]{1,0:T(8,128)(2,1)S(1)}, u32[]{:S(2)}, u32[]{:S(2)}) collective-permute-start(bf16[32,768]{1,0:T(8,128)(2,1)S(1)} %collective-permute-done.18.refs_6_), channel_id=1, source_target_pairs={{0,4},{4,0},{8,12},{12,8},{16,20},{20,16},{24,28},{28,24},{1,5},{5... | collective-permute-start | bytes 147464 | tf_op jit(solution)/shard_map/ppermute | solution.py:24
  65.1 4.1 %collective-permute-start.23 = (bf16[32,768]{1,0:T(8,128)(2,1)S(1)}, bf16[32,768]{1,0:T(8,128)(2,1)S(1)}, u32[]{:S(2)}, u32[]{:S(2)}) collective-permute-start(bf16[32,768]{1,0:T(8,128)(2,1)S(1)} %collective-permute-done.19.refs_7_), channel_id=1, source_target_pairs={{0,4},{4,0},{8,12},{12,8},{16,20},{20,16},{24,28},{28,24},{1,5},{5... | collective-permute-start | bytes 147464 | tf_op jit(solution)/shard_map/ppermute | solution.py:24
  66.6 6.0 %collective-permute-start.24 = (bf16[32,768]{1,0:T(8,128)(2,1)S(1)}, bf16[32,768]{1,0:T(8,128)(2,1)S(1)}, u32[]{:S(2)}, u32[]{:S(2)}) collective-permute-start(bf16[32,768]{1,0:T(8,128)(2,1)S(1)} %collective-permute-done.20.refs_8_), channel_id=1, source_target_pairs={{0,1},{1,0},{2,3},{3,2},{4,5},{5,4},{6,7},{7,6},{8,9},{9,8},{10,11... | collective-permute-start | bytes 147464 | tf_op jit(solution)/shard_map/ppermute | solution.py:19
  67.1 5.5 %collective-permute-start.25 = (bf16[32,768]{1,0:T(8,128)(2,1)S(1)}, bf16[32,768]{1,0:T(8,128)(2,1)S(1)}, u32[]{:S(2)}, u32[]{:S(2)}) collective-permute-start(bf16[32,768]{1,0:T(8,128)(2,1)S(1)} %collective-permute-done.21.refs_9_), channel_id=1, source_target_pairs={{0,1},{1,0},{2,3},{3,2},{4,5},{5,4},{6,7},{7,6},{8,9},{9,8},{10,11... | collective-permute-start | bytes 147464 | tf_op jit(solution)/shard_map/ppermute | solution.py:19
  68.7 4.0 %collective-permute-start.26 = (bf16[32,768]{1,0:T(8,128)(2,1)S(1)}, bf16[32,768]{1,0:T(8,128)(2,1)S(1)}, u32[]{:S(2)}, u32[]{:S(2)}) collective-permute-start(bf16[32,768]{1,0:T(8,128)(2,1)S(1)} %collective-permute-done.22.refs_10_), channel_id=1, source_target_pairs={{0,1},{1,0},{2,3},{3,2},{4,5},{5,4},{6,7},{7,6},{8,9},{9,8},{10,11... | collective-permute-start | bytes 147464 | tf_op jit(solution)/shard_map/ppermute | solution.py:19
  69.2 3.5 %collective-permute-start.27 = (bf16[32,768]{1,0:T(8,128)(2,1)S(1)}, bf16[32,768]{1,0:T(8,128)(2,1)S(1)}, u32[]{:S(2)}, u32[]{:S(2)}) collective-permute-start(bf16[32,768]{1,0:T(8,128)(2,1)S(1)} %collective-permute-done.23.refs_11_), channel_id=1, source_target_pairs={{0,1},{1,0},{2,3},{3,2},{4,5},{5,4},{6,7},{7,6},{8,9},{9,8},{10,11... | collective-permute-start | bytes 147464 | tf_op jit(solution)/shard_map/ppermute | solution.py:19
  77.1 14.9 %all-to-all-start.1 = ((bf16[32,32,128]{2,1,0:T(8,128)(2,1)}), bf16[32,32,128]{2,1,0:T(8,128)(2,1)S(1)}, u32[]{:S(2)}, u32[]{:S(2)}) async-start(bf16[32,32,128]{2,1,0:T(8,128)(2,1)} %get-tuple-element.74), calls=%async_computation.1 | async-start | bytes 524288 | tf_op jit(solution)/shard_map/all_to_all | solution.py:34
  81.1 9.8 %collective-permute-start.32 = (bf16[16,6144]{1,0:T(8,128)(2,1)S(1)}, bf16[16,6144]{1,0:T(8,128)(2,1)S(1)}, u32[]{:S(2)}, u32[]{:S(2)}) collective-permute-start(bf16[16,6144]{1,0:T(8,128)(2,1)S(1)} %get-tuple-element.73), channel_id=1, source_target_pairs={{0,2},{2,0},{1,3},{3,1},{4,6},{6,4},{5,7},{7,5},{8,10},{10,8},{9,1... | collective-permute-start | bytes 589832 | tf_op jit(solution)/shard_map/ppermute | solution.py:579
  (7 other events, 25.8 us)

commit v4 on v3

--- a/solution.py
+++ b/solution.py
@@ -24,10 +24,15 @@
     return lax.ppermute(block, axis, [(i, i ^ apart_by) for i in range(count)])
 
 
-def gather_eight(block):
+def gather_eight(block, *meanwhile):
     near = across(block, "dp", 1)
     far = [across(block, "dp", bits) for bits in NEAR[1:4]]
-    return [block, *far, near, *[across(other, "dp", 1) for other in far]]
+    far, meanwhile = lax.optimization_barrier((far, meanwhile))
+    return [block, *far, near, *[across(other, "dp", 1) for other in far]], *meanwhile
+
+
+def order_of(place, blocks, eight):
+    return [lax.bitwise_xor(place, NEAR[k]) if eight else k for k in range(blocks)]
 
 
 def exchange(blocks, axis):
@@ -74,6 +79,33 @@
 def apart(wide):
     rank = wide.shape[1] // 2
     return jnp.concatenate([wide[:, :rank], wide[:, rank:]], axis=0)
+
+
+def near_kernel(here_ref, tokens_ref, factor_ref, router_ref, tokens_out, factor_out, route_out, router_near, sems):
+    pairs = ((tokens_ref, tokens_out), (factor_ref, factor_out), (router_ref, router_near))
+    copies = [pltpu.make_async_copy(*pair, sems.at[i]) for i, pair in enumerate(pairs)]
+    for copy in copies:
+        copy.start()
+    for copy in copies:
+        copy.wait()
+    picked = lax.broadcasted_iota(jnp.int32, (router_near.shape[0], 1), 0) == here_ref[1]
+    route_out[...] = jnp.sum(jnp.where(picked, router_near[...].astype(f32), 0.0), axis=0, keepdims=True)
+
+
+def brought_near(tokens, factor, router, here):
+    return pl.pallas_call(
+        near_kernel,
+        in_specs=[pl.BlockSpec(memory_space=pltpu.SMEM)] + [pl.BlockSpec(memory_space=pl.ANY)] * 3,
+        out_specs=vmem(3),
+        out_shape=[
+            struct(tokens.shape, bf16),
+            struct(factor.shape, bf16),
+            struct((1, router.shape[1]), f32),
+        ],
+        scratch_shapes=[pltpu.VMEM(router.shape, bf16), pltpu.SemaphoreType.DMA((3,))],
+        compiler_params=params(),
+        name="near",
+    )(here, *[pltpu.with_memory_space_constraint(array, pltpu.HBM) for array in (tokens, factor, router)])
 
 
 def pack_kernel(n_blocks, placer_ref, *refs):
@@ -108,8 +140,10 @@
         at = pl.ds(pl.multiple_of(place_ref[0] * depth, depth), depth)
     else:
         at = slice(None)
+    capacity = parts[0].shape[0]
+    rows = dot_last(jnp.concatenate([r[:, at] for r in parts], axis=0), factor_ref[...])
     for step in range(n_parts):
-        piece = beside(dot_last(parts[step][:, at], factor_ref[...]))
+        piece = beside(rows[step * capacity : (step + 1) * capacity])
         group = lax.rem(place_ref[1] + step, n_parts)
         for i in range(out_ref.shape[0] // (2 * n_parts)):
             spot = (i * n_parts + group) * 2
@@ -117,7 +151,7 @@
             out_ref[spot + 1] = piece
 
 
-def low_pieces(parts, factor, place, group, n_dp):
+def low_pieces(parts, factor, here, place, n_dp):
     rank, depth = factor.shape
     capacity = parts[0].shape[0]
     if depth % 128:
@@ -129,7 +163,7 @@
         out_shape=struct((n_dp * len(parts) * 2, capacity // 2, 2 * rank), f32),
         compiler_params=params(),
         name="low_pieces",
-    )(jnp.stack([place, group]), *parts, factor)
+    )(here, *parts, factor)
 
 
 def lift_kernel(n_parts, *refs):
@@ -173,7 +207,9 @@
     count = capacity * len(parts)
     return pl.pallas_call(
         functools.partial(lift_kernel, len(parts)),
-        in_specs=vmem(len(parts)) + [pl.BlockSpec(memory_space=pl.ANY)] * 2 + vmem(1),
+        in_specs=vmem(len(parts))
+        + [pl.BlockSpec(memory_space=pl.ANY)] * 2
+        + vmem(1),
         out_specs=vmem(3),
         scratch_shapes=[
             pltpu.VMEM(gate_weight.shape, bf16),
@@ -213,9 +249,9 @@
     copies = bring(weight_ref, down_ref, sems, [k * wide for k in range(blocks)])
     groups = low_ref.shape[1]
     sums = []
-    for core in (place_ref[1], 1 - place_ref[1]):
+    for core in (place_ref[2], 1 - place_ref[2]):
         for step in range(groups):
-            group = lax.rem(place_ref[0] - step + groups, groups)
+            group = lax.rem(place_ref[1] - step + groups, groups)
             sums.append(apart(jnp.sum(low_ref[:, group, core], axis=0)))
     low = jnp.concatenate(sums, axis=0).astype(bf16)
     pre = base_ref[...] + adapter_scale * dot(low, factor_ref[...])
@@ -231,30 +267,34 @@
         other_ref[k] = partial[half:]
 
 
-def down(base, lifted, low_parts, factor, down_weight, blocks, group, core):
+def down(base, lifted, low_parts, factor, down_weight, blocks, here):
     count, units = base.shape
     half, width = count // 2, down_weight.shape[1]
     shape = struct((blocks, half, width // blocks), bf16)
-    return pl.pallas_call(
+    *outs, kept = pl.pallas_call(
         down_kernel,
         in_specs=[pl.BlockSpec(memory_space=pltpu.SMEM)] + vmem(4) + [pl.BlockSpec(memory_space=pl.ANY)],
-        out_specs=vmem(4),
-        scratch_shapes=[
+        out_specs=vmem(5),
+        scratch_shapes=[pltpu.SemaphoreType.DMA((blocks,))],
+        out_shape=(
+            shape,
+            shape,
+            struct((count, units), f32),
+            struct((count, factor.shape[0]), bf16),
             pltpu.VMEM((blocks, units, width // blocks), bf16),
-            pltpu.SemaphoreType.DMA((blocks,)),
-        ],
-        out_shape=(shape, shape, struct((count, units), f32), struct((count, factor.shape[0]), bf16)),
+        ),
         cost_estimate=cost(2 * count * width * units, 2 * width * units),
         compiler_params=params(),
         name="down",
     )(
-        jnp.stack([group, core]),
+        here,
         base,
         lifted,
         low_parts,
         factor,
         pltpu.with_memory_space_constraint(down_weight, pltpu.HBM),
     )
+    return *outs, pltpu.with_memory_space_constraint(kept, pltpu.VMEM)
 
 
 def fold_core_kernel(place_ref, own_ref, got_ref, keep_ref, far_ref, near_ref):
@@ -270,7 +310,7 @@
         out_ref[k % 2] = folded(at + 1 - bit)
 
 
-def fold_core(own, got, place):
+def fold_core(own, got, here):
     shapes = [struct((count, *own.shape[1:]), bf16) for count in (4, 2, 2)]
     return pl.pallas_call(
         fold_core_kernel,
@@ -279,7 +319,7 @@
         out_shape=shapes,
         compiler_params=params(),
         name="fold_core",
-    )(place.reshape(1), own, got)
+    )(here, own, got)
 
 
 def fold_near_kernel(first, keep_ref, got_ref, *out_refs):
@@ -317,139 +357,109 @@
     )(*terms, gate)
 
 
-def back_sum(parts, owns, others, starts, gate_ref, weight_ref, down_ref, back_ref, sems, loss_factor):
+def back_sum(parts, owns, others, order, gate_ref, down_ref, loss_factor):
     wide = owns[0].shape[1]
-    copies = bring(weight_ref, down_ref, sems, starts)
     scale = loss_factor * gate_ref[...]
-    for k, (own, other) in enumerate(zip(owns, others)):
-        at = pl.ds(starts[k], wide)
+    total = 0.0
+    for block, own, other in zip(order, owns, others):
+        start = block * wide
+        at = pl.ds(start if isinstance(start, int) else pl.multiple_of(start, wide), wide)
         mixed = jnp.concatenate([own[...], other[...]], axis=0).astype(f32)
         rows = jnp.concatenate([r[:, at] for r in parts], axis=0).astype(f32)
-        back_ref[k] = (scale * (mixed - rows)).astype(bf16)
-    for copy in copies:
-        copy.wait()
-    total = dot_last(down_ref[0], back_ref[0])
-    for k in range(1, len(copies)):
-        total = total + dot_last(down_ref[k], back_ref[k])
+        back = (scale * (mixed - rows)).astype(bf16)
+        total = total + dot_last(down_ref[block], back)
     return total
 
 
-def back_first_kernel(n_parts, n_blocks, loss_factor, order_ref, *refs):
+def back_first_kernel(n_parts, n_blocks, eight, loss_factor, here_ref, *refs):
     parts, refs = refs[:n_parts], refs[n_parts:]
     owns, others, refs = refs[:n_blocks], refs[n_blocks : 2 * n_blocks], refs[2 * n_blocks :]
-    gate_ref, weight_ref, out_ref, *scratch = refs
-    wide = owns[0].shape[1]
-    starts = [pl.multiple_of(order_ref[k] * wide, wide) for k in range(n_blocks)]
-    out_ref[...] = back_sum(parts, owns, others, starts, gate_ref, weight_ref, *scratch, loss_factor)
-
-
-def back_last_kernel(n_parts, n_blocks, loss_factor, order_ref, *refs):
+    gate_ref, down_ref, out_ref = refs
+    order = order_of(here_ref[0], n_blocks, eight)
+    out_ref[...] = back_sum(parts, owns, others, order, gate_ref, down_ref, loss_factor)
+
+
+def back_last_kernel(n_parts, n_blocks, eight, loss_factor, here_ref, *refs):
     parts, refs = refs[:n_parts], refs[n_parts:]
     owns, refs = refs[: 2 * n_blocks], refs[2 * n_blocks :]
     others, refs = refs[:n_blocks], refs[n_blocks:]
-    gate_ref, weight_ref, first_ref, pre_ref, lifted_ref, low_ref, factor_ref = refs[:7]
-    low_out, grad_ref, *homes = refs[7:-3]
+    gate_ref, down_ref, first_ref, pre_ref, lifted_ref, low_ref, factor_ref = refs[:7]
+    low_out, grad_ref, *homes = refs[7:]
     half, wide = owns[0].shape
     capacity = half // len(homes)
-    starts = [pl.multiple_of(order_ref[k] * wide, wide) for k in range(2 * n_blocks)]
+    order = order_of(here_ref[0], 2 * n_blocks, eight)
     pre = pre_ref[...]
     sig = sigmoid(pre)
     slope = lifted_ref[...] * (sig * (1.0 + pre * (1.0 - sig)))
-    total = back_sum(
-        parts, owns[n_blocks:], others, starts[n_blocks:], gate_ref, weight_ref, *refs[-3:], loss_factor
+    total = first_ref[...] + back_sum(
+        parts, owns[n_blocks:], others, order[n_blocks:], gate_ref, down_ref, loss_factor
     )
-    back_pre = ((first_ref[...] + total).T * slope).astype(bf16)
+    back_pre = (total.T * slope).astype(bf16)
     back_low = beside(adapter_scale * dot_last(back_pre, factor_ref[...])).astype(bf16)
     for i in range(low_out.shape[0]):
         low_out[i] = back_low
     grad_ref[...] = adapter_scale * dot_first(low_ref[...], back_pre)
-    for k, own in enumerate(owns):
+    for block, own in zip(order, owns):
+        start = block * wide
+        at = pl.ds(start if isinstance(start, int) else pl.multiple_of(start, wide), wide)
         for step, home in enumerate(homes):
-            home[:, pl.ds(starts[k], wide)] = own[step * capacity : (step + 1) * capacity]
-
-
-def back_scratch(blocks, units, count, wide):
-    return [
-        pltpu.VMEM((blocks, units, wide), bf16),
-        pltpu.VMEM((blocks, count, wide), bf16),
-        pltpu.SemaphoreType.DMA((blocks,)),
-    ]
-
-
-def back_first(parts, owns, others, order, gate, down_weight, loss_factor):
-    units = down_weight.shape[0]
+            home[:, at] = own[step * capacity : (step + 1) * capacity]
+
+
+def back_first(parts, owns, others, here, eight, gate, kept, loss_factor):
+    units = kept.shape[1]
     count, blocks, wide = gate.shape[0], len(owns), owns[0].shape[1]
     return pl.pallas_call(
-        functools.partial(back_first_kernel, len(parts), blocks, loss_factor),
-        in_specs=[pl.BlockSpec(memory_space=pltpu.SMEM)]
-        + vmem(len(parts) + 2 * blocks + 1)
-        + [pl.BlockSpec(memory_space=pl.ANY)],
+        functools.partial(back_first_kernel, len(parts), blocks, eight, loss_factor),
+        in_specs=[pl.BlockSpec(memory_space=pltpu.SMEM)] + vmem(len(parts) + 2 * blocks + 2),
         out_specs=vmem(1)[0],
         out_shape=struct((units, count), f32),
-        scratch_shapes=back_scratch(blocks, units, count, wide),
         cost_estimate=cost(2 * count * blocks * wide * units, 2 * blocks * wide * units),
         compiler_params=params(),
         name="back_first",
-    )(order, *parts, *owns, *others, gate, pltpu.with_memory_space_constraint(down_weight, pltpu.HBM))
-
-
-def back_last(parts, owns, others, order, gate, down_weight, first, pre, lifted, low, factor, loss_factor, copies):
+    )(here, *parts, *owns, *others, gate, kept)
+
+
+def back_last(parts, owns, others, here, eight, gate, kept, first, pre, lifted, low, factor, loss_factor, copies):
     capacity, width = parts[0].shape
     half, wide = owns[0].shape
     count, units = pre.shape
     rank, blocks = factor.shape[0], len(others)
     homes = half // capacity
     return pl.pallas_call(
-        functools.partial(back_last_kernel, len(parts), blocks, loss_factor),
-        in_specs=[pl.BlockSpec(memory_space=pltpu.SMEM)]
-        + vmem(len(parts) + 3 * blocks + 1)
-        + [pl.BlockSpec(memory_space=pl.ANY)]
-        + vmem(5),
+        functools.partial(back_last_kernel, len(parts), blocks, eight, loss_factor),
+        in_specs=[pl.BlockSpec(memory_space=pltpu.SMEM)] + vmem(len(parts) + 3 * blocks + 7),
         out_specs=vmem(2 + homes),
         out_shape=(
             struct((copies, half, 2 * rank), bf16),
             struct((rank, units), f32),
             *[struct((capacity, width), bf16)] * homes,
         ),
-        scratch_shapes=back_scratch(blocks, units, count, wide),
         cost_estimate=cost(2 * count * blocks * wide * units, 2 * blocks * wide * units),
         compiler_params=params(),
         name="back_last",
-    )(
-        order,
-        *parts,
-        *owns,
-        *others,
-        gate,
-        pltpu.with_memory_space_constraint(down_weight, pltpu.HBM),
-        first,
-        pre,
-        lifted,
-        low,
-        factor,
-    )
+    )(here, *parts, *owns, *others, gate, kept, first, pre, lifted, low, factor)
 
 
 def factor_kernel(place_ref, low_ref, piece_ref, out_ref):
-    rank = out_ref.shape[0]
+    rank, share = out_ref.shape
     groups = piece_ref.shape[0]
-    group, core = place_ref[0], place_ref[1]
-    total = 0.0
-    for g in range(groups):
-        mine = jnp.sum(low_ref[:, g, core].astype(f32), axis=0)
-        theirs = jnp.sum(low_ref[:, g, 1 - core].astype(f32), axis=0)
-        low = jnp.concatenate(
-            [mine[:, :rank] + theirs[:, rank:], mine[:, rank:] + theirs[:, :rank]], axis=0
-        )
-        high = low.astype(bf16)
-        rest = (low - high.astype(f32)).astype(bf16)
-        piece = piece_ref[lax.rem(group - g + groups, groups)]
-        total = total + dot_first(high, piece) + dot_first(rest, piece)
-    out_ref[...] = total
-
-
-def factor_gradient(lows, pieces, group, core):
-    rank, share = lows.shape[-1] // 2, pieces.shape[2]
+    group, core = place_ref[1], place_ref[2]
+    lows, rows = [], []
+    for step in range(groups):
+        source = lax.rem(group - step + groups, groups)
+        mine = jnp.sum(low_ref[:, source, core].astype(f32), axis=0)
+        theirs = jnp.sum(low_ref[:, source, 1 - core].astype(f32), axis=0)
+        lows += [mine[:, :rank] + theirs[:, rank:], mine[:, rank:] + theirs[:, :rank]]
+        rows.append(piece_ref[step, :, :share])
+    low = jnp.concatenate(lows, axis=0)
+    high = low.astype(bf16)
+    rest = (low - high.astype(f32)).astype(bf16)
+    out_ref[...] = dot_first(jnp.concatenate([high, rest], axis=0), jnp.concatenate(rows + rows, axis=0))
+
+
+def factor_gradient(lows, pieces, share, here):
+    rank = lows.shape[-1] // 2
     return pl.pallas_call(
         factor_kernel,
         in_specs=[pl.BlockSpec(memory_space=pltpu.SMEM)] + vmem(2),
@@ -457,7 +467,7 @@
         out_shape=struct((rank, share), f32),
         compiler_params=params(),
         name="factor_gradient",
-    )(jnp.stack([group, core]), lows, pieces)
+    )(here, lows, pieces)
 
 
 def shards(
@@ -487,27 +497,32 @@
     blocks = 8
     eight = n_dp == blocks
 
+    here = jnp.stack([place, group, core])
+
     labels = expert_choice_table[0]
     index = jnp.arange(col_rows, dtype=jnp.int32)
-    before = (labels[None, :] == labels[:, None]) & (index[None, :] < index[:, None])
+    number = index
+    if eight:
+        order = lax.bitwise_xor(jnp.array(NEAR, jnp.int32), place)
+        number = (order[:, None] * tok_rows + jnp.arange(tok_rows)[None, :]).reshape(col_rows)
+        labels = jnp.sum(jnp.where(number[:, None] == index[None, :], labels[None, :], 0), axis=1)
+    before = (labels[None, :] == labels[:, None]) & (number[None, :] < number[:, None])
     ordinal = jnp.sum(before.astype(jnp.int32), axis=1)
     ahead = lax.rem(labels - group + groups, groups)
     target = ahead * capacity + ordinal
+    placer = (index[:, None] == target[None, :]).astype(bf16)
+    tokens_near, factor, own_route = brought_near(tokens, adapter_down_shared.T, router.T, here)
     if eight:
-        order = lax.bitwise_xor(jnp.array(NEAR, jnp.int32), place)
-        column = gather_eight(tokens)
-        spread_out = target.reshape(n_dp, tok_rows)
-        arrived = jnp.sum(
-            jnp.where(order[:, None, None] == jnp.arange(n_dp)[None, :, None], spread_out[None], 0), axis=1
-        ).reshape(col_rows)
+        column, placer, tokens_near, factor, own_route = gather_eight(
+            tokens, placer, tokens_near, factor, own_route
+        )
+        column[0] = tokens_near
+        column, placer, factor = lax.optimization_barrier((column, placer, factor))
+        own_target = target[:tok_rows]
     else:
-        order = jnp.arange(blocks, dtype=jnp.int32)
         column = exchange(jnp.broadcast_to(tokens[None], (n_dp, tok_rows, width)), "dp")
         column = [column.reshape(col_rows, width)]
-        arrived = target
-    placer = (index[:, None] == arrived[None, :]).astype(bf16)
-    own_route = lax.dynamic_slice_in_dim(router.T, group, 1, 0).astype(f32)
-    column, placer, own_route = lax.optimization_barrier((column, placer, own_route))
+        own_target = lax.dynamic_slice_in_dim(target, place * tok_rows, tok_rows, 0)
     packed = pack(placer, column, capacity)
     parts = [packed[0]]
     for step in range(1, groups):
@@ -515,33 +530,34 @@
         parts.append(lax.ppermute(packed[step], "x", route))
     parts = parts + [swap(part, "core") for part in parts]
 
-    low_parts = low_pieces(packed, adapter_down_shared.T, place, group, n_dp)
+    low_parts = low_pieces(packed, factor, here, place, n_dp)
     low_parts = exchange(low_parts, every).reshape(n_dp, groups, 2, capacity // 2, 2 * rank)
     base, lifted, gate = lift(parts, gate_weight, up_weight, own_route)
     low_parts, gate = lax.optimization_barrier((low_parts, gate))
-    own, other, pre, low = down(
-        base, lifted, low_parts, adapter_gate_factor, down_weight, blocks, group, core
+    own, other, pre, low, kept = down(
+        base, lifted, low_parts, adapter_gate_factor, down_weight, blocks, here
     )
 
     rows = jnp.concatenate(parts, axis=0)
+    numbers = jnp.broadcast_to(own_target.astype(bf16)[None], (2 * half, tok_rows))
     pieces = []
     for step in range(groups):
         to = lax.rem(group + step, groups)
         at = ((place * groups + to) * 2 + core) * share
-        piece = lax.dynamic_slice_in_dim(rows, at, share, 1)
+        piece = jnp.concatenate([lax.dynamic_slice_in_dim(rows, at, share, 1), numbers], axis=1)
         route = [(i, (i + step) % groups) for i in range(groups)]
         pieces.append(lax.ppermute(piece, "x", route) if step else piece)
     pieces = jnp.stack(pieces)
 
     got = swap(other, "core")
     if eight:
-        keep, far, near = fold_core(own, got, place)
+        keep, far, near = fold_core(own, got, here)
         far, near = across(far, "dp", 1), across(near, "dp", 1)
         two, three = fold_near(keep, far, 2)
         mine, one = fold_near(keep, near, 0)
         terms = [mine, across(one, "dp", 2), across(two, "dp", 4), across(three, "dp", 6)]
         terms, pieces = lax.optimization_barrier((terms, pieces))
-        owns = gather_eight(mix(terms, gate))
+        (owns,) = gather_eight(mix(terms, gate))
     else:
         summed = (own.astype(f32) + got.astype(f32)).astype(bf16)
         summed = summed.transpose(1, 0, 2).reshape(half, n_dp, wide).transpose(1, 0, 2)
@@ -553,15 +569,16 @@
     others = [swap(block, "core") for block in owns]
 
     first = back_first(
-        parts, owns[: blocks // 2], others[: blocks // 2], order, gate, down_weight, loss_factor
+        parts, owns[: blocks // 2], others[: blocks // 2], here, eight, gate, kept, loss_factor
     )
     back_low, grad_b, *homes = back_last(
         parts,
         owns,
         others[blocks // 2 :],
-        order,
+        here,
+        eight,
         gate,
-        down_weight,
+        kept,
         first,
         pre,
         lifted,
@@ -572,16 +589,18 @@
     )
     lows = exchange(back_low, every).reshape(n_dp, groups, 2, half, 2 * rank)
 
-    own_target = lax.dynamic_slice_in_dim(target, place * tok_rows, tok_rows, 0)
     result = jnp.zeros((tok_rows, width), f32)
     for step in range(groups):
-        route = [(i, (i - step) % groups) for i in range(groups)]
-        returned = lax.ppermute(homes[step], "x", route) if step else homes[0]
         spot = index[step * capacity : (step + 1) * capacity]
-        chooser = (own_target[:, None] == spot[None, :]).astype(bf16)
-        result = result + dot(chooser, returned)
-
-    grad_a = factor_gradient(lows, pieces, group, core)
+        wanted = pieces[step, 0, share:].astype(jnp.int32)
+        chooser = (wanted[:, None] == spot[None, :]).astype(bf16)
+        chosen = dot(chooser, homes[step])
+        if step:
+            route = [(i, (i - step) % groups) for i in range(groups)]
+            chosen = lax.ppermute(chosen.astype(bf16), "x", route).astype(f32)
+        result = result + chosen
+
+    grad_a = factor_gradient(lows, pieces, share, here)
     return (result.astype(bf16), grad_a.T, grad_b.T)
 
 

time: 94 us -> 89.1 us (0.948)
  local copies, waits for them, and re-layouts: 2.41 us -> 0.4 us
  Pallas kernels: 20.5 us -> 18.9 us
  other arithmetic: 3.44 us -> 1.96 us
    ppermute x1, waiting for transfers between devices: 7.79 us -> 3.43 us  [shards(): chosen = lax.ppermute(chosen.astype(bf16), 'x', route).astype(f32)]
    all_to_all x2, waiting for transfers between devices: 1.3 us -> 5.56 us  [exchange(): return lax.all_to_all(blocks, axis, 0, 0, tiled=True)]
    pallas_call x2 -> x3, Pallas kernels: 7.83 us -> 5.72 us  [the longest x1 2.58 us: back_last(): pl.pallas_call(functools.partial(back_last_kernel, len(parts), blocks, ei...]
    unnamed x11 -> x5, local copies, waits for them, and re-layouts: 1.74 us -> 0.05 us
    ppermute x19, starting transfers between devices: 24.5 us -> 25.7 us  [across(): return lax.ppermute(block, axis, [(i, i ^ apart_by) for i in range(count)])]
  transfers between devices with their start and end apart: 35 -> 35, of which waited for: 14 -> 17; matrix products, arithmetic and copies ran while one was open for 6% -> 4% of each run, Pallas kernels for 11% -> 11%
where the time goes in v4:
time: 89.1 us; the launch traced here: 88.8 us
  starting transfers between devices  38.7 us (43%)
  waiting for transfers between devices  26.9 us (30%)
  Pallas kernels  18.9 us (21%)
  other arithmetic  1.96 us (2%)
  matrix products  1.06 us (1%)
    ppermute x19, starting transfers between devices, across(): return lax.ppermute(block, axis, [(i, i ^ apart_by) for i in range(count)])  25.7 us
    ppermute x19, waiting for transfers between devices, across(): return lax.ppermute(block, axis, [(i, i ^ apart_by) for i in range(count)])  15.4 us
    all_to_all x2, starting transfers between devices, exchange(): return lax.all_to_all(blocks, axis, 0, 0, tiled=True)  7.27 us
    all_to_all x2, waiting for transfers between devices, exchange(): return lax.all_to_all(blocks, axis, 0, 0, tiled=True)  5.56 us
    pallas_call x1, Pallas kernels, lift(): pl.pallas_call(functools.partial(lift_kernel, len(parts)), in_specs=vmem(...  5.41 us
    pallas_call x1, Pallas kernels, down(): pl.pallas_call(down_kernel, in_specs=[pl.BlockSpec(memory_space=pltpu.SME...  3.86 us
    ppermute x1, waiting for transfers between devices, shards(): chosen = lax.ppermute(chosen.astype(bf16), 'x', route).astype(f32)  3.43 us
    pallas_call x1, Pallas kernels, back_last(): pl.pallas_call(functools.partial(back_last_kernel, len(parts), blocks, ei...  2.58 us
  transfers between devices with their start and end apart: 35, of which 17 were waited for; matrix products, arithmetic and copies ran while one was open for 4% of the time, Pallas kernels for 11%

profile of v4, /device:TPU:0, one launch (start us, length us, event | category | flops | bytes accessed | tf_op | source)
XLA Modules:
  0.0 88.8 jit_solution(15846619817118228786)
XLA Ops:
  0.6 3.1 %collective-permute-start = (bf16[4,6144]{1,0:T(4,128)(2,1)}, bf16[4,6144]{1,0:T(4,128)(2,1)S(1)}, u32[]{:S(2)}, u32[]{:S(2)}) collective-permute-start(bf16[4,6144]{1,0:T(4,128)(2,1)} %tokens_ref.1), channel_id=1, source_target_pairs={{0,8},{4,12},{8,0},{12,4},{16,24},{20,28},{24,16},{28,20},{1,9},{5... | collective-permute-start | bytes 147464 | tf_op jit(solution)/shard_map/ppermute | solution.py:24
  3.7 2.6 %collective-permute-start.1 = (bf16[4,6144]{1,0:T(4,128)(2,1)}, bf16[4,6144]{1,0:T(4,128)(2,1)S(1)}, u32[]{:S(2)}, u32[]{:S(2)}) collective-permute-start(bf16[4,6144]{1,0:T(4,128)(2,1)} %tokens_ref.1), channel_id=1, source_target_pairs={{0,16},{4,20},{8,24},{12,28},{16,0},{20,4},{24,8},{28,12},{1,17},{... | collective-permute-start | bytes 147464 | tf_op jit(solution)/shard_map/ppermute | solution.py:24
  6.3 1.7 %collective-permute-start.3 = (bf16[4,6144]{1,0:T(4,128)(2,1)}, bf16[4,6144]{1,0:T(4,128)(2,1)S(1)}, u32[]{:S(2)}, u32[]{:S(2)}) collective-permute-start(bf16[4,6144]{1,0:T(4,128)(2,1)} %tokens_ref.1), channel_id=1, source_target_pairs={{0,4},{4,0},{8,12},{12,8},{16,20},{20,16},{24,28},{28,24},{1,5},{5... | collective-permute-start | bytes 147464 | tf_op jit(solution)/shard_map/ppermute | solution.py:24
  10.0 1.6 %near.1 = (bf16[4,6144]{1,0:T(4,128)(2,1)S(1)}, bf16[64,768]{1,0:T(8,128)(2,1)S(1)}, f32[1,6144]{1,0:T(1,128)S(1)}) custom-call(s32[3]{0:T(128)S(1)} %pad_add_fusion.here_ref.place_ref, bf16[4,6144]{1,0:T(4,128)(2,1)} %tokens_ref.1, bf16[64,768]{1,0:T(8,128)(2,1)} %bitcast.25, bf16[2,6144]{1,0:T(2,128)(2,1)} %bitcast.28), custom_call_target="tpu_custom_call" | custom-call | tf_op jit(solution)/shard_map/near/pallas_call | solution.py:96
  12.4 1.5 %collective-permute-start.4 = (bf16[4,6144]{1,0:T(4,128)(2,1)S(1)}, bf16[4,6144]{1,0:T(4,128)(2,1)S(1)}, u32[]{:S(2)}, u32[]{:S(2)}) collective-permute-start(bf16[4,6144]{1,0:T(4,128)(2,1)S(1)} %collective-permute-done.refs_1_), channel_id=1, source_target_pairs={{0,4},{4,0},{8,12},{12,8},{16,20},{20,16},{24,28},{28,24},{1,5},{5... | collective-permute-start | bytes 147464 | tf_op jit(solution)/shard_map/ppermute | solution.py:24
  14.4 1.5 %collective-permute-start.6 = (bf16[4,6144]{1,0:T(4,128)(2,1)S(1)}, bf16[4,6144]{1,0:T(4,128)(2,1)S(1)}, u32[]{:S(2)}, u32[]{:S(2)}) collective-permute-start(bf16[4,6144]{1,0:T(4,128)(2,1)S(1)} %collective-permute-done.2.refs_3_), channel_id=1, source_target_pairs={{0,4},{4,0},{8,12},{12,8},{16,20},{20,16},{24,28},{28,24},{1,5},{5... | collective-permute-start | bytes 147464 | tf_op jit(solution)/shard_map/ppermute | solution.py:24
  16.5 1.5 %collective-permute-done.5.refs_6_ = bf16[4,6144]{1,0:T(4,128)(2,1)S(1)} collective-permute-done((bf16[4,6144]{1,0:T(4,128)(2,1)S(1)}, bf16[4,6144]{1,0:T(4,128)(2,1)S(1)}, u32[]{:S(2)}, u32[]{:S(2)}) %collective-permute-start.5) | collective-permute-done | bytes 49184 | tf_op jit(solution)/shard_map/ppermute | solution.py:24
  18.8 1.6 %collective-permute-start.7 = (bf16[16,6144]{1,0:T(8,128)(2,1)S(1)}, bf16[16,6144]{1,0:T(8,128)(2,1)S(1)}, u32[]{:S(2)}, u32[]{:S(2)}) collective-permute-start(bf16[16,6144]{1,0:T(8,128)(2,1)S(1)} %get-tuple-element.73.refs_1_), channel_id=1, source_target_pairs={{0,2},{2,0},{1,3},{3,1},{4,6},{6,4},{5,7},{7,5},{8,10},{10,8},{9,1... | collective-permute-start | bytes 589832 | tf_op jit(solution)/shard_map/ppermute | solution.py:530
  20.5 1.4 %low_pieces.1 = f32[32,8,128]{2,1,0:T(8,128)} custom-call(s32[3]{0:T(128)S(1)} %pad_add_fusion.here_ref.place_ref, bf16[16,6144]{1,0:T(8,128)(2,1)S(1)} %get-tuple-element.72.refs_0_, bf16[16,6144]{1,0:T(8,128)(2,1)S(1)} %get-tuple-element.73.refs_1_, bf16[64,768]{1,0:T(8,128)(2,1)S(1)} %get-tuple-element.77.refs_2_), custom_call_target="tpu_custom_call" | custom-call | tf_op jit(solution)/shard_map/low_pieces/pallas_call | solution.py:159
  21.9 3.3 %all-to-all-start = ((f32[32,8,128]{2,1,0:T(8,128)}), f32[32,8,128]{2,1,0:T(8,128)S(1)}, u32[]{:S(2)}, u32[]{:S(2)}) async-start(f32[32,8,128]{2,1,0:T(8,128)} %low_pieces.1), calls=%async_computation | async-start | bytes 262144 | tf_op jit(solution)/shard_map/all_to_all | solution.py:39
  26.7 5.4 %lift.1 = (f32[64,512]{1,0:T(8,128)S(1)}, f32[64,512]{1,0:T(8,128)S(1)}, f32[64,1]{1,0:T(8,128)S(1)}) custom-call(bf16[16,6144]{1,0:T(8,128)(2,1)S(1)} %get-tuple-element.72.refs_0_, bf16[16,6144]{1,0:T(8,128)(2,1)S(1)} %collective-permute-done.7.refs_1_, bf16[16,6144]{1,0:T(8,128)(2,1)S(1)} %collective-permute-done.8.refs_2_, ...), custom_call_target="tpu_custom_call" | custom-call | flops 805306368 | bytes 12582912 | tf_op jit(solution)/shard_map/lift/pallas_call | solution.py:208
  33.4 3.9 %down.1 = (bf16[8,32,768]{2,1,0:T(8,128)(2,1)S(1)}, bf16[8,32,768]{2,1,0:T(8,128)(2,1)S(1)}, f32[64,512]{1,0:T(8,128)S(1)}, bf16[64,64]{1,0:T(8,128)(2,1)S(1)}, bf16[8,512,768]{2,1,0:T(8,128)(2,1)S(1)}) custom-call(s32[3]{0:T(128)S(1)} %pad_add_fusion.here_ref.place_ref, f32[64,512]{1,0:T(8,128)S(1)} %get-tuple-element.75.base_ref, ...), custom_call_target="tpu_custom_call" | custom-call | flops 402653184 | bytes 6291456 | tf_op jit(solution)/shard_map/down/pallas_call | solution.py:274
  37.7 1.4 %collective-permute-done.10.got_ref = bf16[8,32,768]{2,1,0:T(8,128)(2,1)S(1)} collective-permute-done((bf16[8,32,768]{2,1,0:T(8,128)(2,1)S(1)}, bf16[8,32,768]{2,1,0:T(8,128)(2,1)S(1)}, u32[]{:S(2)}, u32[]{:S(2)}) %collective-permute-start.10) | collective-permute-done | bytes 393248 | tf_op jit(solution)/shard_map/ppermute | solution.py:19
  40.5 1.4 %collective-permute-start.11 = (bf16[2,32,768]{2,1,0:T(8,128)(2,1)S(1)}, bf16[2,32,768]{2,1,0:T(8,128)(2,1)S(1)}, u32[]{:S(2)}, u32[]{:S(2)}) collective-permute-start(bf16[2,32,768]{2,1,0:T(8,128)(2,1)S(1)} %get-tuple-element.83), channel_id=1, source_target_pairs={{0,4},{4,0},{8,12},{12,8},{16,20},{20,16},{24,28},{28,24},{1,5},{5... | collective-permute-start | bytes 294920 | tf_op jit(solution)/shard_map/ppermute | solution.py:24
  42.4 3.0 %collective-permute-done.13.got_ref = bf16[2,32,768]{2,1,0:T(8,128)(2,1)S(1)} collective-permute-done((bf16[2,32,768]{2,1,0:T(8,128)(2,1)S(1)}, bf16[2,32,768]{2,1,0:T(8,128)(2,1)S(1)}, u32[]{:S(2)}, u32[]{:S(2)}) %collective-permute-start.13) | collective-permute-done | bytes 98336 | tf_op jit(solution)/shard_map/ppermute | solution.py:24
  45.5 1.5 %collective-permute-start.14 = (bf16[32,768]{1,0:T(8,128)(2,1)S(1)}, bf16[32,768]{1,0:T(8,128)(2,1)S(1)}, u32[]{:S(2)}, u32[]{:S(2)}) collective-permute-start(bf16[32,768]{1,0:T(8,128)(2,1)S(1)} %get-tuple-element.87), channel_id=1, source_target_pairs={{0,16},{4,20},{8,24},{12,28},{16,0},{20,4},{24,8},{28,12},{1,17},{... | collective-permute-start | bytes 147464 | tf_op jit(solution)/shard_map/ppermute | solution.py:24
  46.9 1.6 %collective-permute-start.15 = (bf16[32,768]{1,0:T(8,128)(2,1)S(1)}, bf16[32,768]{1,0:T(8,128)(2,1)S(1)}, u32[]{:S(2)}, u32[]{:S(2)}) collective-permute-start(bf16[32,768]{1,0:T(8,128)(2,1)S(1)} %get-tuple-element.88), channel_id=1, source_target_pairs={{0,24},{4,28},{8,16},{12,20},{16,8},{20,12},{24,0},{28,4},{1,25},{... | collective-permute-start | bytes 147464 | tf_op jit(solution)/shard_map/ppermute | solution.py:24
  49.1 2.0 %collective-permute-done.14.refs_2_ = bf16[32,768]{1,0:T(8,128)(2,1)S(1)} collective-permute-done((bf16[32,768]{1,0:T(8,128)(2,1)S(1)}, bf16[32,768]{1,0:T(8,128)(2,1)S(1)}, u32[]{:S(2)}, u32[]{:S(2)}) %collective-permute-start.14) | collective-permute-done | bytes 49184 | tf_op jit(solution)/shard_map/ppermute | solution.py:24
  51.2 1.8 %collective-permute-done.15.refs_3_ = bf16[32,768]{1,0:T(8,128)(2,1)S(1)} collective-permute-done((bf16[32,768]{1,0:T(8,128)(2,1)S(1)}, bf16[32,768]{1,0:T(8,128)(2,1)S(1)}, u32[]{:S(2)}, u32[]{:S(2)}) %collective-permute-start.15) | collective-permute-done | bytes 49184 | tf_op jit(solution)/shard_map/ppermute | solution.py:24
  53.6 2.3 %collective-permute-start.18 = (bf16[32,768]{1,0:T(8,128)(2,1)S(1)}, bf16[32,768]{1,0:T(8,128)(2,1)S(1)}, u32[]{:S(2)}, u32[]{:S(2)}) collective-permute-start(bf16[32,768]{1,0:T(8,128)(2,1)S(1)} %mix.1.refs_4_), channel_id=1, source_target_pairs={{0,16},{4,20},{8,24},{12,28},{16,0},{20,4},{24,8},{28,12},{1,17},{... | collective-permute-start | bytes 147464 | tf_op jit(solution)/shard_map/ppermute | solution.py:24
  55.8 2.1 %collective-permute-start.19 = (bf16[32,768]{1,0:T(8,128)(2,1)S(1)}, bf16[32,768]{1,0:T(8,128)(2,1)S(1)}, u32[]{:S(2)}, u32[]{:S(2)}) collective-permute-start(bf16[32,768]{1,0:T(8,128)(2,1)S(1)} %mix.1.refs_4_), channel_id=1, source_target_pairs={{0,24},{4,28},{8,16},{12,20},{16,8},{20,12},{24,0},{28,4},{1,25},{... | collective-permute-start | bytes 147464 | tf_op jit(solution)/shard_map/ppermute | solution.py:24
  59.1 2.6 %collective-permute-done.19.refs_7_ = bf16[32,768]{1,0:T(8,128)(2,1)S(1)} collective-permute-done((bf16[32,768]{1,0:T(8,128)(2,1)S(1)}, bf16[32,768]{1,0:T(8,128)(2,1)S(1)}, u32[]{:S(2)}, u32[]{:S(2)}) %collective-permute-start.19) | collective-permute-done | bytes 49184 | tf_op jit(solution)/shard_map/ppermute | solution.py:24
  62.2 1.5 %collective-permute-start.21 = (bf16[32,768]{1,0:T(8,128)(2,1)S(1)}, bf16[32,768]{1,0:T(8,128)(2,1)S(1)}, u32[]{:S(2)}, u32[]{:S(2)}) collective-permute-start(bf16[32,768]{1,0:T(8,128)(2,1)S(1)} %collective-permute-done.17.refs_5_), channel_id=1, source_target_pairs={{0,4},{4,0},{8,12},{12,8},{16,20},{20,16},{24,28},{28,24},{1,5},{5... | collective-permute-start | bytes 147464 | tf_op jit(solution)/shard_map/ppermute | solution.py:24
  64.3 1.5 %collective-permute-start.23 = (bf16[32,768]{1,0:T(8,128)(2,1)S(1)}, bf16[32,768]{1,0:T(8,128)(2,1)S(1)}, u32[]{:S(2)}, u32[]{:S(2)}) collective-permute-start(bf16[32,768]{1,0:T(8,128)(2,1)S(1)} %collective-permute-done.19.refs_7_), channel_id=1, source_target_pairs={{0,4},{4,0},{8,12},{12,8},{16,20},{20,16},{24,28},{28,24},{1,5},{5... | collective-permute-start | bytes 147464 | tf_op jit(solution)/shard_map/ppermute | solution.py:24
  66.6 1.3 %collective-permute-done.22.refs_10_ = bf16[32,768]{1,0:T(8,128)(2,1)S(1)} collective-permute-done((bf16[32,768]{1,0:T(8,128)(2,1)S(1)}, bf16[32,768]{1,0:T(8,128)(2,1)S(1)}, u32[]{:S(2)}, u32[]{:S(2)}) %collective-permute-start.22) | collective-permute-done | bytes 49184 | tf_op jit(solution)/shard_map/ppermute | solution.py:24
  68.5 1.6 %back_first.1.refs_18_ = f32[512,64]{1,0:T(8,128)S(1)} custom-call(s32[3]{0:T(128)S(1)} %pad_add_fusion.here_ref.place_ref, bf16[16,6144]{1,0:T(8,128)(2,1)S(1)} %get-tuple-element.72.refs_0_, bf16[16,6144]{1,0:T(8,128)(2,1)S(1)} %collective-permute-done.7.refs_1_, bf16[16,6144]{1,0:T(8,128)(2,1)S(1)} %collective-permute-done.8.refs_2_, ...), custom_call_target="tpu_custom_call" | custom-call | flops 201326592 | bytes 3145728 | tf_op jit(solution)/shard_map/back_first/pallas_call | solution.py:412
  70.1 2.6 %back_last.1 = (bf16[32,32,128]{2,1,0:T(8,128)(2,1)}, f32[64,512]{1,0:T(8,128)}, bf16[16,6144]{1,0:T(8,128)(2,1)S(1)}, bf16[16,6144]{1,0:T(8,128)(2,1)S(1)}) custom-call(s32[3]{0:T(128)S(1)} %pad_add_fusion.here_ref.place_ref, bf16[16,6144]{1,0:T(8,128)(2,1)S(1)} %get-tuple-element.72.refs_0_, bf16[16,6144]{1,0:T(8,128)(2,1)S(1)} %collective-permute-done.7.refs_1_, ...), custom_call_target="tpu_custom_call" | custom-call | flops 201326592 | bytes 3145728 | tf_op jit(solution)/shard_map/back_last/pallas_call | solution.py:429
  72.7 4.0 %all-to-all-start.1 = ((bf16[32,32,128]{2,1,0:T(8,128)(2,1)}), bf16[32,32,128]{2,1,0:T(8,128)(2,1)S(1)}, u32[]{:S(2)}, u32[]{:S(2)}) async-start(bf16[32,32,128]{2,1,0:T(8,128)(2,1)} %get-tuple-element.103), calls=%async_computation.1 | async-start | bytes 524288 | tf_op jit(solution)/shard_map/all_to_all | solution.py:39
  76.9 1.8 %collective-permute-start.32 = (bf16[4,6144]{1,0:T(4,128)(2,1)S(1)}, bf16[4,6144]{1,0:T(4,128)(2,1)S(1)}, u32[]{:S(2)}, u32[]{:S(2)}) collective-permute-start(bf16[4,6144]{1,0:T(4,128)(2,1)S(1)} %convolution_convert_fusion), channel_id=1, source_target_pairs={{0,2},{2,0},{1,3},{3,1},{4,6},{6,4},{5,7},{7,5},{8,10},{10,8},{9,1... | collective-permute-start | bytes 147464 | tf_op jit(solution)/shard_map/ppermute | solution.py:600
  78.8 3.4 %collective-permute-done.32 = bf16[4,6144]{1,0:T(4,128)(2,1)S(1)} collective-permute-done((bf16[4,6144]{1,0:T(4,128)(2,1)S(1)}, bf16[4,6144]{1,0:T(4,128)(2,1)S(1)}, u32[]{:S(2)}, u32[]{:S(2)}) %collective-permute-start.32) | collective-permute-done | bytes 49184 | tf_op jit(solution)/shard_map/ppermute | solution.py:600
  83.0 4.3 %all-to-all-done.1 = bf16[32,32,128]{2,1,0:T(8,128)(2,1)S(1)} async-done(((bf16[32,32,128]{2,1,0:T(8,128)(2,1)}), bf16[32,32,128]{2,1,0:T(8,128)(2,1)S(1)}, u32[]{:S(2)}, u32[]{:S(2)}) %all-to-all-start.1) | async-done | bytes 262176 | tf_op jit(solution)/shard_map/all_to_all | solution.py:39
  87.3 1.5 %factor_gradient.1 = f32[64,192]{1,0:T(8,128)} custom-call(s32[3]{0:T(128)S(1)} %pad_add_fusion.here_ref.place_ref, bf16[8,2,2,32,128]{4,3,2,1,0:T(8,128)(2,1)S(1)} %bitcast.23, bf16[2,64,196]{2,1,0:T(8,128)(2,1)S(1)} %pad_maximum_fusion.piece_ref), custom_call_target="tpu_custom_call" | custom-call | tf_op jit(solution)/shard_map/factor_gradient/pallas_call | solution.py:463
  (74 shorter events, 15.6 us)
Async XLA Ops:
  0.6 11.0 %collective-permute-start = (bf16[4,6144]{1,0:T(4,128)(2,1)}, bf16[4,6144]{1,0:T(4,128)(2,1)S(1)}, u32[]{:S(2)}, u32[]{:S(2)}) collective-permute-start(bf16[4,6144]{1,0:T(4,128)(2,1)} %tokens_ref.1), channel_id=1, source_target_pairs={{0,8},{4,12},{8,0},{12,4},{16,24},{20,28},{24,16},{28,20},{1,9},{5... | collective-permute-start | bytes 147464 | tf_op jit(solution)/shard_map/ppermute | solution.py:24
  3.7 7.9 %collective-permute-start.1 = (bf16[4,6144]{1,0:T(4,128)(2,1)}, bf16[4,6144]{1,0:T(4,128)(2,1)S(1)}, u32[]{:S(2)}, u32[]{:S(2)}) collective-permute-start(bf16[4,6144]{1,0:T(4,128)(2,1)} %tokens_ref.1), channel_id=1, source_target_pairs={{0,16},{4,20},{8,24},{12,28},{16,0},{20,4},{24,8},{28,12},{1,17},{... | collective-permute-start | bytes 147464 | tf_op jit(solution)/shard_map/ppermute | solution.py:24
  6.3 6.1 %collective-permute-start.2 = (bf16[4,6144]{1,0:T(4,128)(2,1)}, bf16[4,6144]{1,0:T(4,128)(2,1)S(1)}, u32[]{:S(2)}, u32[]{:S(2)}) collective-permute-start(bf16[4,6144]{1,0:T(4,128)(2,1)} %tokens_ref.1), channel_id=1, source_target_pairs={{0,24},{4,28},{8,16},{12,20},{16,8},{20,12},{24,0},{28,4},{1,25},{... | collective-permute-start | bytes 147464 | tf_op jit(solution)/shard_map/ppermute | solution.py:24
  6.3 9.7 %collective-permute-start.3 = (bf16[4,6144]{1,0:T(4,128)(2,1)}, bf16[4,6144]{1,0:T(4,128)(2,1)S(1)}, u32[]{:S(2)}, u32[]{:S(2)}) collective-permute-start(bf16[4,6144]{1,0:T(4,128)(2,1)} %tokens_ref.1), channel_id=1, source_target_pairs={{0,4},{4,0},{8,12},{12,8},{16,20},{20,16},{24,28},{28,24},{1,5},{5... | collective-permute-start | bytes 147464 | tf_op jit(solution)/shard_map/ppermute | solution.py:24
  12.4 4.1 %collective-permute-start.4 = (bf16[4,6144]{1,0:T(4,128)(2,1)S(1)}, bf16[4,6144]{1,0:T(4,128)(2,1)S(1)}, u32[]{:S(2)}, u32[]{:S(2)}) collective-permute-start(bf16[4,6144]{1,0:T(4,128)(2,1)S(1)} %collective-permute-done.refs_1_), channel_id=1, source_target_pairs={{0,4},{4,0},{8,12},{12,8},{16,20},{20,16},{24,28},{28,24},{1,5},{5... | collective-permute-start | bytes 147464 | tf_op jit(solution)/shard_map/ppermute | solution.py:24
  13.9 4.1 %collective-permute-start.5 = (bf16[4,6144]{1,0:T(4,128)(2,1)S(1)}, bf16[4,6144]{1,0:T(4,128)(2,1)S(1)}, u32[]{:S(2)}, u32[]{:S(2)}) collective-permute-start(bf16[4,6144]{1,0:T(4,128)(2,1)S(1)} %collective-permute-done.1.refs_2_), channel_id=1, source_target_pairs={{0,4},{4,0},{8,12},{12,8},{16,20},{20,16},{24,28},{28,24},{1,5},{5... | collective-permute-start | bytes 147464 | tf_op jit(solution)/shard_map/ppermute | solution.py:24
  14.4 4.1 %collective-permute-start.6 = (bf16[4,6144]{1,0:T(4,128)(2,1)S(1)}, bf16[4,6144]{1,0:T(4,128)(2,1)S(1)}, u32[]{:S(2)}, u32[]{:S(2)}) collective-permute-start(bf16[4,6144]{1,0:T(4,128)(2,1)S(1)} %collective-permute-done.2.refs_3_), channel_id=1, source_target_pairs={{0,4},{4,0},{8,12},{12,8},{16,20},{20,16},{24,28},{28,24},{1,5},{5... | collective-permute-start | bytes 147464 | tf_op jit(solution)/shard_map/ppermute | solution.py:24
  18.8 6.4 %collective-permute-start.7 = (bf16[16,6144]{1,0:T(8,128)(2,1)S(1)}, bf16[16,6144]{1,0:T(8,128)(2,1)S(1)}, u32[]{:S(2)}, u32[]{:S(2)}) collective-permute-start(bf16[16,6144]{1,0:T(8,128)(2,1)S(1)} %get-tuple-element.73.refs_1_), channel_id=1, source_target_pairs={{0,2},{2,0},{1,3},{3,1},{4,6},{6,4},{5,7},{7,5},{8,10},{10,8},{9,1... | collective-permute-start | bytes 589832 | tf_op jit(solution)/shard_map/ppermute | solution.py:530
  20.4 5.2 %collective-permute-start.8 = (bf16[16,6144]{1,0:T(8,128)(2,1)S(1)}, bf16[16,6144]{1,0:T(8,128)(2,1)S(1)}, u32[]{:S(2)}, u32[]{:S(2)}) collective-permute-start(bf16[16,6144]{1,0:T(8,128)(2,1)S(1)} %get-tuple-element.72.refs_0_), channel_id=1, source_target_pairs={{0,1},{1,0},{2,3},{3,2},{4,5},{5,4},{6,7},{7,6},{8,9},{9,8},{10,11... | collective-permute-start | bytes 589832 | tf_op jit(solution)/shard_map/ppermute | solution.py:19
  21.9 11.5 %all-to-all-start = ((f32[32,8,128]{2,1,0:T(8,128)}), f32[32,8,128]{2,1,0:T(8,128)S(1)}, u32[]{:S(2)}, u32[]{:S(2)}) async-start(f32[32,8,128]{2,1,0:T(8,128)} %low_pieces.1), calls=%async_computation | async-start | bytes 262144 | tf_op jit(solution)/shard_map/all_to_all | solution.py:39
  39.7 5.7 %collective-permute-start.13 = (bf16[2,32,768]{2,1,0:T(8,128)(2,1)S(1)}, bf16[2,32,768]{2,1,0:T(8,128)(2,1)S(1)}, u32[]{:S(2)}, u32[]{:S(2)}) collective-permute-start(bf16[2,32,768]{2,1,0:T(8,128)(2,1)S(1)} %get-tuple-element.86), channel_id=1, source_target_pairs={{0,4},{4,0},{8,12},{12,8},{16,20},{20,16},{24,28},{28,24},{1,5},{5... | collective-permute-start | bytes 294920 | tf_op jit(solution)/shard_map/ppermute | solution.py:24
  40.5 8.1 %collective-permute-start.11 = (bf16[2,32,768]{2,1,0:T(8,128)(2,1)S(1)}, bf16[2,32,768]{2,1,0:T(8,128)(2,1)S(1)}, u32[]{:S(2)}, u32[]{:S(2)}) collective-permute-start(bf16[2,32,768]{2,1,0:T(8,128)(2,1)S(1)} %get-tuple-element.83), channel_id=1, source_target_pairs={{0,4},{4,0},{8,12},{12,8},{16,20},{20,16},{24,28},{28,24},{1,5},{5... | collective-permute-start | bytes 294920 | tf_op jit(solution)/shard_map/ppermute | solution.py:24
  41.9 7.3 %collective-permute-start.16 = (bf16[64,196]{1,0:T(8,128)(2,1)S(1)}, bf16[64,196]{1,0:T(8,128)(2,1)S(1)}, u32[]{:S(2)}, u32[]{:S(2)}) collective-permute-start(bf16[64,196]{1,0:T(8,128)(2,1)S(1)} %get-tuple-element.112), channel_id=1, source_target_pairs={{0,2},{2,0},{1,3},{3,1},{4,6},{6,4},{5,7},{7,5},{8,10},{10,8},{9,1... | collective-permute-start | bytes 75272 | tf_op jit(solution)/shard_map/ppermute | solution.py:549
  45.5 5.7 %collective-permute-start.14 = (bf16[32,768]{1,0:T(8,128)(2,1)S(1)}, bf16[32,768]{1,0:T(8,128)(2,1)S(1)}, u32[]{:S(2)}, u32[]{:S(2)}) collective-permute-start(bf16[32,768]{1,0:T(8,128)(2,1)S(1)} %get-tuple-element.87), channel_id=1, source_target_pairs={{0,16},{4,20},{8,24},{12,28},{16,0},{20,4},{24,8},{28,12},{1,17},{... | collective-permute-start | bytes 147464 | tf_op jit(solution)/shard_map/ppermute | solution.py:24
  46.9 6.0 %collective-permute-start.15 = (bf16[32,768]{1,0:T(8,128)(2,1)S(1)}, bf16[32,768]{1,0:T(8,128)(2,1)S(1)}, u32[]{:S(2)}, u32[]{:S(2)}) collective-permute-start(bf16[32,768]{1,0:T(8,128)(2,1)S(1)} %get-tuple-element.88), channel_id=1, source_target_pairs={{0,24},{4,28},{8,16},{12,20},{16,8},{20,12},{24,0},{28,4},{1,25},{... | collective-permute-start | bytes 147464 | tf_op jit(solution)/shard_map/ppermute | solution.py:24
  48.6 4.9 %collective-permute-start.12 = (bf16[32,768]{1,0:T(8,128)(2,1)S(1)}, bf16[32,768]{1,0:T(8,128)(2,1)S(1)}, u32[]{:S(2)}, u32[]{:S(2)}) collective-permute-start(bf16[32,768]{1,0:T(8,128)(2,1)S(1)} %get-tuple-element.85), channel_id=1, source_target_pairs={{0,8},{4,12},{8,0},{12,4},{16,24},{20,28},{24,16},{28,20},{1,9},{5... | collective-permute-start | bytes 147464 | tf_op jit(solution)/shard_map/ppermute | solution.py:24
  53.5 5.5 %collective-permute-start.17 = (bf16[32,768]{1,0:T(8,128)(2,1)S(1)}, bf16[32,768]{1,0:T(8,128)(2,1)S(1)}, u32[]{:S(2)}, u32[]{:S(2)}) collective-permute-start(bf16[32,768]{1,0:T(8,128)(2,1)S(1)} %mix.1.refs_4_), channel_id=1, source_target_pairs={{0,8},{4,12},{8,0},{12,4},{16,24},{20,28},{24,16},{28,20},{1,9},{5... | collective-permute-start | bytes 147464 | tf_op jit(solution)/shard_map/ppermute | solution.py:24
  53.6 5.5 %collective-permute-start.18 = (bf16[32,768]{1,0:T(8,128)(2,1)S(1)}, bf16[32,768]{1,0:T(8,128)(2,1)S(1)}, u32[]{:S(2)}, u32[]{:S(2)}) collective-permute-start(bf16[32,768]{1,0:T(8,128)(2,1)S(1)} %mix.1.refs_4_), channel_id=1, source_target_pairs={{0,16},{4,20},{8,24},{12,28},{16,0},{20,4},{24,8},{28,12},{1,17},{... | collective-permute-start | bytes 147464 | tf_op jit(solution)/shard_map/ppermute | solution.py:24
  55.8 5.9 %collective-permute-start.19 = (bf16[32,768]{1,0:T(8,128)(2,1)S(1)}, bf16[32,768]{1,0:T(8,128)(2,1)S(1)}, u32[]{:S(2)}, u32[]{:S(2)}) collective-permute-start(bf16[32,768]{1,0:T(8,128)(2,1)S(1)} %mix.1.refs_4_), channel_id=1, source_target_pairs={{0,24},{4,28},{8,16},{12,20},{16,8},{20,12},{24,0},{28,4},{1,25},{... | collective-permute-start | bytes 147464 | tf_op jit(solution)/shard_map/ppermute | solution.py:24
  57.9 5.8 %collective-permute-start.28 = (bf16[32,768]{1,0:T(8,128)(2,1)S(1)}, bf16[32,768]{1,0:T(8,128)(2,1)S(1)}, u32[]{:S(2)}, u32[]{:S(2)}) collective-permute-start(bf16[32,768]{1,0:T(8,128)(2,1)S(1)} %mix.1.refs_4_), channel_id=1, source_target_pairs={{0,1},{1,0},{2,3},{3,2},{4,5},{5,4},{6,7},{7,6},{8,9},{9,8},{10,11... | collective-permute-start | bytes 147464 | tf_op jit(solution)/shard_map/ppermute | solution.py:19
  57.9 6.3 %collective-permute-start.20 = (bf16[32,768]{1,0:T(8,128)(2,1)S(1)}, bf16[32,768]{1,0:T(8,128)(2,1)S(1)}, u32[]{:S(2)}, u32[]{:S(2)}) collective-permute-start(bf16[32,768]{1,0:T(8,128)(2,1)S(1)} %mix.1.refs_4_), channel_id=1, source_target_pairs={{0,4},{4,0},{8,12},{12,8},{16,20},{20,16},{24,28},{28,24},{1,5},{5... | collective-permute-start | bytes 147464 | tf_op jit(solution)/shard_map/ppermute | solution.py:24
  61.7 4.1 %collective-permute-start.29 = (bf16[32,768]{1,0:T(8,128)(2,1)S(1)}, bf16[32,768]{1,0:T(8,128)(2,1)S(1)}, u32[]{:S(2)}, u32[]{:S(2)}) collective-permute-start(bf16[32,768]{1,0:T(8,128)(2,1)S(1)} %collective-permute-done.17.refs_5_), channel_id=1, source_target_pairs={{0,1},{1,0},{2,3},{3,2},{4,5},{5,4},{6,7},{7,6},{8,9},{9,8},{10,11... | collective-permute-start | bytes 147464 | tf_op jit(solution)/shard_map/ppermute | solution.py:19
  61.7 4.1 %collective-permute-start.30 = (bf16[32,768]{1,0:T(8,128)(2,1)S(1)}, bf16[32,768]{1,0:T(8,128)(2,1)S(1)}, u32[]{:S(2)}, u32[]{:S(2)}) collective-permute-start(bf16[32,768]{1,0:T(8,128)(2,1)S(1)} %collective-permute-done.18.refs_6_), channel_id=1, source_target_pairs={{0,1},{1,0},{2,3},{3,2},{4,5},{5,4},{6,7},{7,6},{8,9},{9,8},{10,11... | collective-permute-start | bytes 147464 | tf_op jit(solution)/shard_map/ppermute | solution.py:19
  62.2 4.3 %collective-permute-start.21 = (bf16[32,768]{1,0:T(8,128)(2,1)S(1)}, bf16[32,768]{1,0:T(8,128)(2,1)S(1)}, u32[]{:S(2)}, u32[]{:S(2)}) collective-permute-start(bf16[32,768]{1,0:T(8,128)(2,1)S(1)} %collective-permute-done.17.refs_5_), channel_id=1, source_target_pairs={{0,4},{4,0},{8,12},{12,8},{16,20},{20,16},{24,28},{28,24},{1,5},{5... | collective-permute-start | bytes 147464 | tf_op jit(solution)/shard_map/ppermute | solution.py:24
  63.8 4.2 %collective-permute-start.22 = (bf16[32,768]{1,0:T(8,128)(2,1)S(1)}, bf16[32,768]{1,0:T(8,128)(2,1)S(1)}, u32[]{:S(2)}, u32[]{:S(2)}) collective-permute-start(bf16[32,768]{1,0:T(8,128)(2,1)S(1)} %collective-permute-done.18.refs_6_), channel_id=1, source_target_pairs={{0,4},{4,0},{8,12},{12,8},{16,20},{20,16},{24,28},{28,24},{1,5},{5... | collective-permute-start | bytes 147464 | tf_op jit(solution)/shard_map/ppermute | solution.py:24
  64.3 4.2 %collective-permute-start.23 = (bf16[32,768]{1,0:T(8,128)(2,1)S(1)}, bf16[32,768]{1,0:T(8,128)(2,1)S(1)}, u32[]{:S(2)}, u32[]{:S(2)}) collective-permute-start(bf16[32,768]{1,0:T(8,128)(2,1)S(1)} %collective-permute-done.19.refs_7_), channel_id=1, source_target_pairs={{0,4},{4,0},{8,12},{12,8},{16,20},{20,16},{24,28},{28,24},{1,5},{5... | collective-permute-start | bytes 147464 | tf_op jit(solution)/shard_map/ppermute | solution.py:24
  65.9 2.7 %collective-permute-start.31 = (bf16[32,768]{1,0:T(8,128)(2,1)S(1)}, bf16[32,768]{1,0:T(8,128)(2,1)S(1)}, u32[]{:S(2)}, u32[]{:S(2)}) collective-permute-start(bf16[32,768]{1,0:T(8,128)(2,1)S(1)} %collective-permute-done.19.refs_7_), channel_id=1, source_target_pairs={{0,1},{1,0},{2,3},{3,2},{4,5},{5,4},{6,7},{7,6},{8,9},{9,8},{10,11... | collective-permute-start | bytes 147464 | tf_op jit(solution)/shard_map/ppermute | solution.py:19
  65.9 4.2 %collective-permute-start.24 = (bf16[32,768]{1,0:T(8,128)(2,1)S(1)}, bf16[32,768]{1,0:T(8,128)(2,1)S(1)}, u32[]{:S(2)}, u32[]{:S(2)}) collective-permute-start(bf16[32,768]{1,0:T(8,128)(2,1)S(1)} %collective-permute-done.20.refs_8_), channel_id=1, source_target_pairs={{0,1},{1,0},{2,3},{3,2},{4,5},{5,4},{6,7},{7,6},{8,9},{9,8},{10,11... | collective-permute-start | bytes 147464 | tf_op jit(solution)/shard_map/ppermute | solution.py:19
  66.6 3.5 %collective-permute-start.25 = (bf16[32,768]{1,0:T(8,128)(2,1)S(1)}, bf16[32,768]{1,0:T(8,128)(2,1)S(1)}, u32[]{:S(2)}, u32[]{:S(2)}) collective-permute-start(bf16[32,768]{1,0:T(8,128)(2,1)S(1)} %collective-permute-done.21.refs_9_), channel_id=1, source_target_pairs={{0,1},{1,0},{2,3},{3,2},{4,5},{5,4},{6,7},{7,6},{8,9},{9,8},{10,11... | collective-permute-start | bytes 147464 | tf_op jit(solution)/shard_map/ppermute | solution.py:19
  67.9 2.2 %collective-permute-start.26 = (bf16[32,768]{1,0:T(8,128)(2,1)S(1)}, bf16[32,768]{1,0:T(8,128)(2,1)S(1)}, u32[]{:S(2)}, u32[]{:S(2)}) collective-permute-start(bf16[32,768]{1,0:T(8,128)(2,1)S(1)} %collective-permute-done.22.refs_10_), channel_id=1, source_target_pairs={{0,1},{1,0},{2,3},{3,2},{4,5},{5,4},{6,7},{7,6},{8,9},{9,8},{10,11... | collective-permute-start | bytes 147464 | tf_op jit(solution)/shard_map/ppermute | solution.py:19
  72.7 14.6 %all-to-all-start.1 = ((bf16[32,32,128]{2,1,0:T(8,128)(2,1)}), bf16[32,32,128]{2,1,0:T(8,128)(2,1)S(1)}, u32[]{:S(2)}, u32[]{:S(2)}) async-start(bf16[32,32,128]{2,1,0:T(8,128)(2,1)} %get-tuple-element.103), calls=%async_computation.1 | async-start | bytes 524288 | tf_op jit(solution)/shard_map/all_to_all | solution.py:39
  76.9 5.3 %collective-permute-start.32 = (bf16[4,6144]{1,0:T(4,128)(2,1)S(1)}, bf16[4,6144]{1,0:T(4,128)(2,1)S(1)}, u32[]{:S(2)}, u32[]{:S(2)}) collective-permute-start(bf16[4,6144]{1,0:T(4,128)(2,1)S(1)} %convolution_convert_fusion), channel_id=1, source_target_pairs={{0,2},{2,0},{1,3},{3,1},{4,6},{6,4},{5,7},{7,5},{8,10},{10,8},{9,1... | collective-permute-start | bytes 147464 | tf_op jit(solution)/shard_map/ppermute | solution.py:600
  (4 other events, 12.8 us)

commit v5 on v4

--- a/solution.py
+++ b/solution.py
@@ -27,12 +27,13 @@
 def gather_eight(block, *meanwhile):
     near = across(block, "dp", 1)
     far = [across(block, "dp", bits) for bits in NEAR[1:4]]
-    far, meanwhile = lax.optimization_barrier((far, meanwhile))
+    if meanwhile:
+        far[0], meanwhile = lax.optimization_barrier((far[0], meanwhile))
     return [block, *far, near, *[across(other, "dp", 1) for other in far]], *meanwhile
 
 
-def order_of(place, blocks, eight):
-    return [lax.bitwise_xor(place, NEAR[k]) if eight else k for k in range(blocks)]
+def order_of(place, blocks, eight, first=0):
+    return [lax.bitwise_xor(place, NEAR[k]) if eight else k for k in range(first, first + blocks)]
 
 
 def exchange(blocks, axis):
@@ -143,7 +144,7 @@
     capacity = parts[0].shape[0]
     rows = dot_last(jnp.concatenate([r[:, at] for r in parts], axis=0), factor_ref[...])
     for step in range(n_parts):
-        piece = beside(rows[step * capacity : (step + 1) * capacity])
+        piece = beside(rows[step * capacity : (step + 1) * capacity]).astype(bf16)
         group = lax.rem(place_ref[1] + step, n_parts)
         for i in range(out_ref.shape[0] // (2 * n_parts)):
             spot = (i * n_parts + group) * 2
@@ -160,7 +161,7 @@
         functools.partial(low_kernel, len(parts)),
         in_specs=[pl.BlockSpec(memory_space=pltpu.SMEM)] + vmem(len(parts) + 1),
         out_specs=vmem(1)[0],
-        out_shape=struct((n_dp * len(parts) * 2, capacity // 2, 2 * rank), f32),
+        out_shape=struct((n_dp * len(parts) * 2, capacity // 2, 2 * rank), bf16),
         compiler_params=params(),
         name="low_pieces",
     )(here, *parts, factor)
@@ -243,7 +244,7 @@
 
 
 def down_kernel(
-    place_ref, base_ref, lifted_ref, low_ref, factor_ref, weight_ref, own_ref, other_ref, pre_ref, low_out, down_ref, sems
+    place_ref, base_ref, lifted_ref, low_ref, factor_ref, weight_ref, own_ref, other_ref, slope_ref, low_out, down_ref, sems
 ):
     blocks, half, wide = own_ref.shape
     copies = bring(weight_ref, down_ref, sems, [k * wide for k in range(blocks)])
@@ -252,12 +253,14 @@
     for core in (place_ref[2], 1 - place_ref[2]):
         for step in range(groups):
             group = lax.rem(place_ref[1] - step + groups, groups)
-            sums.append(apart(jnp.sum(low_ref[:, group, core], axis=0)))
+            sums.append(apart(jnp.sum(low_ref[:, group, core].astype(f32), axis=0)))
     low = jnp.concatenate(sums, axis=0).astype(bf16)
     pre = base_ref[...] + adapter_scale * dot(low, factor_ref[...])
     low_out[...] = low
-    pre_ref[...] = pre
-    hidden = (pre * sigmoid(pre) * lifted_ref[...]).astype(bf16)
+    lifted = lifted_ref[...]
+    sig = sigmoid(pre)
+    slope_ref[...] = (lifted * (sig * (1.0 + pre * (1.0 - sig)))).T
+    hidden = (pre * sig * lifted).astype(bf16)
     for k in range(blocks):
         if k % 2 == 0:
             copies[k].wait()
@@ -279,7 +282,7 @@
         out_shape=(
             shape,
             shape,
-            struct((count, units), f32),
+            struct((units, count), f32),
             struct((count, factor.shape[0]), bf16),
             pltpu.VMEM((blocks, units, width // blocks), bf16),
         ),
@@ -381,29 +384,45 @@
 
 def back_last_kernel(n_parts, n_blocks, eight, loss_factor, here_ref, *refs):
     parts, refs = refs[:n_parts], refs[n_parts:]
-    owns, refs = refs[: 2 * n_blocks], refs[2 * n_blocks :]
-    others, refs = refs[:n_blocks], refs[n_blocks:]
-    gate_ref, down_ref, first_ref, pre_ref, lifted_ref, low_ref, factor_ref = refs[:7]
-    low_out, grad_ref, *homes = refs[7:]
+    owns, others, refs = refs[:n_blocks], refs[n_blocks : 2 * n_blocks], refs[2 * n_blocks :]
+    gate_ref, down_ref, first_ref, slope_ref, factor_ref, low_out, back_out = refs
+    order = order_of(here_ref[0], n_blocks, eight, n_blocks)
+    total = first_ref[...] + back_sum(parts, owns, others, order, gate_ref, down_ref, loss_factor)
+    back_pre = (total * slope_ref[...]).astype(bf16)
+    back_low = beside(adapter_scale * dot(factor_ref[...], back_pre)).astype(bf16)
+    for i in range(low_out.shape[0]):
+        low_out[i] = back_low
+    back_out[...] = back_pre
+
+
+def rest_kernel(n_blocks, eight, here_ref, *refs):
+    owns, (back_ref, low_ref, grad_ref, *homes) = refs[:n_blocks], refs[n_blocks:]
     half, wide = owns[0].shape
     capacity = half // len(homes)
-    order = order_of(here_ref[0], 2 * n_blocks, eight)
-    pre = pre_ref[...]
-    sig = sigmoid(pre)
-    slope = lifted_ref[...] * (sig * (1.0 + pre * (1.0 - sig)))
-    total = first_ref[...] + back_sum(
-        parts, owns[n_blocks:], others, order[n_blocks:], gate_ref, down_ref, loss_factor
+    grad_ref[...] = adapter_scale * lax.dot_general(
+        low_ref[...], back_ref[...], (((0,), (1,)), ((), ())), preferred_element_type=f32
     )
-    back_pre = (total.T * slope).astype(bf16)
-    back_low = beside(adapter_scale * dot_last(back_pre, factor_ref[...])).astype(bf16)
-    for i in range(low_out.shape[0]):
-        low_out[i] = back_low
-    grad_ref[...] = adapter_scale * dot_first(low_ref[...], back_pre)
-    for block, own in zip(order, owns):
+    for block, own in zip(order_of(here_ref[0], n_blocks, eight), owns):
         start = block * wide
         at = pl.ds(start if isinstance(start, int) else pl.multiple_of(start, wide), wide)
         for step, home in enumerate(homes):
             home[:, at] = own[step * capacity : (step + 1) * capacity]
+
+
+def rest(owns, here, eight, back_pre, low, capacity):
+    half, wide = owns[0].shape
+    homes = half // capacity
+    return pl.pallas_call(
+        functools.partial(rest_kernel, len(owns), eight),
+        in_specs=[pl.BlockSpec(memory_space=pltpu.SMEM)] + vmem(len(owns) + 2),
+        out_specs=vmem(1 + homes),
+        out_shape=(
+            struct((low.shape[1], back_pre.shape[0]), f32),
+            *[struct((capacity, wide * len(owns)), bf16)] * homes,
+        ),
+        compiler_params=params(),
+        name="rest",
+    )(here, *owns, back_pre, low)
 
 
 def back_first(parts, owns, others, here, eight, gate, kept, loss_factor):
@@ -420,46 +439,41 @@
     )(here, *parts, *owns, *others, gate, kept)
 
 
-def back_last(parts, owns, others, here, eight, gate, kept, first, pre, lifted, low, factor, loss_factor, copies):
-    capacity, width = parts[0].shape
-    half, wide = owns[0].shape
-    count, units = pre.shape
+def back_last(parts, owns, others, here, eight, gate, kept, first, slope, factor, loss_factor, copies):
+    wide = owns[0].shape[1]
+    units, count = slope.shape
     rank, blocks = factor.shape[0], len(others)
-    homes = half // capacity
     return pl.pallas_call(
         functools.partial(back_last_kernel, len(parts), blocks, eight, loss_factor),
-        in_specs=[pl.BlockSpec(memory_space=pltpu.SMEM)] + vmem(len(parts) + 3 * blocks + 7),
-        out_specs=vmem(2 + homes),
-        out_shape=(
-            struct((copies, half, 2 * rank), bf16),
-            struct((rank, units), f32),
-            *[struct((capacity, width), bf16)] * homes,
-        ),
+        in_specs=[pl.BlockSpec(memory_space=pltpu.SMEM)] + vmem(len(parts) + 2 * blocks + 5),
+        out_specs=vmem(2),
+        out_shape=(struct((copies, rank // 2, 2 * count), bf16), struct((units, count), bf16)),
         cost_estimate=cost(2 * count * blocks * wide * units, 2 * blocks * wide * units),
         compiler_params=params(),
         name="back_last",
-    )(here, *parts, *owns, *others, gate, kept, first, pre, lifted, low, factor)
+    )(here, *parts, *owns, *others, gate, kept, first, slope, factor)
 
 
 def factor_kernel(place_ref, low_ref, piece_ref, out_ref):
-    rank, share = out_ref.shape
-    groups = piece_ref.shape[0]
+    share = out_ref.shape[1]
+    groups, count = piece_ref.shape[:2]
+    half = count // 2
     group, core = place_ref[1], place_ref[2]
     lows, rows = [], []
     for step in range(groups):
         source = lax.rem(group - step + groups, groups)
-        mine = jnp.sum(low_ref[:, source, core].astype(f32), axis=0)
-        theirs = jnp.sum(low_ref[:, source, 1 - core].astype(f32), axis=0)
-        lows += [mine[:, :rank] + theirs[:, rank:], mine[:, rank:] + theirs[:, :rank]]
+        mine = apart(jnp.sum(low_ref[:, source, core].astype(f32), axis=0))
+        theirs = apart(jnp.sum(low_ref[:, source, 1 - core].astype(f32), axis=0))
+        lows.append(mine + jnp.concatenate([theirs[:, half:], theirs[:, :half]], axis=1))
         rows.append(piece_ref[step, :, :share])
-    low = jnp.concatenate(lows, axis=0)
+    low = jnp.concatenate(lows, axis=1)
     high = low.astype(bf16)
     rest = (low - high.astype(f32)).astype(bf16)
-    out_ref[...] = dot_first(jnp.concatenate([high, rest], axis=0), jnp.concatenate(rows + rows, axis=0))
+    out_ref[...] = dot(jnp.concatenate([high, rest], axis=1), jnp.concatenate(rows + rows, axis=0))
 
 
 def factor_gradient(lows, pieces, share, here):
-    rank = lows.shape[-1] // 2
+    rank = 2 * lows.shape[3]
     return pl.pallas_call(
         factor_kernel,
         in_specs=[pl.BlockSpec(memory_space=pltpu.SMEM)] + vmem(2),
@@ -513,11 +527,9 @@
     placer = (index[:, None] == target[None, :]).astype(bf16)
     tokens_near, factor, own_route = brought_near(tokens, adapter_down_shared.T, router.T, here)
     if eight:
-        column, placer, tokens_near, factor, own_route = gather_eight(
-            tokens, placer, tokens_near, factor, own_route
-        )
+        column, placer = gather_eight(tokens, placer)
         column[0] = tokens_near
-        column, placer, factor = lax.optimization_barrier((column, placer, factor))
+        column, placer, factor, own_route = lax.optimization_barrier((column, placer, factor, own_route))
         own_target = target[:tok_rows]
     else:
         column = exchange(jnp.broadcast_to(tokens[None], (n_dp, tok_rows, width)), "dp")
@@ -534,7 +546,7 @@
     low_parts = exchange(low_parts, every).reshape(n_dp, groups, 2, capacity // 2, 2 * rank)
     base, lifted, gate = lift(parts, gate_weight, up_weight, own_route)
     low_parts, gate = lax.optimization_barrier((low_parts, gate))
-    own, other, pre, low, kept = down(
+    own, other, slope, low, kept = down(
         base, lifted, low_parts, adapter_gate_factor, down_weight, blocks, here
     )
 
@@ -571,23 +583,22 @@
     first = back_first(
         parts, owns[: blocks // 2], others[: blocks // 2], here, eight, gate, kept, loss_factor
     )
-    back_low, grad_b, *homes = back_last(
+    back_low, back_pre = back_last(
         parts,
-        owns,
+        owns[blocks // 2 :],
         others[blocks // 2 :],
         here,
         eight,
         gate,
         kept,
         first,
-        pre,
-        lifted,
-        low,
+        slope,
         adapter_gate_factor,
         loss_factor,
         devices,
     )
-    lows = exchange(back_low, every).reshape(n_dp, groups, 2, half, 2 * rank)
+    lows = exchange(back_low, every).reshape(n_dp, groups, 2, rank // 2, 4 * half)
+    grad_b, *homes = rest(owns, here, eight, back_pre, low, capacity)
 
     result = jnp.zeros((tok_rows, width), f32)
     for step in range(groups):

time: 89.1 us -> 86.9 us (0.975)
  waiting for transfers between devices: 26.9 us -> 21.5 us
  starting transfers between devices: 38.7 us -> 40.5 us
  Pallas kernels: 18.9 us -> 20.3 us
    ppermute x19, waiting for transfers between devices: 15.4 us -> 12 us  [across(): return lax.ppermute(block, axis, [(i, i ^ apart_by) for i in range(count)])]
    all_to_all x2, waiting for transfers between devices: 5.56 us -> 3.6 us  [exchange(): return lax.all_to_all(blocks, axis, 0, 0, tiled=True)]
    pallas_call x0 -> x1, Pallas kernels: none -> 1.39 us  [rest(): pl.pallas_call(functools.partial(rest_kernel, len(owns), eight), in_specs...]
  transfers between devices with their start and end apart: 35 -> 35, of which waited for: 17 -> 14; matrix products, arithmetic and copies ran while one was open for 4% -> 4% of each run, Pallas kernels for 11% -> 13%
where the time goes in v5:
time: 86.9 us; the launch traced here: 86.6 us
  starting transfers between devices  40.5 us (47%)
  waiting for transfers between devices  21.5 us (25%)
  Pallas kernels  20.3 us (23%)
  other arithmetic  1.95 us (2%)
  matrix products  1.06 us (1%)
  between operations  0.91 us (1%)
    ppermute x19, starting transfers between devices, across(): return lax.ppermute(block, axis, [(i, i ^ apart_by) for i in range(count)])  26.4 us
    ppermute x19, waiting for transfers between devices, across(): return lax.ppermute(block, axis, [(i, i ^ apart_by) for i in range(count)])  12 us
    all_to_all x2, starting transfers between devices, exchange(): return lax.all_to_all(blocks, axis, 0, 0, tiled=True)  7.71 us
    pallas_call x1, Pallas kernels, lift(): pl.pallas_call(functools.partial(lift_kernel, len(parts)), in_specs=vmem(...  5.41 us
    pallas_call x1, Pallas kernels, down(): pl.pallas_call(down_kernel, in_specs=[pl.BlockSpec(memory_space=pltpu.SME...  3.89 us
    all_to_all x2, waiting for transfers between devices, exchange(): return lax.all_to_all(blocks, axis, 0, 0, tiled=True)  3.6 us
    ppermute x1, waiting for transfers between devices, shards(): chosen = lax.ppermute(chosen.astype(bf16), 'x', route).astype(f32)  3.18 us
    ppermute x11, waiting for transfers between devices, swap(): return lax.ppermute(block, axis, [(0, 1), (1, 0)])  2.64 us
  transfers between devices with their start and end apart: 35, of which 14 were waited for; matrix products, arithmetic and copies ran while one was open for 4% of the time, Pallas kernels for 13%

profile of v5, /device:TPU:0, one launch (start us, length us, event | category | flops | bytes accessed | tf_op | source)
XLA Modules:
  0.0 86.6 jit_solution(2227283505552274227)
XLA Ops:
  0.6 3.1 %collective-permute-start = (bf16[4,6144]{1,0:T(4,128)(2,1)}, bf16[4,6144]{1,0:T(4,128)(2,1)S(1)}, u32[]{:S(2)}, u32[]{:S(2)}) collective-permute-start(bf16[4,6144]{1,0:T(4,128)(2,1)} %tokens_ref.1), channel_id=1, source_target_pairs={{0,8},{4,12},{8,0},{12,4},{16,24},{20,28},{24,16},{28,20},{1,9},{5... | collective-permute-start | bytes 147464 | tf_op jit(solution)/shard_map/ppermute | solution.py:24
  3.7 2.6 %collective-permute-start.1 = (bf16[4,6144]{1,0:T(4,128)(2,1)}, bf16[4,6144]{1,0:T(4,128)(2,1)S(1)}, u32[]{:S(2)}, u32[]{:S(2)}) collective-permute-start(bf16[4,6144]{1,0:T(4,128)(2,1)} %tokens_ref.1), channel_id=1, source_target_pairs={{0,16},{4,20},{8,24},{12,28},{16,0},{20,4},{24,8},{28,12},{1,17},{... | collective-permute-start | bytes 147464 | tf_op jit(solution)/shard_map/ppermute | solution.py:24
  6.3 1.7 %collective-permute-start.3 = (bf16[4,6144]{1,0:T(4,128)(2,1)}, bf16[4,6144]{1,0:T(4,128)(2,1)S(1)}, u32[]{:S(2)}, u32[]{:S(2)}) collective-permute-start(bf16[4,6144]{1,0:T(4,128)(2,1)} %tokens_ref.1), channel_id=1, source_target_pairs={{0,4},{4,0},{8,12},{12,8},{16,20},{20,16},{24,28},{28,24},{1,5},{5... | collective-permute-start | bytes 147464 | tf_op jit(solution)/shard_map/ppermute | solution.py:24
  10.3 1.7 %collective-permute-start.5 = (bf16[4,6144]{1,0:T(4,128)(2,1)S(1)}, bf16[4,6144]{1,0:T(4,128)(2,1)S(1)}, u32[]{:S(2)}, u32[]{:S(2)}) collective-permute-start(bf16[4,6144]{1,0:T(4,128)(2,1)S(1)} %collective-permute-done.1.refs_2_), channel_id=1, source_target_pairs={{0,4},{4,0},{8,12},{12,8},{16,20},{20,16},{24,28},{28,24},{1,5},{5... | collective-permute-start | bytes 147464 | tf_op jit(solution)/shard_map/ppermute | solution.py:24
  12.4 1.5 %collective-permute-start.6 = (bf16[4,6144]{1,0:T(4,128)(2,1)S(1)}, bf16[4,6144]{1,0:T(4,128)(2,1)S(1)}, u32[]{:S(2)}, u32[]{:S(2)}) collective-permute-start(bf16[4,6144]{1,0:T(4,128)(2,1)S(1)} %collective-permute-done.2.refs_3_), channel_id=1, source_target_pairs={{0,4},{4,0},{8,12},{12,8},{16,20},{20,16},{24,28},{28,24},{1,5},{5... | collective-permute-start | bytes 147464 | tf_op jit(solution)/shard_map/ppermute | solution.py:24
  14.1 1.6 %near.1 = (bf16[4,6144]{1,0:T(4,128)(2,1)S(1)}, bf16[64,768]{1,0:T(8,128)(2,1)S(1)}, f32[1,6144]{1,0:T(1,128)S(1)}) custom-call(s32[3]{0:T(128)S(1)} %pad_add_fusion.here_ref.place_ref, bf16[4,6144]{1,0:T(4,128)(2,1)} %tokens_ref.1, bf16[64,768]{1,0:T(8,128)(2,1)} %bitcast.25, bf16[2,6144]{1,0:T(2,128)(2,1)} %bitcast.28), custom_call_target="tpu_custom_call" | custom-call | tf_op jit(solution)/shard_map/near/pallas_call | solution.py:97
  16.8 1.6 %collective-permute-start.7 = (bf16[16,6144]{1,0:T(8,128)(2,1)S(1)}, bf16[16,6144]{1,0:T(8,128)(2,1)S(1)}, u32[]{:S(2)}, u32[]{:S(2)}) collective-permute-start(bf16[16,6144]{1,0:T(8,128)(2,1)S(1)} %get-tuple-element.63.refs_1_), channel_id=1, source_target_pairs={{0,2},{2,0},{1,3},{3,1},{4,6},{6,4},{5,7},{7,5},{8,10},{10,8},{9,1... | collective-permute-start | bytes 589832 | tf_op jit(solution)/shard_map/ppermute | solution.py:542
  18.4 1.4 %low_pieces.1 = bf16[32,8,128]{2,1,0:T(8,128)(2,1)} custom-call(s32[3]{0:T(128)S(1)} %pad_add_fusion.here_ref.place_ref, bf16[16,6144]{1,0:T(8,128)(2,1)S(1)} %get-tuple-element.62.refs_0_, bf16[16,6144]{1,0:T(8,128)(2,1)S(1)} %get-tuple-element.63.refs_1_, bf16[64,768]{1,0:T(8,128)(2,1)S(1)} %get-tuple-element.67.refs_2_), custom_call_target="tpu_custom_call" | custom-call | tf_op jit(solution)/shard_map/low_pieces/pallas_call | solution.py:160
  19.8 3.7 %all-to-all-start = ((bf16[32,8,128]{2,1,0:T(8,128)(2,1)}), bf16[32,8,128]{2,1,0:T(8,128)(2,1)S(1)}, u32[]{:S(2)}, u32[]{:S(2)}) async-start(bf16[32,8,128]{2,1,0:T(8,128)(2,1)} %low_pieces.1), calls=%async_computation | async-start | bytes 131072 | tf_op jit(solution)/shard_map/all_to_all | solution.py:40
  25.0 5.4 %lift.1 = (f32[64,512]{1,0:T(8,128)S(1)}, f32[64,512]{1,0:T(8,128)S(1)}, f32[64,1]{1,0:T(8,128)S(1)}) custom-call(bf16[16,6144]{1,0:T(8,128)(2,1)S(1)} %get-tuple-element.62.refs_0_, bf16[16,6144]{1,0:T(8,128)(2,1)S(1)} %collective-permute-done.7.refs_1_, bf16[16,6144]{1,0:T(8,128)(2,1)S(1)} %collective-permute-done.8.refs_2_, ...), custom_call_target="tpu_custom_call" | custom-call | flops 805306368 | bytes 12582912 | tf_op jit(solution)/shard_map/lift/pallas_call | solution.py:209
  30.9 3.9 %down.1 = (bf16[8,32,768]{2,1,0:T(8,128)(2,1)S(1)}, bf16[8,32,768]{2,1,0:T(8,128)(2,1)S(1)}, f32[512,64]{1,0:T(8,128)S(1)}, bf16[64,64]{1,0:T(8,128)(2,1)S(1)}, bf16[8,512,768]{2,1,0:T(8,128)(2,1)S(1)}) custom-call(s32[3]{0:T(128)S(1)} %pad_add_fusion.here_ref.place_ref, f32[64,512]{1,0:T(8,128)S(1)} %get-tuple-element.65.base_ref, ...), custom_call_target="tpu_custom_call" | custom-call | flops 402653184 | bytes 6291456 | tf_op jit(solution)/shard_map/down/pallas_call | solution.py:277
  35.1 1.5 %collective-permute-done.10.got_ref = bf16[8,32,768]{2,1,0:T(8,128)(2,1)S(1)} collective-permute-done((bf16[8,32,768]{2,1,0:T(8,128)(2,1)S(1)}, bf16[8,32,768]{2,1,0:T(8,128)(2,1)S(1)}, u32[]{:S(2)}, u32[]{:S(2)}) %collective-permute-start.10) | collective-permute-done | bytes 393248 | tf_op jit(solution)/shard_map/ppermute | solution.py:19
  39.4 1.4 %collective-permute-start.16 = (bf16[64,196]{1,0:T(8,128)(2,1)S(1)}, bf16[64,196]{1,0:T(8,128)(2,1)S(1)}, u32[]{:S(2)}, u32[]{:S(2)}) collective-permute-start(bf16[64,196]{1,0:T(8,128)(2,1)S(1)} %get-tuple-element.100), channel_id=1, source_target_pairs={{0,2},{2,0},{1,3},{3,1},{4,6},{6,4},{5,7},{7,5},{8,10},{10,8},{9,1... | collective-permute-start | bytes 75272 | tf_op jit(solution)/shard_map/ppermute | solution.py:561
  40.8 2.2 %collective-permute-done.13.got_ref = bf16[2,32,768]{2,1,0:T(8,128)(2,1)S(1)} collective-permute-done((bf16[2,32,768]{2,1,0:T(8,128)(2,1)S(1)}, bf16[2,32,768]{2,1,0:T(8,128)(2,1)S(1)}, u32[]{:S(2)}, u32[]{:S(2)}) %collective-permute-start.13) | collective-permute-done | bytes 98336 | tf_op jit(solution)/shard_map/ppermute | solution.py:24
  43.0 2.3 %collective-permute-start.14 = (bf16[32,768]{1,0:T(8,128)(2,1)S(1)}, bf16[32,768]{1,0:T(8,128)(2,1)S(1)}, u32[]{:S(2)}, u32[]{:S(2)}) collective-permute-start(bf16[32,768]{1,0:T(8,128)(2,1)S(1)} %get-tuple-element.77), channel_id=1, source_target_pairs={{0,16},{4,20},{8,24},{12,28},{16,0},{20,4},{24,8},{28,12},{1,17},{... | collective-permute-start | bytes 147464 | tf_op jit(solution)/shard_map/ppermute | solution.py:24
  45.3 1.5 %collective-permute-start.15 = (bf16[32,768]{1,0:T(8,128)(2,1)S(1)}, bf16[32,768]{1,0:T(8,128)(2,1)S(1)}, u32[]{:S(2)}, u32[]{:S(2)}) collective-permute-start(bf16[32,768]{1,0:T(8,128)(2,1)S(1)} %get-tuple-element.78), channel_id=1, source_target_pairs={{0,24},{4,28},{8,16},{12,20},{16,8},{20,12},{24,0},{28,4},{1,25},{... | collective-permute-start | bytes 147464 | tf_op jit(solution)/shard_map/ppermute | solution.py:24
  46.9 2.2 %collective-permute-done.14.refs_2_ = bf16[32,768]{1,0:T(8,128)(2,1)S(1)} collective-permute-done((bf16[32,768]{1,0:T(8,128)(2,1)S(1)}, bf16[32,768]{1,0:T(8,128)(2,1)S(1)}, u32[]{:S(2)}, u32[]{:S(2)}) %collective-permute-start.14) | collective-permute-done | bytes 49184 | tf_op jit(solution)/shard_map/ppermute | solution.py:24
  49.1 2.2 %collective-permute-done.15.refs_3_ = bf16[32,768]{1,0:T(8,128)(2,1)S(1)} collective-permute-done((bf16[32,768]{1,0:T(8,128)(2,1)S(1)}, bf16[32,768]{1,0:T(8,128)(2,1)S(1)}, u32[]{:S(2)}, u32[]{:S(2)}) %collective-permute-start.15) | collective-permute-done | bytes 49184 | tf_op jit(solution)/shard_map/ppermute | solution.py:24
  51.6 2.6 %collective-permute-start.18 = (bf16[32,768]{1,0:T(8,128)(2,1)S(1)}, bf16[32,768]{1,0:T(8,128)(2,1)S(1)}, u32[]{:S(2)}, u32[]{:S(2)}) collective-permute-start(bf16[32,768]{1,0:T(8,128)(2,1)S(1)} %mix.1.refs_4_.refs_0_), channel_id=1, source_target_pairs={{0,16},{4,20},{8,24},{12,28},{16,0},{20,4},{24,8},{28,12},{1,17},{... | collective-permute-start | bytes 147464 | tf_op jit(solution)/shard_map/ppermute | solution.py:24
  54.2 1.7 %collective-permute-start.19 = (bf16[32,768]{1,0:T(8,128)(2,1)S(1)}, bf16[32,768]{1,0:T(8,128)(2,1)S(1)}, u32[]{:S(2)}, u32[]{:S(2)}) collective-permute-start(bf16[32,768]{1,0:T(8,128)(2,1)S(1)} %mix.1.refs_4_.refs_0_), channel_id=1, source_target_pairs={{0,24},{4,28},{8,16},{12,20},{16,8},{20,12},{24,0},{28,4},{1,25},{... | collective-permute-start | bytes 147464 | tf_op jit(solution)/shard_map/ppermute | solution.py:24
  56.0 1.5 %collective-permute-start.20 = (bf16[32,768]{1,0:T(8,128)(2,1)S(1)}, bf16[32,768]{1,0:T(8,128)(2,1)S(1)}, u32[]{:S(2)}, u32[]{:S(2)}) collective-permute-start(bf16[32,768]{1,0:T(8,128)(2,1)S(1)} %mix.1.refs_4_.refs_0_), channel_id=1, source_target_pairs={{0,4},{4,0},{8,12},{12,8},{16,20},{20,16},{24,28},{28,24},{1,5},{5... | collective-permute-start | bytes 147464 | tf_op jit(solution)/shard_map/ppermute | solution.py:24
  57.9 2.2 %collective-permute-done.19.refs_7_.refs_3_ = bf16[32,768]{1,0:T(8,128)(2,1)S(1)} collective-permute-done((bf16[32,768]{1,0:T(8,128)(2,1)S(1)}, bf16[32,768]{1,0:T(8,128)(2,1)S(1)}, u32[]{:S(2)}, u32[]{:S(2)}) %collective-permute-start.19) | collective-permute-done | bytes 49184 | tf_op jit(solution)/shard_map/ppermute | solution.py:24
  60.1 1.5 %collective-permute-start.21 = (bf16[32,768]{1,0:T(8,128)(2,1)S(1)}, bf16[32,768]{1,0:T(8,128)(2,1)S(1)}, u32[]{:S(2)}, u32[]{:S(2)}) collective-permute-start(bf16[32,768]{1,0:T(8,128)(2,1)S(1)} %collective-permute-done.17.refs_5_.refs_1_), channel_id=1, source_target_pairs={{0,4},{4,0},{8,12},{12,8},{16,20},{20,16},{24,28},{28,24},{1,5},{5... | collective-permute-start | bytes 147464 | tf_op jit(solution)/shard_map/ppermute | solution.py:24
  62.1 1.5 %collective-permute-start.23 = (bf16[32,768]{1,0:T(8,128)(2,1)S(1)}, bf16[32,768]{1,0:T(8,128)(2,1)S(1)}, u32[]{:S(2)}, u32[]{:S(2)}) collective-permute-start(bf16[32,768]{1,0:T(8,128)(2,1)S(1)} %collective-permute-done.19.refs_7_.refs_3_), channel_id=1, source_target_pairs={{0,4},{4,0},{8,12},{12,8},{16,20},{20,16},{24,28},{28,24},{1,5},{5... | collective-permute-start | bytes 147464 | tf_op jit(solution)/shard_map/ppermute | solution.py:24
  66.3 1.6 %back_first.1.refs_14_ = f32[512,64]{1,0:T(8,128)S(1)} custom-call(s32[3]{0:T(128)S(1)} %pad_add_fusion.here_ref.place_ref, bf16[16,6144]{1,0:T(8,128)(2,1)S(1)} %get-tuple-element.62.refs_0_, bf16[16,6144]{1,0:T(8,128)(2,1)S(1)} %collective-permute-done.7.refs_1_, bf16[16,6144]{1,0:T(8,128)(2,1)S(1)} %collective-permute-done.8.refs_2_, ...), custom_call_target="tpu_custom_call" | custom-call | flops 201326592 | bytes 3145728 | tf_op jit(solution)/shard_map/back_first/pallas_call | solution.py:431
  67.9 2.5 %back_last.1 = (bf16[32,32,128]{2,1,0:T(8,128)(2,1)}, bf16[512,64]{1,0:T(8,128)(2,1)S(1)}) custom-call(s32[3]{0:T(128)S(1)} %pad_add_fusion.here_ref.place_ref, bf16[16,6144]{1,0:T(8,128)(2,1)S(1)} %get-tuple-element.62.refs_0_, bf16[16,6144]{1,0:T(8,128)(2,1)S(1)} %collective-permute-done.7.refs_1_, bf16[16,6144]{1,0:T(8,128)(2,1)S(1)} %collective-permute-done.8.refs_2_, ...), custom_call_target="tpu_custom_call" | custom-call | flops 201326592 | bytes 3145728 | tf_op jit(solution)/shard_map/back_last/pallas_call | solution.py:446
  70.5 4.0 %all-to-all-start.1 = ((bf16[32,32,128]{2,1,0:T(8,128)(2,1)}), bf16[32,32,128]{2,1,0:T(8,128)(2,1)S(1)}, u32[]{:S(2)}, u32[]{:S(2)}) async-start(bf16[32,32,128]{2,1,0:T(8,128)(2,1)} %get-tuple-element.91), calls=%async_computation.1 | async-start | bytes 524288 | tf_op jit(solution)/shard_map/all_to_all | solution.py:40
  74.5 1.4 %rest.1 = (f32[64,512]{1,0:T(8,128)}, bf16[16,6144]{1,0:T(8,128)(2,1)S(1)}, bf16[16,6144]{1,0:T(8,128)(2,1)S(1)}) custom-call(s32[3]{0:T(128)S(1)} %pad_add_fusion.here_ref.place_ref, bf16[32,768]{1,0:T(8,128)(2,1)S(1)} %mix.1.refs_4_.refs_0_, bf16[32,768]{1,0:T(8,128)(2,1)S(1)} %collective-permute-done.17.refs_5_.refs_1_, ...), custom_call_target="tpu_custom_call" | custom-call | tf_op jit(solution)/shard_map/rest/pallas_call | solution.py:415
  76.1 1.8 %collective-permute-start.32 = (bf16[4,6144]{1,0:T(4,128)(2,1)S(1)}, bf16[4,6144]{1,0:T(4,128)(2,1)S(1)}, u32[]{:S(2)}, u32[]{:S(2)}) collective-permute-start(bf16[4,6144]{1,0:T(4,128)(2,1)S(1)} %convolution_convert_fusion), channel_id=1, source_target_pairs={{0,2},{2,0},{1,3},{3,1},{4,6},{6,4},{5,7},{7,5},{8,10},{10,8},{9,1... | collective-permute-start | bytes 147464 | tf_op jit(solution)/shard_map/ppermute | solution.py:611
  77.9 3.2 %collective-permute-done.32 = bf16[4,6144]{1,0:T(4,128)(2,1)S(1)} collective-permute-done((bf16[4,6144]{1,0:T(4,128)(2,1)S(1)}, bf16[4,6144]{1,0:T(4,128)(2,1)S(1)}, u32[]{:S(2)}, u32[]{:S(2)}) %collective-permute-start.32) | collective-permute-done | bytes 49184 | tf_op jit(solution)/shard_map/ppermute | solution.py:611
  82.0 3.1 %all-to-all-done.1 = bf16[32,32,128]{2,1,0:T(8,128)(2,1)S(1)} async-done(((bf16[32,32,128]{2,1,0:T(8,128)(2,1)}), bf16[32,32,128]{2,1,0:T(8,128)(2,1)S(1)}, u32[]{:S(2)}, u32[]{:S(2)}) %all-to-all-start.1) | async-done | bytes 262176 | tf_op jit(solution)/shard_map/all_to_all | solution.py:40
  85.1 1.5 %factor_gradient.1 = f32[64,192]{1,0:T(8,128)} custom-call(s32[3]{0:T(128)S(1)} %pad_add_fusion.here_ref.place_ref, bf16[8,2,2,32,128]{4,3,2,1,0:T(8,128)(2,1)S(1)} %bitcast.23, bf16[2,64,196]{2,1,0:T(8,128)(2,1)S(1)} %pad_maximum_fusion.piece_ref), custom_call_target="tpu_custom_call" | custom-call | tf_op jit(solution)/shard_map/factor_gradient/pallas_call | solution.py:477
  (75 shorter events, 14.2 us)
Async XLA Ops:
  0.6 9.3 %collective-permute-start = (bf16[4,6144]{1,0:T(4,128)(2,1)}, bf16[4,6144]{1,0:T(4,128)(2,1)S(1)}, u32[]{:S(2)}, u32[]{:S(2)}) collective-permute-start(bf16[4,6144]{1,0:T(4,128)(2,1)} %tokens_ref.1), channel_id=1, source_target_pairs={{0,8},{4,12},{8,0},{12,4},{16,24},{20,28},{24,16},{28,20},{1,9},{5... | collective-permute-start | bytes 147464 | tf_op jit(solution)/shard_map/ppermute | solution.py:24
  3.7 6.6 %collective-permute-start.1 = (bf16[4,6144]{1,0:T(4,128)(2,1)}, bf16[4,6144]{1,0:T(4,128)(2,1)S(1)}, u32[]{:S(2)}, u32[]{:S(2)}) collective-permute-start(bf16[4,6144]{1,0:T(4,128)(2,1)} %tokens_ref.1), channel_id=1, source_target_pairs={{0,16},{4,20},{8,24},{12,28},{16,0},{20,4},{24,8},{28,12},{1,17},{... | collective-permute-start | bytes 147464 | tf_op jit(solution)/shard_map/ppermute | solution.py:24
  6.3 6.1 %collective-permute-start.2 = (bf16[4,6144]{1,0:T(4,128)(2,1)}, bf16[4,6144]{1,0:T(4,128)(2,1)S(1)}, u32[]{:S(2)}, u32[]{:S(2)}) collective-permute-start(bf16[4,6144]{1,0:T(4,128)(2,1)} %tokens_ref.1), channel_id=1, source_target_pairs={{0,24},{4,28},{8,16},{12,20},{16,8},{20,12},{24,0},{28,4},{1,25},{... | collective-permute-start | bytes 147464 | tf_op jit(solution)/shard_map/ppermute | solution.py:24
  6.3 9.3 %collective-permute-start.3 = (bf16[4,6144]{1,0:T(4,128)(2,1)}, bf16[4,6144]{1,0:T(4,128)(2,1)S(1)}, u32[]{:S(2)}, u32[]{:S(2)}) collective-permute-start(bf16[4,6144]{1,0:T(4,128)(2,1)} %tokens_ref.1), channel_id=1, source_target_pairs={{0,4},{4,0},{8,12},{12,8},{16,20},{20,16},{24,28},{28,24},{1,5},{5... | collective-permute-start | bytes 147464 | tf_op jit(solution)/shard_map/ppermute | solution.py:24
  9.9 5.7 %collective-permute-start.4 = (bf16[4,6144]{1,0:T(4,128)(2,1)S(1)}, bf16[4,6144]{1,0:T(4,128)(2,1)S(1)}, u32[]{:S(2)}, u32[]{:S(2)}) collective-permute-start(bf16[4,6144]{1,0:T(4,128)(2,1)S(1)} %collective-permute-done.refs_1_), channel_id=1, source_target_pairs={{0,4},{4,0},{8,12},{12,8},{16,20},{20,16},{24,28},{28,24},{1,5},{5... | collective-permute-start | bytes 147464 | tf_op jit(solution)/shard_map/ppermute | solution.py:24
  10.3 5.4 %collective-permute-start.5 = (bf16[4,6144]{1,0:T(4,128)(2,1)S(1)}, bf16[4,6144]{1,0:T(4,128)(2,1)S(1)}, u32[]{:S(2)}, u32[]{:S(2)}) collective-permute-start(bf16[4,6144]{1,0:T(4,128)(2,1)S(1)} %collective-permute-done.1.refs_2_), channel_id=1, source_target_pairs={{0,4},{4,0},{8,12},{12,8},{16,20},{20,16},{24,28},{28,24},{1,5},{5... | collective-permute-start | bytes 147464 | tf_op jit(solution)/shard_map/ppermute | solution.py:24
  12.4 4.1 %collective-permute-start.6 = (bf16[4,6144]{1,0:T(4,128)(2,1)S(1)}, bf16[4,6144]{1,0:T(4,128)(2,1)S(1)}, u32[]{:S(2)}, u32[]{:S(2)}) collective-permute-start(bf16[4,6144]{1,0:T(4,128)(2,1)S(1)} %collective-permute-done.2.refs_3_), channel_id=1, source_target_pairs={{0,4},{4,0},{8,12},{12,8},{16,20},{20,16},{24,28},{28,24},{1,5},{5... | collective-permute-start | bytes 147464 | tf_op jit(solution)/shard_map/ppermute | solution.py:24
  16.8 6.8 %collective-permute-start.7 = (bf16[16,6144]{1,0:T(8,128)(2,1)S(1)}, bf16[16,6144]{1,0:T(8,128)(2,1)S(1)}, u32[]{:S(2)}, u32[]{:S(2)}) collective-permute-start(bf16[16,6144]{1,0:T(8,128)(2,1)S(1)} %get-tuple-element.63.refs_1_), channel_id=1, source_target_pairs={{0,2},{2,0},{1,3},{3,1},{4,6},{6,4},{5,7},{7,5},{8,10},{10,8},{9,1... | collective-permute-start | bytes 589832 | tf_op jit(solution)/shard_map/ppermute | solution.py:542
  18.3 5.5 %collective-permute-start.8 = (bf16[16,6144]{1,0:T(8,128)(2,1)S(1)}, bf16[16,6144]{1,0:T(8,128)(2,1)S(1)}, u32[]{:S(2)}, u32[]{:S(2)}) collective-permute-start(bf16[16,6144]{1,0:T(8,128)(2,1)S(1)} %get-tuple-element.62.refs_0_), channel_id=1, source_target_pairs={{0,1},{1,0},{2,3},{3,2},{4,5},{5,4},{6,7},{7,6},{8,9},{9,8},{10,11... | collective-permute-start | bytes 589832 | tf_op jit(solution)/shard_map/ppermute | solution.py:19
  19.8 11.1 %all-to-all-start = ((bf16[32,8,128]{2,1,0:T(8,128)(2,1)}), bf16[32,8,128]{2,1,0:T(8,128)(2,1)S(1)}, u32[]{:S(2)}, u32[]{:S(2)}) async-start(bf16[32,8,128]{2,1,0:T(8,128)(2,1)} %low_pieces.1), calls=%async_computation | async-start | bytes 131072 | tf_op jit(solution)/shard_map/all_to_all | solution.py:40
  37.3 5.7 %collective-permute-start.13 = (bf16[2,32,768]{2,1,0:T(8,128)(2,1)S(1)}, bf16[2,32,768]{2,1,0:T(8,128)(2,1)S(1)}, u32[]{:S(2)}, u32[]{:S(2)}) collective-permute-start(bf16[2,32,768]{2,1,0:T(8,128)(2,1)S(1)} %get-tuple-element.76), channel_id=1, source_target_pairs={{0,4},{4,0},{8,12},{12,8},{16,20},{20,16},{24,28},{28,24},{1,5},{5... | collective-permute-start | bytes 294920 | tf_op jit(solution)/shard_map/ppermute | solution.py:24
  38.6 8.1 %collective-permute-start.11 = (bf16[2,32,768]{2,1,0:T(8,128)(2,1)S(1)}, bf16[2,32,768]{2,1,0:T(8,128)(2,1)S(1)}, u32[]{:S(2)}, u32[]{:S(2)}) collective-permute-start(bf16[2,32,768]{2,1,0:T(8,128)(2,1)S(1)} %get-tuple-element.73), channel_id=1, source_target_pairs={{0,4},{4,0},{8,12},{12,8},{16,20},{20,16},{24,28},{28,24},{1,5},{5... | collective-permute-start | bytes 294920 | tf_op jit(solution)/shard_map/ppermute | solution.py:24
  39.4 7.5 %collective-permute-start.16 = (bf16[64,196]{1,0:T(8,128)(2,1)S(1)}, bf16[64,196]{1,0:T(8,128)(2,1)S(1)}, u32[]{:S(2)}, u32[]{:S(2)}) collective-permute-start(bf16[64,196]{1,0:T(8,128)(2,1)S(1)} %get-tuple-element.100), channel_id=1, source_target_pairs={{0,2},{2,0},{1,3},{3,1},{4,6},{6,4},{5,7},{7,5},{8,10},{10,8},{9,1... | collective-permute-start | bytes 75272 | tf_op jit(solution)/shard_map/ppermute | solution.py:561
  43.0 6.1 %collective-permute-start.14 = (bf16[32,768]{1,0:T(8,128)(2,1)S(1)}, bf16[32,768]{1,0:T(8,128)(2,1)S(1)}, u32[]{:S(2)}, u32[]{:S(2)}) collective-permute-start(bf16[32,768]{1,0:T(8,128)(2,1)S(1)} %get-tuple-element.77), channel_id=1, source_target_pairs={{0,16},{4,20},{8,24},{12,28},{16,0},{20,4},{24,8},{28,12},{1,17},{... | collective-permute-start | bytes 147464 | tf_op jit(solution)/shard_map/ppermute | solution.py:24
  45.3 6.0 %collective-permute-start.15 = (bf16[32,768]{1,0:T(8,128)(2,1)S(1)}, bf16[32,768]{1,0:T(8,128)(2,1)S(1)}, u32[]{:S(2)}, u32[]{:S(2)}) collective-permute-start(bf16[32,768]{1,0:T(8,128)(2,1)S(1)} %get-tuple-element.78), channel_id=1, source_target_pairs={{0,24},{4,28},{8,16},{12,20},{16,8},{20,12},{24,0},{28,4},{1,25},{... | collective-permute-start | bytes 147464 | tf_op jit(solution)/shard_map/ppermute | solution.py:24
  46.8 4.7 %collective-permute-start.12 = (bf16[32,768]{1,0:T(8,128)(2,1)S(1)}, bf16[32,768]{1,0:T(8,128)(2,1)S(1)}, u32[]{:S(2)}, u32[]{:S(2)}) collective-permute-start(bf16[32,768]{1,0:T(8,128)(2,1)S(1)} %get-tuple-element.75), channel_id=1, source_target_pairs={{0,8},{4,12},{8,0},{12,4},{16,24},{20,28},{24,16},{28,20},{1,9},{5... | collective-permute-start | bytes 147464 | tf_op jit(solution)/shard_map/ppermute | solution.py:24
  51.5 5.9 %collective-permute-start.17 = (bf16[32,768]{1,0:T(8,128)(2,1)S(1)}, bf16[32,768]{1,0:T(8,128)(2,1)S(1)}, u32[]{:S(2)}, u32[]{:S(2)}) collective-permute-start(bf16[32,768]{1,0:T(8,128)(2,1)S(1)} %mix.1.refs_4_.refs_0_), channel_id=1, source_target_pairs={{0,8},{4,12},{8,0},{12,4},{16,24},{20,28},{24,16},{28,20},{1,9},{5... | collective-permute-start | bytes 147464 | tf_op jit(solution)/shard_map/ppermute | solution.py:24
  51.6 6.1 %collective-permute-start.18 = (bf16[32,768]{1,0:T(8,128)(2,1)S(1)}, bf16[32,768]{1,0:T(8,128)(2,1)S(1)}, u32[]{:S(2)}, u32[]{:S(2)}) collective-permute-start(bf16[32,768]{1,0:T(8,128)(2,1)S(1)} %mix.1.refs_4_.refs_0_), channel_id=1, source_target_pairs={{0,16},{4,20},{8,24},{12,28},{16,0},{20,4},{24,8},{28,12},{1,17},{... | collective-permute-start | bytes 147464 | tf_op jit(solution)/shard_map/ppermute | solution.py:24
  54.2 5.9 %collective-permute-start.19 = (bf16[32,768]{1,0:T(8,128)(2,1)S(1)}, bf16[32,768]{1,0:T(8,128)(2,1)S(1)}, u32[]{:S(2)}, u32[]{:S(2)}) collective-permute-start(bf16[32,768]{1,0:T(8,128)(2,1)S(1)} %mix.1.refs_4_.refs_0_), channel_id=1, source_target_pairs={{0,24},{4,28},{8,16},{12,20},{16,8},{20,12},{24,0},{28,4},{1,25},{... | collective-permute-start | bytes 147464 | tf_op jit(solution)/shard_map/ppermute | solution.py:24
  56.0 5.6 %collective-permute-start.28 = (bf16[32,768]{1,0:T(8,128)(2,1)S(1)}, bf16[32,768]{1,0:T(8,128)(2,1)S(1)}, u32[]{:S(2)}, u32[]{:S(2)}) collective-permute-start(bf16[32,768]{1,0:T(8,128)(2,1)S(1)} %mix.1.refs_4_.refs_0_), channel_id=1, source_target_pairs={{0,1},{1,0},{2,3},{3,2},{4,5},{5,4},{6,7},{7,6},{8,9},{9,8},{10,11... | collective-permute-start | bytes 147464 | tf_op jit(solution)/shard_map/ppermute | solution.py:19
  56.0 6.2 %collective-permute-start.20 = (bf16[32,768]{1,0:T(8,128)(2,1)S(1)}, bf16[32,768]{1,0:T(8,128)(2,1)S(1)}, u32[]{:S(2)}, u32[]{:S(2)}) collective-permute-start(bf16[32,768]{1,0:T(8,128)(2,1)S(1)} %mix.1.refs_4_.refs_0_), channel_id=1, source_target_pairs={{0,4},{4,0},{8,12},{12,8},{16,20},{20,16},{24,28},{28,24},{1,5},{5... | collective-permute-start | bytes 147464 | tf_op jit(solution)/shard_map/ppermute | solution.py:24
  57.4 6.3 %collective-permute-start.29 = (bf16[32,768]{1,0:T(8,128)(2,1)S(1)}, bf16[32,768]{1,0:T(8,128)(2,1)S(1)}, u32[]{:S(2)}, u32[]{:S(2)}) collective-permute-start(bf16[32,768]{1,0:T(8,128)(2,1)S(1)} %collective-permute-done.17.refs_5_.refs_1_), channel_id=1, source_target_pairs={{0,1},{1,0},{2,3},{3,2},{4,5},{5,4},{6,7},{7,6},{8,9},{9,8},{10,11... | collective-permute-start | bytes 147464 | tf_op jit(solution)/shard_map/ppermute | solution.py:19
  57.6 6.1 %collective-permute-start.30 = (bf16[32,768]{1,0:T(8,128)(2,1)S(1)}, bf16[32,768]{1,0:T(8,128)(2,1)S(1)}, u32[]{:S(2)}, u32[]{:S(2)}) collective-permute-start(bf16[32,768]{1,0:T(8,128)(2,1)S(1)} %collective-permute-done.18.refs_6_.refs_2_), channel_id=1, source_target_pairs={{0,1},{1,0},{2,3},{3,2},{4,5},{5,4},{6,7},{7,6},{8,9},{9,8},{10,11... | collective-permute-start | bytes 147464 | tf_op jit(solution)/shard_map/ppermute | solution.py:19
  60.1 4.1 %collective-permute-start.21 = (bf16[32,768]{1,0:T(8,128)(2,1)S(1)}, bf16[32,768]{1,0:T(8,128)(2,1)S(1)}, u32[]{:S(2)}, u32[]{:S(2)}) collective-permute-start(bf16[32,768]{1,0:T(8,128)(2,1)S(1)} %collective-permute-done.17.refs_5_.refs_1_), channel_id=1, source_target_pairs={{0,4},{4,0},{8,12},{12,8},{16,20},{20,16},{24,28},{28,24},{1,5},{5... | collective-permute-start | bytes 147464 | tf_op jit(solution)/shard_map/ppermute | solution.py:24
  61.6 4.1 %collective-permute-start.22 = (bf16[32,768]{1,0:T(8,128)(2,1)S(1)}, bf16[32,768]{1,0:T(8,128)(2,1)S(1)}, u32[]{:S(2)}, u32[]{:S(2)}) collective-permute-start(bf16[32,768]{1,0:T(8,128)(2,1)S(1)} %collective-permute-done.18.refs_6_.refs_2_), channel_id=1, source_target_pairs={{0,4},{4,0},{8,12},{12,8},{16,20},{20,16},{24,28},{28,24},{1,5},{5... | collective-permute-start | bytes 147464 | tf_op jit(solution)/shard_map/ppermute | solution.py:24
  62.1 4.1 %collective-permute-start.23 = (bf16[32,768]{1,0:T(8,128)(2,1)S(1)}, bf16[32,768]{1,0:T(8,128)(2,1)S(1)}, u32[]{:S(2)}, u32[]{:S(2)}) collective-permute-start(bf16[32,768]{1,0:T(8,128)(2,1)S(1)} %collective-permute-done.19.refs_7_.refs_3_), channel_id=1, source_target_pairs={{0,4},{4,0},{8,12},{12,8},{16,20},{20,16},{24,28},{28,24},{1,5},{5... | collective-permute-start | bytes 147464 | tf_op jit(solution)/shard_map/ppermute | solution.py:24
  63.7 2.6 %collective-permute-start.31 = (bf16[32,768]{1,0:T(8,128)(2,1)S(1)}, bf16[32,768]{1,0:T(8,128)(2,1)S(1)}, u32[]{:S(2)}, u32[]{:S(2)}) collective-permute-start(bf16[32,768]{1,0:T(8,128)(2,1)S(1)} %collective-permute-done.19.refs_7_.refs_3_), channel_id=1, source_target_pairs={{0,1},{1,0},{2,3},{3,2},{4,5},{5,4},{6,7},{7,6},{8,9},{9,8},{10,11... | collective-permute-start | bytes 147464 | tf_op jit(solution)/shard_map/ppermute | solution.py:19
  63.7 4.2 %collective-permute-start.24 = (bf16[32,768]{1,0:T(8,128)(2,1)S(1)}, bf16[32,768]{1,0:T(8,128)(2,1)S(1)}, u32[]{:S(2)}, u32[]{:S(2)}) collective-permute-start(bf16[32,768]{1,0:T(8,128)(2,1)S(1)} %collective-permute-done.20.refs_4_), channel_id=1, source_target_pairs={{0,1},{1,0},{2,3},{3,2},{4,5},{5,4},{6,7},{7,6},{8,9},{9,8},{10,11... | collective-permute-start | bytes 147464 | tf_op jit(solution)/shard_map/ppermute | solution.py:19
  64.2 3.7 %collective-permute-start.25 = (bf16[32,768]{1,0:T(8,128)(2,1)S(1)}, bf16[32,768]{1,0:T(8,128)(2,1)S(1)}, u32[]{:S(2)}, u32[]{:S(2)}) collective-permute-start(bf16[32,768]{1,0:T(8,128)(2,1)S(1)} %collective-permute-done.21.refs_5_), channel_id=1, source_target_pairs={{0,1},{1,0},{2,3},{3,2},{4,5},{5,4},{6,7},{7,6},{8,9},{9,8},{10,11... | collective-permute-start | bytes 147464 | tf_op jit(solution)/shard_map/ppermute | solution.py:19
  65.7 2.2 %collective-permute-start.26 = (bf16[32,768]{1,0:T(8,128)(2,1)S(1)}, bf16[32,768]{1,0:T(8,128)(2,1)S(1)}, u32[]{:S(2)}, u32[]{:S(2)}) collective-permute-start(bf16[32,768]{1,0:T(8,128)(2,1)S(1)} %collective-permute-done.22.refs_6_), channel_id=1, source_target_pairs={{0,1},{1,0},{2,3},{3,2},{4,5},{5,4},{6,7},{7,6},{8,9},{9,8},{10,11... | collective-permute-start | bytes 147464 | tf_op jit(solution)/shard_map/ppermute | solution.py:19
  70.5 14.6 %all-to-all-start.1 = ((bf16[32,32,128]{2,1,0:T(8,128)(2,1)}), bf16[32,32,128]{2,1,0:T(8,128)(2,1)S(1)}, u32[]{:S(2)}, u32[]{:S(2)}) async-start(bf16[32,32,128]{2,1,0:T(8,128)(2,1)} %get-tuple-element.91), calls=%async_computation.1 | async-start | bytes 524288 | tf_op jit(solution)/shard_map/all_to_all | solution.py:40
  76.1 5.0 %collective-permute-start.32 = (bf16[4,6144]{1,0:T(4,128)(2,1)S(1)}, bf16[4,6144]{1,0:T(4,128)(2,1)S(1)}, u32[]{:S(2)}, u32[]{:S(2)}) collective-permute-start(bf16[4,6144]{1,0:T(4,128)(2,1)S(1)} %convolution_convert_fusion), channel_id=1, source_target_pairs={{0,2},{2,0},{1,3},{3,1},{4,6},{6,4},{5,7},{7,5},{8,10},{10,8},{9,1... | collective-permute-start | bytes 147464 | tf_op jit(solution)/shard_map/ppermute | solution.py:611
  (4 other events, 12.0 us)

commit v6 on v5

--- a/solution.py
+++ b/solution.py
@@ -62,6 +62,21 @@
 
 def vmem(count):
     return [pl.BlockSpec(memory_space=pltpu.VMEM)] * count
+
+
+class Here:
+    def __init__(self, refs):
+        self.refs = refs
+
+    def __getitem__(self, which):
+        return self.refs[which][0]
+
+
+def seated(kernel):
+    def run(place_ref, group_ref, core_ref, *refs):
+        kernel(Here((place_ref, group_ref, core_ref)), *refs)
+
+    return run
 
 
 def params():
@@ -95,8 +110,8 @@
 
 def brought_near(tokens, factor, router, here):
     return pl.pallas_call(
-        near_kernel,
-        in_specs=[pl.BlockSpec(memory_space=pltpu.SMEM)] + [pl.BlockSpec(memory_space=pl.ANY)] * 3,
+        seated(near_kernel),
+        in_specs=[pl.BlockSpec(memory_space=pltpu.SMEM)] * 3 + [pl.BlockSpec(memory_space=pl.ANY)] * 3,
         out_specs=vmem(3),
         out_shape=[
             struct(tokens.shape, bf16),
@@ -106,7 +121,7 @@
         scratch_shapes=[pltpu.VMEM(router.shape, bf16), pltpu.SemaphoreType.DMA((3,))],
         compiler_params=params(),
         name="near",
-    )(here, *[pltpu.with_memory_space_constraint(array, pltpu.HBM) for array in (tokens, factor, router)])
+    )(*here, *[pltpu.with_memory_space_constraint(array, pltpu.HBM) for array in (tokens, factor, router)])
 
 
 def pack_kernel(n_blocks, placer_ref, *refs):
@@ -158,13 +173,13 @@
     if depth % 128:
         parts = [lax.dynamic_slice_in_dim(part, place * depth, depth, 1) for part in parts]
     return pl.pallas_call(
-        functools.partial(low_kernel, len(parts)),
-        in_specs=[pl.BlockSpec(memory_space=pltpu.SMEM)] + vmem(len(parts) + 1),
+        seated(functools.partial(low_kernel, len(parts))),
+        in_specs=[pl.BlockSpec(memory_space=pltpu.SMEM)] * 3 + vmem(len(parts) + 1),
         out_specs=vmem(1)[0],
         out_shape=struct((n_dp * len(parts) * 2, capacity // 2, 2 * rank), bf16),
         compiler_params=params(),
         name="low_pieces",
-    )(here, *parts, factor)
+    )(*here, *parts, factor)
 
 
 def lift_kernel(n_parts, *refs):
@@ -275,8 +290,8 @@
     half, width = count // 2, down_weight.shape[1]
     shape = struct((blocks, half, width // blocks), bf16)
     *outs, kept = pl.pallas_call(
-        down_kernel,
-        in_specs=[pl.BlockSpec(memory_space=pltpu.SMEM)] + vmem(4) + [pl.BlockSpec(memory_space=pl.ANY)],
+        seated(down_kernel),
+        in_specs=[pl.BlockSpec(memory_space=pltpu.SMEM)] * 3 + vmem(4) + [pl.BlockSpec(memory_space=pl.ANY)],
         out_specs=vmem(5),
         scratch_shapes=[pltpu.SemaphoreType.DMA((blocks,))],
         out_shape=(
@@ -290,7 +305,7 @@
         compiler_params=params(),
         name="down",
     )(
-        here,
+        *here,
         base,
         lifted,
         low_parts,
@@ -316,13 +331,13 @@
 def fold_core(own, got, here):
     shapes = [struct((count, *own.shape[1:]), bf16) for count in (4, 2, 2)]
     return pl.pallas_call(
-        fold_core_kernel,
-        in_specs=[pl.BlockSpec(memory_space=pltpu.SMEM)] + vmem(2),
+        seated(fold_core_kernel),
+        in_specs=[pl.BlockSpec(memory_space=pltpu.SMEM)] * 3 + vmem(2),
         out_specs=vmem(3),
         out_shape=shapes,
         compiler_params=params(),
         name="fold_core",
-    )(here, own, got)
+    )(*here, own, got)
 
 
 def fold_near_kernel(first, keep_ref, got_ref, *out_refs):
@@ -413,8 +428,8 @@
     half, wide = owns[0].shape
     homes = half // capacity
     return pl.pallas_call(
-        functools.partial(rest_kernel, len(owns), eight),
-        in_specs=[pl.BlockSpec(memory_space=pltpu.SMEM)] + vmem(len(owns) + 2),
+        seated(functools.partial(rest_kernel, len(owns), eight)),
+        in_specs=[pl.BlockSpec(memory_space=pltpu.SMEM)] * 3 + vmem(len(owns) + 2),
         out_specs=vmem(1 + homes),
         out_shape=(
             struct((low.shape[1], back_pre.shape[0]), f32),
@@ -422,21 +437,21 @@
         ),
         compiler_params=params(),
         name="rest",
-    )(here, *owns, back_pre, low)
+    )(*here, *owns, back_pre, low)
 
 
 def back_first(parts, owns, others, here, eight, gate, kept, loss_factor):
     units = kept.shape[1]
     count, blocks, wide = gate.shape[0], len(owns), owns[0].shape[1]
     return pl.pallas_call(
-        functools.partial(back_first_kernel, len(parts), blocks, eight, loss_factor),
-        in_specs=[pl.BlockSpec(memory_space=pltpu.SMEM)] + vmem(len(parts) + 2 * blocks + 2),
+        seated(functools.partial(back_first_kernel, len(parts), blocks, eight, loss_factor)),
+        in_specs=[pl.BlockSpec(memory_space=pltpu.SMEM)] * 3 + vmem(len(parts) + 2 * blocks + 2),
         out_specs=vmem(1)[0],
         out_shape=struct((units, count), f32),
         cost_estimate=cost(2 * count * blocks * wide * units, 2 * blocks * wide * units),
         compiler_params=params(),
         name="back_first",
-    )(here, *parts, *owns, *others, gate, kept)
+    )(*here, *parts, *owns, *others, gate, kept)
 
 
 def back_last(parts, owns, others, here, eight, gate, kept, first, slope, factor, loss_factor, copies):
@@ -444,14 +459,14 @@
     units, count = slope.shape
     rank, blocks = factor.shape[0], len(others)
     return pl.pallas_call(
-        functools.partial(back_last_kernel, len(parts), blocks, eight, loss_factor),
-        in_specs=[pl.BlockSpec(memory_space=pltpu.SMEM)] + vmem(len(parts) + 2 * blocks + 5),
+        seated(functools.partial(back_last_kernel, len(parts), blocks, eight, loss_factor)),
+        in_specs=[pl.BlockSpec(memory_space=pltpu.SMEM)] * 3 + vmem(len(parts) + 2 * blocks + 5),
         out_specs=vmem(2),
         out_shape=(struct((copies, rank // 2, 2 * count), bf16), struct((units, count), bf16)),
         cost_estimate=cost(2 * count * blocks * wide * units, 2 * blocks * wide * units),
         compiler_params=params(),
         name="back_last",
-    )(here, *parts, *owns, *others, gate, kept, first, slope, factor)
+    )(*here, *parts, *owns, *others, gate, kept, first, slope, factor)
 
 
 def factor_kernel(place_ref, low_ref, piece_ref, out_ref):
@@ -475,13 +490,13 @@
 def factor_gradient(lows, pieces, share, here):
     rank = 2 * lows.shape[3]
     return pl.pallas_call(
-        factor_kernel,
-        in_specs=[pl.BlockSpec(memory_space=pltpu.SMEM)] + vmem(2),
+        seated(factor_kernel),
+        in_specs=[pl.BlockSpec(memory_space=pltpu.SMEM)] * 3 + vmem(2),
         out_specs=vmem(1)[0],
         out_shape=struct((rank, share), f32),
         compiler_params=params(),
         name="factor_gradient",
-    )(here, lows, pieces)
+    )(*here, lows, pieces)
 
 
 def shards(
@@ -511,7 +526,7 @@
     blocks = 8
     eight = n_dp == blocks
 
-    here = jnp.stack([place, group, core])
+    here = (place.reshape(1), group.reshape(1), core.reshape(1))
 
     labels = expert_choice_table[0]
     index = jnp.arange(col_rows, dtype=jnp.int32)

time: 86.9 us -> 83.7 us (0.963)
  Pallas kernels: 20.3 us -> 16 us
  waiting for transfers between devices: 21.5 us -> 22.7 us
    pallas_call x8, Pallas kernels: 14.5 us -> 10.2 us  [the longest x1 3.35 us: down(): pl.pallas_call(seated(down_kernel), in_specs=[pl.BlockSpec(memory_space=p...]
  transfers between devices with their start and end apart: 35 -> 35, of which waited for: 14 -> 15; matrix products, arithmetic and copies ran while one was open for 4% -> 4% of each run, Pallas kernels for 13% -> 11%
where the time goes in v6:
time: 83.7 us; the launch traced here: 83.3 us
  starting transfers between devices  40.4 us (48%)
  waiting for transfers between devices  22.7 us (27%)
  Pallas kernels  16 us (19%)
  other arithmetic  1.88 us (2%)
  matrix products  1.06 us (1%)
  between operations  0.89 us (1%)
    ppermute x19, starting transfers between devices, across(): return lax.ppermute(block, axis, [(i, i ^ apart_by) for i in range(count)])  26.4 us
    ppermute x19, waiting for transfers between devices, across(): return lax.ppermute(block, axis, [(i, i ^ apart_by) for i in range(count)])  12.7 us
    all_to_all x2, starting transfers between devices, exchange(): return lax.all_to_all(blocks, axis, 0, 0, tiled=True)  7.62 us
    pallas_call x1, Pallas kernels, lift(): pl.pallas_call(functools.partial(lift_kernel, len(parts)), in_specs=vmem(...  5.41 us
    all_to_all x2, waiting for transfers between devices, exchange(): return lax.all_to_all(blocks, axis, 0, 0, tiled=True)  4.15 us
    pallas_call x1, Pallas kernels, down(): pl.pallas_call(seated(down_kernel), in_specs=[pl.BlockSpec(memory_space=p...  3.35 us
    ppermute x1, waiting for transfers between devices, shards(): chosen = lax.ppermute(chosen.astype(bf16), 'x', route).astype(f32)  3.17 us
    ppermute x11, waiting for transfers between devices, swap(): return lax.ppermute(block, axis, [(0, 1), (1, 0)])  2.72 us
  transfers between devices with their start and end apart: 35, of which 15 were waited for; matrix products, arithmetic and copies ran while one was open for 4% of the time, Pallas kernels for 11%

profile of v6, /device:TPU:0, one launch (start us, length us, event | category | flops | bytes accessed | tf_op | source)
XLA Modules:
  0.0 83.3 jit_solution(17778558247110765710)
XLA Ops:
  0.6 3.1 %collective-permute-start = (bf16[4,6144]{1,0:T(4,128)(2,1)}, bf16[4,6144]{1,0:T(4,128)(2,1)S(1)}, u32[]{:S(2)}, u32[]{:S(2)}) collective-permute-start(bf16[4,6144]{1,0:T(4,128)(2,1)} %refs_0_.1), channel_id=1, source_target_pairs={{0,8},{4,12},{8,0},{12,4},{16,24},{20,28},{24,16},{28,20},{1,9},{5... | collective-permute-start | bytes 147464 | tf_op jit(solution)/shard_map/ppermute | solution.py:24
  3.7 2.6 %collective-permute-start.1 = (bf16[4,6144]{1,0:T(4,128)(2,1)}, bf16[4,6144]{1,0:T(4,128)(2,1)S(1)}, u32[]{:S(2)}, u32[]{:S(2)}) collective-permute-start(bf16[4,6144]{1,0:T(4,128)(2,1)} %refs_0_.1), channel_id=1, source_target_pairs={{0,16},{4,20},{8,24},{12,28},{16,0},{20,4},{24,8},{28,12},{1,17},{... | collective-permute-start | bytes 147464 | tf_op jit(solution)/shard_map/ppermute | solution.py:24
  6.3 1.7 %collective-permute-start.3 = (bf16[4,6144]{1,0:T(4,128)(2,1)}, bf16[4,6144]{1,0:T(4,128)(2,1)S(1)}, u32[]{:S(2)}, u32[]{:S(2)}) collective-permute-start(bf16[4,6144]{1,0:T(4,128)(2,1)} %refs_0_.1), channel_id=1, source_target_pairs={{0,4},{4,0},{8,12},{12,8},{16,20},{20,16},{24,28},{28,24},{1,5},{5... | collective-permute-start | bytes 147464 | tf_op jit(solution)/shard_map/ppermute | solution.py:24
  10.3 1.7 %collective-permute-start.5 = (bf16[4,6144]{1,0:T(4,128)(2,1)S(1)}, bf16[4,6144]{1,0:T(4,128)(2,1)S(1)}, u32[]{:S(2)}, u32[]{:S(2)}) collective-permute-start(bf16[4,6144]{1,0:T(4,128)(2,1)S(1)} %collective-permute-done.1.refs_2_), channel_id=1, source_target_pairs={{0,4},{4,0},{8,12},{12,8},{16,20},{20,16},{24,28},{28,24},{1,5},{5... | collective-permute-start | bytes 147464 | tf_op jit(solution)/shard_map/ppermute | solution.py:24
  12.4 1.5 %collective-permute-start.6 = (bf16[4,6144]{1,0:T(4,128)(2,1)S(1)}, bf16[4,6144]{1,0:T(4,128)(2,1)S(1)}, u32[]{:S(2)}, u32[]{:S(2)}) collective-permute-start(bf16[4,6144]{1,0:T(4,128)(2,1)S(1)} %collective-permute-done.2.refs_3_), channel_id=1, source_target_pairs={{0,4},{4,0},{8,12},{12,8},{16,20},{20,16},{24,28},{28,24},{1,5},{5... | collective-permute-start | bytes 147464 | tf_op jit(solution)/shard_map/ppermute | solution.py:24
  15.1 1.4 %collective-permute-done.6.refs_7_ = bf16[4,6144]{1,0:T(4,128)(2,1)S(1)} collective-permute-done((bf16[4,6144]{1,0:T(4,128)(2,1)S(1)}, bf16[4,6144]{1,0:T(4,128)(2,1)S(1)}, u32[]{:S(2)}, u32[]{:S(2)}) %collective-permute-start.6) | collective-permute-done | bytes 49184 | tf_op jit(solution)/shard_map/ppermute | solution.py:24
  16.8 1.6 %collective-permute-start.7 = (bf16[16,6144]{1,0:T(8,128)(2,1)S(1)}, bf16[16,6144]{1,0:T(8,128)(2,1)S(1)}, u32[]{:S(2)}, u32[]{:S(2)}) collective-permute-start(bf16[16,6144]{1,0:T(8,128)(2,1)S(1)} %get-tuple-element.63.refs_1_), channel_id=1, source_target_pairs={{0,2},{2,0},{1,3},{3,1},{4,6},{6,4},{5,7},{7,5},{8,10},{10,8},{9,1... | collective-permute-start | bytes 589832 | tf_op jit(solution)/shard_map/ppermute | solution.py:557
  19.3 3.7 %all-to-all-start = ((bf16[32,8,128]{2,1,0:T(8,128)(2,1)}), bf16[32,8,128]{2,1,0:T(8,128)(2,1)S(1)}, u32[]{:S(2)}, u32[]{:S(2)}) async-start(bf16[32,8,128]{2,1,0:T(8,128)(2,1)} %low_pieces.1), calls=%async_computation | async-start | bytes 131072 | tf_op jit(solution)/shard_map/all_to_all | solution.py:40
  23.4 1.1 %collective-permute-done.9.refs_3_ = bf16[16,6144]{1,0:T(8,128)(2,1)S(1)} collective-permute-done((bf16[16,6144]{1,0:T(8,128)(2,1)S(1)}, bf16[16,6144]{1,0:T(8,128)(2,1)S(1)}, u32[]{:S(2)}, u32[]{:S(2)}) %collective-permute-start.9) | collective-permute-done | bytes 196640 | tf_op jit(solution)/shard_map/ppermute | solution.py:19
  24.5 5.4 %lift.1 = (f32[64,512]{1,0:T(8,128)S(1)}, f32[64,512]{1,0:T(8,128)S(1)}, f32[64,1]{1,0:T(8,128)S(1)}) custom-call(bf16[16,6144]{1,0:T(8,128)(2,1)S(1)} %get-tuple-element.62.refs_0_, bf16[16,6144]{1,0:T(8,128)(2,1)S(1)} %collective-permute-done.7.refs_1_, bf16[16,6144]{1,0:T(8,128)(2,1)S(1)} %collective-permute-done.8.refs_2_, ...), custom_call_target="tpu_custom_call" | custom-call | flops 805306368 | bytes 12582912 | tf_op jit(solution)/shard_map/lift/pallas_call | solution.py:224
  30.4 3.4 %down.1 = (bf16[8,32,768]{2,1,0:T(8,128)(2,1)S(1)}, bf16[8,32,768]{2,1,0:T(8,128)(2,1)S(1)}, f32[512,64]{1,0:T(8,128)S(1)}, bf16[64,64]{1,0:T(8,128)(2,1)S(1)}, bf16[8,512,768]{2,1,0:T(8,128)(2,1)S(1)}) custom-call(s32[1]{0:T(128)} %bitcast.place_ref, s32[1]{0:T(128)} %bitcast.1.group_ref, s32[1]{0:T(128)} %bitcast.2.core_ref, ...), custom_call_target="tpu_custom_call" | custom-call | flops 402653184 | bytes 6291456 | tf_op jit(solution)/shard_map/down/pallas_call | solution.py:292
  34.0 1.5 %collective-permute-done.10.refs_1_ = bf16[8,32,768]{2,1,0:T(8,128)(2,1)S(1)} collective-permute-done((bf16[8,32,768]{2,1,0:T(8,128)(2,1)S(1)}, bf16[8,32,768]{2,1,0:T(8,128)(2,1)S(1)}, u32[]{:S(2)}, u32[]{:S(2)}) %collective-permute-start.10) | collective-permute-done | bytes 393248 | tf_op jit(solution)/shard_map/ppermute | solution.py:19
  35.6 1.4 %collective-permute-start.13 = (bf16[2,32,768]{2,1,0:T(8,128)(2,1)S(1)}, bf16[2,32,768]{2,1,0:T(8,128)(2,1)S(1)}, u32[]{:S(2)}, u32[]{:S(2)}) collective-permute-start(bf16[2,32,768]{2,1,0:T(8,128)(2,1)S(1)} %get-tuple-element.76), channel_id=1, source_target_pairs={{0,4},{4,0},{8,12},{12,8},{16,20},{20,16},{24,28},{28,24},{1,5},{5... | collective-permute-start | bytes 294920 | tf_op jit(solution)/shard_map/ppermute | solution.py:24
  37.7 1.4 %collective-permute-start.16 = (bf16[64,196]{1,0:T(8,128)(2,1)S(1)}, bf16[64,196]{1,0:T(8,128)(2,1)S(1)}, u32[]{:S(2)}, u32[]{:S(2)}) collective-permute-start(bf16[64,196]{1,0:T(8,128)(2,1)S(1)} %get-tuple-element.100), channel_id=1, source_target_pairs={{0,2},{2,0},{1,3},{3,1},{4,6},{6,4},{5,7},{7,5},{8,10},{10,8},{9,1... | collective-permute-start | bytes 75272 | tf_op jit(solution)/shard_map/ppermute | solution.py:576
  39.1 2.2 %collective-permute-done.13.got_ref = bf16[2,32,768]{2,1,0:T(8,128)(2,1)S(1)} collective-permute-done((bf16[2,32,768]{2,1,0:T(8,128)(2,1)S(1)}, bf16[2,32,768]{2,1,0:T(8,128)(2,1)S(1)}, u32[]{:S(2)}, u32[]{:S(2)}) %collective-permute-start.13) | collective-permute-done | bytes 98336 | tf_op jit(solution)/shard_map/ppermute | solution.py:24
  41.4 2.3 %collective-permute-start.14 = (bf16[32,768]{1,0:T(8,128)(2,1)S(1)}, bf16[32,768]{1,0:T(8,128)(2,1)S(1)}, u32[]{:S(2)}, u32[]{:S(2)}) collective-permute-start(bf16[32,768]{1,0:T(8,128)(2,1)S(1)} %get-tuple-element.77), channel_id=1, source_target_pairs={{0,16},{4,20},{8,24},{12,28},{16,0},{20,4},{24,8},{28,12},{1,17},{... | collective-permute-start | bytes 147464 | tf_op jit(solution)/shard_map/ppermute | solution.py:24
  43.6 1.5 %collective-permute-start.15 = (bf16[32,768]{1,0:T(8,128)(2,1)S(1)}, bf16[32,768]{1,0:T(8,128)(2,1)S(1)}, u32[]{:S(2)}, u32[]{:S(2)}) collective-permute-start(bf16[32,768]{1,0:T(8,128)(2,1)S(1)} %get-tuple-element.78), channel_id=1, source_target_pairs={{0,24},{4,28},{8,16},{12,20},{16,8},{20,12},{24,0},{28,4},{1,25},{... | collective-permute-start | bytes 147464 | tf_op jit(solution)/shard_map/ppermute | solution.py:24
  45.3 2.2 %collective-permute-done.14.refs_2_ = bf16[32,768]{1,0:T(8,128)(2,1)S(1)} collective-permute-done((bf16[32,768]{1,0:T(8,128)(2,1)S(1)}, bf16[32,768]{1,0:T(8,128)(2,1)S(1)}, u32[]{:S(2)}, u32[]{:S(2)}) %collective-permute-start.14) | collective-permute-done | bytes 49184 | tf_op jit(solution)/shard_map/ppermute | solution.py:24
  47.5 2.2 %collective-permute-done.15.refs_3_ = bf16[32,768]{1,0:T(8,128)(2,1)S(1)} collective-permute-done((bf16[32,768]{1,0:T(8,128)(2,1)S(1)}, bf16[32,768]{1,0:T(8,128)(2,1)S(1)}, u32[]{:S(2)}, u32[]{:S(2)}) %collective-permute-start.15) | collective-permute-done | bytes 49184 | tf_op jit(solution)/shard_map/ppermute | solution.py:24
  49.9 2.6 %collective-permute-start.18 = (bf16[32,768]{1,0:T(8,128)(2,1)S(1)}, bf16[32,768]{1,0:T(8,128)(2,1)S(1)}, u32[]{:S(2)}, u32[]{:S(2)}) collective-permute-start(bf16[32,768]{1,0:T(8,128)(2,1)S(1)} %mix.1.refs_4_.refs_0_), channel_id=1, source_target_pairs={{0,16},{4,20},{8,24},{12,28},{16,0},{20,4},{24,8},{28,12},{1,17},{... | collective-permute-start | bytes 147464 | tf_op jit(solution)/shard_map/ppermute | solution.py:24
  52.6 1.7 %collective-permute-start.19 = (bf16[32,768]{1,0:T(8,128)(2,1)S(1)}, bf16[32,768]{1,0:T(8,128)(2,1)S(1)}, u32[]{:S(2)}, u32[]{:S(2)}) collective-permute-start(bf16[32,768]{1,0:T(8,128)(2,1)S(1)} %mix.1.refs_4_.refs_0_), channel_id=1, source_target_pairs={{0,24},{4,28},{8,16},{12,20},{16,8},{20,12},{24,0},{28,4},{1,25},{... | collective-permute-start | bytes 147464 | tf_op jit(solution)/shard_map/ppermute | solution.py:24
  54.3 1.5 %collective-permute-start.20 = (bf16[32,768]{1,0:T(8,128)(2,1)S(1)}, bf16[32,768]{1,0:T(8,128)(2,1)S(1)}, u32[]{:S(2)}, u32[]{:S(2)}) collective-permute-start(bf16[32,768]{1,0:T(8,128)(2,1)S(1)} %mix.1.refs_4_.refs_0_), channel_id=1, source_target_pairs={{0,4},{4,0},{8,12},{12,8},{16,20},{20,16},{24,28},{28,24},{1,5},{5... | collective-permute-start | bytes 147464 | tf_op jit(solution)/shard_map/ppermute | solution.py:24
  56.3 2.2 %collective-permute-done.19.refs_7_.refs_3_ = bf16[32,768]{1,0:T(8,128)(2,1)S(1)} collective-permute-done((bf16[32,768]{1,0:T(8,128)(2,1)S(1)}, bf16[32,768]{1,0:T(8,128)(2,1)S(1)}, u32[]{:S(2)}, u32[]{:S(2)}) %collective-permute-start.19) | collective-permute-done | bytes 49184 | tf_op jit(solution)/shard_map/ppermute | solution.py:24
  58.5 1.5 %collective-permute-start.21 = (bf16[32,768]{1,0:T(8,128)(2,1)S(1)}, bf16[32,768]{1,0:T(8,128)(2,1)S(1)}, u32[]{:S(2)}, u32[]{:S(2)}) collective-permute-start(bf16[32,768]{1,0:T(8,128)(2,1)S(1)} %collective-permute-done.17.refs_5_.refs_1_), channel_id=1, source_target_pairs={{0,4},{4,0},{8,12},{12,8},{16,20},{20,16},{24,28},{28,24},{1,5},{5... | collective-permute-start | bytes 147464 | tf_op jit(solution)/shard_map/ppermute | solution.py:24
  60.5 1.5 %collective-permute-start.23 = (bf16[32,768]{1,0:T(8,128)(2,1)S(1)}, bf16[32,768]{1,0:T(8,128)(2,1)S(1)}, u32[]{:S(2)}, u32[]{:S(2)}) collective-permute-start(bf16[32,768]{1,0:T(8,128)(2,1)S(1)} %collective-permute-done.19.refs_7_.refs_3_), channel_id=1, source_target_pairs={{0,4},{4,0},{8,12},{12,8},{16,20},{20,16},{24,28},{28,24},{1,5},{5... | collective-permute-start | bytes 147464 | tf_op jit(solution)/shard_map/ppermute | solution.py:24
  62.7 1.4 %collective-permute-done.22.refs_6_ = bf16[32,768]{1,0:T(8,128)(2,1)S(1)} collective-permute-done((bf16[32,768]{1,0:T(8,128)(2,1)S(1)}, bf16[32,768]{1,0:T(8,128)(2,1)S(1)}, u32[]{:S(2)}, u32[]{:S(2)}) %collective-permute-start.22) | collective-permute-done | bytes 49184 | tf_op jit(solution)/shard_map/ppermute | solution.py:24
  64.7 1.0 %back_first.1.refs_14_ = f32[512,64]{1,0:T(8,128)S(1)} custom-call(s32[1]{0:T(128)} %bitcast.place_ref, s32[1]{0:T(128)} %bitcast.1.group_ref, s32[1]{0:T(128)} %bitcast.2.core_ref, bf16[16,6144]{1,0:T(8,128)(2,1)S(1)} %get-tuple-element.62.refs_0_, bf16[16,6144]{1,0:T(8,128)(2,1)S(1)} %collective-permute-done.7.refs_1_, ...), custom_call_target="tpu_custom_call" | custom-call | flops 201326592 | bytes 3145728 | tf_op jit(solution)/shard_map/back_first/pallas_call | solution.py:446
  65.8 2.0 %back_last.1 = (bf16[32,32,128]{2,1,0:T(8,128)(2,1)}, bf16[512,64]{1,0:T(8,128)(2,1)S(1)}) custom-call(s32[1]{0:T(128)} %bitcast.place_ref, s32[1]{0:T(128)} %bitcast.1.group_ref, s32[1]{0:T(128)} %bitcast.2.core_ref, bf16[16,6144]{1,0:T(8,128)(2,1)S(1)} %get-tuple-element.62.refs_0_, bf16[16,6144]{1,0:T(8,128)(2,1)S(1)} %collective-permute-done.7.refs_1_, ...), custom_call_target="tpu_custom_call" | custom-call | flops 201326592 | bytes 3145728 | tf_op jit(solution)/shard_map/back_last/pallas_call | solution.py:461
  67.8 3.9 %all-to-all-start.1 = ((bf16[32,32,128]{2,1,0:T(8,128)(2,1)}), bf16[32,32,128]{2,1,0:T(8,128)(2,1)S(1)}, u32[]{:S(2)}, u32[]{:S(2)}) async-start(bf16[32,32,128]{2,1,0:T(8,128)(2,1)} %get-tuple-element.91), calls=%async_computation.1 | async-start | bytes 524288 | tf_op jit(solution)/shard_map/all_to_all | solution.py:40
  72.8 1.8 %collective-permute-start.32 = (bf16[4,6144]{1,0:T(4,128)(2,1)S(1)}, bf16[4,6144]{1,0:T(4,128)(2,1)S(1)}, u32[]{:S(2)}, u32[]{:S(2)}) collective-permute-start(bf16[4,6144]{1,0:T(4,128)(2,1)S(1)} %convolution_convert_fusion), channel_id=1, source_target_pairs={{0,2},{2,0},{1,3},{3,1},{4,6},{6,4},{5,7},{7,5},{8,10},{10,8},{9,1... | collective-permute-start | bytes 147464 | tf_op jit(solution)/shard_map/ppermute | solution.py:626
  74.7 3.2 %collective-permute-done.32 = bf16[4,6144]{1,0:T(4,128)(2,1)S(1)} collective-permute-done((bf16[4,6144]{1,0:T(4,128)(2,1)S(1)}, bf16[4,6144]{1,0:T(4,128)(2,1)S(1)}, u32[]{:S(2)}, u32[]{:S(2)}) %collective-permute-start.32) | collective-permute-done | bytes 49184 | tf_op jit(solution)/shard_map/ppermute | solution.py:626
  78.7 3.7 %all-to-all-done.1 = bf16[32,32,128]{2,1,0:T(8,128)(2,1)S(1)} async-done(((bf16[32,32,128]{2,1,0:T(8,128)(2,1)}), bf16[32,32,128]{2,1,0:T(8,128)(2,1)S(1)}, u32[]{:S(2)}, u32[]{:S(2)}) %all-to-all-start.1) | async-done | bytes 262176 | tf_op jit(solution)/shard_map/all_to_all | solution.py:40
  (74 shorter events, 12.7 us)
Async XLA Ops:
  0.6 9.3 %collective-permute-start = (bf16[4,6144]{1,0:T(4,128)(2,1)}, bf16[4,6144]{1,0:T(4,128)(2,1)S(1)}, u32[]{:S(2)}, u32[]{:S(2)}) collective-permute-start(bf16[4,6144]{1,0:T(4,128)(2,1)} %refs_0_.1), channel_id=1, source_target_pairs={{0,8},{4,12},{8,0},{12,4},{16,24},{20,28},{24,16},{28,20},{1,9},{5... | collective-permute-start | bytes 147464 | tf_op jit(solution)/shard_map/ppermute | solution.py:24
  3.7 6.6 %collective-permute-start.1 = (bf16[4,6144]{1,0:T(4,128)(2,1)}, bf16[4,6144]{1,0:T(4,128)(2,1)S(1)}, u32[]{:S(2)}, u32[]{:S(2)}) collective-permute-start(bf16[4,6144]{1,0:T(4,128)(2,1)} %refs_0_.1), channel_id=1, source_target_pairs={{0,16},{4,20},{8,24},{12,28},{16,0},{20,4},{24,8},{28,12},{1,17},{... | collective-permute-start | bytes 147464 | tf_op jit(solution)/shard_map/ppermute | solution.py:24
  6.3 6.1 %collective-permute-start.2 = (bf16[4,6144]{1,0:T(4,128)(2,1)}, bf16[4,6144]{1,0:T(4,128)(2,1)S(1)}, u32[]{:S(2)}, u32[]{:S(2)}) collective-permute-start(bf16[4,6144]{1,0:T(4,128)(2,1)} %refs_0_.1), channel_id=1, source_target_pairs={{0,24},{4,28},{8,16},{12,20},{16,8},{20,12},{24,0},{28,4},{1,25},{... | collective-permute-start | bytes 147464 | tf_op jit(solution)/shard_map/ppermute | solution.py:24
  6.3 8.7 %collective-permute-start.3 = (bf16[4,6144]{1,0:T(4,128)(2,1)}, bf16[4,6144]{1,0:T(4,128)(2,1)S(1)}, u32[]{:S(2)}, u32[]{:S(2)}) collective-permute-start(bf16[4,6144]{1,0:T(4,128)(2,1)} %refs_0_.1), channel_id=1, source_target_pairs={{0,4},{4,0},{8,12},{12,8},{16,20},{20,16},{24,28},{28,24},{1,5},{5... | collective-permute-start | bytes 147464 | tf_op jit(solution)/shard_map/ppermute | solution.py:24
  9.9 5.1 %collective-permute-start.4 = (bf16[4,6144]{1,0:T(4,128)(2,1)S(1)}, bf16[4,6144]{1,0:T(4,128)(2,1)S(1)}, u32[]{:S(2)}, u32[]{:S(2)}) collective-permute-start(bf16[4,6144]{1,0:T(4,128)(2,1)S(1)} %collective-permute-done.refs_1_), channel_id=1, source_target_pairs={{0,4},{4,0},{8,12},{12,8},{16,20},{20,16},{24,28},{28,24},{1,5},{5... | collective-permute-start | bytes 147464 | tf_op jit(solution)/shard_map/ppermute | solution.py:24
  10.3 4.8 %collective-permute-start.5 = (bf16[4,6144]{1,0:T(4,128)(2,1)S(1)}, bf16[4,6144]{1,0:T(4,128)(2,1)S(1)}, u32[]{:S(2)}, u32[]{:S(2)}) collective-permute-start(bf16[4,6144]{1,0:T(4,128)(2,1)S(1)} %collective-permute-done.1.refs_2_), channel_id=1, source_target_pairs={{0,4},{4,0},{8,12},{12,8},{16,20},{20,16},{24,28},{28,24},{1,5},{5... | collective-permute-start | bytes 147464 | tf_op jit(solution)/shard_map/ppermute | solution.py:24
  12.4 4.1 %collective-permute-start.6 = (bf16[4,6144]{1,0:T(4,128)(2,1)S(1)}, bf16[4,6144]{1,0:T(4,128)(2,1)S(1)}, u32[]{:S(2)}, u32[]{:S(2)}) collective-permute-start(bf16[4,6144]{1,0:T(4,128)(2,1)S(1)} %collective-permute-done.2.refs_3_), channel_id=1, source_target_pairs={{0,4},{4,0},{8,12},{12,8},{16,20},{20,16},{24,28},{28,24},{1,5},{5... | collective-permute-start | bytes 147464 | tf_op jit(solution)/shard_map/ppermute | solution.py:24
  16.8 6.2 %collective-permute-start.7 = (bf16[16,6144]{1,0:T(8,128)(2,1)S(1)}, bf16[16,6144]{1,0:T(8,128)(2,1)S(1)}, u32[]{:S(2)}, u32[]{:S(2)}) collective-permute-start(bf16[16,6144]{1,0:T(8,128)(2,1)S(1)} %get-tuple-element.63.refs_1_), channel_id=1, source_target_pairs={{0,2},{2,0},{1,3},{3,1},{4,6},{6,4},{5,7},{7,5},{8,10},{10,8},{9,1... | collective-permute-start | bytes 589832 | tf_op jit(solution)/shard_map/ppermute | solution.py:557
  18.3 5.0 %collective-permute-start.8 = (bf16[16,6144]{1,0:T(8,128)(2,1)S(1)}, bf16[16,6144]{1,0:T(8,128)(2,1)S(1)}, u32[]{:S(2)}, u32[]{:S(2)}) collective-permute-start(bf16[16,6144]{1,0:T(8,128)(2,1)S(1)} %get-tuple-element.62.refs_0_), channel_id=1, source_target_pairs={{0,1},{1,0},{2,3},{3,2},{4,5},{5,4},{6,7},{7,6},{8,9},{9,8},{10,11... | collective-permute-start | bytes 589832 | tf_op jit(solution)/shard_map/ppermute | solution.py:19
  19.3 11.1 %all-to-all-start = ((bf16[32,8,128]{2,1,0:T(8,128)(2,1)}), bf16[32,8,128]{2,1,0:T(8,128)(2,1)S(1)}, u32[]{:S(2)}, u32[]{:S(2)}) async-start(bf16[32,8,128]{2,1,0:T(8,128)(2,1)} %low_pieces.1), calls=%async_computation | async-start | bytes 131072 | tf_op jit(solution)/shard_map/all_to_all | solution.py:40
  33.7 1.8 %collective-permute-start.10 = (bf16[8,32,768]{2,1,0:T(8,128)(2,1)S(1)}, bf16[8,32,768]{2,1,0:T(8,128)(2,1)S(1)}, u32[]{:S(2)}, u32[]{:S(2)}) collective-permute-start(bf16[8,32,768]{2,1,0:T(8,128)(2,1)S(1)} %get-tuple-element.71), channel_id=1, source_target_pairs={{0,1},{1,0},{2,3},{3,2},{4,5},{5,4},{6,7},{7,6},{8,9},{9,8},{10,11... | collective-permute-start | bytes 1179656 | tf_op jit(solution)/shard_map/ppermute | solution.py:19
  35.6 5.7 %collective-permute-start.13 = (bf16[2,32,768]{2,1,0:T(8,128)(2,1)S(1)}, bf16[2,32,768]{2,1,0:T(8,128)(2,1)S(1)}, u32[]{:S(2)}, u32[]{:S(2)}) collective-permute-start(bf16[2,32,768]{2,1,0:T(8,128)(2,1)S(1)} %get-tuple-element.76), channel_id=1, source_target_pairs={{0,4},{4,0},{8,12},{12,8},{16,20},{20,16},{24,28},{28,24},{1,5},{5... | collective-permute-start | bytes 294920 | tf_op jit(solution)/shard_map/ppermute | solution.py:24
  37.0 8.1 %collective-permute-start.11 = (bf16[2,32,768]{2,1,0:T(8,128)(2,1)S(1)}, bf16[2,32,768]{2,1,0:T(8,128)(2,1)S(1)}, u32[]{:S(2)}, u32[]{:S(2)}) collective-permute-start(bf16[2,32,768]{2,1,0:T(8,128)(2,1)S(1)} %get-tuple-element.73), channel_id=1, source_target_pairs={{0,4},{4,0},{8,12},{12,8},{16,20},{20,16},{24,28},{28,24},{1,5},{5... | collective-permute-start | bytes 294920 | tf_op jit(solution)/shard_map/ppermute | solution.py:24
  37.7 7.5 %collective-permute-start.16 = (bf16[64,196]{1,0:T(8,128)(2,1)S(1)}, bf16[64,196]{1,0:T(8,128)(2,1)S(1)}, u32[]{:S(2)}, u32[]{:S(2)}) collective-permute-start(bf16[64,196]{1,0:T(8,128)(2,1)S(1)} %get-tuple-element.100), channel_id=1, source_target_pairs={{0,2},{2,0},{1,3},{3,1},{4,6},{6,4},{5,7},{7,5},{8,10},{10,8},{9,1... | collective-permute-start | bytes 75272 | tf_op jit(solution)/shard_map/ppermute | solution.py:576
  41.4 6.1 %collective-permute-start.14 = (bf16[32,768]{1,0:T(8,128)(2,1)S(1)}, bf16[32,768]{1,0:T(8,128)(2,1)S(1)}, u32[]{:S(2)}, u32[]{:S(2)}) collective-permute-start(bf16[32,768]{1,0:T(8,128)(2,1)S(1)} %get-tuple-element.77), channel_id=1, source_target_pairs={{0,16},{4,20},{8,24},{12,28},{16,0},{20,4},{24,8},{28,12},{1,17},{... | collective-permute-start | bytes 147464 | tf_op jit(solution)/shard_map/ppermute | solution.py:24
  43.6 6.0 %collective-permute-start.15 = (bf16[32,768]{1,0:T(8,128)(2,1)S(1)}, bf16[32,768]{1,0:T(8,128)(2,1)S(1)}, u32[]{:S(2)}, u32[]{:S(2)}) collective-permute-start(bf16[32,768]{1,0:T(8,128)(2,1)S(1)} %get-tuple-element.78), channel_id=1, source_target_pairs={{0,24},{4,28},{8,16},{12,20},{16,8},{20,12},{24,0},{28,4},{1,25},{... | collective-permute-start | bytes 147464 | tf_op jit(solution)/shard_map/ppermute | solution.py:24
  45.1 4.7 %collective-permute-start.12 = (bf16[32,768]{1,0:T(8,128)(2,1)S(1)}, bf16[32,768]{1,0:T(8,128)(2,1)S(1)}, u32[]{:S(2)}, u32[]{:S(2)}) collective-permute-start(bf16[32,768]{1,0:T(8,128)(2,1)S(1)} %get-tuple-element.75), channel_id=1, source_target_pairs={{0,8},{4,12},{8,0},{12,4},{16,24},{20,28},{24,16},{28,20},{1,9},{5... | collective-permute-start | bytes 147464 | tf_op jit(solution)/shard_map/ppermute | solution.py:24
  49.9 5.9 %collective-permute-start.17 = (bf16[32,768]{1,0:T(8,128)(2,1)S(1)}, bf16[32,768]{1,0:T(8,128)(2,1)S(1)}, u32[]{:S(2)}, u32[]{:S(2)}) collective-permute-start(bf16[32,768]{1,0:T(8,128)(2,1)S(1)} %mix.1.refs_4_.refs_0_), channel_id=1, source_target_pairs={{0,8},{4,12},{8,0},{12,4},{16,24},{20,28},{24,16},{28,20},{1,9},{5... | collective-permute-start | bytes 147464 | tf_op jit(solution)/shard_map/ppermute | solution.py:24
  49.9 6.1 %collective-permute-start.18 = (bf16[32,768]{1,0:T(8,128)(2,1)S(1)}, bf16[32,768]{1,0:T(8,128)(2,1)S(1)}, u32[]{:S(2)}, u32[]{:S(2)}) collective-permute-start(bf16[32,768]{1,0:T(8,128)(2,1)S(1)} %mix.1.refs_4_.refs_0_), channel_id=1, source_target_pairs={{0,16},{4,20},{8,24},{12,28},{16,0},{20,4},{24,8},{28,12},{1,17},{... | collective-permute-start | bytes 147464 | tf_op jit(solution)/shard_map/ppermute | solution.py:24
  52.6 5.9 %collective-permute-start.19 = (bf16[32,768]{1,0:T(8,128)(2,1)S(1)}, bf16[32,768]{1,0:T(8,128)(2,1)S(1)}, u32[]{:S(2)}, u32[]{:S(2)}) collective-permute-start(bf16[32,768]{1,0:T(8,128)(2,1)S(1)} %mix.1.refs_4_.refs_0_), channel_id=1, source_target_pairs={{0,24},{4,28},{8,16},{12,20},{16,8},{20,12},{24,0},{28,4},{1,25},{... | collective-permute-start | bytes 147464 | tf_op jit(solution)/shard_map/ppermute | solution.py:24
  54.3 5.6 %collective-permute-start.28 = (bf16[32,768]{1,0:T(8,128)(2,1)S(1)}, bf16[32,768]{1,0:T(8,128)(2,1)S(1)}, u32[]{:S(2)}, u32[]{:S(2)}) collective-permute-start(bf16[32,768]{1,0:T(8,128)(2,1)S(1)} %mix.1.refs_4_.refs_0_), channel_id=1, source_target_pairs={{0,1},{1,0},{2,3},{3,2},{4,5},{5,4},{6,7},{7,6},{8,9},{9,8},{10,11... | collective-permute-start | bytes 147464 | tf_op jit(solution)/shard_map/ppermute | solution.py:19
  54.3 6.2 %collective-permute-start.20 = (bf16[32,768]{1,0:T(8,128)(2,1)S(1)}, bf16[32,768]{1,0:T(8,128)(2,1)S(1)}, u32[]{:S(2)}, u32[]{:S(2)}) collective-permute-start(bf16[32,768]{1,0:T(8,128)(2,1)S(1)} %mix.1.refs_4_.refs_0_), channel_id=1, source_target_pairs={{0,4},{4,0},{8,12},{12,8},{16,20},{20,16},{24,28},{28,24},{1,5},{5... | collective-permute-start | bytes 147464 | tf_op jit(solution)/shard_map/ppermute | solution.py:24
  55.8 6.3 %collective-permute-start.29 = (bf16[32,768]{1,0:T(8,128)(2,1)S(1)}, bf16[32,768]{1,0:T(8,128)(2,1)S(1)}, u32[]{:S(2)}, u32[]{:S(2)}) collective-permute-start(bf16[32,768]{1,0:T(8,128)(2,1)S(1)} %collective-permute-done.17.refs_5_.refs_1_), channel_id=1, source_target_pairs={{0,1},{1,0},{2,3},{3,2},{4,5},{5,4},{6,7},{7,6},{8,9},{9,8},{10,11... | collective-permute-start | bytes 147464 | tf_op jit(solution)/shard_map/ppermute | solution.py:19
  56.0 6.1 %collective-permute-start.30 = (bf16[32,768]{1,0:T(8,128)(2,1)S(1)}, bf16[32,768]{1,0:T(8,128)(2,1)S(1)}, u32[]{:S(2)}, u32[]{:S(2)}) collective-permute-start(bf16[32,768]{1,0:T(8,128)(2,1)S(1)} %collective-permute-done.18.refs_6_.refs_2_), channel_id=1, source_target_pairs={{0,1},{1,0},{2,3},{3,2},{4,5},{5,4},{6,7},{7,6},{8,9},{9,8},{10,11... | collective-permute-start | bytes 147464 | tf_op jit(solution)/shard_map/ppermute | solution.py:19
  58.5 4.1 %collective-permute-start.21 = (bf16[32,768]{1,0:T(8,128)(2,1)S(1)}, bf16[32,768]{1,0:T(8,128)(2,1)S(1)}, u32[]{:S(2)}, u32[]{:S(2)}) collective-permute-start(bf16[32,768]{1,0:T(8,128)(2,1)S(1)} %collective-permute-done.17.refs_5_.refs_1_), channel_id=1, source_target_pairs={{0,4},{4,0},{8,12},{12,8},{16,20},{20,16},{24,28},{28,24},{1,5},{5... | collective-permute-start | bytes 147464 | tf_op jit(solution)/shard_map/ppermute | solution.py:24
  59.9 4.1 %collective-permute-start.22 = (bf16[32,768]{1,0:T(8,128)(2,1)S(1)}, bf16[32,768]{1,0:T(8,128)(2,1)S(1)}, u32[]{:S(2)}, u32[]{:S(2)}) collective-permute-start(bf16[32,768]{1,0:T(8,128)(2,1)S(1)} %collective-permute-done.18.refs_6_.refs_2_), channel_id=1, source_target_pairs={{0,4},{4,0},{8,12},{12,8},{16,20},{20,16},{24,28},{28,24},{1,5},{5... | collective-permute-start | bytes 147464 | tf_op jit(solution)/shard_map/ppermute | solution.py:24
  60.5 4.1 %collective-permute-start.23 = (bf16[32,768]{1,0:T(8,128)(2,1)S(1)}, bf16[32,768]{1,0:T(8,128)(2,1)S(1)}, u32[]{:S(2)}, u32[]{:S(2)}) collective-permute-start(bf16[32,768]{1,0:T(8,128)(2,1)S(1)} %collective-permute-done.19.refs_7_.refs_3_), channel_id=1, source_target_pairs={{0,4},{4,0},{8,12},{12,8},{16,20},{20,16},{24,28},{28,24},{1,5},{5... | collective-permute-start | bytes 147464 | tf_op jit(solution)/shard_map/ppermute | solution.py:24
  62.1 2.6 %collective-permute-start.31 = (bf16[32,768]{1,0:T(8,128)(2,1)S(1)}, bf16[32,768]{1,0:T(8,128)(2,1)S(1)}, u32[]{:S(2)}, u32[]{:S(2)}) collective-permute-start(bf16[32,768]{1,0:T(8,128)(2,1)S(1)} %collective-permute-done.19.refs_7_.refs_3_), channel_id=1, source_target_pairs={{0,1},{1,0},{2,3},{3,2},{4,5},{5,4},{6,7},{7,6},{8,9},{9,8},{10,11... | collective-permute-start | bytes 147464 | tf_op jit(solution)/shard_map/ppermute | solution.py:19
  62.1 3.6 %collective-permute-start.24 = (bf16[32,768]{1,0:T(8,128)(2,1)S(1)}, bf16[32,768]{1,0:T(8,128)(2,1)S(1)}, u32[]{:S(2)}, u32[]{:S(2)}) collective-permute-start(bf16[32,768]{1,0:T(8,128)(2,1)S(1)} %collective-permute-done.20.refs_4_), channel_id=1, source_target_pairs={{0,1},{1,0},{2,3},{3,2},{4,5},{5,4},{6,7},{7,6},{8,9},{9,8},{10,11... | collective-permute-start | bytes 147464 | tf_op jit(solution)/shard_map/ppermute | solution.py:19
  62.6 3.1 %collective-permute-start.25 = (bf16[32,768]{1,0:T(8,128)(2,1)S(1)}, bf16[32,768]{1,0:T(8,128)(2,1)S(1)}, u32[]{:S(2)}, u32[]{:S(2)}) collective-permute-start(bf16[32,768]{1,0:T(8,128)(2,1)S(1)} %collective-permute-done.21.refs_5_), channel_id=1, source_target_pairs={{0,1},{1,0},{2,3},{3,2},{4,5},{5,4},{6,7},{7,6},{8,9},{9,8},{10,11... | collective-permute-start | bytes 147464 | tf_op jit(solution)/shard_map/ppermute | solution.py:19
  67.8 14.5 %all-to-all-start.1 = ((bf16[32,32,128]{2,1,0:T(8,128)(2,1)}), bf16[32,32,128]{2,1,0:T(8,128)(2,1)S(1)}, u32[]{:S(2)}, u32[]{:S(2)}) async-start(bf16[32,32,128]{2,1,0:T(8,128)(2,1)} %get-tuple-element.91), calls=%async_computation.1 | async-start | bytes 524288 | tf_op jit(solution)/shard_map/all_to_all | solution.py:40
  72.8 5.0 %collective-permute-start.32 = (bf16[4,6144]{1,0:T(4,128)(2,1)S(1)}, bf16[4,6144]{1,0:T(4,128)(2,1)S(1)}, u32[]{:S(2)}, u32[]{:S(2)}) collective-permute-start(bf16[4,6144]{1,0:T(4,128)(2,1)S(1)} %convolution_convert_fusion), channel_id=1, source_target_pairs={{0,2},{2,0},{1,3},{3,1},{4,6},{6,4},{5,7},{7,5},{8,10},{10,8},{9,1... | collective-permute-start | bytes 147464 | tf_op jit(solution)/shard_map/ppermute | solution.py:626
  (4 other events, 11.5 us)

commit v7 on v6

--- a/solution.py
+++ b/solution.py
@@ -26,7 +26,7 @@
 
 def gather_eight(block, *meanwhile):
     near = across(block, "dp", 1)
-    far = [across(block, "dp", bits) for bits in NEAR[1:4]]
+    far = [across(block, "dp", bits) for bits in NEAR[3:0:-1]][::-1]
     if meanwhile:
         far[0], meanwhile = lax.optimization_barrier((far[0], meanwhile))
     return [block, *far, near, *[across(other, "dp", 1) for other in far]], *meanwhile
@@ -197,17 +197,14 @@
                 pltpu.make_async_copy(up_ref.at[at], up.at[at], sems.at[1, k]),
             )
         )
-    ahead = 4
-    for pair in copies[:ahead]:
+    for pair in copies:
         pair[0].start()
         pair[1].start()
     pre = lifted = logit = 0.0
     for k in range(steps):
         at = slice(k * chunk, (k + 1) * chunk)
-        for i in (0, 1):
-            copies[k][i].wait()
-            if k + ahead < steps:
-                copies[k + ahead][i].start()
+        copies[k][0].wait()
+        copies[k][1].wait()
         rows = jnp.concatenate([r[:, at] for r in parts], axis=0)
         pre = pre + dot(rows, weight[at])
         lifted = lifted + dot(rows, up[at])
@@ -551,13 +548,14 @@
         column = [column.reshape(col_rows, width)]
         own_target = lax.dynamic_slice_in_dim(target, place * tok_rows, tok_rows, 0)
     packed = pack(placer, column, capacity)
+    low_parts = low_pieces(packed, factor, here, place, n_dp)
+    packed, low_parts = lax.optimization_barrier((packed, low_parts))
     parts = [packed[0]]
     for step in range(1, groups):
         route = [(i, (i + step) % groups) for i in range(groups)]
         parts.append(lax.ppermute(packed[step], "x", route))
     parts = parts + [swap(part, "core") for part in parts]
 
-    low_parts = low_pieces(packed, factor, here, place, n_dp)
     low_parts = exchange(low_parts, every).reshape(n_dp, groups, 2, capacity // 2, 2 * rank)
     base, lifted, gate = lift(parts, gate_weight, up_weight, own_route)
     low_parts, gate = lax.optimization_barrier((low_parts, gate))
@@ -579,11 +577,11 @@
     got = swap(other, "core")
     if eight:
         keep, far, near = fold_core(own, got, here)
-        far, near = across(far, "dp", 1), across(near, "dp", 1)
+        far, near, pieces = lax.optimization_barrier((across(far, "dp", 1), near, pieces))
+        near = across(near, "dp", 1)
         two, three = fold_near(keep, far, 2)
         mine, one = fold_near(keep, near, 0)
         terms = [mine, across(one, "dp", 2), across(two, "dp", 4), across(three, "dp", 6)]
-        terms, pieces = lax.optimization_barrier((terms, pieces))
         (owns,) = gather_eight(mix(terms, gate))
     else:
         summed = (own.astype(f32) + got.astype(f32)).astype(bf16)

time: 83.7 us -> 83.2 us (level)
  starting transfers between devices: 40.4 us -> 39.4 us
  waiting for transfers between devices: 22.7 us -> 23.6 us
    ppermute x1, waiting for transfers between devices: 0.01 us -> 1.17 us  [shards(): pieces.append(lax.ppermute(piece, 'x', route) if step else piece)]
    ppermute x11, waiting for transfers between devices: 2.72 us -> 1.82 us  [swap(): return lax.ppermute(block, axis, [(0, 1), (1, 0)])]
  transfers between devices with their start and end apart: 35 -> 35, of which waited for: 15 -> 17; matrix products, arithmetic and copies ran while one was open for 4% -> 4% of each run, Pallas kernels for 11% -> 10%
where the time goes in v7:
time: 83.2 us; the launch traced here: 82.9 us
  starting transfers between devices  39.4 us (47%)
  waiting for transfers between devices  23.6 us (28%)
  Pallas kernels  15.6 us (19%)
  other arithmetic  1.88 us (2%)
  matrix products  1.06 us (1%)
  between operations  0.88 us (1%)
    ppermute x19, starting transfers between devices, across(): return lax.ppermute(block, axis, [(i, i ^ apart_by) for i in range(count)])  26.7 us
    ppermute x19, waiting for transfers between devices, across(): return lax.ppermute(block, axis, [(i, i ^ apart_by) for i in range(count)])  12.9 us
    all_to_all x2, starting transfers between devices, exchange(): return lax.all_to_all(blocks, axis, 0, 0, tiled=True)  6.96 us
    pallas_call x1, Pallas kernels, lift(): pl.pallas_call(functools.partial(lift_kernel, len(parts)), in_specs=vmem(...  5.07 us
    all_to_all x2, waiting for transfers between devices, exchange(): return lax.all_to_all(blocks, axis, 0, 0, tiled=True)  4.17 us
    pallas_call x1, Pallas kernels, down(): pl.pallas_call(seated(down_kernel), in_specs=[pl.BlockSpec(memory_space=p...  3.35 us
    ppermute x1, waiting for transfers between devices, shards(): chosen = lax.ppermute(chosen.astype(bf16), 'x', route).astype(f32)  3.17 us
    pallas_call x1, Pallas kernels, back_last(): pl.pallas_call(seated(functools.partial(back_last_kernel, len(parts), blo...  1.99 us
  transfers between devices with their start and end apart: 35, of which 17 were waited for; matrix products, arithmetic and copies ran while one was open for 4% of the time, Pallas kernels for 10%

profile of v7, /device:TPU:0, one launch (start us, length us, event | category | flops | bytes accessed | tf_op | source)
XLA Modules:
  0.0 82.9 jit_solution(15254077613019298010)
XLA Ops:
  0.6 3.1 %collective-permute-start = (bf16[4,6144]{1,0:T(4,128)(2,1)}, bf16[4,6144]{1,0:T(4,128)(2,1)S(1)}, u32[]{:S(2)}, u32[]{:S(2)}) collective-permute-start(bf16[4,6144]{1,0:T(4,128)(2,1)} %refs_0_.1), channel_id=1, source_target_pairs={{0,8},{4,12},{8,0},{12,4},{16,24},{20,28},{24,16},{28,20},{1,9},{5... | collective-permute-start | bytes 147464 | tf_op jit(solution)/shard_map/ppermute | solution.py:24
  3.7 2.6 %collective-permute-start.1 = (bf16[4,6144]{1,0:T(4,128)(2,1)}, bf16[4,6144]{1,0:T(4,128)(2,1)S(1)}, u32[]{:S(2)}, u32[]{:S(2)}) collective-permute-start(bf16[4,6144]{1,0:T(4,128)(2,1)} %refs_0_.1), channel_id=1, source_target_pairs={{0,16},{4,20},{8,24},{12,28},{16,0},{20,4},{24,8},{28,12},{1,17},{... | collective-permute-start | bytes 147464 | tf_op jit(solution)/shard_map/ppermute | solution.py:24
  6.3 1.7 %collective-permute-start.3 = (bf16[4,6144]{1,0:T(4,128)(2,1)}, bf16[4,6144]{1,0:T(4,128)(2,1)S(1)}, u32[]{:S(2)}, u32[]{:S(2)}) collective-permute-start(bf16[4,6144]{1,0:T(4,128)(2,1)} %refs_0_.1), channel_id=1, source_target_pairs={{0,4},{4,0},{8,12},{12,8},{16,20},{20,16},{24,28},{28,24},{1,5},{5... | collective-permute-start | bytes 147464 | tf_op jit(solution)/shard_map/ppermute | solution.py:24
  10.3 1.7 %collective-permute-start.5 = (bf16[4,6144]{1,0:T(4,128)(2,1)S(1)}, bf16[4,6144]{1,0:T(4,128)(2,1)S(1)}, u32[]{:S(2)}, u32[]{:S(2)}) collective-permute-start(bf16[4,6144]{1,0:T(4,128)(2,1)S(1)} %collective-permute-done.1.refs_2_), channel_id=1, source_target_pairs={{0,4},{4,0},{8,12},{12,8},{16,20},{20,16},{24,28},{28,24},{1,5},{5... | collective-permute-start | bytes 147464 | tf_op jit(solution)/shard_map/ppermute | solution.py:24
  12.4 1.5 %collective-permute-start.6 = (bf16[4,6144]{1,0:T(4,128)(2,1)S(1)}, bf16[4,6144]{1,0:T(4,128)(2,1)S(1)}, u32[]{:S(2)}, u32[]{:S(2)}) collective-permute-start(bf16[4,6144]{1,0:T(4,128)(2,1)S(1)} %collective-permute-done.2.refs_3_), channel_id=1, source_target_pairs={{0,4},{4,0},{8,12},{12,8},{16,20},{20,16},{24,28},{28,24},{1,5},{5... | collective-permute-start | bytes 147464 | tf_op jit(solution)/shard_map/ppermute | solution.py:24
  15.1 1.4 %collective-permute-done.6.refs_7_ = bf16[4,6144]{1,0:T(4,128)(2,1)S(1)} collective-permute-done((bf16[4,6144]{1,0:T(4,128)(2,1)S(1)}, bf16[4,6144]{1,0:T(4,128)(2,1)S(1)}, u32[]{:S(2)}, u32[]{:S(2)}) %collective-permute-start.6) | collective-permute-done | bytes 49184 | tf_op jit(solution)/shard_map/ppermute | solution.py:24
  17.6 1.5 %collective-permute-start.7 = (bf16[16,6144]{1,0:T(8,128)(2,1)S(1)}, bf16[16,6144]{1,0:T(8,128)(2,1)S(1)}, u32[]{:S(2)}, u32[]{:S(2)}) collective-permute-start(bf16[16,6144]{1,0:T(8,128)(2,1)S(1)} %get-tuple-element.67.refs_1_), channel_id=1, source_target_pairs={{0,2},{2,0},{1,3},{3,1},{4,6},{6,4},{5,7},{7,5},{8,10},{10,8},{9,1... | collective-permute-start | bytes 589832 | tf_op jit(solution)/shard_map/ppermute | solution.py:556
  19.2 3.7 %all-to-all-start = ((bf16[32,8,128]{2,1,0:T(8,128)(2,1)}), bf16[32,8,128]{2,1,0:T(8,128)(2,1)S(1)}, u32[]{:S(2)}, u32[]{:S(2)}) async-start(bf16[32,8,128]{2,1,0:T(8,128)(2,1)} %low_pieces.1), calls=%async_computation | async-start | bytes 131072 | tf_op jit(solution)/shard_map/all_to_all | solution.py:40
  23.4 1.4 %collective-permute-done.9.refs_3_ = bf16[16,6144]{1,0:T(8,128)(2,1)S(1)} collective-permute-done((bf16[16,6144]{1,0:T(8,128)(2,1)S(1)}, bf16[16,6144]{1,0:T(8,128)(2,1)S(1)}, u32[]{:S(2)}, u32[]{:S(2)}) %collective-permute-start.9) | collective-permute-done | bytes 196640 | tf_op jit(solution)/shard_map/ppermute | solution.py:19
  24.7 5.1 %lift.1 = (f32[64,512]{1,0:T(8,128)S(1)}, f32[64,512]{1,0:T(8,128)S(1)}, f32[64,1]{1,0:T(8,128)S(1)}) custom-call(bf16[16,6144]{1,0:T(8,128)(2,1)S(1)} %get-tuple-element.66.refs_0_, bf16[16,6144]{1,0:T(8,128)(2,1)S(1)} %collective-permute-done.7.refs_1_, bf16[16,6144]{1,0:T(8,128)(2,1)S(1)} %collective-permute-done.8.refs_2_, ...), custom_call_target="tpu_custom_call" | custom-call | flops 805306368 | bytes 12582912 | tf_op jit(solution)/shard_map/lift/pallas_call | solution.py:221
  30.3 3.4 %down.1 = (bf16[8,32,768]{2,1,0:T(8,128)(2,1)S(1)}, bf16[8,32,768]{2,1,0:T(8,128)(2,1)S(1)}, f32[512,64]{1,0:T(8,128)S(1)}, bf16[64,64]{1,0:T(8,128)(2,1)S(1)}, bf16[8,512,768]{2,1,0:T(8,128)(2,1)S(1)}) custom-call(s32[1]{0:T(128)} %bitcast.place_ref, s32[1]{0:T(128)} %bitcast.1.group_ref, s32[1]{0:T(128)} %bitcast.2.core_ref, ...), custom_call_target="tpu_custom_call" | custom-call | flops 402653184 | bytes 6291456 | tf_op jit(solution)/shard_map/down/pallas_call | solution.py:289
  34.0 1.1 %collective-permute-start.12 = (bf16[64,196]{1,0:T(8,128)(2,1)S(1)}, bf16[64,196]{1,0:T(8,128)(2,1)S(1)}, u32[]{:S(2)}, u32[]{:S(2)}) collective-permute-start(bf16[64,196]{1,0:T(8,128)(2,1)S(1)} %get-tuple-element.102), channel_id=1, source_target_pairs={{0,2},{2,0},{1,3},{3,1},{4,6},{6,4},{5,7},{7,5},{8,10},{10,8},{9,1... | collective-permute-start | bytes 75272 | tf_op jit(solution)/shard_map/ppermute | solution.py:574
  35.6 1.2 %collective-permute-start.11 = (bf16[2,32,768]{2,1,0:T(8,128)(2,1)S(1)}, bf16[2,32,768]{2,1,0:T(8,128)(2,1)S(1)}, u32[]{:S(2)}, u32[]{:S(2)}) collective-permute-start(bf16[2,32,768]{2,1,0:T(8,128)(2,1)S(1)} %get-tuple-element.76), channel_id=1, source_target_pairs={{0,4},{4,0},{8,12},{12,8},{16,20},{20,16},{24,28},{28,24},{1,5},{5... | collective-permute-start | bytes 294920 | tf_op jit(solution)/shard_map/ppermute | solution.py:24
  36.8 1.2 %collective-permute-done.12 = bf16[64,196]{1,0:T(8,128)(2,1)S(1)} collective-permute-done((bf16[64,196]{1,0:T(8,128)(2,1)S(1)}, bf16[64,196]{1,0:T(8,128)(2,1)S(1)}, u32[]{:S(2)}, u32[]{:S(2)}) %collective-permute-start.12) | collective-permute-done | bytes 25120 | tf_op jit(solution)/shard_map/ppermute | solution.py:574
  38.0 2.5 %collective-permute-done.11.got_ref = bf16[2,32,768]{2,1,0:T(8,128)(2,1)S(1)} collective-permute-done((bf16[2,32,768]{2,1,0:T(8,128)(2,1)S(1)}, bf16[2,32,768]{2,1,0:T(8,128)(2,1)S(1)}, u32[]{:S(2)}, u32[]{:S(2)}) %collective-permute-start.11) | collective-permute-done | bytes 98336 | tf_op jit(solution)/shard_map/ppermute | solution.py:24
  40.5 1.1 %collective-permute-start.13 = (bf16[2,32,768]{2,1,0:T(8,128)(2,1)S(1)}, bf16[2,32,768]{2,1,0:T(8,128)(2,1)S(1)}, u32[]{:S(2)}, u32[]{:S(2)}) collective-permute-start(bf16[2,32,768]{2,1,0:T(8,128)(2,1)S(1)} %get-tuple-element.80), channel_id=1, source_target_pairs={{0,4},{4,0},{8,12},{12,8},{16,20},{20,16},{24,28},{28,24},{1,5},{5... | collective-permute-start | bytes 294920 | tf_op jit(solution)/shard_map/ppermute | solution.py:24
  41.6 2.4 %collective-permute-start.15 = (bf16[32,768]{1,0:T(8,128)(2,1)S(1)}, bf16[32,768]{1,0:T(8,128)(2,1)S(1)}, u32[]{:S(2)}, u32[]{:S(2)}) collective-permute-start(bf16[32,768]{1,0:T(8,128)(2,1)S(1)} %get-tuple-element.84), channel_id=1, source_target_pairs={{0,16},{4,20},{8,24},{12,28},{16,0},{20,4},{24,8},{28,12},{1,17},{... | collective-permute-start | bytes 147464 | tf_op jit(solution)/shard_map/ppermute | solution.py:24
  44.0 1.4 %collective-permute-start.16 = (bf16[32,768]{1,0:T(8,128)(2,1)S(1)}, bf16[32,768]{1,0:T(8,128)(2,1)S(1)}, u32[]{:S(2)}, u32[]{:S(2)}) collective-permute-start(bf16[32,768]{1,0:T(8,128)(2,1)S(1)} %get-tuple-element.85), channel_id=1, source_target_pairs={{0,24},{4,28},{8,16},{12,20},{16,8},{20,12},{24,0},{28,4},{1,25},{... | collective-permute-start | bytes 147464 | tf_op jit(solution)/shard_map/ppermute | solution.py:24
  46.2 2.0 %collective-permute-done.15.refs_2_ = bf16[32,768]{1,0:T(8,128)(2,1)S(1)} collective-permute-done((bf16[32,768]{1,0:T(8,128)(2,1)S(1)}, bf16[32,768]{1,0:T(8,128)(2,1)S(1)}, u32[]{:S(2)}, u32[]{:S(2)}) %collective-permute-start.15) | collective-permute-done | bytes 49184 | tf_op jit(solution)/shard_map/ppermute | solution.py:24
  48.2 1.8 %collective-permute-done.16.refs_3_ = bf16[32,768]{1,0:T(8,128)(2,1)S(1)} collective-permute-done((bf16[32,768]{1,0:T(8,128)(2,1)S(1)}, bf16[32,768]{1,0:T(8,128)(2,1)S(1)}, u32[]{:S(2)}, u32[]{:S(2)}) %collective-permute-start.16) | collective-permute-done | bytes 49184 | tf_op jit(solution)/shard_map/ppermute | solution.py:24
  50.4 2.4 %collective-permute-start.18 = (bf16[32,768]{1,0:T(8,128)(2,1)S(1)}, bf16[32,768]{1,0:T(8,128)(2,1)S(1)}, u32[]{:S(2)}, u32[]{:S(2)}) collective-permute-start(bf16[32,768]{1,0:T(8,128)(2,1)S(1)} %mix.1.refs_4_.refs_0_), channel_id=1, source_target_pairs={{0,16},{4,20},{8,24},{12,28},{16,0},{20,4},{24,8},{28,12},{1,17},{... | collective-permute-start | bytes 147464 | tf_op jit(solution)/shard_map/ppermute | solution.py:24
  52.8 1.8 %collective-permute-start.19 = (bf16[32,768]{1,0:T(8,128)(2,1)S(1)}, bf16[32,768]{1,0:T(8,128)(2,1)S(1)}, u32[]{:S(2)}, u32[]{:S(2)}) collective-permute-start(bf16[32,768]{1,0:T(8,128)(2,1)S(1)} %mix.1.refs_4_.refs_0_), channel_id=1, source_target_pairs={{0,24},{4,28},{8,16},{12,20},{16,8},{20,12},{24,0},{28,4},{1,25},{... | collective-permute-start | bytes 147464 | tf_op jit(solution)/shard_map/ppermute | solution.py:24
  55.9 2.8 %collective-permute-done.19.refs_7_.refs_3_ = bf16[32,768]{1,0:T(8,128)(2,1)S(1)} collective-permute-done((bf16[32,768]{1,0:T(8,128)(2,1)S(1)}, bf16[32,768]{1,0:T(8,128)(2,1)S(1)}, u32[]{:S(2)}, u32[]{:S(2)}) %collective-permute-start.19) | collective-permute-done | bytes 49184 | tf_op jit(solution)/shard_map/ppermute | solution.py:24
  58.7 1.5 %collective-permute-start.21 = (bf16[32,768]{1,0:T(8,128)(2,1)S(1)}, bf16[32,768]{1,0:T(8,128)(2,1)S(1)}, u32[]{:S(2)}, u32[]{:S(2)}) collective-permute-start(bf16[32,768]{1,0:T(8,128)(2,1)S(1)} %collective-permute-done.17.refs_5_.refs_1_), channel_id=1, source_target_pairs={{0,4},{4,0},{8,12},{12,8},{16,20},{20,16},{24,28},{28,24},{1,5},{5... | collective-permute-start | bytes 147464 | tf_op jit(solution)/shard_map/ppermute | solution.py:24
  60.8 1.5 %collective-permute-start.23 = (bf16[32,768]{1,0:T(8,128)(2,1)S(1)}, bf16[32,768]{1,0:T(8,128)(2,1)S(1)}, u32[]{:S(2)}, u32[]{:S(2)}) collective-permute-start(bf16[32,768]{1,0:T(8,128)(2,1)S(1)} %collective-permute-done.19.refs_7_.refs_3_), channel_id=1, source_target_pairs={{0,4},{4,0},{8,12},{12,8},{16,20},{20,16},{24,28},{28,24},{1,5},{5... | collective-permute-start | bytes 147464 | tf_op jit(solution)/shard_map/ppermute | solution.py:24
  62.9 1.4 %collective-permute-done.22.refs_6_ = bf16[32,768]{1,0:T(8,128)(2,1)S(1)} collective-permute-done((bf16[32,768]{1,0:T(8,128)(2,1)S(1)}, bf16[32,768]{1,0:T(8,128)(2,1)S(1)}, u32[]{:S(2)}, u32[]{:S(2)}) %collective-permute-start.22) | collective-permute-done | bytes 49184 | tf_op jit(solution)/shard_map/ppermute | solution.py:24
  64.9 1.0 %back_first.1.refs_14_ = f32[512,64]{1,0:T(8,128)S(1)} custom-call(s32[1]{0:T(128)} %bitcast.place_ref, s32[1]{0:T(128)} %bitcast.1.group_ref, s32[1]{0:T(128)} %bitcast.2.core_ref, bf16[16,6144]{1,0:T(8,128)(2,1)S(1)} %get-tuple-element.66.refs_0_, bf16[16,6144]{1,0:T(8,128)(2,1)S(1)} %collective-permute-done.7.refs_1_, ...), custom_call_target="tpu_custom_call" | custom-call | flops 201326592 | bytes 3145728 | tf_op jit(solution)/shard_map/back_first/pallas_call | solution.py:443
  66.1 2.0 %back_last.1 = (bf16[32,32,128]{2,1,0:T(8,128)(2,1)}, bf16[512,64]{1,0:T(8,128)(2,1)S(1)}) custom-call(s32[1]{0:T(128)} %bitcast.place_ref, s32[1]{0:T(128)} %bitcast.1.group_ref, s32[1]{0:T(128)} %bitcast.2.core_ref, bf16[16,6144]{1,0:T(8,128)(2,1)S(1)} %get-tuple-element.66.refs_0_, bf16[16,6144]{1,0:T(8,128)(2,1)S(1)} %collective-permute-done.7.refs_1_, ...), custom_call_target="tpu_custom_call" | custom-call | flops 201326592 | bytes 3145728 | tf_op jit(solution)/shard_map/back_last/pallas_call | solution.py:458
  68.1 3.3 %all-to-all-start.1 = ((bf16[32,32,128]{2,1,0:T(8,128)(2,1)}), bf16[32,32,128]{2,1,0:T(8,128)(2,1)S(1)}, u32[]{:S(2)}, u32[]{:S(2)}) async-start(bf16[32,32,128]{2,1,0:T(8,128)(2,1)} %get-tuple-element.93), calls=%async_computation.1 | async-start | bytes 524288 | tf_op jit(solution)/shard_map/all_to_all | solution.py:40
  72.4 1.8 %collective-permute-start.32 = (bf16[4,6144]{1,0:T(4,128)(2,1)S(1)}, bf16[4,6144]{1,0:T(4,128)(2,1)S(1)}, u32[]{:S(2)}, u32[]{:S(2)}) collective-permute-start(bf16[4,6144]{1,0:T(4,128)(2,1)S(1)} %convolution_convert_fusion), channel_id=1, source_target_pairs={{0,2},{2,0},{1,3},{3,1},{4,6},{6,4},{5,7},{7,5},{8,10},{10,8},{9,1... | collective-permute-start | bytes 147464 | tf_op jit(solution)/shard_map/ppermute | solution.py:624
  74.3 3.2 %collective-permute-done.32 = bf16[4,6144]{1,0:T(4,128)(2,1)S(1)} collective-permute-done((bf16[4,6144]{1,0:T(4,128)(2,1)S(1)}, bf16[4,6144]{1,0:T(4,128)(2,1)S(1)}, u32[]{:S(2)}, u32[]{:S(2)}) %collective-permute-start.32) | collective-permute-done | bytes 49184 | tf_op jit(solution)/shard_map/ppermute | solution.py:624
  78.3 3.7 %all-to-all-done.1 = bf16[32,32,128]{2,1,0:T(8,128)(2,1)S(1)} async-done(((bf16[32,32,128]{2,1,0:T(8,128)(2,1)}), bf16[32,32,128]{2,1,0:T(8,128)(2,1)S(1)}, u32[]{:S(2)}, u32[]{:S(2)}) %all-to-all-start.1) | async-done | bytes 262176 | tf_op jit(solution)/shard_map/all_to_all | solution.py:40
  (74 shorter events, 13.9 us)
Async XLA Ops:
  0.6 9.3 %collective-permute-start = (bf16[4,6144]{1,0:T(4,128)(2,1)}, bf16[4,6144]{1,0:T(4,128)(2,1)S(1)}, u32[]{:S(2)}, u32[]{:S(2)}) collective-permute-start(bf16[4,6144]{1,0:T(4,128)(2,1)} %refs_0_.1), channel_id=1, source_target_pairs={{0,8},{4,12},{8,0},{12,4},{16,24},{20,28},{24,16},{28,20},{1,9},{5... | collective-permute-start | bytes 147464 | tf_op jit(solution)/shard_map/ppermute | solution.py:24
  3.7 6.6 %collective-permute-start.1 = (bf16[4,6144]{1,0:T(4,128)(2,1)}, bf16[4,6144]{1,0:T(4,128)(2,1)S(1)}, u32[]{:S(2)}, u32[]{:S(2)}) collective-permute-start(bf16[4,6144]{1,0:T(4,128)(2,1)} %refs_0_.1), channel_id=1, source_target_pairs={{0,16},{4,20},{8,24},{12,28},{16,0},{20,4},{24,8},{28,12},{1,17},{... | collective-permute-start | bytes 147464 | tf_op jit(solution)/shard_map/ppermute | solution.py:24
  6.3 6.1 %collective-permute-start.2 = (bf16[4,6144]{1,0:T(4,128)(2,1)}, bf16[4,6144]{1,0:T(4,128)(2,1)S(1)}, u32[]{:S(2)}, u32[]{:S(2)}) collective-permute-start(bf16[4,6144]{1,0:T(4,128)(2,1)} %refs_0_.1), channel_id=1, source_target_pairs={{0,24},{4,28},{8,16},{12,20},{16,8},{20,12},{24,0},{28,4},{1,25},{... | collective-permute-start | bytes 147464 | tf_op jit(solution)/shard_map/ppermute | solution.py:24
  6.3 8.7 %collective-permute-start.3 = (bf16[4,6144]{1,0:T(4,128)(2,1)}, bf16[4,6144]{1,0:T(4,128)(2,1)S(1)}, u32[]{:S(2)}, u32[]{:S(2)}) collective-permute-start(bf16[4,6144]{1,0:T(4,128)(2,1)} %refs_0_.1), channel_id=1, source_target_pairs={{0,4},{4,0},{8,12},{12,8},{16,20},{20,16},{24,28},{28,24},{1,5},{5... | collective-permute-start | bytes 147464 | tf_op jit(solution)/shard_map/ppermute | solution.py:24
  9.9 5.1 %collective-permute-start.4 = (bf16[4,6144]{1,0:T(4,128)(2,1)S(1)}, bf16[4,6144]{1,0:T(4,128)(2,1)S(1)}, u32[]{:S(2)}, u32[]{:S(2)}) collective-permute-start(bf16[4,6144]{1,0:T(4,128)(2,1)S(1)} %collective-permute-done.refs_1_), channel_id=1, source_target_pairs={{0,4},{4,0},{8,12},{12,8},{16,20},{20,16},{24,28},{28,24},{1,5},{5... | collective-permute-start | bytes 147464 | tf_op jit(solution)/shard_map/ppermute | solution.py:24
  10.3 4.8 %collective-permute-start.5 = (bf16[4,6144]{1,0:T(4,128)(2,1)S(1)}, bf16[4,6144]{1,0:T(4,128)(2,1)S(1)}, u32[]{:S(2)}, u32[]{:S(2)}) collective-permute-start(bf16[4,6144]{1,0:T(4,128)(2,1)S(1)} %collective-permute-done.1.refs_2_), channel_id=1, source_target_pairs={{0,4},{4,0},{8,12},{12,8},{16,20},{20,16},{24,28},{28,24},{1,5},{5... | collective-permute-start | bytes 147464 | tf_op jit(solution)/shard_map/ppermute | solution.py:24
  12.4 4.1 %collective-permute-start.6 = (bf16[4,6144]{1,0:T(4,128)(2,1)S(1)}, bf16[4,6144]{1,0:T(4,128)(2,1)S(1)}, u32[]{:S(2)}, u32[]{:S(2)}) collective-permute-start(bf16[4,6144]{1,0:T(4,128)(2,1)S(1)} %collective-permute-done.2.refs_3_), channel_id=1, source_target_pairs={{0,4},{4,0},{8,12},{12,8},{16,20},{20,16},{24,28},{28,24},{1,5},{5... | collective-permute-start | bytes 147464 | tf_op jit(solution)/shard_map/ppermute | solution.py:24
  17.6 5.7 %collective-permute-start.7 = (bf16[16,6144]{1,0:T(8,128)(2,1)S(1)}, bf16[16,6144]{1,0:T(8,128)(2,1)S(1)}, u32[]{:S(2)}, u32[]{:S(2)}) collective-permute-start(bf16[16,6144]{1,0:T(8,128)(2,1)S(1)} %get-tuple-element.67.refs_1_), channel_id=1, source_target_pairs={{0,2},{2,0},{1,3},{3,1},{4,6},{6,4},{5,7},{7,5},{8,10},{10,8},{9,1... | collective-permute-start | bytes 589832 | tf_op jit(solution)/shard_map/ppermute | solution.py:556
  19.1 4.2 %collective-permute-start.8 = (bf16[16,6144]{1,0:T(8,128)(2,1)S(1)}, bf16[16,6144]{1,0:T(8,128)(2,1)S(1)}, u32[]{:S(2)}, u32[]{:S(2)}) collective-permute-start(bf16[16,6144]{1,0:T(8,128)(2,1)S(1)} %get-tuple-element.66.refs_0_), channel_id=1, source_target_pairs={{0,1},{1,0},{2,3},{3,2},{4,5},{5,4},{6,7},{7,6},{8,9},{9,8},{10,11... | collective-permute-start | bytes 589832 | tf_op jit(solution)/shard_map/ppermute | solution.py:19
  19.2 11.1 %all-to-all-start = ((bf16[32,8,128]{2,1,0:T(8,128)(2,1)}), bf16[32,8,128]{2,1,0:T(8,128)(2,1)S(1)}, u32[]{:S(2)}, u32[]{:S(2)}) async-start(bf16[32,8,128]{2,1,0:T(8,128)(2,1)} %low_pieces.1), calls=%async_computation | async-start | bytes 131072 | tf_op jit(solution)/shard_map/all_to_all | solution.py:40
  33.7 1.8 %collective-permute-start.10 = (bf16[8,32,768]{2,1,0:T(8,128)(2,1)S(1)}, bf16[8,32,768]{2,1,0:T(8,128)(2,1)S(1)}, u32[]{:S(2)}, u32[]{:S(2)}) collective-permute-start(bf16[8,32,768]{2,1,0:T(8,128)(2,1)S(1)} %get-tuple-element.75), channel_id=1, source_target_pairs={{0,1},{1,0},{2,3},{3,2},{4,5},{5,4},{6,7},{7,6},{8,9},{9,8},{10,11... | collective-permute-start | bytes 1179656 | tf_op jit(solution)/shard_map/ppermute | solution.py:19
  34.0 4.0 %collective-permute-start.12 = (bf16[64,196]{1,0:T(8,128)(2,1)S(1)}, bf16[64,196]{1,0:T(8,128)(2,1)S(1)}, u32[]{:S(2)}, u32[]{:S(2)}) collective-permute-start(bf16[64,196]{1,0:T(8,128)(2,1)S(1)} %get-tuple-element.102), channel_id=1, source_target_pairs={{0,2},{2,0},{1,3},{3,1},{4,6},{6,4},{5,7},{7,5},{8,10},{10,8},{9,1... | collective-permute-start | bytes 75272 | tf_op jit(solution)/shard_map/ppermute | solution.py:574
  35.6 4.9 %collective-permute-start.11 = (bf16[2,32,768]{2,1,0:T(8,128)(2,1)S(1)}, bf16[2,32,768]{2,1,0:T(8,128)(2,1)S(1)}, u32[]{:S(2)}, u32[]{:S(2)}) collective-permute-start(bf16[2,32,768]{2,1,0:T(8,128)(2,1)S(1)} %get-tuple-element.76), channel_id=1, source_target_pairs={{0,4},{4,0},{8,12},{12,8},{16,20},{20,16},{24,28},{28,24},{1,5},{5... | collective-permute-start | bytes 294920 | tf_op jit(solution)/shard_map/ppermute | solution.py:24
  40.5 5.0 %collective-permute-start.13 = (bf16[2,32,768]{2,1,0:T(8,128)(2,1)S(1)}, bf16[2,32,768]{2,1,0:T(8,128)(2,1)S(1)}, u32[]{:S(2)}, u32[]{:S(2)}) collective-permute-start(bf16[2,32,768]{2,1,0:T(8,128)(2,1)S(1)} %get-tuple-element.80), channel_id=1, source_target_pairs={{0,4},{4,0},{8,12},{12,8},{16,20},{20,16},{24,28},{28,24},{1,5},{5... | collective-permute-start | bytes 294920 | tf_op jit(solution)/shard_map/ppermute | solution.py:24
  41.6 6.6 %collective-permute-start.15 = (bf16[32,768]{1,0:T(8,128)(2,1)S(1)}, bf16[32,768]{1,0:T(8,128)(2,1)S(1)}, u32[]{:S(2)}, u32[]{:S(2)}) collective-permute-start(bf16[32,768]{1,0:T(8,128)(2,1)S(1)} %get-tuple-element.84), channel_id=1, source_target_pairs={{0,16},{4,20},{8,24},{12,28},{16,0},{20,4},{24,8},{28,12},{1,17},{... | collective-permute-start | bytes 147464 | tf_op jit(solution)/shard_map/ppermute | solution.py:24
  44.0 6.0 %collective-permute-start.16 = (bf16[32,768]{1,0:T(8,128)(2,1)S(1)}, bf16[32,768]{1,0:T(8,128)(2,1)S(1)}, u32[]{:S(2)}, u32[]{:S(2)}) collective-permute-start(bf16[32,768]{1,0:T(8,128)(2,1)S(1)} %get-tuple-element.85), channel_id=1, source_target_pairs={{0,24},{4,28},{8,16},{12,20},{16,8},{20,12},{24,0},{28,4},{1,25},{... | collective-permute-start | bytes 147464 | tf_op jit(solution)/shard_map/ppermute | solution.py:24
  45.5 4.7 %collective-permute-start.14 = (bf16[32,768]{1,0:T(8,128)(2,1)S(1)}, bf16[32,768]{1,0:T(8,128)(2,1)S(1)}, u32[]{:S(2)}, u32[]{:S(2)}) collective-permute-start(bf16[32,768]{1,0:T(8,128)(2,1)S(1)} %get-tuple-element.82), channel_id=1, source_target_pairs={{0,8},{4,12},{8,0},{12,4},{16,24},{20,28},{24,16},{28,20},{1,9},{5... | collective-permute-start | bytes 147464 | tf_op jit(solution)/shard_map/ppermute | solution.py:24
  50.2 5.2 %collective-permute-start.17 = (bf16[32,768]{1,0:T(8,128)(2,1)S(1)}, bf16[32,768]{1,0:T(8,128)(2,1)S(1)}, u32[]{:S(2)}, u32[]{:S(2)}) collective-permute-start(bf16[32,768]{1,0:T(8,128)(2,1)S(1)} %mix.1.refs_4_.refs_0_), channel_id=1, source_target_pairs={{0,8},{4,12},{8,0},{12,4},{16,24},{20,28},{24,16},{28,20},{1,9},{5... | collective-permute-start | bytes 147464 | tf_op jit(solution)/shard_map/ppermute | solution.py:24
  50.4 5.2 %collective-permute-start.18 = (bf16[32,768]{1,0:T(8,128)(2,1)S(1)}, bf16[32,768]{1,0:T(8,128)(2,1)S(1)}, u32[]{:S(2)}, u32[]{:S(2)}) collective-permute-start(bf16[32,768]{1,0:T(8,128)(2,1)S(1)} %mix.1.refs_4_.refs_0_), channel_id=1, source_target_pairs={{0,16},{4,20},{8,24},{12,28},{16,0},{20,4},{24,8},{28,12},{1,17},{... | collective-permute-start | bytes 147464 | tf_op jit(solution)/shard_map/ppermute | solution.py:24
  52.8 5.9 %collective-permute-start.19 = (bf16[32,768]{1,0:T(8,128)(2,1)S(1)}, bf16[32,768]{1,0:T(8,128)(2,1)S(1)}, u32[]{:S(2)}, u32[]{:S(2)}) collective-permute-start(bf16[32,768]{1,0:T(8,128)(2,1)S(1)} %mix.1.refs_4_.refs_0_), channel_id=1, source_target_pairs={{0,24},{4,28},{8,16},{12,20},{16,8},{20,12},{24,0},{28,4},{1,25},{... | collective-permute-start | bytes 147464 | tf_op jit(solution)/shard_map/ppermute | solution.py:24
  54.6 5.6 %collective-permute-start.28 = (bf16[32,768]{1,0:T(8,128)(2,1)S(1)}, bf16[32,768]{1,0:T(8,128)(2,1)S(1)}, u32[]{:S(2)}, u32[]{:S(2)}) collective-permute-start(bf16[32,768]{1,0:T(8,128)(2,1)S(1)} %mix.1.refs_4_.refs_0_), channel_id=1, source_target_pairs={{0,1},{1,0},{2,3},{3,2},{4,5},{5,4},{6,7},{7,6},{8,9},{9,8},{10,11... | collective-permute-start | bytes 147464 | tf_op jit(solution)/shard_map/ppermute | solution.py:19
  54.6 6.1 %collective-permute-start.20 = (bf16[32,768]{1,0:T(8,128)(2,1)S(1)}, bf16[32,768]{1,0:T(8,128)(2,1)S(1)}, u32[]{:S(2)}, u32[]{:S(2)}) collective-permute-start(bf16[32,768]{1,0:T(8,128)(2,1)S(1)} %mix.1.refs_4_.refs_0_), channel_id=1, source_target_pairs={{0,4},{4,0},{8,12},{12,8},{16,20},{20,16},{24,28},{28,24},{1,5},{5... | collective-permute-start | bytes 147464 | tf_op jit(solution)/shard_map/ppermute | solution.py:24
  55.4 6.9 %collective-permute-start.29 = (bf16[32,768]{1,0:T(8,128)(2,1)S(1)}, bf16[32,768]{1,0:T(8,128)(2,1)S(1)}, u32[]{:S(2)}, u32[]{:S(2)}) collective-permute-start(bf16[32,768]{1,0:T(8,128)(2,1)S(1)} %collective-permute-done.17.refs_5_.refs_1_), channel_id=1, source_target_pairs={{0,1},{1,0},{2,3},{3,2},{4,5},{5,4},{6,7},{7,6},{8,9},{9,8},{10,11... | collective-permute-start | bytes 147464 | tf_op jit(solution)/shard_map/ppermute | solution.py:19
  55.7 6.7 %collective-permute-start.30 = (bf16[32,768]{1,0:T(8,128)(2,1)S(1)}, bf16[32,768]{1,0:T(8,128)(2,1)S(1)}, u32[]{:S(2)}, u32[]{:S(2)}) collective-permute-start(bf16[32,768]{1,0:T(8,128)(2,1)S(1)} %collective-permute-done.18.refs_6_.refs_2_), channel_id=1, source_target_pairs={{0,1},{1,0},{2,3},{3,2},{4,5},{5,4},{6,7},{7,6},{8,9},{9,8},{10,11... | collective-permute-start | bytes 147464 | tf_op jit(solution)/shard_map/ppermute | solution.py:19
  58.7 4.1 %collective-permute-start.21 = (bf16[32,768]{1,0:T(8,128)(2,1)S(1)}, bf16[32,768]{1,0:T(8,128)(2,1)S(1)}, u32[]{:S(2)}, u32[]{:S(2)}) collective-permute-start(bf16[32,768]{1,0:T(8,128)(2,1)S(1)} %collective-permute-done.17.refs_5_.refs_1_), channel_id=1, source_target_pairs={{0,4},{4,0},{8,12},{12,8},{16,20},{20,16},{24,28},{28,24},{1,5},{5... | collective-permute-start | bytes 147464 | tf_op jit(solution)/shard_map/ppermute | solution.py:24
  60.2 4.1 %collective-permute-start.22 = (bf16[32,768]{1,0:T(8,128)(2,1)S(1)}, bf16[32,768]{1,0:T(8,128)(2,1)S(1)}, u32[]{:S(2)}, u32[]{:S(2)}) collective-permute-start(bf16[32,768]{1,0:T(8,128)(2,1)S(1)} %collective-permute-done.18.refs_6_.refs_2_), channel_id=1, source_target_pairs={{0,4},{4,0},{8,12},{12,8},{16,20},{20,16},{24,28},{28,24},{1,5},{5... | collective-permute-start | bytes 147464 | tf_op jit(solution)/shard_map/ppermute | solution.py:24
  60.8 4.1 %collective-permute-start.23 = (bf16[32,768]{1,0:T(8,128)(2,1)S(1)}, bf16[32,768]{1,0:T(8,128)(2,1)S(1)}, u32[]{:S(2)}, u32[]{:S(2)}) collective-permute-start(bf16[32,768]{1,0:T(8,128)(2,1)S(1)} %collective-permute-done.19.refs_7_.refs_3_), channel_id=1, source_target_pairs={{0,4},{4,0},{8,12},{12,8},{16,20},{20,16},{24,28},{28,24},{1,5},{5... | collective-permute-start | bytes 147464 | tf_op jit(solution)/shard_map/ppermute | solution.py:24
  62.3 2.6 %collective-permute-start.31 = (bf16[32,768]{1,0:T(8,128)(2,1)S(1)}, bf16[32,768]{1,0:T(8,128)(2,1)S(1)}, u32[]{:S(2)}, u32[]{:S(2)}) collective-permute-start(bf16[32,768]{1,0:T(8,128)(2,1)S(1)} %collective-permute-done.19.refs_7_.refs_3_), channel_id=1, source_target_pairs={{0,1},{1,0},{2,3},{3,2},{4,5},{5,4},{6,7},{7,6},{8,9},{9,8},{10,11... | collective-permute-start | bytes 147464 | tf_op jit(solution)/shard_map/ppermute | solution.py:19
  62.4 3.6 %collective-permute-start.24 = (bf16[32,768]{1,0:T(8,128)(2,1)S(1)}, bf16[32,768]{1,0:T(8,128)(2,1)S(1)}, u32[]{:S(2)}, u32[]{:S(2)}) collective-permute-start(bf16[32,768]{1,0:T(8,128)(2,1)S(1)} %collective-permute-done.20.refs_4_), channel_id=1, source_target_pairs={{0,1},{1,0},{2,3},{3,2},{4,5},{5,4},{6,7},{7,6},{8,9},{9,8},{10,11... | collective-permute-start | bytes 147464 | tf_op jit(solution)/shard_map/ppermute | solution.py:19
  62.9 3.1 %collective-permute-start.25 = (bf16[32,768]{1,0:T(8,128)(2,1)S(1)}, bf16[32,768]{1,0:T(8,128)(2,1)S(1)}, u32[]{:S(2)}, u32[]{:S(2)}) collective-permute-start(bf16[32,768]{1,0:T(8,128)(2,1)S(1)} %collective-permute-done.21.refs_5_), channel_id=1, source_target_pairs={{0,1},{1,0},{2,3},{3,2},{4,5},{5,4},{6,7},{7,6},{8,9},{9,8},{10,11... | collective-permute-start | bytes 147464 | tf_op jit(solution)/shard_map/ppermute | solution.py:19
  68.1 13.9 %all-to-all-start.1 = ((bf16[32,32,128]{2,1,0:T(8,128)(2,1)}), bf16[32,32,128]{2,1,0:T(8,128)(2,1)S(1)}, u32[]{:S(2)}, u32[]{:S(2)}) async-start(bf16[32,32,128]{2,1,0:T(8,128)(2,1)} %get-tuple-element.93), calls=%async_computation.1 | async-start | bytes 524288 | tf_op jit(solution)/shard_map/all_to_all | solution.py:40
  72.4 5.0 %collective-permute-start.32 = (bf16[4,6144]{1,0:T(4,128)(2,1)S(1)}, bf16[4,6144]{1,0:T(4,128)(2,1)S(1)}, u32[]{:S(2)}, u32[]{:S(2)}) collective-permute-start(bf16[4,6144]{1,0:T(4,128)(2,1)S(1)} %convolution_convert_fusion), channel_id=1, source_target_pairs={{0,2},{2,0},{1,3},{3,1},{4,6},{6,4},{5,7},{7,5},{8,10},{10,8},{9,1... | collective-permute-start | bytes 147464 | tf_op jit(solution)/shard_map/ppermute | solution.py:624
  (4 other events, 11.3 us)

commit v8 on v7

--- a/solution.py
+++ b/solution.py
@@ -30,6 +30,16 @@
     if meanwhile:
         far[0], meanwhile = lax.optimization_barrier((far[0], meanwhile))
     return [block, *far, near, *[across(other, "dp", 1) for other in far]], *meanwhile
+
+
+def gather_pairs(block):
+    near = across(block, "dp", 1)
+    line = stack_three([across(block, "dp", bits) for bits in NEAR[3:0:-1]][::-1])
+    return (block, line), (near, across(line, "dp", 1))
+
+
+def views(single, line):
+    return [single, *[line.at[k] for k in range(line.shape[0])]]
 
 
 def order_of(place, blocks, eight, first=0):
@@ -353,6 +363,22 @@
     )(keep, got)
 
 
+def stack_kernel(*refs):
+    for k, ref in enumerate(refs[:-1]):
+        refs[-1][k] = ref[...]
+
+
+def stack_three(arrays):
+    return pl.pallas_call(
+        stack_kernel,
+        in_specs=vmem(len(arrays)),
+        out_specs=vmem(1)[0],
+        out_shape=struct((len(arrays), *arrays[0].shape), bf16),
+        compiler_params=params(),
+        name="stack",
+    )(*arrays)
+
+
 def mix_kernel(n_terms, *refs):
     gate_ref, out_ref = refs[n_terms:]
     total = refs[0][...].astype(f32)
@@ -388,7 +414,7 @@
 
 def back_first_kernel(n_parts, n_blocks, eight, loss_factor, here_ref, *refs):
     parts, refs = refs[:n_parts], refs[n_parts:]
-    owns, others, refs = refs[:n_blocks], refs[n_blocks : 2 * n_blocks], refs[2 * n_blocks :]
+    owns, others, refs = views(*refs[:2]), views(*refs[2:4]), refs[4:]
     gate_ref, down_ref, out_ref = refs
     order = order_of(here_ref[0], n_blocks, eight)
     out_ref[...] = back_sum(parts, owns, others, order, gate_ref, down_ref, loss_factor)
@@ -396,7 +422,7 @@
 
 def back_last_kernel(n_parts, n_blocks, eight, loss_factor, here_ref, *refs):
     parts, refs = refs[:n_parts], refs[n_parts:]
-    owns, others, refs = refs[:n_blocks], refs[n_blocks : 2 * n_blocks], refs[2 * n_blocks :]
+    owns, others, refs = views(*refs[:2]), views(*refs[2:4]), refs[4:]
     gate_ref, down_ref, first_ref, slope_ref, factor_ref, low_out, back_out = refs
     order = order_of(here_ref[0], n_blocks, eight, n_blocks)
     total = first_ref[...] + back_sum(parts, owns, others, order, gate_ref, down_ref, loss_factor)
@@ -408,7 +434,8 @@
 
 
 def rest_kernel(n_blocks, eight, here_ref, *refs):
-    owns, (back_ref, low_ref, grad_ref, *homes) = refs[:n_blocks], refs[n_blocks:]
+    owns = views(*refs[:2]) + views(*refs[2:4])
+    back_ref, low_ref, grad_ref, *homes = refs[4:]
     half, wide = owns[0].shape
     capacity = half // len(homes)
     grad_ref[...] = adapter_scale * lax.dot_general(
@@ -423,14 +450,14 @@
 
 def rest(owns, here, eight, back_pre, low, capacity):
     half, wide = owns[0].shape
-    homes = half // capacity
-    return pl.pallas_call(
-        seated(functools.partial(rest_kernel, len(owns), eight)),
+    homes, blocks = half // capacity, 2 * (1 + owns[1].shape[0])
+    return pl.pallas_call(
+        seated(functools.partial(rest_kernel, blocks, eight)),
         in_specs=[pl.BlockSpec(memory_space=pltpu.SMEM)] * 3 + vmem(len(owns) + 2),
         out_specs=vmem(1 + homes),
         out_shape=(
             struct((low.shape[1], back_pre.shape[0]), f32),
-            *[struct((capacity, wide * len(owns)), bf16)] * homes,
+            *[struct((capacity, wide * blocks), bf16)] * homes,
         ),
         compiler_params=params(),
         name="rest",
@@ -439,10 +466,10 @@
 
 def back_first(parts, owns, others, here, eight, gate, kept, loss_factor):
     units = kept.shape[1]
-    count, blocks, wide = gate.shape[0], len(owns), owns[0].shape[1]
+    count, blocks, wide = gate.shape[0], 1 + owns[1].shape[0], owns[0].shape[1]
     return pl.pallas_call(
         seated(functools.partial(back_first_kernel, len(parts), blocks, eight, loss_factor)),
-        in_specs=[pl.BlockSpec(memory_space=pltpu.SMEM)] * 3 + vmem(len(parts) + 2 * blocks + 2),
+        in_specs=[pl.BlockSpec(memory_space=pltpu.SMEM)] * 3 + vmem(len(parts) + 6),
         out_specs=vmem(1)[0],
         out_shape=struct((units, count), f32),
         cost_estimate=cost(2 * count * blocks * wide * units, 2 * blocks * wide * units),
@@ -454,10 +481,10 @@
 def back_last(parts, owns, others, here, eight, gate, kept, first, slope, factor, loss_factor, copies):
     wide = owns[0].shape[1]
     units, count = slope.shape
-    rank, blocks = factor.shape[0], len(others)
+    rank, blocks = factor.shape[0], 1 + others[1].shape[0]
     return pl.pallas_call(
         seated(functools.partial(back_last_kernel, len(parts), blocks, eight, loss_factor)),
-        in_specs=[pl.BlockSpec(memory_space=pltpu.SMEM)] * 3 + vmem(len(parts) + 2 * blocks + 5),
+        in_specs=[pl.BlockSpec(memory_space=pltpu.SMEM)] * 3 + vmem(len(parts) + 9),
         out_specs=vmem(2),
         out_shape=(struct((copies, rank // 2, 2 * count), bf16), struct((units, count), bf16)),
         cost_estimate=cost(2 * count * blocks * wide * units, 2 * blocks * wide * units),
@@ -582,7 +609,7 @@
         two, three = fold_near(keep, far, 2)
         mine, one = fold_near(keep, near, 0)
         terms = [mine, across(one, "dp", 2), across(two, "dp", 4), across(three, "dp", 6)]
-        (owns,) = gather_eight(mix(terms, gate))
+        owns = gather_pairs(mix(terms, gate))
     else:
         summed = (own.astype(f32) + got.astype(f32)).astype(bf16)
         summed = summed.transpose(1, 0, 2).reshape(half, n_dp, wide).transpose(1, 0, 2)
@@ -591,15 +618,16 @@
         mixed = exchange(jnp.broadcast_to(mixed[None], (n_dp, half, wide)), "dp")
         mixed = mixed.transpose(1, 0, 2).reshape(half, width)
         owns = [mixed[:, i * (width // blocks) : (i + 1) * (width // blocks)] for i in range(blocks)]
-    others = [swap(block, "core") for block in owns]
+        owns = [(owns[k], jnp.stack(owns[k + 1 : k + blocks // 2])) for k in (0, blocks // 2)]
+    others = [[swap(block, "core") for block in pair] for pair in owns]
 
     first = back_first(
-        parts, owns[: blocks // 2], others[: blocks // 2], here, eight, gate, kept, loss_factor
+        parts, owns[0], others[0], here, eight, gate, kept, loss_factor
     )
     back_low, back_pre = back_last(
         parts,
-        owns[blocks // 2 :],
-        others[blocks // 2 :],
+        owns[1],
+        others[1],
         here,
         eight,
         gate,
@@ -611,7 +639,7 @@
         devices,
     )
     lows = exchange(back_low, every).reshape(n_dp, groups, 2, rank // 2, 4 * half)
-    grad_b, *homes = rest(owns, here, eight, back_pre, low, capacity)
+    grad_b, *homes = rest([*owns[0], *owns[1]], here, eight, back_pre, low, capacity)
 
     result = jnp.zeros((tok_rows, width), f32)
     for step in range(groups):

time: 83.2 us -> 83.2 us (level)
  waiting for transfers between devices: 23.6 us -> 26 us
  starting transfers between devices: 39.4 us -> 37.1 us
    ppermute x19 -> x17, waiting for transfers between devices: 12.9 us -> 15.4 us  [across(): return lax.ppermute(block, axis, [(i, i ^ apart_by) for i in range(count)])]
    ppermute x19 -> x17, starting transfers between devices: 26.7 us -> 24.5 us  [across(): return lax.ppermute(block, axis, [(i, i ^ apart_by) for i in range(count)])]
    ppermute x11 -> x7, waiting for transfers between devices: 1.82 us -> 1.73 us  [swap(): return lax.ppermute(block, axis, [(0, 1), (1, 0)])]
  transfers between devices with their start and end apart: 35 -> 29, of which waited for: 17 -> 16; matrix products, arithmetic and copies ran while one was open for 4% -> 4% of each run, Pallas kernels for 10% -> 10%
where the time goes in v8:
time: 83.2 us; the launch traced here: 82.9 us
  starting transfers between devices  37.1 us (45%)
  waiting for transfers between devices  26 us (31%)
  Pallas kernels  15.7 us (19%)
  other arithmetic  1.88 us (2%)
  matrix products  1.06 us (1%)
  between operations  0.85 us (1%)
    ppermute x17, starting transfers between devices, across(): return lax.ppermute(block, axis, [(i, i ^ apart_by) for i in range(count)])  24.5 us
    ppermute x17, waiting for transfers between devices, across(): return lax.ppermute(block, axis, [(i, i ^ apart_by) for i in range(count)])  15.4 us
    all_to_all x2, starting transfers between devices, exchange(): return lax.all_to_all(blocks, axis, 0, 0, tiled=True)  6.9 us
    pallas_call x1, Pallas kernels, lift(): pl.pallas_call(functools.partial(lift_kernel, len(parts)), in_specs=vmem(...  5.07 us
    all_to_all x2, waiting for transfers between devices, exchange(): return lax.all_to_all(blocks, axis, 0, 0, tiled=True)  4.17 us
    pallas_call x1, Pallas kernels, down(): pl.pallas_call(seated(down_kernel), in_specs=[pl.BlockSpec(memory_space=p...  3.35 us
    ppermute x1, waiting for transfers between devices, shards(): chosen = lax.ppermute(chosen.astype(bf16), 'x', route).astype(f32)  3.17 us
    pallas_call x1, Pallas kernels, back_last(): pl.pallas_call(seated(functools.partial(back_last_kernel, len(parts), blo...  2 us
  transfers between devices with their start and end apart: 29, of which 16 were waited for; matrix products, arithmetic and copies ran while one was open for 4% of the time, Pallas kernels for 10%

profile of v8, /device:TPU:0, one launch (start us, length us, event | category | flops | bytes accessed | tf_op | source)
XLA Modules:
  0.0 82.9 jit_solution(12849892900561655446)
XLA Ops:
  0.6 3.1 %collective-permute-start = (bf16[4,6144]{1,0:T(4,128)(2,1)}, bf16[4,6144]{1,0:T(4,128)(2,1)S(1)}, u32[]{:S(2)}, u32[]{:S(2)}) collective-permute-start(bf16[4,6144]{1,0:T(4,128)(2,1)} %refs_0_.1), channel_id=1, source_target_pairs={{0,8},{4,12},{8,0},{12,4},{16,24},{20,28},{24,16},{28,20},{1,9},{5... | collective-permute-start | bytes 147464 | tf_op jit(solution)/shard_map/ppermute | solution.py:24
  3.7 2.6 %collective-permute-start.1 = (bf16[4,6144]{1,0:T(4,128)(2,1)}, bf16[4,6144]{1,0:T(4,128)(2,1)S(1)}, u32[]{:S(2)}, u32[]{:S(2)}) collective-permute-start(bf16[4,6144]{1,0:T(4,128)(2,1)} %refs_0_.1), channel_id=1, source_target_pairs={{0,16},{4,20},{8,24},{12,28},{16,0},{20,4},{24,8},{28,12},{1,17},{... | collective-permute-start | bytes 147464 | tf_op jit(solution)/shard_map/ppermute | solution.py:24
  6.3 1.7 %collective-permute-start.3 = (bf16[4,6144]{1,0:T(4,128)(2,1)}, bf16[4,6144]{1,0:T(4,128)(2,1)S(1)}, u32[]{:S(2)}, u32[]{:S(2)}) collective-permute-start(bf16[4,6144]{1,0:T(4,128)(2,1)} %refs_0_.1), channel_id=1, source_target_pairs={{0,4},{4,0},{8,12},{12,8},{16,20},{20,16},{24,28},{28,24},{1,5},{5... | collective-permute-start | bytes 147464 | tf_op jit(solution)/shard_map/ppermute | solution.py:24
  10.3 1.7 %collective-permute-start.5 = (bf16[4,6144]{1,0:T(4,128)(2,1)S(1)}, bf16[4,6144]{1,0:T(4,128)(2,1)S(1)}, u32[]{:S(2)}, u32[]{:S(2)}) collective-permute-start(bf16[4,6144]{1,0:T(4,128)(2,1)S(1)} %collective-permute-done.1.refs_2_), channel_id=1, source_target_pairs={{0,4},{4,0},{8,12},{12,8},{16,20},{20,16},{24,28},{28,24},{1,5},{5... | collective-permute-start | bytes 147464 | tf_op jit(solution)/shard_map/ppermute | solution.py:24
  12.4 1.5 %collective-permute-start.6 = (bf16[4,6144]{1,0:T(4,128)(2,1)S(1)}, bf16[4,6144]{1,0:T(4,128)(2,1)S(1)}, u32[]{:S(2)}, u32[]{:S(2)}) collective-permute-start(bf16[4,6144]{1,0:T(4,128)(2,1)S(1)} %collective-permute-done.2.refs_3_), channel_id=1, source_target_pairs={{0,4},{4,0},{8,12},{12,8},{16,20},{20,16},{24,28},{28,24},{1,5},{5... | collective-permute-start | bytes 147464 | tf_op jit(solution)/shard_map/ppermute | solution.py:24
  14.0 1.0 %near.1 = (bf16[4,6144]{1,0:T(4,128)(2,1)S(1)}, bf16[64,768]{1,0:T(8,128)(2,1)S(1)}, f32[1,6144]{1,0:T(1,128)S(1)}) custom-call(s32[1]{0:T(128)} %bitcast.place_ref, s32[1]{0:T(128)} %bitcast.1.group_ref, s32[1]{0:T(128)} %bitcast.2.core_ref, bf16[4,6144]{1,0:T(4,128)(2,1)} %refs_0_.1, bf16[64,768]{1,0:T(8,128)(2,1)} %bitcast.25, bf16[2,6144]{1,0:T(2,128)(2,1)} %bitcast.28), custom_call_target="tpu_custom_call" | custom-call | tf_op jit(solution)/shard_map/near/pallas_call | solution.py:122
  15.1 1.4 %collective-permute-done.6.refs_7_ = bf16[4,6144]{1,0:T(4,128)(2,1)S(1)} collective-permute-done((bf16[4,6144]{1,0:T(4,128)(2,1)S(1)}, bf16[4,6144]{1,0:T(4,128)(2,1)S(1)}, u32[]{:S(2)}, u32[]{:S(2)}) %collective-permute-start.6) | collective-permute-done | bytes 49184 | tf_op jit(solution)/shard_map/ppermute | solution.py:24
  17.6 1.5 %collective-permute-start.7 = (bf16[16,6144]{1,0:T(8,128)(2,1)S(1)}, bf16[16,6144]{1,0:T(8,128)(2,1)S(1)}, u32[]{:S(2)}, u32[]{:S(2)}) collective-permute-start(bf16[16,6144]{1,0:T(8,128)(2,1)S(1)} %get-tuple-element.67.refs_1_), channel_id=1, source_target_pairs={{0,2},{2,0},{1,3},{3,1},{4,6},{6,4},{5,7},{7,5},{8,10},{10,8},{9,1... | collective-permute-start | bytes 589832 | tf_op jit(solution)/shard_map/ppermute | solution.py:583
  19.2 3.7 %all-to-all-start = ((bf16[32,8,128]{2,1,0:T(8,128)(2,1)}), bf16[32,8,128]{2,1,0:T(8,128)(2,1)S(1)}, u32[]{:S(2)}, u32[]{:S(2)}) async-start(bf16[32,8,128]{2,1,0:T(8,128)(2,1)} %low_pieces.1), calls=%async_computation | async-start | bytes 131072 | tf_op jit(solution)/shard_map/all_to_all | solution.py:50
  23.4 1.4 %collective-permute-done.9.refs_3_ = bf16[16,6144]{1,0:T(8,128)(2,1)S(1)} collective-permute-done((bf16[16,6144]{1,0:T(8,128)(2,1)S(1)}, bf16[16,6144]{1,0:T(8,128)(2,1)S(1)}, u32[]{:S(2)}, u32[]{:S(2)}) %collective-permute-start.9) | collective-permute-done | bytes 196640 | tf_op jit(solution)/shard_map/ppermute | solution.py:19
  24.7 5.1 %lift.1 = (f32[64,512]{1,0:T(8,128)S(1)}, f32[64,512]{1,0:T(8,128)S(1)}, f32[64,1]{1,0:T(8,128)S(1)}) custom-call(bf16[16,6144]{1,0:T(8,128)(2,1)S(1)} %get-tuple-element.66.refs_0_, bf16[16,6144]{1,0:T(8,128)(2,1)S(1)} %collective-permute-done.7.refs_1_, bf16[16,6144]{1,0:T(8,128)(2,1)S(1)} %collective-permute-done.8.refs_2_, ...), custom_call_target="tpu_custom_call" | custom-call | flops 805306368 | bytes 12582912 | tf_op jit(solution)/shard_map/lift/pallas_call | solution.py:231
  30.3 3.4 %down.1 = (bf16[8,32,768]{2,1,0:T(8,128)(2,1)S(1)}, bf16[8,32,768]{2,1,0:T(8,128)(2,1)S(1)}, f32[512,64]{1,0:T(8,128)S(1)}, bf16[64,64]{1,0:T(8,128)(2,1)S(1)}, bf16[8,512,768]{2,1,0:T(8,128)(2,1)S(1)}) custom-call(s32[1]{0:T(128)} %bitcast.place_ref, s32[1]{0:T(128)} %bitcast.1.group_ref, s32[1]{0:T(128)} %bitcast.2.core_ref, ...), custom_call_target="tpu_custom_call" | custom-call | flops 402653184 | bytes 6291456 | tf_op jit(solution)/shard_map/down/pallas_call | solution.py:299
  34.0 1.1 %collective-permute-start.12 = (bf16[64,196]{1,0:T(8,128)(2,1)S(1)}, bf16[64,196]{1,0:T(8,128)(2,1)S(1)}, u32[]{:S(2)}, u32[]{:S(2)}) collective-permute-start(bf16[64,196]{1,0:T(8,128)(2,1)S(1)} %get-tuple-element.102), channel_id=1, source_target_pairs={{0,2},{2,0},{1,3},{3,1},{4,6},{6,4},{5,7},{7,5},{8,10},{10,8},{9,1... | collective-permute-start | bytes 75272 | tf_op jit(solution)/shard_map/ppermute | solution.py:601
  35.6 1.2 %collective-permute-start.11 = (bf16[2,32,768]{2,1,0:T(8,128)(2,1)S(1)}, bf16[2,32,768]{2,1,0:T(8,128)(2,1)S(1)}, u32[]{:S(2)}, u32[]{:S(2)}) collective-permute-start(bf16[2,32,768]{2,1,0:T(8,128)(2,1)S(1)} %get-tuple-element.76), channel_id=1, source_target_pairs={{0,4},{4,0},{8,12},{12,8},{16,20},{20,16},{24,28},{28,24},{1,5},{5... | collective-permute-start | bytes 294920 | tf_op jit(solution)/shard_map/ppermute | solution.py:24
  36.8 1.2 %collective-permute-done.12 = bf16[64,196]{1,0:T(8,128)(2,1)S(1)} collective-permute-done((bf16[64,196]{1,0:T(8,128)(2,1)S(1)}, bf16[64,196]{1,0:T(8,128)(2,1)S(1)}, u32[]{:S(2)}, u32[]{:S(2)}) %collective-permute-start.12) | collective-permute-done | bytes 25120 | tf_op jit(solution)/shard_map/ppermute | solution.py:601
  38.0 2.5 %collective-permute-done.11.got_ref = bf16[2,32,768]{2,1,0:T(8,128)(2,1)S(1)} collective-permute-done((bf16[2,32,768]{2,1,0:T(8,128)(2,1)S(1)}, bf16[2,32,768]{2,1,0:T(8,128)(2,1)S(1)}, u32[]{:S(2)}, u32[]{:S(2)}) %collective-permute-start.11) | collective-permute-done | bytes 98336 | tf_op jit(solution)/shard_map/ppermute | solution.py:24
  40.5 1.1 %collective-permute-start.13 = (bf16[2,32,768]{2,1,0:T(8,128)(2,1)S(1)}, bf16[2,32,768]{2,1,0:T(8,128)(2,1)S(1)}, u32[]{:S(2)}, u32[]{:S(2)}) collective-permute-start(bf16[2,32,768]{2,1,0:T(8,128)(2,1)S(1)} %get-tuple-element.80), channel_id=1, source_target_pairs={{0,4},{4,0},{8,12},{12,8},{16,20},{20,16},{24,28},{28,24},{1,5},{5... | collective-permute-start | bytes 294920 | tf_op jit(solution)/shard_map/ppermute | solution.py:24
  41.6 2.4 %collective-permute-start.15 = (bf16[32,768]{1,0:T(8,128)(2,1)S(1)}, bf16[32,768]{1,0:T(8,128)(2,1)S(1)}, u32[]{:S(2)}, u32[]{:S(2)}) collective-permute-start(bf16[32,768]{1,0:T(8,128)(2,1)S(1)} %get-tuple-element.84), channel_id=1, source_target_pairs={{0,16},{4,20},{8,24},{12,28},{16,0},{20,4},{24,8},{28,12},{1,17},{... | collective-permute-start | bytes 147464 | tf_op jit(solution)/shard_map/ppermute | solution.py:24
  44.0 1.4 %collective-permute-start.16 = (bf16[32,768]{1,0:T(8,128)(2,1)S(1)}, bf16[32,768]{1,0:T(8,128)(2,1)S(1)}, u32[]{:S(2)}, u32[]{:S(2)}) collective-permute-start(bf16[32,768]{1,0:T(8,128)(2,1)S(1)} %get-tuple-element.85), channel_id=1, source_target_pairs={{0,24},{4,28},{8,16},{12,20},{16,8},{20,12},{24,0},{28,4},{1,25},{... | collective-permute-start | bytes 147464 | tf_op jit(solution)/shard_map/ppermute | solution.py:24
  46.2 2.0 %collective-permute-done.15.refs_2_ = bf16[32,768]{1,0:T(8,128)(2,1)S(1)} collective-permute-done((bf16[32,768]{1,0:T(8,128)(2,1)S(1)}, bf16[32,768]{1,0:T(8,128)(2,1)S(1)}, u32[]{:S(2)}, u32[]{:S(2)}) %collective-permute-start.15) | collective-permute-done | bytes 49184 | tf_op jit(solution)/shard_map/ppermute | solution.py:24
  48.2 1.8 %collective-permute-done.16.refs_3_ = bf16[32,768]{1,0:T(8,128)(2,1)S(1)} collective-permute-done((bf16[32,768]{1,0:T(8,128)(2,1)S(1)}, bf16[32,768]{1,0:T(8,128)(2,1)S(1)}, u32[]{:S(2)}, u32[]{:S(2)}) %collective-permute-start.16) | collective-permute-done | bytes 49184 | tf_op jit(solution)/shard_map/ppermute | solution.py:24
  50.4 2.4 %collective-permute-start.18 = (bf16[32,768]{1,0:T(8,128)(2,1)S(1)}, bf16[32,768]{1,0:T(8,128)(2,1)S(1)}, u32[]{:S(2)}, u32[]{:S(2)}) collective-permute-start(bf16[32,768]{1,0:T(8,128)(2,1)S(1)} %mix.1.refs_4_.refs_0_), channel_id=1, source_target_pairs={{0,16},{4,20},{8,24},{12,28},{16,0},{20,4},{24,8},{28,12},{1,17},{... | collective-permute-start | bytes 147464 | tf_op jit(solution)/shard_map/ppermute | solution.py:24
  52.8 1.8 %collective-permute-start.19 = (bf16[32,768]{1,0:T(8,128)(2,1)S(1)}, bf16[32,768]{1,0:T(8,128)(2,1)S(1)}, u32[]{:S(2)}, u32[]{:S(2)}) collective-permute-start(bf16[32,768]{1,0:T(8,128)(2,1)S(1)} %mix.1.refs_4_.refs_0_), channel_id=1, source_target_pairs={{0,24},{4,28},{8,16},{12,20},{16,8},{20,12},{24,0},{28,4},{1,25},{... | collective-permute-start | bytes 147464 | tf_op jit(solution)/shard_map/ppermute | solution.py:24
  55.7 3.1 %collective-permute-done.19.refs_2_ = bf16[32,768]{1,0:T(8,128)(2,1)S(1)} collective-permute-done((bf16[32,768]{1,0:T(8,128)(2,1)S(1)}, bf16[32,768]{1,0:T(8,128)(2,1)S(1)}, u32[]{:S(2)}, u32[]{:S(2)}) %collective-permute-start.19) | collective-permute-done | bytes 49184 | tf_op jit(solution)/shard_map/ppermute | solution.py:24
  58.7 1.6 %collective-permute-start.21 = (bf16[3,32,768]{2,1,0:T(8,128)(2,1)S(1)}, bf16[3,32,768]{2,1,0:T(8,128)(2,1)S(1)}, u32[]{:S(2)}, u32[]{:S(2)}) collective-permute-start(bf16[3,32,768]{2,1,0:T(8,128)(2,1)S(1)} %stack.13.refs_5_.refs_1_), channel_id=1, source_target_pairs={{0,4},{4,0},{8,12},{12,8},{16,20},{20,16},{24,28},{28,24},{1,5},{5... | collective-permute-start | bytes 442376 | tf_op jit(solution)/shard_map/ppermute | solution.py:24
  61.4 3.1 %collective-permute-done.20.refs_4_.refs_2_ = bf16[32,768]{1,0:T(8,128)(2,1)S(1)} collective-permute-done((bf16[32,768]{1,0:T(8,128)(2,1)S(1)}, bf16[32,768]{1,0:T(8,128)(2,1)S(1)}, u32[]{:S(2)}, u32[]{:S(2)}) %collective-permute-start.20) | collective-permute-done | bytes 49184 | tf_op jit(solution)/shard_map/ppermute | solution.py:24
  65.1 1.0 %back_first.1.refs_10_ = f32[512,64]{1,0:T(8,128)S(1)} custom-call(s32[1]{0:T(128)} %bitcast.place_ref, s32[1]{0:T(128)} %bitcast.1.group_ref, s32[1]{0:T(128)} %bitcast.2.core_ref, bf16[16,6144]{1,0:T(8,128)(2,1)S(1)} %get-tuple-element.66.refs_0_, bf16[16,6144]{1,0:T(8,128)(2,1)S(1)} %collective-permute-done.7.refs_1_, ...), custom_call_target="tpu_custom_call" | custom-call | flops 201326592 | bytes 3145728 | tf_op jit(solution)/shard_map/back_first/pallas_call | solution.py:470
  66.1 2.0 %back_last.1 = (bf16[32,32,128]{2,1,0:T(8,128)(2,1)}, bf16[512,64]{1,0:T(8,128)(2,1)S(1)}) custom-call(s32[1]{0:T(128)} %bitcast.place_ref, s32[1]{0:T(128)} %bitcast.1.group_ref, s32[1]{0:T(128)} %bitcast.2.core_ref, bf16[16,6144]{1,0:T(8,128)(2,1)S(1)} %get-tuple-element.66.refs_0_, bf16[16,6144]{1,0:T(8,128)(2,1)S(1)} %collective-permute-done.7.refs_1_, ...), custom_call_target="tpu_custom_call" | custom-call | flops 201326592 | bytes 3145728 | tf_op jit(solution)/shard_map/back_last/pallas_call | solution.py:485
  68.1 3.2 %all-to-all-start.1 = ((bf16[32,32,128]{2,1,0:T(8,128)(2,1)}), bf16[32,32,128]{2,1,0:T(8,128)(2,1)S(1)}, u32[]{:S(2)}, u32[]{:S(2)}) async-start(bf16[32,32,128]{2,1,0:T(8,128)(2,1)} %get-tuple-element.93), calls=%async_computation.1 | async-start | bytes 524288 | tf_op jit(solution)/shard_map/all_to_all | solution.py:50
  72.4 1.8 %collective-permute-start.26 = (bf16[4,6144]{1,0:T(4,128)(2,1)S(1)}, bf16[4,6144]{1,0:T(4,128)(2,1)S(1)}, u32[]{:S(2)}, u32[]{:S(2)}) collective-permute-start(bf16[4,6144]{1,0:T(4,128)(2,1)S(1)} %convolution_convert_fusion), channel_id=1, source_target_pairs={{0,2},{2,0},{1,3},{3,1},{4,6},{6,4},{5,7},{7,5},{8,10},{10,8},{9,1... | collective-permute-start | bytes 147464 | tf_op jit(solution)/shard_map/ppermute | solution.py:652
  74.2 3.2 %collective-permute-done.26 = bf16[4,6144]{1,0:T(4,128)(2,1)S(1)} collective-permute-done((bf16[4,6144]{1,0:T(4,128)(2,1)S(1)}, bf16[4,6144]{1,0:T(4,128)(2,1)S(1)}, u32[]{:S(2)}, u32[]{:S(2)}) %collective-permute-start.26) | collective-permute-done | bytes 49184 | tf_op jit(solution)/shard_map/ppermute | solution.py:652
  78.3 3.7 %all-to-all-done.1 = bf16[32,32,128]{2,1,0:T(8,128)(2,1)S(1)} async-done(((bf16[32,32,128]{2,1,0:T(8,128)(2,1)}), bf16[32,32,128]{2,1,0:T(8,128)(2,1)S(1)}, u32[]{:S(2)}, u32[]{:S(2)}) %all-to-all-start.1) | async-done | bytes 262176 | tf_op jit(solution)/shard_map/all_to_all | solution.py:50
  (63 shorter events, 12.4 us)
Async XLA Ops:
  0.6 9.3 %collective-permute-start = (bf16[4,6144]{1,0:T(4,128)(2,1)}, bf16[4,6144]{1,0:T(4,128)(2,1)S(1)}, u32[]{:S(2)}, u32[]{:S(2)}) collective-permute-start(bf16[4,6144]{1,0:T(4,128)(2,1)} %refs_0_.1), channel_id=1, source_target_pairs={{0,8},{4,12},{8,0},{12,4},{16,24},{20,28},{24,16},{28,20},{1,9},{5... | collective-permute-start | bytes 147464 | tf_op jit(solution)/shard_map/ppermute | solution.py:24
  3.7 6.6 %collective-permute-start.1 = (bf16[4,6144]{1,0:T(4,128)(2,1)}, bf16[4,6144]{1,0:T(4,128)(2,1)S(1)}, u32[]{:S(2)}, u32[]{:S(2)}) collective-permute-start(bf16[4,6144]{1,0:T(4,128)(2,1)} %refs_0_.1), channel_id=1, source_target_pairs={{0,16},{4,20},{8,24},{12,28},{16,0},{20,4},{24,8},{28,12},{1,17},{... | collective-permute-start | bytes 147464 | tf_op jit(solution)/shard_map/ppermute | solution.py:24
  6.3 6.1 %collective-permute-start.2 = (bf16[4,6144]{1,0:T(4,128)(2,1)}, bf16[4,6144]{1,0:T(4,128)(2,1)S(1)}, u32[]{:S(2)}, u32[]{:S(2)}) collective-permute-start(bf16[4,6144]{1,0:T(4,128)(2,1)} %refs_0_.1), channel_id=1, source_target_pairs={{0,24},{4,28},{8,16},{12,20},{16,8},{20,12},{24,0},{28,4},{1,25},{... | collective-permute-start | bytes 147464 | tf_op jit(solution)/shard_map/ppermute | solution.py:24
  6.3 8.7 %collective-permute-start.3 = (bf16[4,6144]{1,0:T(4,128)(2,1)}, bf16[4,6144]{1,0:T(4,128)(2,1)S(1)}, u32[]{:S(2)}, u32[]{:S(2)}) collective-permute-start(bf16[4,6144]{1,0:T(4,128)(2,1)} %refs_0_.1), channel_id=1, source_target_pairs={{0,4},{4,0},{8,12},{12,8},{16,20},{20,16},{24,28},{28,24},{1,5},{5... | collective-permute-start | bytes 147464 | tf_op jit(solution)/shard_map/ppermute | solution.py:24
  9.9 5.1 %collective-permute-start.4 = (bf16[4,6144]{1,0:T(4,128)(2,1)S(1)}, bf16[4,6144]{1,0:T(4,128)(2,1)S(1)}, u32[]{:S(2)}, u32[]{:S(2)}) collective-permute-start(bf16[4,6144]{1,0:T(4,128)(2,1)S(1)} %collective-permute-done.refs_1_), channel_id=1, source_target_pairs={{0,4},{4,0},{8,12},{12,8},{16,20},{20,16},{24,28},{28,24},{1,5},{5... | collective-permute-start | bytes 147464 | tf_op jit(solution)/shard_map/ppermute | solution.py:24
  10.3 4.8 %collective-permute-start.5 = (bf16[4,6144]{1,0:T(4,128)(2,1)S(1)}, bf16[4,6144]{1,0:T(4,128)(2,1)S(1)}, u32[]{:S(2)}, u32[]{:S(2)}) collective-permute-start(bf16[4,6144]{1,0:T(4,128)(2,1)S(1)} %collective-permute-done.1.refs_2_), channel_id=1, source_target_pairs={{0,4},{4,0},{8,12},{12,8},{16,20},{20,16},{24,28},{28,24},{1,5},{5... | collective-permute-start | bytes 147464 | tf_op jit(solution)/shard_map/ppermute | solution.py:24
  12.4 4.1 %collective-permute-start.6 = (bf16[4,6144]{1,0:T(4,128)(2,1)S(1)}, bf16[4,6144]{1,0:T(4,128)(2,1)S(1)}, u32[]{:S(2)}, u32[]{:S(2)}) collective-permute-start(bf16[4,6144]{1,0:T(4,128)(2,1)S(1)} %collective-permute-done.2.refs_3_), channel_id=1, source_target_pairs={{0,4},{4,0},{8,12},{12,8},{16,20},{20,16},{24,28},{28,24},{1,5},{5... | collective-permute-start | bytes 147464 | tf_op jit(solution)/shard_map/ppermute | solution.py:24
  17.6 5.7 %collective-permute-start.7 = (bf16[16,6144]{1,0:T(8,128)(2,1)S(1)}, bf16[16,6144]{1,0:T(8,128)(2,1)S(1)}, u32[]{:S(2)}, u32[]{:S(2)}) collective-permute-start(bf16[16,6144]{1,0:T(8,128)(2,1)S(1)} %get-tuple-element.67.refs_1_), channel_id=1, source_target_pairs={{0,2},{2,0},{1,3},{3,1},{4,6},{6,4},{5,7},{7,5},{8,10},{10,8},{9,1... | collective-permute-start | bytes 589832 | tf_op jit(solution)/shard_map/ppermute | solution.py:583
  19.1 4.2 %collective-permute-start.8 = (bf16[16,6144]{1,0:T(8,128)(2,1)S(1)}, bf16[16,6144]{1,0:T(8,128)(2,1)S(1)}, u32[]{:S(2)}, u32[]{:S(2)}) collective-permute-start(bf16[16,6144]{1,0:T(8,128)(2,1)S(1)} %get-tuple-element.66.refs_0_), channel_id=1, source_target_pairs={{0,1},{1,0},{2,3},{3,2},{4,5},{5,4},{6,7},{7,6},{8,9},{9,8},{10,11... | collective-permute-start | bytes 589832 | tf_op jit(solution)/shard_map/ppermute | solution.py:19
  19.2 11.1 %all-to-all-start = ((bf16[32,8,128]{2,1,0:T(8,128)(2,1)}), bf16[32,8,128]{2,1,0:T(8,128)(2,1)S(1)}, u32[]{:S(2)}, u32[]{:S(2)}) async-start(bf16[32,8,128]{2,1,0:T(8,128)(2,1)} %low_pieces.1), calls=%async_computation | async-start | bytes 131072 | tf_op jit(solution)/shard_map/all_to_all | solution.py:50
  23.3 1.4 %collective-permute-start.9 = (bf16[16,6144]{1,0:T(8,128)(2,1)S(1)}, bf16[16,6144]{1,0:T(8,128)(2,1)S(1)}, u32[]{:S(2)}, u32[]{:S(2)}) collective-permute-start(bf16[16,6144]{1,0:T(8,128)(2,1)S(1)} %collective-permute-done.7.refs_1_), channel_id=1, source_target_pairs={{0,1},{1,0},{2,3},{3,2},{4,5},{5,4},{6,7},{7,6},{8,9},{9,8},{10,11... | collective-permute-start | bytes 589832 | tf_op jit(solution)/shard_map/ppermute | solution.py:19
  23.4 7.0 %copy-start = (bf16[64,512]{1,0:T(8,128)(2,1)S(1)}, bf16[64,512]{1,0:T(8,128)(2,1)}, u32[]{:S(2)}) copy-start(bf16[64,512]{1,0:T(8,128)(2,1)} %refs_12_.1) | copy-start | bytes 196612
  33.7 1.8 %collective-permute-start.10 = (bf16[8,32,768]{2,1,0:T(8,128)(2,1)S(1)}, bf16[8,32,768]{2,1,0:T(8,128)(2,1)S(1)}, u32[]{:S(2)}, u32[]{:S(2)}) collective-permute-start(bf16[8,32,768]{2,1,0:T(8,128)(2,1)S(1)} %get-tuple-element.75), channel_id=1, source_target_pairs={{0,1},{1,0},{2,3},{3,2},{4,5},{5,4},{6,7},{7,6},{8,9},{9,8},{10,11... | collective-permute-start | bytes 1179656 | tf_op jit(solution)/shard_map/ppermute | solution.py:19
  34.0 4.0 %collective-permute-start.12 = (bf16[64,196]{1,0:T(8,128)(2,1)S(1)}, bf16[64,196]{1,0:T(8,128)(2,1)S(1)}, u32[]{:S(2)}, u32[]{:S(2)}) collective-permute-start(bf16[64,196]{1,0:T(8,128)(2,1)S(1)} %get-tuple-element.102), channel_id=1, source_target_pairs={{0,2},{2,0},{1,3},{3,1},{4,6},{6,4},{5,7},{7,5},{8,10},{10,8},{9,1... | collective-permute-start | bytes 75272 | tf_op jit(solution)/shard_map/ppermute | solution.py:601
  35.6 4.9 %collective-permute-start.11 = (bf16[2,32,768]{2,1,0:T(8,128)(2,1)S(1)}, bf16[2,32,768]{2,1,0:T(8,128)(2,1)S(1)}, u32[]{:S(2)}, u32[]{:S(2)}) collective-permute-start(bf16[2,32,768]{2,1,0:T(8,128)(2,1)S(1)} %get-tuple-element.76), channel_id=1, source_target_pairs={{0,4},{4,0},{8,12},{12,8},{16,20},{20,16},{24,28},{28,24},{1,5},{5... | collective-permute-start | bytes 294920 | tf_op jit(solution)/shard_map/ppermute | solution.py:24
  40.5 5.0 %collective-permute-start.13 = (bf16[2,32,768]{2,1,0:T(8,128)(2,1)S(1)}, bf16[2,32,768]{2,1,0:T(8,128)(2,1)S(1)}, u32[]{:S(2)}, u32[]{:S(2)}) collective-permute-start(bf16[2,32,768]{2,1,0:T(8,128)(2,1)S(1)} %get-tuple-element.80), channel_id=1, source_target_pairs={{0,4},{4,0},{8,12},{12,8},{16,20},{20,16},{24,28},{28,24},{1,5},{5... | collective-permute-start | bytes 294920 | tf_op jit(solution)/shard_map/ppermute | solution.py:24
  41.6 6.6 %collective-permute-start.15 = (bf16[32,768]{1,0:T(8,128)(2,1)S(1)}, bf16[32,768]{1,0:T(8,128)(2,1)S(1)}, u32[]{:S(2)}, u32[]{:S(2)}) collective-permute-start(bf16[32,768]{1,0:T(8,128)(2,1)S(1)} %get-tuple-element.84), channel_id=1, source_target_pairs={{0,16},{4,20},{8,24},{12,28},{16,0},{20,4},{24,8},{28,12},{1,17},{... | collective-permute-start | bytes 147464 | tf_op jit(solution)/shard_map/ppermute | solution.py:24
  44.0 6.0 %collective-permute-start.16 = (bf16[32,768]{1,0:T(8,128)(2,1)S(1)}, bf16[32,768]{1,0:T(8,128)(2,1)S(1)}, u32[]{:S(2)}, u32[]{:S(2)}) collective-permute-start(bf16[32,768]{1,0:T(8,128)(2,1)S(1)} %get-tuple-element.85), channel_id=1, source_target_pairs={{0,24},{4,28},{8,16},{12,20},{16,8},{20,12},{24,0},{28,4},{1,25},{... | collective-permute-start | bytes 147464 | tf_op jit(solution)/shard_map/ppermute | solution.py:24
  45.5 4.7 %collective-permute-start.14 = (bf16[32,768]{1,0:T(8,128)(2,1)S(1)}, bf16[32,768]{1,0:T(8,128)(2,1)S(1)}, u32[]{:S(2)}, u32[]{:S(2)}) collective-permute-start(bf16[32,768]{1,0:T(8,128)(2,1)S(1)} %get-tuple-element.82), channel_id=1, source_target_pairs={{0,8},{4,12},{8,0},{12,4},{16,24},{20,28},{24,16},{28,20},{1,9},{5... | collective-permute-start | bytes 147464 | tf_op jit(solution)/shard_map/ppermute | solution.py:24
  50.2 4.4 %collective-permute-start.17 = (bf16[32,768]{1,0:T(8,128)(2,1)S(1)}, bf16[32,768]{1,0:T(8,128)(2,1)S(1)}, u32[]{:S(2)}, u32[]{:S(2)}) collective-permute-start(bf16[32,768]{1,0:T(8,128)(2,1)S(1)} %mix.1.refs_4_.refs_0_), channel_id=1, source_target_pairs={{0,8},{4,12},{8,0},{12,4},{16,24},{20,28},{24,16},{28,20},{1,9},{5... | collective-permute-start | bytes 147464 | tf_op jit(solution)/shard_map/ppermute | solution.py:24
  50.4 5.2 %collective-permute-start.18 = (bf16[32,768]{1,0:T(8,128)(2,1)S(1)}, bf16[32,768]{1,0:T(8,128)(2,1)S(1)}, u32[]{:S(2)}, u32[]{:S(2)}) collective-permute-start(bf16[32,768]{1,0:T(8,128)(2,1)S(1)} %mix.1.refs_4_.refs_0_), channel_id=1, source_target_pairs={{0,16},{4,20},{8,24},{12,28},{16,0},{20,4},{24,8},{28,12},{1,17},{... | collective-permute-start | bytes 147464 | tf_op jit(solution)/shard_map/ppermute | solution.py:24
  52.8 5.9 %collective-permute-start.19 = (bf16[32,768]{1,0:T(8,128)(2,1)S(1)}, bf16[32,768]{1,0:T(8,128)(2,1)S(1)}, u32[]{:S(2)}, u32[]{:S(2)}) collective-permute-start(bf16[32,768]{1,0:T(8,128)(2,1)S(1)} %mix.1.refs_4_.refs_0_), channel_id=1, source_target_pairs={{0,24},{4,28},{8,16},{12,20},{16,8},{20,12},{24,0},{28,4},{1,25},{... | collective-permute-start | bytes 147464 | tf_op jit(solution)/shard_map/ppermute | solution.py:24
  58.7 5.7 %collective-permute-start.21 = (bf16[3,32,768]{2,1,0:T(8,128)(2,1)S(1)}, bf16[3,32,768]{2,1,0:T(8,128)(2,1)S(1)}, u32[]{:S(2)}, u32[]{:S(2)}) collective-permute-start(bf16[3,32,768]{2,1,0:T(8,128)(2,1)S(1)} %stack.13.refs_5_.refs_1_), channel_id=1, source_target_pairs={{0,4},{4,0},{8,12},{12,8},{16,20},{20,16},{24,28},{28,24},{1,5},{5... | collective-permute-start | bytes 442376 | tf_op jit(solution)/shard_map/ppermute | solution.py:24
  60.3 4.2 %collective-permute-start.20 = (bf16[32,768]{1,0:T(8,128)(2,1)S(1)}, bf16[32,768]{1,0:T(8,128)(2,1)S(1)}, u32[]{:S(2)}, u32[]{:S(2)}) collective-permute-start(bf16[32,768]{1,0:T(8,128)(2,1)S(1)} %mix.1.refs_4_.refs_0_), channel_id=1, source_target_pairs={{0,4},{4,0},{8,12},{12,8},{16,20},{20,16},{24,28},{28,24},{1,5},{5... | collective-permute-start | bytes 147464 | tf_op jit(solution)/shard_map/ppermute | solution.py:24
  60.9 4.2 %collective-permute-start.24 = (bf16[32,768]{1,0:T(8,128)(2,1)S(1)}, bf16[32,768]{1,0:T(8,128)(2,1)S(1)}, u32[]{:S(2)}, u32[]{:S(2)}) collective-permute-start(bf16[32,768]{1,0:T(8,128)(2,1)S(1)} %mix.1.refs_4_.refs_0_), channel_id=1, source_target_pairs={{0,1},{1,0},{2,3},{3,2},{4,5},{5,4},{6,7},{7,6},{8,9},{9,8},{10,11... | collective-permute-start | bytes 147464 | tf_op jit(solution)/shard_map/ppermute | solution.py:19
  60.9 4.2 %collective-permute-start.25 = (bf16[3,32,768]{2,1,0:T(8,128)(2,1)S(1)}, bf16[3,32,768]{2,1,0:T(8,128)(2,1)S(1)}, u32[]{:S(2)}, u32[]{:S(2)}) collective-permute-start(bf16[3,32,768]{2,1,0:T(8,128)(2,1)S(1)} %stack.13.refs_5_.refs_1_), channel_id=1, source_target_pairs={{0,1},{1,0},{2,3},{3,2},{4,5},{5,4},{6,7},{7,6},{8,9},{9,8},{10,11... | collective-permute-start | bytes 442376 | tf_op jit(solution)/shard_map/ppermute | solution.py:19
  64.5 1.6 %collective-permute-start.22 = (bf16[32,768]{1,0:T(8,128)(2,1)S(1)}, bf16[32,768]{1,0:T(8,128)(2,1)S(1)}, u32[]{:S(2)}, u32[]{:S(2)}) collective-permute-start(bf16[32,768]{1,0:T(8,128)(2,1)S(1)} %collective-permute-done.20.refs_4_.refs_2_), channel_id=1, source_target_pairs={{0,1},{1,0},{2,3},{3,2},{4,5},{5,4},{6,7},{7,6},{8,9},{9,8},{10,11... | collective-permute-start | bytes 147464 | tf_op jit(solution)/shard_map/ppermute | solution.py:19
  64.5 1.6 %collective-permute-start.23 = (bf16[3,32,768]{2,1,0:T(8,128)(2,1)S(1)}, bf16[3,32,768]{2,1,0:T(8,128)(2,1)S(1)}, u32[]{:S(2)}, u32[]{:S(2)}) collective-permute-start(bf16[3,32,768]{2,1,0:T(8,128)(2,1)S(1)} %collective-permute-done.21.refs_5_.refs_3_), channel_id=1, source_target_pairs={{0,1},{1,0},{2,3},{3,2},{4,5},{5,4},{6,7},{7,6},{8,9},{9,8},{10,11... | collective-permute-start | bytes 442376 | tf_op jit(solution)/shard_map/ppermute | solution.py:19
  68.1 13.8 %all-to-all-start.1 = ((bf16[32,32,128]{2,1,0:T(8,128)(2,1)}), bf16[32,32,128]{2,1,0:T(8,128)(2,1)S(1)}, u32[]{:S(2)}, u32[]{:S(2)}) async-start(bf16[32,32,128]{2,1,0:T(8,128)(2,1)} %get-tuple-element.93), calls=%async_computation.1 | async-start | bytes 524288 | tf_op jit(solution)/shard_map/all_to_all | solution.py:50
  72.4 5.0 %collective-permute-start.26 = (bf16[4,6144]{1,0:T(4,128)(2,1)S(1)}, bf16[4,6144]{1,0:T(4,128)(2,1)S(1)}, u32[]{:S(2)}, u32[]{:S(2)}) collective-permute-start(bf16[4,6144]{1,0:T(4,128)(2,1)S(1)} %convolution_convert_fusion), channel_id=1, source_target_pairs={{0,2},{2,0},{1,3},{3,1},{4,6},{6,4},{5,7},{7,5},{8,10},{10,8},{9,1... | collective-permute-start | bytes 147464 | tf_op jit(solution)/shard_map/ppermute | solution.py:652

commit v9 on v8

--- a/solution.py
+++ b/solution.py
@@ -237,7 +237,7 @@
         scratch_shapes=[
             pltpu.VMEM(gate_weight.shape, bf16),
             pltpu.VMEM(up_weight.shape, bf16),
-            pltpu.SemaphoreType.DMA((2, 12)),
+            pltpu.SemaphoreType.DMA((2, 8)),
         ],
         out_shape=(
             struct((count, units), f32),

time: 83.2 us -> 83.2 us (level)
  no operation moved by 1% of the time
where the time goes in v9:
time: 83.2 us; the launch traced here: 83 us
  starting transfers between devices  37.2 us (45%)
  waiting for transfers between devices  25.9 us (31%)
  Pallas kernels  15.7 us (19%)
  other arithmetic  1.88 us (2%)
  matrix products  1.06 us (1%)
  between operations  0.85 us (1%)
    ppermute x17, starting transfers between devices, across(): return lax.ppermute(block, axis, [(i, i ^ apart_by) for i in range(count)])  24.5 us
    ppermute x17, waiting for transfers between devices, across(): return lax.ppermute(block, axis, [(i, i ^ apart_by) for i in range(count)])  15.4 us
    all_to_all x2, starting transfers between devices, exchange(): return lax.all_to_all(blocks, axis, 0, 0, tiled=True)  6.9 us
    pallas_call x1, Pallas kernels, lift(): pl.pallas_call(functools.partial(lift_kernel, len(parts)), in_specs=vmem(...  5.11 us
    all_to_all x2, waiting for transfers between devices, exchange(): return lax.all_to_all(blocks, axis, 0, 0, tiled=True)  4.14 us
    pallas_call x1, Pallas kernels, down(): pl.pallas_call(seated(down_kernel), in_specs=[pl.BlockSpec(memory_space=p...  3.35 us
    ppermute x1, waiting for transfers between devices, shards(): chosen = lax.ppermute(chosen.astype(bf16), 'x', route).astype(f32)  3.18 us
    pallas_call x1, Pallas kernels, back_last(): pl.pallas_call(seated(functools.partial(back_last_kernel, len(parts), blo...  1.99 us
  transfers between devices with their start and end apart: 29, of which 16 were waited for; matrix products, arithmetic and copies ran while one was open for 4% of the time, Pallas kernels for 10%

profile of v9, /device:TPU:0, one launch (start us, length us, event | category | flops | bytes accessed | tf_op | source)
XLA Modules:
  0.0 83.0 jit_solution(5053995130595446110)
XLA Ops:
  0.6 3.1 %collective-permute-start = (bf16[4,6144]{1,0:T(4,128)(2,1)}, bf16[4,6144]{1,0:T(4,128)(2,1)S(1)}, u32[]{:S(2)}, u32[]{:S(2)}) collective-permute-start(bf16[4,6144]{1,0:T(4,128)(2,1)} %refs_0_.1), channel_id=1, source_target_pairs={{0,8},{4,12},{8,0},{12,4},{16,24},{20,28},{24,16},{28,20},{1,9},{5... | collective-permute-start | bytes 147464 | tf_op jit(solution)/shard_map/ppermute | solution.py:24
  3.7 2.6 %collective-permute-start.1 = (bf16[4,6144]{1,0:T(4,128)(2,1)}, bf16[4,6144]{1,0:T(4,128)(2,1)S(1)}, u32[]{:S(2)}, u32[]{:S(2)}) collective-permute-start(bf16[4,6144]{1,0:T(4,128)(2,1)} %refs_0_.1), channel_id=1, source_target_pairs={{0,16},{4,20},{8,24},{12,28},{16,0},{20,4},{24,8},{28,12},{1,17},{... | collective-permute-start | bytes 147464 | tf_op jit(solution)/shard_map/ppermute | solution.py:24
  6.3 1.7 %collective-permute-start.3 = (bf16[4,6144]{1,0:T(4,128)(2,1)}, bf16[4,6144]{1,0:T(4,128)(2,1)S(1)}, u32[]{:S(2)}, u32[]{:S(2)}) collective-permute-start(bf16[4,6144]{1,0:T(4,128)(2,1)} %refs_0_.1), channel_id=1, source_target_pairs={{0,4},{4,0},{8,12},{12,8},{16,20},{20,16},{24,28},{28,24},{1,5},{5... | collective-permute-start | bytes 147464 | tf_op jit(solution)/shard_map/ppermute | solution.py:24
  10.3 1.7 %collective-permute-start.5 = (bf16[4,6144]{1,0:T(4,128)(2,1)S(1)}, bf16[4,6144]{1,0:T(4,128)(2,1)S(1)}, u32[]{:S(2)}, u32[]{:S(2)}) collective-permute-start(bf16[4,6144]{1,0:T(4,128)(2,1)S(1)} %collective-permute-done.1.refs_2_), channel_id=1, source_target_pairs={{0,4},{4,0},{8,12},{12,8},{16,20},{20,16},{24,28},{28,24},{1,5},{5... | collective-permute-start | bytes 147464 | tf_op jit(solution)/shard_map/ppermute | solution.py:24
  12.4 1.5 %collective-permute-start.6 = (bf16[4,6144]{1,0:T(4,128)(2,1)S(1)}, bf16[4,6144]{1,0:T(4,128)(2,1)S(1)}, u32[]{:S(2)}, u32[]{:S(2)}) collective-permute-start(bf16[4,6144]{1,0:T(4,128)(2,1)S(1)} %collective-permute-done.2.refs_3_), channel_id=1, source_target_pairs={{0,4},{4,0},{8,12},{12,8},{16,20},{20,16},{24,28},{28,24},{1,5},{5... | collective-permute-start | bytes 147464 | tf_op jit(solution)/shard_map/ppermute | solution.py:24
  14.0 1.0 %near.1 = (bf16[4,6144]{1,0:T(4,128)(2,1)S(1)}, bf16[64,768]{1,0:T(8,128)(2,1)S(1)}, f32[1,6144]{1,0:T(1,128)S(1)}) custom-call(s32[1]{0:T(128)} %bitcast.place_ref, s32[1]{0:T(128)} %bitcast.1.group_ref, s32[1]{0:T(128)} %bitcast.2.core_ref, bf16[4,6144]{1,0:T(4,128)(2,1)} %refs_0_.1, bf16[64,768]{1,0:T(8,128)(2,1)} %bitcast.25, bf16[2,6144]{1,0:T(2,128)(2,1)} %bitcast.28), custom_call_target="tpu_custom_call" | custom-call | tf_op jit(solution)/shard_map/near/pallas_call | solution.py:122
  15.1 1.4 %collective-permute-done.6.refs_7_ = bf16[4,6144]{1,0:T(4,128)(2,1)S(1)} collective-permute-done((bf16[4,6144]{1,0:T(4,128)(2,1)S(1)}, bf16[4,6144]{1,0:T(4,128)(2,1)S(1)}, u32[]{:S(2)}, u32[]{:S(2)}) %collective-permute-start.6) | collective-permute-done | bytes 49184 | tf_op jit(solution)/shard_map/ppermute | solution.py:24
  17.6 1.5 %collective-permute-start.7 = (bf16[16,6144]{1,0:T(8,128)(2,1)S(1)}, bf16[16,6144]{1,0:T(8,128)(2,1)S(1)}, u32[]{:S(2)}, u32[]{:S(2)}) collective-permute-start(bf16[16,6144]{1,0:T(8,128)(2,1)S(1)} %get-tuple-element.67.refs_1_), channel_id=1, source_target_pairs={{0,2},{2,0},{1,3},{3,1},{4,6},{6,4},{5,7},{7,5},{8,10},{10,8},{9,1... | collective-permute-start | bytes 589832 | tf_op jit(solution)/shard_map/ppermute | solution.py:583
  19.2 3.7 %all-to-all-start = ((bf16[32,8,128]{2,1,0:T(8,128)(2,1)}), bf16[32,8,128]{2,1,0:T(8,128)(2,1)S(1)}, u32[]{:S(2)}, u32[]{:S(2)}) async-start(bf16[32,8,128]{2,1,0:T(8,128)(2,1)} %low_pieces.1), calls=%async_computation | async-start | bytes 131072 | tf_op jit(solution)/shard_map/all_to_all | solution.py:50
  23.4 1.4 %collective-permute-done.9.refs_3_ = bf16[16,6144]{1,0:T(8,128)(2,1)S(1)} collective-permute-done((bf16[16,6144]{1,0:T(8,128)(2,1)S(1)}, bf16[16,6144]{1,0:T(8,128)(2,1)S(1)}, u32[]{:S(2)}, u32[]{:S(2)}) %collective-permute-start.9) | collective-permute-done | bytes 196640 | tf_op jit(solution)/shard_map/ppermute | solution.py:19
  24.7 5.1 %lift.1 = (f32[64,512]{1,0:T(8,128)S(1)}, f32[64,512]{1,0:T(8,128)S(1)}, f32[64,1]{1,0:T(8,128)S(1)}) custom-call(bf16[16,6144]{1,0:T(8,128)(2,1)S(1)} %get-tuple-element.66.refs_0_, bf16[16,6144]{1,0:T(8,128)(2,1)S(1)} %collective-permute-done.7.refs_1_, bf16[16,6144]{1,0:T(8,128)(2,1)S(1)} %collective-permute-done.8.refs_2_, ...), custom_call_target="tpu_custom_call" | custom-call | flops 805306368 | bytes 12582912 | tf_op jit(solution)/shard_map/lift/pallas_call | solution.py:231
  30.3 3.4 %down.1 = (bf16[8,32,768]{2,1,0:T(8,128)(2,1)S(1)}, bf16[8,32,768]{2,1,0:T(8,128)(2,1)S(1)}, f32[512,64]{1,0:T(8,128)S(1)}, bf16[64,64]{1,0:T(8,128)(2,1)S(1)}, bf16[8,512,768]{2,1,0:T(8,128)(2,1)S(1)}) custom-call(s32[1]{0:T(128)} %bitcast.place_ref, s32[1]{0:T(128)} %bitcast.1.group_ref, s32[1]{0:T(128)} %bitcast.2.core_ref, ...), custom_call_target="tpu_custom_call" | custom-call | flops 402653184 | bytes 6291456 | tf_op jit(solution)/shard_map/down/pallas_call | solution.py:299
  34.0 1.2 %collective-permute-start.12 = (bf16[64,196]{1,0:T(8,128)(2,1)S(1)}, bf16[64,196]{1,0:T(8,128)(2,1)S(1)}, u32[]{:S(2)}, u32[]{:S(2)}) collective-permute-start(bf16[64,196]{1,0:T(8,128)(2,1)S(1)} %get-tuple-element.102), channel_id=1, source_target_pairs={{0,2},{2,0},{1,3},{3,1},{4,6},{6,4},{5,7},{7,5},{8,10},{10,8},{9,1... | collective-permute-start | bytes 75272 | tf_op jit(solution)/shard_map/ppermute | solution.py:601
  35.6 1.3 %collective-permute-start.11 = (bf16[2,32,768]{2,1,0:T(8,128)(2,1)S(1)}, bf16[2,32,768]{2,1,0:T(8,128)(2,1)S(1)}, u32[]{:S(2)}, u32[]{:S(2)}) collective-permute-start(bf16[2,32,768]{2,1,0:T(8,128)(2,1)S(1)} %get-tuple-element.76), channel_id=1, source_target_pairs={{0,4},{4,0},{8,12},{12,8},{16,20},{20,16},{24,28},{28,24},{1,5},{5... | collective-permute-start | bytes 294920 | tf_op jit(solution)/shard_map/ppermute | solution.py:24
  36.9 1.1 %collective-permute-done.12 = bf16[64,196]{1,0:T(8,128)(2,1)S(1)} collective-permute-done((bf16[64,196]{1,0:T(8,128)(2,1)S(1)}, bf16[64,196]{1,0:T(8,128)(2,1)S(1)}, u32[]{:S(2)}, u32[]{:S(2)}) %collective-permute-start.12) | collective-permute-done | bytes 25120 | tf_op jit(solution)/shard_map/ppermute | solution.py:601
  38.0 2.5 %collective-permute-done.11.got_ref = bf16[2,32,768]{2,1,0:T(8,128)(2,1)S(1)} collective-permute-done((bf16[2,32,768]{2,1,0:T(8,128)(2,1)S(1)}, bf16[2,32,768]{2,1,0:T(8,128)(2,1)S(1)}, u32[]{:S(2)}, u32[]{:S(2)}) %collective-permute-start.11) | collective-permute-done | bytes 98336 | tf_op jit(solution)/shard_map/ppermute | solution.py:24
  40.5 1.2 %collective-permute-start.13 = (bf16[2,32,768]{2,1,0:T(8,128)(2,1)S(1)}, bf16[2,32,768]{2,1,0:T(8,128)(2,1)S(1)}, u32[]{:S(2)}, u32[]{:S(2)}) collective-permute-start(bf16[2,32,768]{2,1,0:T(8,128)(2,1)S(1)} %get-tuple-element.80), channel_id=1, source_target_pairs={{0,4},{4,0},{8,12},{12,8},{16,20},{20,16},{24,28},{28,24},{1,5},{5... | collective-permute-start | bytes 294920 | tf_op jit(solution)/shard_map/ppermute | solution.py:24
  41.7 2.4 %collective-permute-start.15 = (bf16[32,768]{1,0:T(8,128)(2,1)S(1)}, bf16[32,768]{1,0:T(8,128)(2,1)S(1)}, u32[]{:S(2)}, u32[]{:S(2)}) collective-permute-start(bf16[32,768]{1,0:T(8,128)(2,1)S(1)} %get-tuple-element.84), channel_id=1, source_target_pairs={{0,16},{4,20},{8,24},{12,28},{16,0},{20,4},{24,8},{28,12},{1,17},{... | collective-permute-start | bytes 147464 | tf_op jit(solution)/shard_map/ppermute | solution.py:24
  44.0 1.4 %collective-permute-start.16 = (bf16[32,768]{1,0:T(8,128)(2,1)S(1)}, bf16[32,768]{1,0:T(8,128)(2,1)S(1)}, u32[]{:S(2)}, u32[]{:S(2)}) collective-permute-start(bf16[32,768]{1,0:T(8,128)(2,1)S(1)} %get-tuple-element.85), channel_id=1, source_target_pairs={{0,24},{4,28},{8,16},{12,20},{16,8},{20,12},{24,0},{28,4},{1,25},{... | collective-permute-start | bytes 147464 | tf_op jit(solution)/shard_map/ppermute | solution.py:24
  46.2 2.0 %collective-permute-done.15.refs_2_ = bf16[32,768]{1,0:T(8,128)(2,1)S(1)} collective-permute-done((bf16[32,768]{1,0:T(8,128)(2,1)S(1)}, bf16[32,768]{1,0:T(8,128)(2,1)S(1)}, u32[]{:S(2)}, u32[]{:S(2)}) %collective-permute-start.15) | collective-permute-done | bytes 49184 | tf_op jit(solution)/shard_map/ppermute | solution.py:24
  48.2 1.8 %collective-permute-done.16.refs_3_ = bf16[32,768]{1,0:T(8,128)(2,1)S(1)} collective-permute-done((bf16[32,768]{1,0:T(8,128)(2,1)S(1)}, bf16[32,768]{1,0:T(8,128)(2,1)S(1)}, u32[]{:S(2)}, u32[]{:S(2)}) %collective-permute-start.16) | collective-permute-done | bytes 49184 | tf_op jit(solution)/shard_map/ppermute | solution.py:24
  50.4 2.4 %collective-permute-start.18 = (bf16[32,768]{1,0:T(8,128)(2,1)S(1)}, bf16[32,768]{1,0:T(8,128)(2,1)S(1)}, u32[]{:S(2)}, u32[]{:S(2)}) collective-permute-start(bf16[32,768]{1,0:T(8,128)(2,1)S(1)} %mix.1.refs_4_.refs_0_), channel_id=1, source_target_pairs={{0,16},{4,20},{8,24},{12,28},{16,0},{20,4},{24,8},{28,12},{1,17},{... | collective-permute-start | bytes 147464 | tf_op jit(solution)/shard_map/ppermute | solution.py:24
  52.9 1.8 %collective-permute-start.19 = (bf16[32,768]{1,0:T(8,128)(2,1)S(1)}, bf16[32,768]{1,0:T(8,128)(2,1)S(1)}, u32[]{:S(2)}, u32[]{:S(2)}) collective-permute-start(bf16[32,768]{1,0:T(8,128)(2,1)S(1)} %mix.1.refs_4_.refs_0_), channel_id=1, source_target_pairs={{0,24},{4,28},{8,16},{12,20},{16,8},{20,12},{24,0},{28,4},{1,25},{... | collective-permute-start | bytes 147464 | tf_op jit(solution)/shard_map/ppermute | solution.py:24
  55.7 3.1 %collective-permute-done.19.refs_2_ = bf16[32,768]{1,0:T(8,128)(2,1)S(1)} collective-permute-done((bf16[32,768]{1,0:T(8,128)(2,1)S(1)}, bf16[32,768]{1,0:T(8,128)(2,1)S(1)}, u32[]{:S(2)}, u32[]{:S(2)}) %collective-permute-start.19) | collective-permute-done | bytes 49184 | tf_op jit(solution)/shard_map/ppermute | solution.py:24
  58.8 1.6 %collective-permute-start.21 = (bf16[3,32,768]{2,1,0:T(8,128)(2,1)S(1)}, bf16[3,32,768]{2,1,0:T(8,128)(2,1)S(1)}, u32[]{:S(2)}, u32[]{:S(2)}) collective-permute-start(bf16[3,32,768]{2,1,0:T(8,128)(2,1)S(1)} %stack.13.refs_5_.refs_1_), channel_id=1, source_target_pairs={{0,4},{4,0},{8,12},{12,8},{16,20},{20,16},{24,28},{28,24},{1,5},{5... | collective-permute-start | bytes 442376 | tf_op jit(solution)/shard_map/ppermute | solution.py:24
  61.5 3.1 %collective-permute-done.20.refs_4_.refs_2_ = bf16[32,768]{1,0:T(8,128)(2,1)S(1)} collective-permute-done((bf16[32,768]{1,0:T(8,128)(2,1)S(1)}, bf16[32,768]{1,0:T(8,128)(2,1)S(1)}, u32[]{:S(2)}, u32[]{:S(2)}) %collective-permute-start.20) | collective-permute-done | bytes 49184 | tf_op jit(solution)/shard_map/ppermute | solution.py:24
  65.1 1.0 %back_first.1.refs_10_ = f32[512,64]{1,0:T(8,128)S(1)} custom-call(s32[1]{0:T(128)} %bitcast.place_ref, s32[1]{0:T(128)} %bitcast.1.group_ref, s32[1]{0:T(128)} %bitcast.2.core_ref, bf16[16,6144]{1,0:T(8,128)(2,1)S(1)} %get-tuple-element.66.refs_0_, bf16[16,6144]{1,0:T(8,128)(2,1)S(1)} %collective-permute-done.7.refs_1_, ...), custom_call_target="tpu_custom_call" | custom-call | flops 201326592 | bytes 3145728 | tf_op jit(solution)/shard_map/back_first/pallas_call | solution.py:470
  66.2 2.0 %back_last.1 = (bf16[32,32,128]{2,1,0:T(8,128)(2,1)}, bf16[512,64]{1,0:T(8,128)(2,1)S(1)}) custom-call(s32[1]{0:T(128)} %bitcast.place_ref, s32[1]{0:T(128)} %bitcast.1.group_ref, s32[1]{0:T(128)} %bitcast.2.core_ref, bf16[16,6144]{1,0:T(8,128)(2,1)S(1)} %get-tuple-element.66.refs_0_, bf16[16,6144]{1,0:T(8,128)(2,1)S(1)} %collective-permute-done.7.refs_1_, ...), custom_call_target="tpu_custom_call" | custom-call | flops 201326592 | bytes 3145728 | tf_op jit(solution)/shard_map/back_last/pallas_call | solution.py:485
  68.2 3.2 %all-to-all-start.1 = ((bf16[32,32,128]{2,1,0:T(8,128)(2,1)}), bf16[32,32,128]{2,1,0:T(8,128)(2,1)S(1)}, u32[]{:S(2)}, u32[]{:S(2)}) async-start(bf16[32,32,128]{2,1,0:T(8,128)(2,1)} %get-tuple-element.93), calls=%async_computation.1 | async-start | bytes 524288 | tf_op jit(solution)/shard_map/all_to_all | solution.py:50
  72.5 1.8 %collective-permute-start.26 = (bf16[4,6144]{1,0:T(4,128)(2,1)S(1)}, bf16[4,6144]{1,0:T(4,128)(2,1)S(1)}, u32[]{:S(2)}, u32[]{:S(2)}) collective-permute-start(bf16[4,6144]{1,0:T(4,128)(2,1)S(1)} %convolution_convert_fusion), channel_id=1, source_target_pairs={{0,2},{2,0},{1,3},{3,1},{4,6},{6,4},{5,7},{7,5},{8,10},{10,8},{9,1... | collective-permute-start | bytes 147464 | tf_op jit(solution)/shard_map/ppermute | solution.py:652
  74.3 3.2 %collective-permute-done.26 = bf16[4,6144]{1,0:T(4,128)(2,1)S(1)} collective-permute-done((bf16[4,6144]{1,0:T(4,128)(2,1)S(1)}, bf16[4,6144]{1,0:T(4,128)(2,1)S(1)}, u32[]{:S(2)}, u32[]{:S(2)}) %collective-permute-start.26) | collective-permute-done | bytes 49184 | tf_op jit(solution)/shard_map/ppermute | solution.py:652
  78.3 3.7 %all-to-all-done.1 = bf16[32,32,128]{2,1,0:T(8,128)(2,1)S(1)} async-done(((bf16[32,32,128]{2,1,0:T(8,128)(2,1)}), bf16[32,32,128]{2,1,0:T(8,128)(2,1)S(1)}, u32[]{:S(2)}, u32[]{:S(2)}) %all-to-all-start.1) | async-done | bytes 262176 | tf_op jit(solution)/shard_map/all_to_all | solution.py:50
  (63 shorter events, 12.3 us)
Async XLA Ops:
  0.6 9.3 %collective-permute-start = (bf16[4,6144]{1,0:T(4,128)(2,1)}, bf16[4,6144]{1,0:T(4,128)(2,1)S(1)}, u32[]{:S(2)}, u32[]{:S(2)}) collective-permute-start(bf16[4,6144]{1,0:T(4,128)(2,1)} %refs_0_.1), channel_id=1, source_target_pairs={{0,8},{4,12},{8,0},{12,4},{16,24},{20,28},{24,16},{28,20},{1,9},{5... | collective-permute-start | bytes 147464 | tf_op jit(solution)/shard_map/ppermute | solution.py:24
  3.7 6.6 %collective-permute-start.1 = (bf16[4,6144]{1,0:T(4,128)(2,1)}, bf16[4,6144]{1,0:T(4,128)(2,1)S(1)}, u32[]{:S(2)}, u32[]{:S(2)}) collective-permute-start(bf16[4,6144]{1,0:T(4,128)(2,1)} %refs_0_.1), channel_id=1, source_target_pairs={{0,16},{4,20},{8,24},{12,28},{16,0},{20,4},{24,8},{28,12},{1,17},{... | collective-permute-start | bytes 147464 | tf_op jit(solution)/shard_map/ppermute | solution.py:24
  6.3 6.1 %collective-permute-start.2 = (bf16[4,6144]{1,0:T(4,128)(2,1)}, bf16[4,6144]{1,0:T(4,128)(2,1)S(1)}, u32[]{:S(2)}, u32[]{:S(2)}) collective-permute-start(bf16[4,6144]{1,0:T(4,128)(2,1)} %refs_0_.1), channel_id=1, source_target_pairs={{0,24},{4,28},{8,16},{12,20},{16,8},{20,12},{24,0},{28,4},{1,25},{... | collective-permute-start | bytes 147464 | tf_op jit(solution)/shard_map/ppermute | solution.py:24
  6.3 8.7 %collective-permute-start.3 = (bf16[4,6144]{1,0:T(4,128)(2,1)}, bf16[4,6144]{1,0:T(4,128)(2,1)S(1)}, u32[]{:S(2)}, u32[]{:S(2)}) collective-permute-start(bf16[4,6144]{1,0:T(4,128)(2,1)} %refs_0_.1), channel_id=1, source_target_pairs={{0,4},{4,0},{8,12},{12,8},{16,20},{20,16},{24,28},{28,24},{1,5},{5... | collective-permute-start | bytes 147464 | tf_op jit(solution)/shard_map/ppermute | solution.py:24
  9.9 5.1 %collective-permute-start.4 = (bf16[4,6144]{1,0:T(4,128)(2,1)S(1)}, bf16[4,6144]{1,0:T(4,128)(2,1)S(1)}, u32[]{:S(2)}, u32[]{:S(2)}) collective-permute-start(bf16[4,6144]{1,0:T(4,128)(2,1)S(1)} %collective-permute-done.refs_1_), channel_id=1, source_target_pairs={{0,4},{4,0},{8,12},{12,8},{16,20},{20,16},{24,28},{28,24},{1,5},{5... | collective-permute-start | bytes 147464 | tf_op jit(solution)/shard_map/ppermute | solution.py:24
  10.3 4.8 %collective-permute-start.5 = (bf16[4,6144]{1,0:T(4,128)(2,1)S(1)}, bf16[4,6144]{1,0:T(4,128)(2,1)S(1)}, u32[]{:S(2)}, u32[]{:S(2)}) collective-permute-start(bf16[4,6144]{1,0:T(4,128)(2,1)S(1)} %collective-permute-done.1.refs_2_), channel_id=1, source_target_pairs={{0,4},{4,0},{8,12},{12,8},{16,20},{20,16},{24,28},{28,24},{1,5},{5... | collective-permute-start | bytes 147464 | tf_op jit(solution)/shard_map/ppermute | solution.py:24
  12.4 4.1 %collective-permute-start.6 = (bf16[4,6144]{1,0:T(4,128)(2,1)S(1)}, bf16[4,6144]{1,0:T(4,128)(2,1)S(1)}, u32[]{:S(2)}, u32[]{:S(2)}) collective-permute-start(bf16[4,6144]{1,0:T(4,128)(2,1)S(1)} %collective-permute-done.2.refs_3_), channel_id=1, source_target_pairs={{0,4},{4,0},{8,12},{12,8},{16,20},{20,16},{24,28},{28,24},{1,5},{5... | collective-permute-start | bytes 147464 | tf_op jit(solution)/shard_map/ppermute | solution.py:24
  17.6 5.7 %collective-permute-start.7 = (bf16[16,6144]{1,0:T(8,128)(2,1)S(1)}, bf16[16,6144]{1,0:T(8,128)(2,1)S(1)}, u32[]{:S(2)}, u32[]{:S(2)}) collective-permute-start(bf16[16,6144]{1,0:T(8,128)(2,1)S(1)} %get-tuple-element.67.refs_1_), channel_id=1, source_target_pairs={{0,2},{2,0},{1,3},{3,1},{4,6},{6,4},{5,7},{7,5},{8,10},{10,8},{9,1... | collective-permute-start | bytes 589832 | tf_op jit(solution)/shard_map/ppermute | solution.py:583
  19.1 4.2 %collective-permute-start.8 = (bf16[16,6144]{1,0:T(8,128)(2,1)S(1)}, bf16[16,6144]{1,0:T(8,128)(2,1)S(1)}, u32[]{:S(2)}, u32[]{:S(2)}) collective-permute-start(bf16[16,6144]{1,0:T(8,128)(2,1)S(1)} %get-tuple-element.66.refs_0_), channel_id=1, source_target_pairs={{0,1},{1,0},{2,3},{3,2},{4,5},{5,4},{6,7},{7,6},{8,9},{9,8},{10,11... | collective-permute-start | bytes 589832 | tf_op jit(solution)/shard_map/ppermute | solution.py:19
  19.2 11.1 %all-to-all-start = ((bf16[32,8,128]{2,1,0:T(8,128)(2,1)}), bf16[32,8,128]{2,1,0:T(8,128)(2,1)S(1)}, u32[]{:S(2)}, u32[]{:S(2)}) async-start(bf16[32,8,128]{2,1,0:T(8,128)(2,1)} %low_pieces.1), calls=%async_computation | async-start | bytes 131072 | tf_op jit(solution)/shard_map/all_to_all | solution.py:50
  23.3 1.4 %collective-permute-start.9 = (bf16[16,6144]{1,0:T(8,128)(2,1)S(1)}, bf16[16,6144]{1,0:T(8,128)(2,1)S(1)}, u32[]{:S(2)}, u32[]{:S(2)}) collective-permute-start(bf16[16,6144]{1,0:T(8,128)(2,1)S(1)} %collective-permute-done.7.refs_1_), channel_id=1, source_target_pairs={{0,1},{1,0},{2,3},{3,2},{4,5},{5,4},{6,7},{7,6},{8,9},{9,8},{10,11... | collective-permute-start | bytes 589832 | tf_op jit(solution)/shard_map/ppermute | solution.py:19
  23.4 7.0 %copy-start = (bf16[64,512]{1,0:T(8,128)(2,1)S(1)}, bf16[64,512]{1,0:T(8,128)(2,1)}, u32[]{:S(2)}) copy-start(bf16[64,512]{1,0:T(8,128)(2,1)} %refs_12_.1) | copy-start | bytes 196612
  33.7 1.8 %collective-permute-start.10 = (bf16[8,32,768]{2,1,0:T(8,128)(2,1)S(1)}, bf16[8,32,768]{2,1,0:T(8,128)(2,1)S(1)}, u32[]{:S(2)}, u32[]{:S(2)}) collective-permute-start(bf16[8,32,768]{2,1,0:T(8,128)(2,1)S(1)} %get-tuple-element.75), channel_id=1, source_target_pairs={{0,1},{1,0},{2,3},{3,2},{4,5},{5,4},{6,7},{7,6},{8,9},{9,8},{10,11... | collective-permute-start | bytes 1179656 | tf_op jit(solution)/shard_map/ppermute | solution.py:19
  34.0 4.0 %collective-permute-start.12 = (bf16[64,196]{1,0:T(8,128)(2,1)S(1)}, bf16[64,196]{1,0:T(8,128)(2,1)S(1)}, u32[]{:S(2)}, u32[]{:S(2)}) collective-permute-start(bf16[64,196]{1,0:T(8,128)(2,1)S(1)} %get-tuple-element.102), channel_id=1, source_target_pairs={{0,2},{2,0},{1,3},{3,1},{4,6},{6,4},{5,7},{7,5},{8,10},{10,8},{9,1... | collective-permute-start | bytes 75272 | tf_op jit(solution)/shard_map/ppermute | solution.py:601
  35.6 4.9 %collective-permute-start.11 = (bf16[2,32,768]{2,1,0:T(8,128)(2,1)S(1)}, bf16[2,32,768]{2,1,0:T(8,128)(2,1)S(1)}, u32[]{:S(2)}, u32[]{:S(2)}) collective-permute-start(bf16[2,32,768]{2,1,0:T(8,128)(2,1)S(1)} %get-tuple-element.76), channel_id=1, source_target_pairs={{0,4},{4,0},{8,12},{12,8},{16,20},{20,16},{24,28},{28,24},{1,5},{5... | collective-permute-start | bytes 294920 | tf_op jit(solution)/shard_map/ppermute | solution.py:24
  40.5 5.0 %collective-permute-start.13 = (bf16[2,32,768]{2,1,0:T(8,128)(2,1)S(1)}, bf16[2,32,768]{2,1,0:T(8,128)(2,1)S(1)}, u32[]{:S(2)}, u32[]{:S(2)}) collective-permute-start(bf16[2,32,768]{2,1,0:T(8,128)(2,1)S(1)} %get-tuple-element.80), channel_id=1, source_target_pairs={{0,4},{4,0},{8,12},{12,8},{16,20},{20,16},{24,28},{28,24},{1,5},{5... | collective-permute-start | bytes 294920 | tf_op jit(solution)/shard_map/ppermute | solution.py:24
  41.7 6.6 %collective-permute-start.15 = (bf16[32,768]{1,0:T(8,128)(2,1)S(1)}, bf16[32,768]{1,0:T(8,128)(2,1)S(1)}, u32[]{:S(2)}, u32[]{:S(2)}) collective-permute-start(bf16[32,768]{1,0:T(8,128)(2,1)S(1)} %get-tuple-element.84), channel_id=1, source_target_pairs={{0,16},{4,20},{8,24},{12,28},{16,0},{20,4},{24,8},{28,12},{1,17},{... | collective-permute-start | bytes 147464 | tf_op jit(solution)/shard_map/ppermute | solution.py:24
  44.0 6.0 %collective-permute-start.16 = (bf16[32,768]{1,0:T(8,128)(2,1)S(1)}, bf16[32,768]{1,0:T(8,128)(2,1)S(1)}, u32[]{:S(2)}, u32[]{:S(2)}) collective-permute-start(bf16[32,768]{1,0:T(8,128)(2,1)S(1)} %get-tuple-element.85), channel_id=1, source_target_pairs={{0,24},{4,28},{8,16},{12,20},{16,8},{20,12},{24,0},{28,4},{1,25},{... | collective-permute-start | bytes 147464 | tf_op jit(solution)/shard_map/ppermute | solution.py:24
  45.5 4.7 %collective-permute-start.14 = (bf16[32,768]{1,0:T(8,128)(2,1)S(1)}, bf16[32,768]{1,0:T(8,128)(2,1)S(1)}, u32[]{:S(2)}, u32[]{:S(2)}) collective-permute-start(bf16[32,768]{1,0:T(8,128)(2,1)S(1)} %get-tuple-element.82), channel_id=1, source_target_pairs={{0,8},{4,12},{8,0},{12,4},{16,24},{20,28},{24,16},{28,20},{1,9},{5... | collective-permute-start | bytes 147464 | tf_op jit(solution)/shard_map/ppermute | solution.py:24
  50.3 4.4 %collective-permute-start.17 = (bf16[32,768]{1,0:T(8,128)(2,1)S(1)}, bf16[32,768]{1,0:T(8,128)(2,1)S(1)}, u32[]{:S(2)}, u32[]{:S(2)}) collective-permute-start(bf16[32,768]{1,0:T(8,128)(2,1)S(1)} %mix.1.refs_4_.refs_0_), channel_id=1, source_target_pairs={{0,8},{4,12},{8,0},{12,4},{16,24},{20,28},{24,16},{28,20},{1,9},{5... | collective-permute-start | bytes 147464 | tf_op jit(solution)/shard_map/ppermute | solution.py:24
  50.4 5.2 %collective-permute-start.18 = (bf16[32,768]{1,0:T(8,128)(2,1)S(1)}, bf16[32,768]{1,0:T(8,128)(2,1)S(1)}, u32[]{:S(2)}, u32[]{:S(2)}) collective-permute-start(bf16[32,768]{1,0:T(8,128)(2,1)S(1)} %mix.1.refs_4_.refs_0_), channel_id=1, source_target_pairs={{0,16},{4,20},{8,24},{12,28},{16,0},{20,4},{24,8},{28,12},{1,17},{... | collective-permute-start | bytes 147464 | tf_op jit(solution)/shard_map/ppermute | solution.py:24
  52.9 5.9 %collective-permute-start.19 = (bf16[32,768]{1,0:T(8,128)(2,1)S(1)}, bf16[32,768]{1,0:T(8,128)(2,1)S(1)}, u32[]{:S(2)}, u32[]{:S(2)}) collective-permute-start(bf16[32,768]{1,0:T(8,128)(2,1)S(1)} %mix.1.refs_4_.refs_0_), channel_id=1, source_target_pairs={{0,24},{4,28},{8,16},{12,20},{16,8},{20,12},{24,0},{28,4},{1,25},{... | collective-permute-start | bytes 147464 | tf_op jit(solution)/shard_map/ppermute | solution.py:24
  58.8 5.7 %collective-permute-start.21 = (bf16[3,32,768]{2,1,0:T(8,128)(2,1)S(1)}, bf16[3,32,768]{2,1,0:T(8,128)(2,1)S(1)}, u32[]{:S(2)}, u32[]{:S(2)}) collective-permute-start(bf16[3,32,768]{2,1,0:T(8,128)(2,1)S(1)} %stack.13.refs_5_.refs_1_), channel_id=1, source_target_pairs={{0,4},{4,0},{8,12},{12,8},{16,20},{20,16},{24,28},{28,24},{1,5},{5... | collective-permute-start | bytes 442376 | tf_op jit(solution)/shard_map/ppermute | solution.py:24
  60.3 4.2 %collective-permute-start.20 = (bf16[32,768]{1,0:T(8,128)(2,1)S(1)}, bf16[32,768]{1,0:T(8,128)(2,1)S(1)}, u32[]{:S(2)}, u32[]{:S(2)}) collective-permute-start(bf16[32,768]{1,0:T(8,128)(2,1)S(1)} %mix.1.refs_4_.refs_0_), channel_id=1, source_target_pairs={{0,4},{4,0},{8,12},{12,8},{16,20},{20,16},{24,28},{28,24},{1,5},{5... | collective-permute-start | bytes 147464 | tf_op jit(solution)/shard_map/ppermute | solution.py:24
  60.9 4.2 %collective-permute-start.24 = (bf16[32,768]{1,0:T(8,128)(2,1)S(1)}, bf16[32,768]{1,0:T(8,128)(2,1)S(1)}, u32[]{:S(2)}, u32[]{:S(2)}) collective-permute-start(bf16[32,768]{1,0:T(8,128)(2,1)S(1)} %mix.1.refs_4_.refs_0_), channel_id=1, source_target_pairs={{0,1},{1,0},{2,3},{3,2},{4,5},{5,4},{6,7},{7,6},{8,9},{9,8},{10,11... | collective-permute-start | bytes 147464 | tf_op jit(solution)/shard_map/ppermute | solution.py:19
  60.9 4.2 %collective-permute-start.25 = (bf16[3,32,768]{2,1,0:T(8,128)(2,1)S(1)}, bf16[3,32,768]{2,1,0:T(8,128)(2,1)S(1)}, u32[]{:S(2)}, u32[]{:S(2)}) collective-permute-start(bf16[3,32,768]{2,1,0:T(8,128)(2,1)S(1)} %stack.13.refs_5_.refs_1_), channel_id=1, source_target_pairs={{0,1},{1,0},{2,3},{3,2},{4,5},{5,4},{6,7},{7,6},{8,9},{9,8},{10,11... | collective-permute-start | bytes 442376 | tf_op jit(solution)/shard_map/ppermute | solution.py:19
  64.5 1.6 %collective-permute-start.22 = (bf16[32,768]{1,0:T(8,128)(2,1)S(1)}, bf16[32,768]{1,0:T(8,128)(2,1)S(1)}, u32[]{:S(2)}, u32[]{:S(2)}) collective-permute-start(bf16[32,768]{1,0:T(8,128)(2,1)S(1)} %collective-permute-done.20.refs_4_.refs_2_), channel_id=1, source_target_pairs={{0,1},{1,0},{2,3},{3,2},{4,5},{5,4},{6,7},{7,6},{8,9},{9,8},{10,11... | collective-permute-start | bytes 147464 | tf_op jit(solution)/shard_map/ppermute | solution.py:19
  64.5 1.6 %collective-permute-start.23 = (bf16[3,32,768]{2,1,0:T(8,128)(2,1)S(1)}, bf16[3,32,768]{2,1,0:T(8,128)(2,1)S(1)}, u32[]{:S(2)}, u32[]{:S(2)}) collective-permute-start(bf16[3,32,768]{2,1,0:T(8,128)(2,1)S(1)} %collective-permute-done.21.refs_5_.refs_3_), channel_id=1, source_target_pairs={{0,1},{1,0},{2,3},{3,2},{4,5},{5,4},{6,7},{7,6},{8,9},{9,8},{10,11... | collective-permute-start | bytes 442376 | tf_op jit(solution)/shard_map/ppermute | solution.py:19
  68.2 13.8 %all-to-all-start.1 = ((bf16[32,32,128]{2,1,0:T(8,128)(2,1)}), bf16[32,32,128]{2,1,0:T(8,128)(2,1)S(1)}, u32[]{:S(2)}, u32[]{:S(2)}) async-start(bf16[32,32,128]{2,1,0:T(8,128)(2,1)} %get-tuple-element.93), calls=%async_computation.1 | async-start | bytes 524288 | tf_op jit(solution)/shard_map/all_to_all | solution.py:50
  72.5 5.0 %collective-permute-start.26 = (bf16[4,6144]{1,0:T(4,128)(2,1)S(1)}, bf16[4,6144]{1,0:T(4,128)(2,1)S(1)}, u32[]{:S(2)}, u32[]{:S(2)}) collective-permute-start(bf16[4,6144]{1,0:T(4,128)(2,1)S(1)} %convolution_convert_fusion), channel_id=1, source_target_pairs={{0,2},{2,0},{1,3},{3,1},{4,6},{6,4},{5,7},{7,5},{8,10},{10,8},{9,1... | collective-permute-start | bytes 147464 | tf_op jit(solution)/shard_map/ppermute | solution.py:652
